TPU v7x, 512 devices: a whole 4x8x8 slice. The times are simulated.
512 devices in a mesh: dp: 8 (over x, z_lo), section: 4 (over z_hi), tensor: 16 (over y, core).
Axes of the slice: x: 4, y: 8, z: 8 (z_hi: 4, z_lo: 2; z = z_hi * 2 + z_lo), core: 2. Of those that a mesh axis runs over, the one named last changes fastest.
Arguments:
- passed_activations: bfloat16 [4, 2048, 3072], P('section', 'dp', 'tensor'), may hold values from -6 to 6
- kept_section_input: bfloat16 [4, 2048, 3072], P('section', 'dp', 'tensor'), may hold values from -47 to 47
- handed_grads: bfloat16 [4, 2048, 3072], P('section', 'dp', 'tensor'), may hold values from -6 to 6
- norm_gain: float32 [4, 3072], P('section'), may hold values from 0.1 to 6
- gate_weight: bfloat16 [4, 3072, 5376], P('section', 'dp', 'tensor'), may hold values from -0.109375 to 0.109375
- up_weight: bfloat16 [4, 3072, 5376], P('section', 'dp', 'tensor'), may hold values from -0.109375 to 0.109375
- down_weight: bfloat16 [4, 5376, 3072], P('section', 'tensor', 'dp'), may hold values from -0.078125 to 0.078125
- routes: int32 [4, 2, 2048, 4], P('section', None, 'dp'), may hold values from 0 to 15, all different within a row
- route_probs: float32 [4, 2, 2048, 4], P('section', None, 'dp'), may hold values from 0.1 to 1
Outputs:
- section_output: bfloat16 [4, 2048, 3072], P('section', 'dp', 'tensor')
- stored_input_gradient: bfloat16 [4, 2048, 3072], P('section', 'dp', 'tensor')
- gate_grad: bfloat16 [4, 3072, 5376], P('section', None, 'tensor')
- up_grad: bfloat16 [4, 3072, 5376], P('section', None, 'tensor')
Inputs may be any that keep to these rules, and one draw needn't show every extreme that they name: `routes`: each row names 4 different experts, and every expert is named somewhere.
All inputs are finite; a program needn't handle non-finite values.
Results may differ from a plain program's by a relative error of at most 0.018.
Values may be sent and summed in bfloat16 or wider, within the bound.
No kernel may reach another device: no remote copies, remote signals or barrier semaphores. Data moves between devices by JAX's collectives and lax.ppermute only.
A program may use at most 128 MiB of HBM per device.

v0:
```python
import jax
import jax.numpy as jnp
from jax import lax
from jax.sharding import PartitionSpec as P

EPS = 1e-05


def from_behind(value, axis, steps):
    count = lax.axis_size(axis)
    pairs = [(source, (source + steps) % count) for source in range(count)]
    return lax.ppermute(value, axis, pairs)


def normalized_input(inputs, norm_scale_weight):
    float_input = inputs.astype(jnp.float32)
    inverse_norm_scale = lax.rsqrt(
        jnp.mean(float_input * float_input, axis=-1, keepdims=True) + EPS
    )
    normalized_values = float_input * inverse_norm_scale
    return (
        inverse_norm_scale,
        (normalized_values * norm_scale_weight[None, :]).astype(jnp.bfloat16),
    )


def combine(route_ids, probs):
    return jnp.sum(jnp.where(route_ids == 0, probs, jnp.zeros_like(probs)), axis=-1)


def backward_rows(normal_rows, dy_rows, weight_rows, w_gate, w_up, w_down):
    gate_b = jnp.dot(normal_rows, w_gate, preferred_element_type=jnp.float32)
    up_b = jnp.dot(normal_rows, w_up, preferred_element_type=jnp.float32)
    hidden_grad = jnp.dot(dy_rows, w_down.T, preferred_element_type=jnp.float32)
    sigmoid_g = jax.nn.sigmoid(gate_b)
    active = gate_b * sigmoid_g
    slope = sigmoid_g * (1.0 + gate_b * (1.0 - sigmoid_g))
    dgate = (hidden_grad * weight_rows[:, None] * up_b * slope).astype(jnp.bfloat16)
    dup = (hidden_grad * weight_rows[:, None] * active).astype(jnp.bfloat16)
    grad_g = jnp.dot(normal_rows.T, dgate, preferred_element_type=jnp.float32)
    grad_u = jnp.dot(normal_rows.T, dup, preferred_element_type=jnp.float32)
    into_sum = jnp.dot(dgate, w_gate.T, preferred_element_type=jnp.float32)
    into_sum = into_sum + jnp.dot(dup, w_up.T, preferred_element_type=jnp.float32)
    return (grad_g, grad_u, into_sum)


def local(
    passed_activations,
    kept_section_input,
    handed_grads,
    norm_gain,
    gate_weight,
    up_weight,
    down_weight,
    routes,
    route_probs,
):
    acts_here = from_behind(passed_activations[0], "section", 1)
    section_gradients = from_behind(handed_grads[0], "section", -1)
    section_saved_input = kept_section_input[0]
    acts_full, saved_full, grads_full = (
        lax.all_gather(acts_here, "tensor", axis=1, tiled=True),
        lax.all_gather(section_saved_input, "tensor", axis=1, tiled=True),
        lax.all_gather(section_gradients, "tensor", axis=1, tiled=True),
    )
    norm_scale_weight = norm_gain[0]
    slice_width = acts_here.shape[1]
    entire_width = acts_full.shape[1]
    gain_here = lax.dynamic_slice_in_dim(
        norm_scale_weight, lax.axis_index("tensor") * slice_width, slice_width
    )
    weight_f = combine(routes[0, 0], route_probs[0, 0])
    weight_b = combine(routes[0, 1], route_probs[0, 1])
    inverse_norm_scale, normalized_rows = normalized_input(acts_full, norm_scale_weight)
    w_gate, w_up, w_down = (
        lax.all_gather(gate_weight[0], "dp", axis=0, tiled=True),
        lax.all_gather(up_weight[0], "dp", axis=0, tiled=True),
        lax.all_gather(down_weight[0], "dp", axis=1, tiled=True),
    )
    gate_pre = jnp.dot(normalized_rows, w_gate, preferred_element_type=jnp.float32)
    up_pre = jnp.dot(normalized_rows, w_up, preferred_element_type=jnp.float32)
    hidden = (jax.nn.silu(gate_pre) * up_pre * weight_f[:, None]).astype(jnp.bfloat16)
    partial_out = jnp.dot(hidden, w_down, preferred_element_type=jnp.float32)
    summed = lax.psum_scatter(
        partial_out.astype(jnp.bfloat16), "tensor", scatter_dimension=1, tiled=True
    ).astype(jnp.float32)
    section_output = (acts_here.astype(jnp.float32) + summed).astype(jnp.bfloat16)
    inverse_norm_backward, normalized_rows_backward = normalized_input(
        saved_full, norm_scale_weight
    )
    grad_g, grad_u, into_sum = backward_rows(
        normalized_rows_backward, grads_full, weight_b, w_gate, w_up, w_down
    )
    dnormal = lax.psum_scatter(
        into_sum.astype(jnp.bfloat16), "tensor", scatter_dimension=1, tiled=True
    ).astype(jnp.float32)
    section_normalized_values = section_saved_input.astype(jnp.float32) * inverse_norm_backward
    normalized_input_gradient = dnormal * gain_here[None, :]
    mean_square_stat = (
        lax.psum(
            jnp.sum(normalized_input_gradient * section_normalized_values, axis=-1, keepdims=True),
            "tensor",
        )
        / entire_width
    )
    stored_input_gradient = (
        section_gradients.astype(jnp.float32)
        + inverse_norm_backward
        * (normalized_input_gradient - section_normalized_values * mean_square_stat)
    ).astype(jnp.bfloat16)
    grad_g, grad_u = (
        lax.psum(grad_g.astype(jnp.bfloat16), "dp").astype(jnp.float32),
        lax.psum(grad_u.astype(jnp.bfloat16), "dp").astype(jnp.float32),
    )
    return (
        section_output[None],
        stored_input_gradient[None],
        grad_g.astype(jnp.bfloat16)[None],
        grad_u.astype(jnp.bfloat16)[None],
    )


def solution(mesh):
    placed = (
        P("section", "dp", "tensor"),
        P("section", "dp", "tensor"),
        P("section", "dp", "tensor"),
        P("section", None),
        P("section", "dp", "tensor"),
        P("section", "dp", "tensor"),
        P("section", "tensor", "dp"),
        P("section", None, "dp", None),
        P("section", None, "dp", None),
    )
    return jax.shard_map(
        local,
        mesh=mesh,
        in_specs=placed,
        out_specs=(
            P("section", "dp", "tensor"),
            P("section", "dp", "tensor"),
            P("section", None, "tensor"),
            P("section", None, "tensor"),
        ),
        check_vma=False,
    )
```

profile of v0, /device:TPU:6, one launch (start us, length us, event | category | flops | bytes accessed | tf_op | source)
XLA Modules:
  0.0 646.6 jit_solution(3368659325298959108)
XLA Ops:
  7.2 0.0 all-gather.21.cloned.1.call-start
  7.2 0.7 all-gather.21.cloned.1.call-update
  7.9 0.0 all-gather.15.cloned.1.call-start
  8.0 0.7 all-gather.15.cloned.1.call-update
  8.7 0.0 all-gather.13.cloned.1.call-start
  8.7 10.9 %collective-permute-start.1 = (bf16[256,192]{0,1:T(8,128)(2,1)}, bf16[256,192]{0,1:T(8,128)(2,1)S(1)}, u32[]{:S(2)}, u32[]{:S(2)}) collective-permute-start(bf16[256,192]{0,1:T(8,128)(2,1)} %bitcast.74), channel_id=1, source_target_pairs={{0,48},{16,0},{32,16},{48,32},{1,49},{17,1},{33,17},{49,33},{2,50}... | collective-permute-start | bytes 294920 | tf_op jit(solution)/shard_map/ppermute | solution.py:12
  19.6 4.5 collective-permute-done.1
  24.1 0.6 copy-done.6
  24.8 0.0 all-gather.19.cloned.1.call-start
  24.8 0.5 all-gather.19.cloned.1.call-update
  25.4 0.0 all-gather.17.cloned.1.call-start
  25.4 0.5 all-gather.17.cloned.1.call-update
  26.0 0.0 all-gather.11.cloned.1.call-start
  26.0 3.1 collective-permute-start
  29.1 7.4 %collective-permute-done = bf16[256,192]{0,1:T(8,128)(2,1)S(1)} collective-permute-done((bf16[256,192]{0,1:T(8,128)(2,1)}, bf16[256,192]{0,1:T(8,128)(2,1)S(1)}, u32[]{:S(2)}, u32[]{:S(2)}) %collective-permute-start) | collective-permute-done | bytes 98336 | tf_op jit(solution)/shard_map/ppermute | solution.py:12
  36.5 0.6 copy-done.8
  37.1 0.0 reduce-scatter.5.cloned.1.call-start
  37.2 0.8 select_reduce_fusion
  37.9 18.2 %all-gather.21.cloned.1.call-done = bf16[1,256,3072]{1,2,0:T(8,128)(2,1)} async-done(((bf16[1,256,192]{1,2,0:T(8,128)(2,1)}), bf16[1,256,3072]{1,2,0:T(8,128)(2,1)}) %all-gather.21.cloned.1.call-update) | async-done | bytes 1572880 | tf_op jit(solution)/shard_map/all_gather | solution.py:63
  56.1 1.8 fusion.6
  58.0 54.8 %all-gather.15.cloned.1.call-done = bf16[1,3072,336]{1,2,0:T(8,128)(2,1)} async-done(((bf16[1,384,336]{1,2,0:T(8,128)(2,1)}), bf16[1,3072,336]{1,2,0:T(8,128)(2,1)}) %all-gather.15.cloned.1.call-update) | async-done | bytes 2064400 | tf_op jit(solution)/shard_map/all_gather | solution.py:76
  112.8 2.9 fusion.21
  115.7 41.5 %all-gather.13.cloned.1.call-done = bf16[256,3072]{0,1:T(8,128)(2,1)} async-done(((bf16[256,192]{0,1:T(8,128)(2,1)}), bf16[256,3072]{0,1:T(8,128)(2,1)}) %all-gather.13.cloned.1.call-update) | async-done | bytes 1572880 | tf_op jit(solution)/shard_map/all_gather | solution.py:64
  157.2 56.4 %all-gather.19.cloned.1.call-done = bf16[1,336,3072]{2,1,0:T(8,128)(2,1)} async-done(((bf16[1,336,384]{2,1,0:T(8,128)(2,1)}), bf16[1,336,3072]{2,1,0:T(8,128)(2,1)}) %all-gather.19.cloned.1.call-update) | async-done | bytes 2064400 | tf_op jit(solution)/shard_map/all_gather | solution.py:78
  213.6 2.8 multiply_convert_fusion
  216.5 55.3 %all-gather.17.cloned.1.call-done = bf16[1,3072,336]{1,2,0:T(8,128)(2,1)} async-done(((bf16[1,384,336]{1,2,0:T(8,128)(2,1)}), bf16[1,3072,336]{1,2,0:T(8,128)(2,1)}) %all-gather.17.cloned.1.call-update) | async-done | bytes 2064400 | tf_op jit(solution)/shard_map/all_gather | solution.py:77
  271.7 2.6 fusion.32
  274.3 1.2 fusion.17
  275.5 0.4 copy-done.2
  275.9 2.4 fusion
  278.3 0.0 reduce-scatter.3.cloned.1.call-start
  278.4 38.2 %all-gather.11.cloned.1.call-done = bf16[256,3072]{0,1:T(8,128)(2,1)} async-done(((bf16[256,192]{0,1:T(8,128)(2,1)}), bf16[256,3072]{0,1:T(8,128)(2,1)}) %all-gather.11.cloned.1.call-update) | async-done | bytes 1572880 | tf_op jit(solution)/shard_map/all_gather | solution.py:62
  316.5 1.8 fusion.3
  318.4 3.7 fusion.13
  322.1 6.3 convolution_convert_fusion.2
  328.5 0.0 all-reduce.3.cloned.1.call-start
  328.5 2.1 fusion.1
  330.6 2.1 fusion.2
  332.8 0.1 constant_dynamic-slice_fusion
  332.9 46.1 %reduce-scatter.5.cloned.1.call-done = bf16[256,192]{0,1:T(8,128)(2,1)} async-done(((bf16[256,3072]{0,1:T(8,128)(2,1)}), bf16[256,192]{0,1:T(8,128)(2,1)}) %reduce-scatter.5.cloned.1.call-update) | async-done | bytes 98320 | tf_op jit(solution)/shard_map/reduce_scatter | solution.py:94
  379.0 1.0 fusion.39
  380.0 23.8 %psum.21 = f32[256,1]{0,1:T(1,128)S(1)} all-reduce(f32[256,1]{0,1:T(1,128)S(1)} %bitcast.73), channel_id=1, replica_groups=mesh['dp'=8,'section'=4,'tensor'=16] {'tensor'}, use_global_device_ids=true, to_apply=%region_7.8 | all-reduce | flops 256 | bytes 2048 | tf_op jit(solution)/shard_map/psum | solution.py:100
  403.8 38.0 %reduce-scatter.3.cloned.1.call-done = bf16[256,192]{0,1:T(8,128)(2,1)} async-done(((bf16[256,3072]{0,1:T(8,128)(2,1)}), bf16[256,192]{0,1:T(8,128)(2,1)}) %reduce-scatter.3.cloned.1.call-update) | async-done | bytes 98320 | tf_op jit(solution)/shard_map/reduce_scatter | solution.py:84
  441.8 1.6 fusion.54
  443.4 1.6 fusion.55
  445.0 190.6 %all-reduce.3.cloned.1.call-done = (bf16[1,3072,336]{1,2,0:T(8,128)(2,1)}, bf16[1,3072,336]{1,2,0:T(8,128)(2,1)}) async-done(((bf16[1,3072,336]{1,2,0:T(8,128)(2,1)}, bf16[1,3072,336]{1,2,0:T(8,128)(2,1)}), (bf16[1,3072,336]{1,2,0:T(8,128)(2,1)}, bf16[1,3072,336]{1,2,0:T(8,128)(2,1)})) %all-reduce.3.cloned.1.call-update) | async-done | bytes 4128784 | tf_op jit(solution)/shard_map/psum | solution.py:112
  635.6 3.2 copy.15
  638.8 1.3 copy.16
  (27 shorter events, 0.1 us)
Async XLA Ops:
  7.2 105.6 %copy-start.10 = (f32[1,3072]{1,0:T(1,128)S(1)}, f32[1,3072]{1,0:T(1,128)}, u32[]{:S(2)}) copy-start(f32[1,3072]{1,0:T(1,128)} %param.12) | copy-start | bytes 36868
  7.2 48.9 %all-gather.21.cloned.1.call-start = ((), (), s32[]{:S(2)}) async-start(), calls=%async_computation.9 | async-start | bytes 1671168 | tf_op jit(solution)/shard_map/all_gather | solution.py:63
  7.9 104.9 %all-gather.15.cloned.1.call-start = ((), (), s32[]{:S(2)}) async-start(), calls=%async_computation.6 | async-start | bytes 2322432 | tf_op jit(solution)/shard_map/all_gather | solution.py:76
  8.7 148.5 %all-gather.13.cloned.1.call-start = ((), (), s32[]{:S(2)}) async-start(), calls=%async_computation.4 | async-start | bytes 1671168 | tf_op jit(solution)/shard_map/all_gather | solution.py:64
  8.7 15.4 %collective-permute-start.1 = (bf16[256,192]{0,1:T(8,128)(2,1)}, bf16[256,192]{0,1:T(8,128)(2,1)S(1)}, u32[]{:S(2)}, u32[]{:S(2)}) collective-permute-start(bf16[256,192]{0,1:T(8,128)(2,1)} %bitcast.74), channel_id=1, source_target_pairs={{0,48},{16,0},{32,16},{48,32},{1,49},{17,1},{33,17},{49,33},{2,50}... | collective-permute-start | bytes 294920 | tf_op jit(solution)/shard_map/ppermute | solution.py:12
  24.1 0.6 copy-start.6
  24.8 188.8 %all-gather.19.cloned.1.call-start = ((), (), s32[]{:S(2)}) async-start(), calls=%async_computation.8 | async-start | bytes 2322432 | tf_op jit(solution)/shard_map/all_gather | solution.py:78
  25.4 246.3 %all-gather.17.cloned.1.call-start = ((), (), s32[]{:S(2)}) async-start(), calls=%async_computation.7 | async-start | bytes 2322432 | tf_op jit(solution)/shard_map/all_gather | solution.py:77
  26.0 290.6 %all-gather.11.cloned.1.call-start = ((), (), s32[]{:S(2)}) async-start(), calls=%async_computation.2 | async-start | bytes 1671168 | tf_op jit(solution)/shard_map/all_gather | solution.py:62
  26.0 10.5 %collective-permute-start = (bf16[256,192]{0,1:T(8,128)(2,1)}, bf16[256,192]{0,1:T(8,128)(2,1)S(1)}, u32[]{:S(2)}, u32[]{:S(2)}) collective-permute-start(bf16[256,192]{0,1:T(8,128)(2,1)} %bitcast.75), channel_id=1, source_target_pairs={{0,16},{16,32},{32,48},{48,0},{1,17},{17,33},{33,49},{49,1},{2,18}... | collective-permute-start | bytes 294920 | tf_op jit(solution)/shard_map/ppermute | solution.py:12
  36.5 0.6 copy-start.8
  37.1 341.9 %reduce-scatter.5.cloned.1.call-start = ((), (), s32[]{:S(2)}) async-start(), calls=%async_computation.5 | async-start | bytes 1671168 | tf_op jit(solution)/shard_map/reduce_scatter | solution.py:94
  213.6 58.1 %copy-start = (bf16[1,256,3072]{1,2,0:T(8,128)(2,1)S(1)}, bf16[1,256,3072]{1,2,0:T(8,128)(2,1)}, u32[]{:S(2)}) copy-start(bf16[1,256,3072]{1,2,0:T(8,128)(2,1)} %all-gather.21.cloned.1.call-done) | copy-start | bytes 4718596
  271.7 2.6 copy-start.1
  274.3 1.6 copy-start.2
  278.3 163.5 %reduce-scatter.3.cloned.1.call-start = ((), (), s32[]{:S(2)}) async-start(), calls=%async_computation.3 | async-start | bytes 1671168 | tf_op jit(solution)/shard_map/reduce_scatter | solution.py:84
  318.4 3.8 copy-start.4
  328.5 307.1 %all-reduce.3.cloned.1.call-start = ((), (), s32[]{:S(2)}) async-start(), calls=%async_computation.10 | async-start | bytes 8257536 | tf_op jit(solution)/shard_map/psum | solution.py:112
  332.8 46.3 %copy-start.5 = (bf16[1,256,192]{1,2,0:T(8,128)(2,1)S(1)}, bf16[1,256,192]{1,2,0:T(8,128)(2,1)}, u32[]{:S(2)}) copy-start(bf16[1,256,192]{1,2,0:T(8,128)(2,1)} %param.10) | copy-start | bytes 294916
  332.8 109.0 %copy-start.9 = (bf16[256,192]{0,1:T(8,128)(2,1)S(1)}, bf16[256,192]{0,1:T(8,128)(2,1)}, u32[]{:S(2)}) copy-start(bf16[256,192]{0,1:T(8,128)(2,1)} %copy-done.8) | copy-start | bytes 294916
  332.8 110.6 %copy-start.7 = (bf16[256,192]{0,1:T(8,128)(2,1)S(1)}, bf16[256,192]{0,1:T(8,128)(2,1)}, u32[]{:S(2)}) copy-start(bf16[256,192]{0,1:T(8,128)(2,1)} %copy-done.6) | copy-start | bytes 294916
  635.6 3.2 copy-start.3
Sparse Core Ops, SparseCore 0:
  10.1 45.9 all-gather.20
  58.2 54.5 all-gather.14
  114.9 42.2 all-gather.12
  159.1 54.4 all-gather.18
  215.5 56.1 all-gather.16
  274.3 42.2 all-gather.10
  319.4 59.6 reduce-scatter.4
  382.1 59.6 reduce-scatter.2
  445.4 190.1 all-reduce.2
where the time goes:
time: 649 us; the launch traced here: 647 us
  waiting for transfers between devices  553 us (85%)
  matrix products  26.1 us (4%)
  blocking collectives  23.8 us (4%)
  starting transfers between devices  14.4 us (2%)
  between operations  13.9 us (2%)
  other arithmetic  8.68 us (1%)
    psum x1, waiting for transfers between devices, local(): lax.psum(grad_g.astype(jnp.bfloat16), 'dp').astype(jnp.float32)  191 us
    all_gather x1, waiting for transfers between devices, local(): lax.all_gather(down_weight[0], 'dp', axis=1, tiled=True)  56.4 us
    all_gather x1, waiting for transfers between devices, local(): lax.all_gather(up_weight[0], 'dp', axis=0, tiled=True)  55.3 us
    all_gather x1, waiting for transfers between devices, local(): lax.all_gather(gate_weight[0], 'dp', axis=0, tiled=True)  54.8 us
    reduce_scatter x1, waiting for transfers between devices, local(): lax.psum_scatter(into_sum.astype(jnp.bfloat16), 'tensor', scatter_dimensi...  46.1 us
    all_gather x1, waiting for transfers between devices, local(): lax.all_gather(section_gradients, 'tensor', axis=1, tiled=True)  41.5 us
    all_gather x1, waiting for transfers between devices, local(): lax.all_gather(acts_here, 'tensor', axis=1, tiled=True)  38.2 us
    reduce_scatter x1, waiting for transfers between devices, local(): lax.psum_scatter(partial_out.astype(jnp.bfloat16), 'tensor', scatter_dime...  38 us
  transfers between devices with their start and end apart: 11, of which 11 were waited for; matrix products, arithmetic and copies ran while one was open for 5% of the time, Pallas kernels for 0%

commit v1 on v0

v1 whole, which is shorter than its diff:
```python
import jax
import jax.numpy as jnp
import numpy as np
from jax import lax
from jax.experimental import pallas as pl
from jax.experimental.pallas import tpu as pltpu
from jax.sharding import Mesh, PartitionSpec as P

EPS = 1e-05
AXES = ("x", "zl", "s", "y", "c")
SIZES = {"x": 4, "zl": 2, "s": 4, "y": 8, "c": 2}
D = 3072
TOK = 256
G = 336
F = 192
N_T = 16
N_DP = 8
DS = D // N_DP
OFFSETS = ((0, 0), (0, 1), (-1, 0), (1, 0), (-1, 1), (1, 1), (2, 0), (2, 1))
VMEM_LIMIT = 50 * 1024 * 1024

VM = pl.BlockSpec(memory_space=pltpu.VMEM)
SM = pl.BlockSpec(memory_space=pltpu.SMEM)
HB = pl.BlockSpec(memory_space=pl.ANY)


def shift(value, **steps):
    axes = tuple(a for a in AXES if a in steps)
    sizes = [SIZES[a] for a in axes]
    pairs = []
    for i in range(int(np.prod(sizes))):
        at = np.unravel_index(i, sizes)
        to = [(at[k] + steps[a]) % sizes[k] for k, a in enumerate(axes)]
        pairs.append((i, int(np.ravel_multi_index(to, sizes))))
    return lax.ppermute(value, axes if len(axes) > 1 else axes[0], pairs)


def swapped(value, step):
    pairs = []
    for e in range(N_DP):
        for y in range(N_DP):
            d = (((y // 2) + step) % 4) * 2 + y % 2
            pairs.append((e * N_DP + y, d * N_DP + e))
    return lax.ppermute(value, ("x", "zl", "y"), pairs)


def gather_ring(own):
    z = shift(own, zl=1)
    behind = shift(own, x=1)
    ahead = shift(own, x=-1)
    z, behind, ahead = lax.optimization_barrier((z, behind, ahead))
    z_behind = shift(z, x=1)
    z_ahead = shift(z, x=-1)
    across = shift(behind, x=1)
    z_across = shift(z_ahead, x=-1)
    return [own, z, behind, ahead, z_behind, z_ahead, across, z_across]


def places():
    x, zl = lax.axis_index("x"), lax.axis_index("zl")
    return jnp.stack([((x + dx) % 4) * 2 + (zl + dz) % 2 for dx, dz in OFFSETS]).astype(jnp.int32)


def normal_into(act_ref, gain_ref, out_ref):
    total = jnp.zeros((1, TOK), jnp.float32)
    for t in range(N_T):
        v = act_ref[t, 0].astype(jnp.float32)
        total = total + jnp.sum(v * v, axis=0, keepdims=True)
    scale = lax.rsqrt(total / D + EPS)
    for t in range(N_T):
        v = act_ref[t, 0].astype(jnp.float32)
        out_ref[t * F : (t + 1) * F, :] = ((v * scale) * gain_ref[t * F : (t + 1) * F, :]).astype(jnp.bfloat16)
    return scale


def inner_kernel(place, *refs):
    w = refs[:N_DP]
    saved, dy, gain, weight, dg_out, dgs_out, scale_out, stat_out, normal = refs[N_DP:]
    scale = normal_into(saved, gain, normal)
    scale_out[...] = scale
    row = weight[...]
    stat = jnp.zeros((1, TOK), jnp.float32)
    step = 112
    for m in range(0, G, step):
        gate = jnp.zeros((step, TOK), jnp.float32)
        up = jnp.zeros((step, TOK), jnp.float32)
        hid = jnp.zeros((step, TOK), jnp.float32)
        for r in range(N_DP):
            d = place[r]
            n = normal[pl.ds(pl.multiple_of(d * DS, DS), DS), :]
            g = dy[pl.ds(2 * d, 2), 0].reshape(DS, TOK)
            gate = gate + jnp.dot(w[r][m : m + step, :], n, preferred_element_type=jnp.float32)
            up = up + jnp.dot(w[r][G + m : G + m + step, :], n, preferred_element_type=jnp.float32)
            hid = hid + jnp.dot(w[r][2 * G + m : 2 * G + m + step, :], g, preferred_element_type=jnp.float32)
        sg = jax.nn.sigmoid(gate)
        hid = hid * row
        dgate = hid * up * (sg * (1.0 + gate * (1.0 - sg)))
        dup = hid * (gate * sg)
        dgate_r, dup_r = dgate.astype(jnp.bfloat16), dup.astype(jnp.bfloat16)
        dg_out[m : m + step, :] = dgate_r
        dg_out[G + m : G + m + step, :] = dup_r
        dgs_out[m : m + step, :] = (dgate * scale).astype(jnp.bfloat16)
        dgs_out[G + m : G + m + step, :] = (dup * scale).astype(jnp.bfloat16)
        stat = stat + jnp.sum(
            dgate_r.astype(jnp.float32) * gate + dup_r.astype(jnp.float32) * up, axis=0, keepdims=True
        )
    stat_out[...] = stat


def outer_kernel(place, *refs):
    w = refs[:N_DP]
    dg, act, gain, weight, stat, out, normal, hidden, dg_t, hid_t = refs[N_DP:]
    normal_into(act, gain, normal)
    row = weight[...]
    step = 112
    for m in range(0, G, step):
        gate = jnp.zeros((step, TOK), jnp.float32)
        up = jnp.zeros((step, TOK), jnp.float32)
        for r in range(N_DP):
            n = normal[pl.ds(pl.multiple_of(place[r] * DS, DS), DS), :]
            gate = gate + jnp.dot(w[r][m : m + step, :], n, preferred_element_type=jnp.float32)
            up = up + jnp.dot(w[r][G + m : G + m + step, :], n, preferred_element_type=jnp.float32)
        hidden[m : m + step, :] = gate * jax.nn.sigmoid(gate) * up * row
    dg_t[...] = dg[...].astype(jnp.float32).T.astype(jnp.bfloat16)
    hid_t[...] = hidden[...].T.astype(jnp.bfloat16)
    for r in range(N_DP):
        at = pl.ds(2 * place[r], 2)
        into = jnp.dot(dg_t[...], w[r][: 2 * G, :], preferred_element_type=jnp.float32)
        out[at, 0:F, :] = into.T.astype(jnp.bfloat16).reshape(2, F, TOK)
        part = jnp.dot(hid_t[...], w[r][2 * G :, :], preferred_element_type=jnp.float32)
        out[at, F : 2 * F, :] = part.T.astype(jnp.bfloat16).reshape(2, F, TOK)
    me = place[N_DP]
    value = stat[...]
    high = value.astype(jnp.bfloat16).astype(jnp.float32)
    rows = lax.broadcasted_iota(jnp.int32, (2 * N_T, TOK), 0)
    block = jnp.where(rows == me, high, jnp.where(rows == me + N_T, value - high, 0.0)).astype(jnp.bfloat16)
    for t in range(N_T):
        out[t, 2 * F :, :] = block


def grad_kernel(place, *refs):
    dgs = refs[:N_DP]
    near, far, gain, near_out, far_out = refs[N_DP:]
    own = place[0]
    opposite = lax.rem(own + 4, N_DP)
    step = 336
    for src, at, out in ((near, own, near_out), (far, opposite, far_out)):
        lanes = gain[:, pl.ds(pl.multiple_of(at * DS, DS), DS)]
        for m in range(0, 2 * G, step):
            total = jnp.zeros((step, DS), jnp.float32)
            for r in range(N_DP):
                v = src[pl.ds(2 * place[r], 2), 0].reshape(DS, TOK)
                total = total + lax.dot_general(
                    dgs[r][m : m + step, :], v, (((1,), (1,)), ((), ())), preferred_element_type=jnp.float32
                )
            out[m : m + step, :] = (total * lanes).astype(jnp.bfloat16)


def assemble_kernel(place, *refs):
    parts = refs[:N_DP]
    gate_out, up_out, sems = refs[N_DP:]
    copies = []
    for r in range(N_DP):
        lanes = pl.ds(pl.multiple_of(place[r] * DS, DS), DS)
        copies.append(pltpu.make_async_copy(parts[r].at[:G, :], gate_out.at[:, lanes], sems.at[2 * r]))
        copies.append(pltpu.make_async_copy(parts[r].at[G:, :], up_out.at[:, lanes], sems.at[2 * r + 1]))
    for copy in copies:
        copy.start()
    for copy in copies:
        copy.wait()


def params():
    return pltpu.CompilerParams(vmem_limit_bytes=VMEM_LIMIT)


def cost(flops, nbytes):
    return pl.CostEstimate(flops=flops, bytes_accessed=nbytes, transcendentals=0)


def of(array, k):
    return pl.BlockSpec((N_T, 1, F, TOK), lambda *_: (0, k, 0, 0), memory_space=pltpu.VMEM)


def combine(route_ids, probs):
    return jnp.sum(jnp.where(route_ids == 0, probs, jnp.zeros_like(probs)), axis=-1)[None, :]


def local(
    passed_activations,
    kept_section_input,
    handed_grads,
    norm_gain,
    gate_weight,
    up_weight,
    down_weight,
    routes,
    route_probs,
):
    place = places()
    here = lax.axis_index("y") * 2 + lax.axis_index("c")
    place_t = jnp.concatenate([place, here[None].astype(jnp.int32)])
    saved_t = kept_section_input[0].T
    acts_t = shift(passed_activations[0].T, s=1)
    dy_t = shift(handed_grads[0].T, s=-1)
    near = swapped(saved_t, 0)
    far = swapped(saved_t, 2)
    weights = gather_ring(jnp.concatenate([gate_weight[0].T, up_weight[0].T, down_weight[0]], axis=0))
    acts = lax.all_gather(
        jnp.concatenate([acts_t, dy_t, saved_t, near, far], axis=0), ("y", "c"), axis=0
    ).reshape(N_T, 5, F, TOK)
    gain = norm_gain[0]
    gain_col = gain[:, None]
    weight_f = combine(routes[0, 0], route_probs[0, 0])
    weight_b = combine(routes[0, 1], route_probs[0, 1])

    bf, f32 = jnp.bfloat16, jnp.float32
    dg, dgs, scale_b, stat = pl.pallas_call(
        inner_kernel,
        grid=(1,),
        in_specs=[SM] + [VM] * N_DP + [of(acts, 2), of(acts, 1), VM, VM],
        out_specs=[VM] * 4,
        out_shape=[
            jax.ShapeDtypeStruct((2 * G, TOK), bf),
            jax.ShapeDtypeStruct((2 * G, TOK), bf),
            jax.ShapeDtypeStruct((1, TOK), f32),
            jax.ShapeDtypeStruct((1, TOK), f32),
        ],
        scratch_shapes=[pltpu.VMEM((D, TOK), bf)],
        compiler_params=params(),
        cost_estimate=cost(6 * D * G * TOK, 12 << 20),
        name="inner",
    )(place, *weights, acts, acts, gain_col, weight_b)
    dgs_all = gather_ring(dgs)
    payload = pl.pallas_call(
        outer_kernel,
        grid=(1,),
        in_specs=[SM] + [VM] * N_DP + [VM, of(acts, 0), VM, VM, VM],
        out_specs=VM,
        out_shape=jax.ShapeDtypeStruct((N_T, 2 * F + 2 * N_T, TOK), bf),
        scratch_shapes=[
            pltpu.VMEM((D, TOK), bf),
            pltpu.VMEM((G, TOK), f32),
            pltpu.VMEM((TOK, 2 * G), bf),
            pltpu.VMEM((TOK, G), bf),
        ],
        compiler_params=params(),
        cost_estimate=cost(10 * D * G * TOK, 12 << 20),
        name="outer",
    )(place_t, *weights, dg, acts, gain_col, weight_f, stat)
    summed = lax.psum_scatter(payload, ("y", "c"), scatter_dimension=0)

    near_grad, far_grad = pl.pallas_call(
        grad_kernel,
        grid=(1,),
        in_specs=[SM] + [VM] * N_DP + [of(acts, 3), of(acts, 4), VM],
        out_specs=[VM, VM],
        out_shape=[jax.ShapeDtypeStruct((2 * G, DS), bf)] * 2,
        compiler_params=params(),
        cost_estimate=cost(8 * DS * G * TOK * N_DP, 8 << 20),
        name="grad",
    )(place, *dgs_all, acts, acts, gain[None, :])
    z = shift(near_grad, zl=1)
    behind = shift(near_grad, x=1)
    ahead = shift(near_grad, x=-1)
    z_far = shift(far_grad, zl=1)
    z_behind = shift(z, x=1)
    z_ahead = shift(z, x=-1)
    parts = [near_grad, z, behind, ahead, z_behind, z_ahead, far_grad, z_far]
    grad_g, grad_u = pl.pallas_call(
        assemble_kernel,
        in_specs=[SM] + [HB] * N_DP,
        out_specs=[HB, HB],
        out_shape=[jax.ShapeDtypeStruct((G, D), bf)] * 2,
        scratch_shapes=[pltpu.SemaphoreType.DMA((2 * N_DP,))],
        compiler_params=params(),
        cost_estimate=cost(0, 8 << 20),
        name="assemble",
    )(place, *parts)

    into = summed[:F].astype(f32)
    mean_stat = jnp.sum(summed[2 * F :].astype(f32), axis=0, keepdims=True) / D
    gain_here = lax.dynamic_slice_in_dim(gain, here * F, F)[:, None]
    output = (acts_t.astype(f32) + summed[F : 2 * F].astype(f32)).astype(bf)
    hat = saved_t.astype(f32) * scale_b
    stored = (dy_t.astype(f32) + scale_b * (into * gain_here - hat * mean_stat)).astype(bf)
    return (output.T[None], stored.T[None], grad_g.T[None], grad_u.T[None])


def solution(mesh):
    fine = Mesh(mesh.devices.reshape(tuple(SIZES[a] for a in AXES)), AXES)
    dp, tensor = ("x", "zl"), ("y", "c")
    placed = (
        P("s", dp, tensor),
        P("s", dp, tensor),
        P("s", dp, tensor),
        P("s", None),
        P("s", dp, tensor),
        P("s", dp, tensor),
        P("s", tensor, dp),
        P("s", None, dp, None),
        P("s", None, dp, None),
    )
    return jax.shard_map(
        local,
        mesh=fine,
        in_specs=placed,
        out_specs=(
            P("s", dp, tensor),
            P("s", dp, tensor),
            P("s", None, tensor),
            P("s", None, tensor),
        ),
        check_vma=False,
    )
```

time: 649 us -> 246 us (0.38)
  the two profiles are of different devices: /device:TPU:6 before, /device:TPU:14 now
where the time goes in v1:
time: 246 us
  starting transfers between devices  86.8 us (35%)
  waiting for transfers between devices  83.9 us (34%)
  Pallas kernels  54.1 us (22%)
  between operations  14.5 us (6%)
  local copies, waits for them, and re-layouts  3.71 us (2%)
  other arithmetic  2.56 us (1%)
    ppermute x22, waiting for transfers between devices, shift(): return lax.ppermute(value, axes if len(axes) > 1 else axes[0], pairs)  81.3 us
    ppermute x22, starting transfers between devices, shift(): return lax.ppermute(value, axes if len(axes) > 1 else axes[0], pairs)  75.6 us
    pallas_call x1, Pallas kernels, local(): pl.pallas_call(assemble_kernel, in_specs=[SM] + [HB] * N_DP, out_specs=[H...  33.1 us
    ppermute x2, starting transfers between devices, swapped(): return lax.ppermute(value, ('x', 'zl', 'y'), pairs)  11.1 us
    pallas_call x1, Pallas kernels, local(): pl.pallas_call(outer_kernel, grid=(1,), in_specs=[SM] + [VM] * N_DP + [VM...  9.59 us
    pallas_call x1, Pallas kernels, local(): pl.pallas_call(inner_kernel, grid=(1,), in_specs=[SM] + [VM] * N_DP + [of...  6.51 us
    pallas_call x1, Pallas kernels, local(): pl.pallas_call(grad_kernel, grid=(1,), in_specs=[SM] + [VM] * N_DP + [of(...  4.94 us
  transfers between devices with their start and end apart: 26, of which 20 were waited for; matrix products, arithmetic and copies ran while one was open for 1% of the time, Pallas kernels for 15%

profile of v1, /device:TPU:14, one launch (start us, length us, event | category | flops | bytes accessed | tf_op | source)
XLA Modules:
  0.0 245.5 jit_solution(2018182719238196828)
XLA Ops:
  7.2 6.2 %collective-permute-start = (bf16[192,256]{1,0:T(8,128)(2,1)}, bf16[192,256]{1,0:T(8,128)(2,1)S(1)}, u32[]{:S(2)}, u32[]{:S(2)}) collective-permute-start(bf16[192,256]{1,0:T(8,128)(2,1)} %bitcast.74), channel_id=1, source_target_pairs={{0,16},{16,32},{32,48},{48,0},{1,17},{17,33},{33,49},{49,1},{2,18}... | collective-permute-start | bytes 294920 | tf_op jit(solution)/shard_map/ppermute | solution.py:35
  13.5 7.8 %collective-permute-start.9 = (bf16[192,256]{1,0:T(8,128)(2,1)}, bf16[192,256]{1,0:T(8,128)(2,1)S(1)}, u32[]{:S(2)}, u32[]{:S(2)}) collective-permute-start(bf16[192,256]{1,0:T(8,128)(2,1)} %bitcast.66), channel_id=1, source_target_pairs={{0,0},{2,64},{4,128},{6,192},{8,256},{10,320},{12,384},{14,448},{6... | collective-permute-start | bytes 294920 | tf_op jit(solution)/shard_map/ppermute | solution.py:44
  21.3 3.3 %collective-permute-start.10 = (bf16[192,256]{1,0:T(8,128)(2,1)}, bf16[192,256]{1,0:T(8,128)(2,1)S(1)}, u32[]{:S(2)}, u32[]{:S(2)}) collective-permute-start(bf16[192,256]{1,0:T(8,128)(2,1)} %bitcast.67), channel_id=1, source_target_pairs={{0,256},{2,320},{4,384},{6,448},{8,0},{10,64},{12,128},{14,192},{6... | collective-permute-start | bytes 294920 | tf_op jit(solution)/shard_map/ppermute | solution.py:44
  24.6 6.8 %collective-permute-start.8 = (bf16[192,256]{1,0:T(8,128)(2,1)}, bf16[192,256]{1,0:T(8,128)(2,1)S(1)}, u32[]{:S(2)}, u32[]{:S(2)}) collective-permute-start(bf16[192,256]{1,0:T(8,128)(2,1)} %bitcast.75), channel_id=1, source_target_pairs={{0,48},{16,0},{32,16},{48,32},{1,49},{17,1},{33,17},{49,33},{2,50}... | collective-permute-start | bytes 294920 | tf_op jit(solution)/shard_map/ppermute | solution.py:35
  31.4 4.8 %collective-permute-done.8 = bf16[192,256]{1,0:T(8,128)(2,1)S(1)} collective-permute-done((bf16[192,256]{1,0:T(8,128)(2,1)}, bf16[192,256]{1,0:T(8,128)(2,1)S(1)}, u32[]{:S(2)}, u32[]{:S(2)}) %collective-permute-start.8) | collective-permute-done | bytes 98336 | tf_op jit(solution)/shard_map/ppermute | solution.py:35
  36.2 0.9 constant_dynamic-update-slice_fusion.2
  37.2 2.5 %collective-permute-done.10 = bf16[192,256]{1,0:T(8,128)(2,1)S(1)} collective-permute-done((bf16[192,256]{1,0:T(8,128)(2,1)}, bf16[192,256]{1,0:T(8,128)(2,1)S(1)}, u32[]{:S(2)}, u32[]{:S(2)}) %collective-permute-start.10) | collective-permute-done | bytes 98336 | tf_op jit(solution)/shard_map/ppermute | solution.py:44
  40.7 1.9 collective-permute-start.1
  42.6 10.0 %collective-permute-start.2 = (bf16[1008,384]{1,0:T(8,128)(2,1)S(1)}, bf16[1008,384]{1,0:T(8,128)(2,1)S(1)}, u32[]{:S(2)}, u32[]{:S(2)}) collective-permute-start(bf16[1008,384]{1,0:T(8,128)(2,1)S(1)} %pad_maximum_fusion.refs_0_), channel_id=1, source_target_pairs={{0,128},{128,256},{256,384},{384,0},{1,129},{129,257},{257,385},{3... | collective-permute-start | bytes 2322440 | tf_op jit(solution)/shard_map/ppermute | solution.py:35
  52.7 1.9 collective-permute-start.3
  54.6 7.2 %collective-permute-done.1.refs_1_ = bf16[1008,384]{1,0:T(8,128)(2,1)S(1)} collective-permute-done((bf16[1008,384]{1,0:T(8,128)(2,1)S(1)}, bf16[1008,384]{1,0:T(8,128)(2,1)S(1)}, u32[]{:S(2)}, u32[]{:S(2)}) %collective-permute-start.1) | collective-permute-done | bytes 774176 | tf_op jit(solution)/shard_map/ppermute | solution.py:35
  61.8 7.0 %collective-permute-done.2.refs_2_ = bf16[1008,384]{1,0:T(8,128)(2,1)S(1)} collective-permute-done((bf16[1008,384]{1,0:T(8,128)(2,1)S(1)}, bf16[1008,384]{1,0:T(8,128)(2,1)S(1)}, u32[]{:S(2)}, u32[]{:S(2)}) %collective-permute-start.2) | collective-permute-done | bytes 774176 | tf_op jit(solution)/shard_map/ppermute | solution.py:35
  68.9 5.3 %collective-permute-done.3.refs_3_ = bf16[1008,384]{1,0:T(8,128)(2,1)S(1)} collective-permute-done((bf16[1008,384]{1,0:T(8,128)(2,1)S(1)}, bf16[1008,384]{1,0:T(8,128)(2,1)S(1)}, u32[]{:S(2)}, u32[]{:S(2)}) %collective-permute-start.3) | collective-permute-done | bytes 774176 | tf_op jit(solution)/shard_map/ppermute | solution.py:35
  74.2 1.9 collective-permute-start.5
  76.1 5.1 %collective-permute-start.4 = (bf16[1008,384]{1,0:T(8,128)(2,1)S(1)}, bf16[1008,384]{1,0:T(8,128)(2,1)}, u32[]{:S(2)}, u32[]{:S(2)}) collective-permute-start(bf16[1008,384]{1,0:T(8,128)(2,1)S(1)} %collective-permute-done.1.refs_1_), channel_id=1, source_target_pairs={{0,128},{128,256},{256,384},{384,0},{1,129},{129,257},{257,385},{3... | collective-permute-start | bytes 2322440 | tf_op jit(solution)/shard_map/ppermute | solution.py:35
  81.2 1.9 collective-permute-start.6
  83.2 11.7 %collective-permute-done.5.refs_5_ = bf16[1008,384]{1,0:T(8,128)(2,1)} collective-permute-done((bf16[1008,384]{1,0:T(8,128)(2,1)S(1)}, bf16[1008,384]{1,0:T(8,128)(2,1)}, u32[]{:S(2)}, u32[]{:S(2)}) %collective-permute-start.5) | collective-permute-done | bytes 774176 | tf_op jit(solution)/shard_map/ppermute | solution.py:35
  94.9 1.9 collective-permute-start.7
  97.1 1.7 copy.13.refs_10_
  99.0 13.6 %collective-permute-done.6.refs_6_ = bf16[1008,384]{1,0:T(8,128)(2,1)} collective-permute-done((bf16[1008,384]{1,0:T(8,128)(2,1)S(1)}, bf16[1008,384]{1,0:T(8,128)(2,1)}, u32[]{:S(2)}, u32[]{:S(2)}) %collective-permute-start.6) | collective-permute-done | bytes 774176 | tf_op jit(solution)/shard_map/ppermute | solution.py:35
  112.6 2.3 collective-permute-done.7.refs_7_
  114.9 6.5 %inner.1 = (bf16[672,256]{1,0:T(8,128)(2,1)S(1)}, bf16[672,256]{1,0:T(8,128)(2,1)S(1)}, f32[1,256]{1,0:T(1,128)S(1)}, f32[1,256]{1,0:T(1,128)S(1)}) custom-call(s32[8]{0:T(128)S(1)} %stack.35.place, bf16[1008,384]{1,0:T(8,128)(2,1)S(1)} %pad_maximum_fusion.refs_0_, bf16[1008,384]{1,0:T(8,128)(2,1)S(1)} %collective-permute-done.1.refs_1_, ...), custom_call_target="tpu_custom_call" | custom-call | flops 1585446912 | bytes 12582912 | tf_op jit(solution)/shard_map/inner/pallas_call | solution.py:218
  121.4 9.6 %outer.1 = bf16[16,416,256]{2,1,0:T(8,128)(2,1)} custom-call(s32[9]{0:T(128)S(1)} %concatenate.10.place, bf16[1008,384]{1,0:T(8,128)(2,1)S(1)} %pad_maximum_fusion.refs_0_, bf16[1008,384]{1,0:T(8,128)(2,1)S(1)} %collective-permute-done.1.refs_1_, bf16[1008,384]{1,0:T(8,128)(2,1)S(1)} %collective-permute-done.2.refs_2_, ...), custom_call_target="tpu_custom_call" | custom-call | flops 2642411520 | bytes 12582912 | tf_op jit(solution)/shard_map/outer/pallas_call | solution.py:235
  131.0 2.8 %collective-permute-start.11 = (bf16[672,256]{1,0:T(8,128)(2,1)S(1)}, bf16[672,256]{1,0:T(8,128)(2,1)S(1)}, u32[]{:S(2)}, u32[]{:S(2)}) collective-permute-start(bf16[672,256]{1,0:T(8,128)(2,1)S(1)} %get-tuple-element.24.refs_0_), channel_id=1, source_target_pairs={{0,64},{64,0},{1,65},{65,1},{2,66},{66,2},{3,67},{67,3},{4,68},{68... | collective-permute-start | bytes 1032200 | tf_op jit(solution)/shard_map/ppermute | solution.py:35
  133.8 3.1 %collective-permute-start.12 = (bf16[672,256]{1,0:T(8,128)(2,1)S(1)}, bf16[672,256]{1,0:T(8,128)(2,1)S(1)}, u32[]{:S(2)}, u32[]{:S(2)}) collective-permute-start(bf16[672,256]{1,0:T(8,128)(2,1)S(1)} %get-tuple-element.24.refs_0_), channel_id=1, source_target_pairs={{0,128},{128,256},{256,384},{384,0},{1,129},{129,257},{257,385},{3... | collective-permute-start | bytes 1032200 | tf_op jit(solution)/shard_map/ppermute | solution.py:35
  136.9 2.7 %collective-permute-start.13 = (bf16[672,256]{1,0:T(8,128)(2,1)S(1)}, bf16[672,256]{1,0:T(8,128)(2,1)S(1)}, u32[]{:S(2)}, u32[]{:S(2)}) collective-permute-start(bf16[672,256]{1,0:T(8,128)(2,1)S(1)} %get-tuple-element.24.refs_0_), channel_id=1, source_target_pairs={{0,384},{128,0},{256,128},{384,256},{1,385},{129,1},{257,129},{385... | collective-permute-start | bytes 1032200 | tf_op jit(solution)/shard_map/ppermute | solution.py:35
  140.1 2.8 %collective-permute-done.12.refs_2_ = bf16[672,256]{1,0:T(8,128)(2,1)S(1)} collective-permute-done((bf16[672,256]{1,0:T(8,128)(2,1)S(1)}, bf16[672,256]{1,0:T(8,128)(2,1)S(1)}, u32[]{:S(2)}, u32[]{:S(2)}) %collective-permute-start.12) | collective-permute-done | bytes 344096 | tf_op jit(solution)/shard_map/ppermute | solution.py:35
  142.9 4.3 %collective-permute-done.13.refs_3_ = bf16[672,256]{1,0:T(8,128)(2,1)S(1)} collective-permute-done((bf16[672,256]{1,0:T(8,128)(2,1)S(1)}, bf16[672,256]{1,0:T(8,128)(2,1)S(1)}, u32[]{:S(2)}, u32[]{:S(2)}) %collective-permute-start.13) | collective-permute-done | bytes 344096 | tf_op jit(solution)/shard_map/ppermute | solution.py:35
  147.2 1.9 collective-permute-start.15
  149.2 5.1 %collective-permute-start.14 = (bf16[672,256]{1,0:T(8,128)(2,1)S(1)}, bf16[672,256]{1,0:T(8,128)(2,1)S(1)}, u32[]{:S(2)}, u32[]{:S(2)}) collective-permute-start(bf16[672,256]{1,0:T(8,128)(2,1)S(1)} %collective-permute-done.11.refs_1_), channel_id=1, source_target_pairs={{0,128},{128,256},{256,384},{384,0},{1,129},{129,257},{257,385},{3... | collective-permute-start | bytes 1032200 | tf_op jit(solution)/shard_map/ppermute | solution.py:35
  154.3 1.9 collective-permute-start.16
  156.2 1.4 collective-permute-done.15.refs_5_
  157.6 2.8 %collective-permute-start.17 = (bf16[672,256]{1,0:T(8,128)(2,1)S(1)}, bf16[672,256]{1,0:T(8,128)(2,1)S(1)}, u32[]{:S(2)}, u32[]{:S(2)}) collective-permute-start(bf16[672,256]{1,0:T(8,128)(2,1)S(1)} %collective-permute-done.15.refs_5_), channel_id=1, source_target_pairs={{0,384},{128,0},{256,128},{384,256},{1,385},{129,1},{257,129},{385... | collective-permute-start | bytes 1032200 | tf_op jit(solution)/shard_map/ppermute | solution.py:35
  160.4 0.9 collective-permute-done.14.refs_4_
  161.3 3.7 %collective-permute-done.16.refs_6_ = bf16[672,256]{1,0:T(8,128)(2,1)S(1)} collective-permute-done((bf16[672,256]{1,0:T(8,128)(2,1)S(1)}, bf16[672,256]{1,0:T(8,128)(2,1)S(1)}, u32[]{:S(2)}, u32[]{:S(2)}) %collective-permute-start.16) | collective-permute-done | bytes 344096 | tf_op jit(solution)/shard_map/ppermute | solution.py:35
  165.0 3.0 %collective-permute-done.17.refs_7_ = bf16[672,256]{1,0:T(8,128)(2,1)S(1)} collective-permute-done((bf16[672,256]{1,0:T(8,128)(2,1)S(1)}, bf16[672,256]{1,0:T(8,128)(2,1)S(1)}, u32[]{:S(2)}, u32[]{:S(2)}) %collective-permute-start.17) | collective-permute-done | bytes 344096 | tf_op jit(solution)/shard_map/ppermute | solution.py:35
  167.9 4.9 %grad.1 = (bf16[672,384]{1,0:T(8,128)(2,1)S(1)}, bf16[672,384]{1,0:T(8,128)(2,1)S(1)}) custom-call(s32[8]{0:T(128)S(1)} %stack.35.place, bf16[672,256]{1,0:T(8,128)(2,1)S(1)} %get-tuple-element.24.refs_0_, bf16[672,256]{1,0:T(8,128)(2,1)S(1)} %collective-permute-done.11.refs_1_, bf16[672,256]{1,0:T(8,128)(2,1)S(1)} %collective-permute-done.12.refs_2_, ...), custom_call_target="tpu_custom_call" | custom-call | flops 2113929216 | bytes 8388608 | tf_op jit(solution)/shard_map/grad/pallas_call | solution.py:253
  172.9 3.3 %collective-permute-start.18 = (bf16[672,384]{1,0:T(8,128)(2,1)S(1)}, bf16[672,384]{1,0:T(8,128)(2,1)S(1)}, u32[]{:S(2)}, u32[]{:S(2)}) collective-permute-start(bf16[672,384]{1,0:T(8,128)(2,1)S(1)} %get-tuple-element.28.refs_0_), channel_id=1, source_target_pairs={{0,64},{64,0},{1,65},{65,1},{2,66},{66,2},{3,67},{67,3},{4,68},{68... | collective-permute-start | bytes 1548296 | tf_op jit(solution)/shard_map/ppermute | solution.py:35
  176.2 1.9 collective-permute-start.19
  178.2 3.9 %collective-permute-start.20 = (bf16[672,384]{1,0:T(8,128)(2,1)S(1)}, bf16[672,384]{1,0:T(8,128)(2,1)S(1)}, u32[]{:S(2)}, u32[]{:S(2)}) collective-permute-start(bf16[672,384]{1,0:T(8,128)(2,1)S(1)} %get-tuple-element.28.refs_0_), channel_id=1, source_target_pairs={{0,384},{128,0},{256,128},{384,256},{1,385},{129,1},{257,129},{385... | collective-permute-start | bytes 1548296 | tf_op jit(solution)/shard_map/ppermute | solution.py:35
  182.1 2.5 %collective-permute-start.23 = (bf16[672,384]{1,0:T(8,128)(2,1)S(1)}, bf16[672,384]{1,0:T(8,128)(2,1)}, u32[]{:S(2)}, u32[]{:S(2)}) collective-permute-start(bf16[672,384]{1,0:T(8,128)(2,1)S(1)} %get-tuple-element.29.refs_6_), channel_id=1, source_target_pairs={{0,64},{64,0},{1,65},{65,1},{2,66},{66,2},{3,67},{67,3},{4,68},{68... | collective-permute-start | bytes 1548296 | tf_op jit(solution)/shard_map/ppermute | solution.py:35
  184.6 4.3 %collective-permute-done.18.refs_1_ = bf16[672,384]{1,0:T(8,128)(2,1)S(1)} collective-permute-done((bf16[672,384]{1,0:T(8,128)(2,1)S(1)}, bf16[672,384]{1,0:T(8,128)(2,1)S(1)}, u32[]{:S(2)}, u32[]{:S(2)}) %collective-permute-start.18) | collective-permute-done | bytes 516128 | tf_op jit(solution)/shard_map/ppermute | solution.py:35
  188.9 1.9 collective-permute-start.21
  190.8 3.9 %collective-permute-start.22 = (bf16[672,384]{1,0:T(8,128)(2,1)S(1)}, bf16[672,384]{1,0:T(8,128)(2,1)}, u32[]{:S(2)}, u32[]{:S(2)}) collective-permute-start(bf16[672,384]{1,0:T(8,128)(2,1)S(1)} %collective-permute-done.18.refs_1_), channel_id=1, source_target_pairs={{0,384},{128,0},{256,128},{384,256},{1,385},{129,1},{257,129},{385... | collective-permute-start | bytes 1548296 | tf_op jit(solution)/shard_map/ppermute | solution.py:35
  195.0 4.8 %collective-permute-done.21.refs_4_ = bf16[672,384]{1,0:T(8,128)(2,1)S(1)} collective-permute-done((bf16[672,384]{1,0:T(8,128)(2,1)S(1)}, bf16[672,384]{1,0:T(8,128)(2,1)S(1)}, u32[]{:S(2)}, u32[]{:S(2)}) %collective-permute-start.21) | collective-permute-done | bytes 516128 | tf_op jit(solution)/shard_map/ppermute | solution.py:35
  199.9 3.2 %collective-permute-done.22.refs_5_ = bf16[672,384]{1,0:T(8,128)(2,1)} collective-permute-done((bf16[672,384]{1,0:T(8,128)(2,1)S(1)}, bf16[672,384]{1,0:T(8,128)(2,1)}, u32[]{:S(2)}, u32[]{:S(2)}) %collective-permute-start.22) | collective-permute-done | bytes 516128 | tf_op jit(solution)/shard_map/ppermute | solution.py:35
  203.1 33.1 %assemble.1 = (bf16[336,3072]{1,0:T(8,128)(2,1)}, bf16[336,3072]{1,0:T(8,128)(2,1)}) custom-call(s32[8]{0:T(128)S(1)} %stack.35.place, bf16[672,384]{1,0:T(8,128)(2,1)S(1)} %get-tuple-element.28.refs_0_, bf16[672,384]{1,0:T(8,128)(2,1)S(1)} %collective-permute-done.18.refs_1_, bf16[672,384]{1,0:T(8,128)(2,1)S(1)} %collective-permute-done.19.refs_2_, ...), custom_call_target="tpu_custom_call" | custom-call | bytes 8388608 | tf_op jit(solution)/shard_map/assemble/pallas_call | solution.py:270
  237.0 1.7 fusion.6
  (48 shorter events, 3.0 us)
Async XLA Ops:
  7.2 33.4 %copy-start.7 = (bf16[1,336,384]{2,1,0:T(8,128)(2,1)S(1)}, bf16[1,336,384]{2,1,0:T(8,128)(2,1)}, u32[]{:S(2)}) copy-start(bf16[1,336,384]{2,1,0:T(8,128)(2,1)} %param.15) | copy-start | bytes 774148
  7.2 33.4 %copy-start.8 = (bf16[1,384,336]{1,2,0:T(8,128)(2,1)S(1)}, bf16[1,384,336]{1,2,0:T(8,128)(2,1)}, u32[]{:S(2)}) copy-start(bf16[1,384,336]{1,2,0:T(8,128)(2,1)} %param.14) | copy-start | bytes 774148
  7.2 33.4 %copy-start.9 = (bf16[1,384,336]{1,2,0:T(8,128)(2,1)S(1)}, bf16[1,384,336]{1,2,0:T(8,128)(2,1)}, u32[]{:S(2)}) copy-start(bf16[1,384,336]{1,2,0:T(8,128)(2,1)} %param.13) | copy-start | bytes 774148
  7.2 107.7 %all-gather.3.cloned.1.call-start = ((), (), s32[]{:S(2)}) async-start(), calls=%async_computation.2 | async-start | bytes 8355840 | tf_op jit(solution)/shard_map/all_gather | solution.py:209
  7.2 24.1 %collective-permute-start = (bf16[192,256]{1,0:T(8,128)(2,1)}, bf16[192,256]{1,0:T(8,128)(2,1)S(1)}, u32[]{:S(2)}, u32[]{:S(2)}) collective-permute-start(bf16[192,256]{1,0:T(8,128)(2,1)} %bitcast.74), channel_id=1, source_target_pairs={{0,16},{16,32},{32,48},{48,0},{1,17},{17,33},{33,49},{49,1},{2,18}... | collective-permute-start | bytes 294920 | tf_op jit(solution)/shard_map/ppermute | solution.py:35
  13.5 23.7 %collective-permute-start.9 = (bf16[192,256]{1,0:T(8,128)(2,1)}, bf16[192,256]{1,0:T(8,128)(2,1)S(1)}, u32[]{:S(2)}, u32[]{:S(2)}) collective-permute-start(bf16[192,256]{1,0:T(8,128)(2,1)} %bitcast.66), channel_id=1, source_target_pairs={{0,0},{2,64},{4,128},{6,192},{8,256},{10,320},{12,384},{14,448},{6... | collective-permute-start | bytes 294920 | tf_op jit(solution)/shard_map/ppermute | solution.py:44
  21.3 18.4 %collective-permute-start.10 = (bf16[192,256]{1,0:T(8,128)(2,1)}, bf16[192,256]{1,0:T(8,128)(2,1)S(1)}, u32[]{:S(2)}, u32[]{:S(2)}) collective-permute-start(bf16[192,256]{1,0:T(8,128)(2,1)} %bitcast.67), channel_id=1, source_target_pairs={{0,256},{2,320},{4,384},{6,448},{8,0},{10,64},{12,128},{14,192},{6... | collective-permute-start | bytes 294920 | tf_op jit(solution)/shard_map/ppermute | solution.py:44
  24.6 11.6 %collective-permute-start.8 = (bf16[192,256]{1,0:T(8,128)(2,1)}, bf16[192,256]{1,0:T(8,128)(2,1)S(1)}, u32[]{:S(2)}, u32[]{:S(2)}) collective-permute-start(bf16[192,256]{1,0:T(8,128)(2,1)} %bitcast.75), channel_id=1, source_target_pairs={{0,48},{16,0},{32,16},{48,32},{1,49},{17,1},{33,17},{49,33},{2,50}... | collective-permute-start | bytes 294920 | tf_op jit(solution)/shard_map/ppermute | solution.py:35
  31.4 5.8 %copy-start.3 = (bf16[192,256]{1,0:T(8,128)(2,1)}, bf16[192,256]{1,0:T(8,128)(2,1)S(1)}, u32[]{:S(2)}) copy-start(bf16[192,256]{1,0:T(8,128)(2,1)S(1)} %collective-permute-done) | copy-start | bytes 294916
  31.4 65.6 %copy-start = (f32[1,3072]{1,0:T(1,128)S(1)}, f32[1,3072]{1,0:T(1,128)}, u32[]{:S(2)}) copy-start(f32[1,3072]{1,0:T(1,128)} %refs_10_.1) | copy-start | bytes 36868
  36.2 4.3 %copy-start.5 = (bf16[192,256]{1,0:T(8,128)(2,1)}, bf16[192,256]{1,0:T(8,128)(2,1)S(1)}, u32[]{:S(2)}) copy-start(bf16[192,256]{1,0:T(8,128)(2,1)S(1)} %collective-permute-done.8) | copy-start | bytes 294916
  39.7 0.8 copy-start.1
  40.5 195.7 %reduce-scatter.2.cloned.1.call-start = ((), (), s32[]{:S(2)}) async-start(), calls=%async_computation.1 | async-start | bytes 3620864 | tf_op jit(solution)/shard_map/reduce_scatter | solution.py:251
  40.6 58.1 %copy-start.10 = (f32[1,2,256,4]{2,3,1,0:T(4,128)S(1)}, f32[1,2,256,4]{2,3,1,0:T(4,128)}, u32[]{:S(2)}) copy-start(f32[1,2,256,4]{2,3,1,0:T(4,128)} %param.17) | copy-start | bytes 24580
  40.6 58.1 %copy-start.11 = (s32[1,2,256,4]{2,3,1,0:T(4,128)S(1)}, s32[1,2,256,4]{2,3,1,0:T(4,128)}, u32[]{:S(2)}) copy-start(s32[1,2,256,4]{2,3,1,0:T(4,128)} %param.16) | copy-start | bytes 24580
  40.7 21.1 %collective-permute-start.1 = (bf16[1008,384]{1,0:T(8,128)(2,1)S(1)}, bf16[1008,384]{1,0:T(8,128)(2,1)S(1)}, u32[]{:S(2)}, u32[]{:S(2)}) collective-permute-start(bf16[1008,384]{1,0:T(8,128)(2,1)S(1)} %pad_maximum_fusion.refs_0_), channel_id=1, source_target_pairs={{0,64},{64,0},{1,65},{65,1},{2,66},{66,2},{3,67},{67,3},{4,68},{68... | collective-permute-start | bytes 2322440 | tf_op jit(solution)/shard_map/ppermute | solution.py:35
  42.6 26.2 %collective-permute-start.2 = (bf16[1008,384]{1,0:T(8,128)(2,1)S(1)}, bf16[1008,384]{1,0:T(8,128)(2,1)S(1)}, u32[]{:S(2)}, u32[]{:S(2)}) collective-permute-start(bf16[1008,384]{1,0:T(8,128)(2,1)S(1)} %pad_maximum_fusion.refs_0_), channel_id=1, source_target_pairs={{0,128},{128,256},{256,384},{384,0},{1,129},{129,257},{257,385},{3... | collective-permute-start | bytes 2322440 | tf_op jit(solution)/shard_map/ppermute | solution.py:35
  52.7 21.5 %collective-permute-start.3 = (bf16[1008,384]{1,0:T(8,128)(2,1)S(1)}, bf16[1008,384]{1,0:T(8,128)(2,1)S(1)}, u32[]{:S(2)}, u32[]{:S(2)}) collective-permute-start(bf16[1008,384]{1,0:T(8,128)(2,1)S(1)} %pad_maximum_fusion.refs_0_), channel_id=1, source_target_pairs={{0,384},{128,0},{256,128},{384,256},{1,385},{129,1},{257,129},{385... | collective-permute-start | bytes 2322440 | tf_op jit(solution)/shard_map/ppermute | solution.py:35
  74.2 20.7 %collective-permute-start.5 = (bf16[1008,384]{1,0:T(8,128)(2,1)S(1)}, bf16[1008,384]{1,0:T(8,128)(2,1)}, u32[]{:S(2)}, u32[]{:S(2)}) collective-permute-start(bf16[1008,384]{1,0:T(8,128)(2,1)S(1)} %collective-permute-done.1.refs_1_), channel_id=1, source_target_pairs={{0,384},{128,0},{256,128},{384,256},{1,385},{129,1},{257,129},{385... | collective-permute-start | bytes 2322440 | tf_op jit(solution)/shard_map/ppermute | solution.py:35
  76.1 22.9 %collective-permute-start.4 = (bf16[1008,384]{1,0:T(8,128)(2,1)S(1)}, bf16[1008,384]{1,0:T(8,128)(2,1)}, u32[]{:S(2)}, u32[]{:S(2)}) collective-permute-start(bf16[1008,384]{1,0:T(8,128)(2,1)S(1)} %collective-permute-done.1.refs_1_), channel_id=1, source_target_pairs={{0,128},{128,256},{256,384},{384,0},{1,129},{129,257},{257,385},{3... | collective-permute-start | bytes 2322440 | tf_op jit(solution)/shard_map/ppermute | solution.py:35
  81.2 31.3 %collective-permute-start.6 = (bf16[1008,384]{1,0:T(8,128)(2,1)S(1)}, bf16[1008,384]{1,0:T(8,128)(2,1)}, u32[]{:S(2)}, u32[]{:S(2)}) collective-permute-start(bf16[1008,384]{1,0:T(8,128)(2,1)S(1)} %collective-permute-done.2.refs_2_), channel_id=1, source_target_pairs={{0,128},{128,256},{256,384},{384,0},{1,129},{129,257},{257,385},{3... | collective-permute-start | bytes 2322440 | tf_op jit(solution)/shard_map/ppermute | solution.py:35
  94.9 20.0 %collective-permute-start.7 = (bf16[1008,384]{1,0:T(8,128)(2,1)}, bf16[1008,384]{1,0:T(8,128)(2,1)}, u32[]{:S(2)}, u32[]{:S(2)}) collective-permute-start(bf16[1008,384]{1,0:T(8,128)(2,1)} %collective-permute-done.5.refs_5_), channel_id=1, source_target_pairs={{0,384},{128,0},{256,128},{384,256},{1,385},{129,1},{257,129},{385... | collective-permute-start | bytes 2322440 | tf_op jit(solution)/shard_map/ppermute | solution.py:35
  131.0 9.1 %collective-permute-start.11 = (bf16[672,256]{1,0:T(8,128)(2,1)S(1)}, bf16[672,256]{1,0:T(8,128)(2,1)S(1)}, u32[]{:S(2)}, u32[]{:S(2)}) collective-permute-start(bf16[672,256]{1,0:T(8,128)(2,1)S(1)} %get-tuple-element.24.refs_0_), channel_id=1, source_target_pairs={{0,64},{64,0},{1,65},{65,1},{2,66},{66,2},{3,67},{67,3},{4,68},{68... | collective-permute-start | bytes 1032200 | tf_op jit(solution)/shard_map/ppermute | solution.py:35
  133.8 9.1 %collective-permute-start.12 = (bf16[672,256]{1,0:T(8,128)(2,1)S(1)}, bf16[672,256]{1,0:T(8,128)(2,1)S(1)}, u32[]{:S(2)}, u32[]{:S(2)}) collective-permute-start(bf16[672,256]{1,0:T(8,128)(2,1)S(1)} %get-tuple-element.24.refs_0_), channel_id=1, source_target_pairs={{0,128},{128,256},{256,384},{384,0},{1,129},{129,257},{257,385},{3... | collective-permute-start | bytes 1032200 | tf_op jit(solution)/shard_map/ppermute | solution.py:35
  136.9 10.4 %collective-permute-start.13 = (bf16[672,256]{1,0:T(8,128)(2,1)S(1)}, bf16[672,256]{1,0:T(8,128)(2,1)S(1)}, u32[]{:S(2)}, u32[]{:S(2)}) collective-permute-start(bf16[672,256]{1,0:T(8,128)(2,1)S(1)} %get-tuple-element.24.refs_0_), channel_id=1, source_target_pairs={{0,384},{128,0},{256,128},{384,256},{1,385},{129,1},{257,129},{385... | collective-permute-start | bytes 1032200 | tf_op jit(solution)/shard_map/ppermute | solution.py:35
  147.2 10.3 %collective-permute-start.15 = (bf16[672,256]{1,0:T(8,128)(2,1)S(1)}, bf16[672,256]{1,0:T(8,128)(2,1)S(1)}, u32[]{:S(2)}, u32[]{:S(2)}) collective-permute-start(bf16[672,256]{1,0:T(8,128)(2,1)S(1)} %collective-permute-done.11.refs_1_), channel_id=1, source_target_pairs={{0,384},{128,0},{256,128},{384,256},{1,385},{129,1},{257,129},{385... | collective-permute-start | bytes 1032200 | tf_op jit(solution)/shard_map/ppermute | solution.py:35
  149.2 12.1 %collective-permute-start.14 = (bf16[672,256]{1,0:T(8,128)(2,1)S(1)}, bf16[672,256]{1,0:T(8,128)(2,1)S(1)}, u32[]{:S(2)}, u32[]{:S(2)}) collective-permute-start(bf16[672,256]{1,0:T(8,128)(2,1)S(1)} %collective-permute-done.11.refs_1_), channel_id=1, source_target_pairs={{0,128},{128,256},{256,384},{384,0},{1,129},{129,257},{257,385},{3... | collective-permute-start | bytes 1032200 | tf_op jit(solution)/shard_map/ppermute | solution.py:35
  154.3 10.7 %collective-permute-start.16 = (bf16[672,256]{1,0:T(8,128)(2,1)S(1)}, bf16[672,256]{1,0:T(8,128)(2,1)S(1)}, u32[]{:S(2)}, u32[]{:S(2)}) collective-permute-start(bf16[672,256]{1,0:T(8,128)(2,1)S(1)} %collective-permute-done.12.refs_2_), channel_id=1, source_target_pairs={{0,128},{128,256},{256,384},{384,0},{1,129},{129,257},{257,385},{3... | collective-permute-start | bytes 1032200 | tf_op jit(solution)/shard_map/ppermute | solution.py:35
  157.6 10.3 %collective-permute-start.17 = (bf16[672,256]{1,0:T(8,128)(2,1)S(1)}, bf16[672,256]{1,0:T(8,128)(2,1)S(1)}, u32[]{:S(2)}, u32[]{:S(2)}) collective-permute-start(bf16[672,256]{1,0:T(8,128)(2,1)S(1)} %collective-permute-done.15.refs_5_), channel_id=1, source_target_pairs={{0,384},{128,0},{256,128},{384,256},{1,385},{129,1},{257,129},{385... | collective-permute-start | bytes 1032200 | tf_op jit(solution)/shard_map/ppermute | solution.py:35
  172.9 16.0 %collective-permute-start.18 = (bf16[672,384]{1,0:T(8,128)(2,1)S(1)}, bf16[672,384]{1,0:T(8,128)(2,1)S(1)}, u32[]{:S(2)}, u32[]{:S(2)}) collective-permute-start(bf16[672,384]{1,0:T(8,128)(2,1)S(1)} %get-tuple-element.28.refs_0_), channel_id=1, source_target_pairs={{0,64},{64,0},{1,65},{65,1},{2,66},{66,2},{3,67},{67,3},{4,68},{68... | collective-permute-start | bytes 1548296 | tf_op jit(solution)/shard_map/ppermute | solution.py:35
  176.2 18.6 %collective-permute-start.19 = (bf16[672,384]{1,0:T(8,128)(2,1)S(1)}, bf16[672,384]{1,0:T(8,128)(2,1)S(1)}, u32[]{:S(2)}, u32[]{:S(2)}) collective-permute-start(bf16[672,384]{1,0:T(8,128)(2,1)S(1)} %get-tuple-element.28.refs_0_), channel_id=1, source_target_pairs={{0,128},{128,256},{256,384},{384,0},{1,129},{129,257},{257,385},{3... | collective-permute-start | bytes 1548296 | tf_op jit(solution)/shard_map/ppermute | solution.py:35
  178.2 16.7 %collective-permute-start.20 = (bf16[672,384]{1,0:T(8,128)(2,1)S(1)}, bf16[672,384]{1,0:T(8,128)(2,1)S(1)}, u32[]{:S(2)}, u32[]{:S(2)}) collective-permute-start(bf16[672,384]{1,0:T(8,128)(2,1)S(1)} %get-tuple-element.28.refs_0_), channel_id=1, source_target_pairs={{0,384},{128,0},{256,128},{384,256},{1,385},{129,1},{257,129},{385... | collective-permute-start | bytes 1548296 | tf_op jit(solution)/shard_map/ppermute | solution.py:35
  182.1 12.9 %collective-permute-start.23 = (bf16[672,384]{1,0:T(8,128)(2,1)S(1)}, bf16[672,384]{1,0:T(8,128)(2,1)}, u32[]{:S(2)}, u32[]{:S(2)}) collective-permute-start(bf16[672,384]{1,0:T(8,128)(2,1)S(1)} %get-tuple-element.29.refs_6_), channel_id=1, source_target_pairs={{0,64},{64,0},{1,65},{65,1},{2,66},{66,2},{3,67},{67,3},{4,68},{68... | collective-permute-start | bytes 1548296 | tf_op jit(solution)/shard_map/ppermute | solution.py:35
  188.9 11.0 %collective-permute-start.21 = (bf16[672,384]{1,0:T(8,128)(2,1)S(1)}, bf16[672,384]{1,0:T(8,128)(2,1)S(1)}, u32[]{:S(2)}, u32[]{:S(2)}) collective-permute-start(bf16[672,384]{1,0:T(8,128)(2,1)S(1)} %collective-permute-done.18.refs_1_), channel_id=1, source_target_pairs={{0,128},{128,256},{256,384},{384,0},{1,129},{129,257},{257,385},{3... | collective-permute-start | bytes 1548296 | tf_op jit(solution)/shard_map/ppermute | solution.py:35
  190.8 12.3 %collective-permute-start.22 = (bf16[672,384]{1,0:T(8,128)(2,1)S(1)}, bf16[672,384]{1,0:T(8,128)(2,1)}, u32[]{:S(2)}, u32[]{:S(2)}) collective-permute-start(bf16[672,384]{1,0:T(8,128)(2,1)S(1)} %collective-permute-done.18.refs_1_), channel_id=1, source_target_pairs={{0,384},{128,0},{256,128},{384,256},{1,385},{129,1},{257,129},{385... | collective-permute-start | bytes 1548296 | tf_op jit(solution)/shard_map/ppermute | solution.py:35
  194.8 42.1 %copy-start.2 = (bf16[1,256,192]{1,2,0:T(8,128)(2,1)S(1)}, bf16[1,256,192]{1,2,0:T(8,128)(2,1)}, u32[]{:S(2)}) copy-start(bf16[1,256,192]{1,2,0:T(8,128)(2,1)} %param.10) | copy-start | bytes 294916
  194.8 42.1 %copy-start.4 = (bf16[192,256]{1,0:T(8,128)(2,1)S(1)}, bf16[192,256]{1,0:T(8,128)(2,1)}, u32[]{:S(2)}) copy-start(bf16[192,256]{1,0:T(8,128)(2,1)} %copy-done.3) | copy-start | bytes 294916
  194.8 42.2 %copy-start.6 = (bf16[192,256]{1,0:T(8,128)(2,1)S(1)}, bf16[192,256]{1,0:T(8,128)(2,1)}, u32[]{:S(2)}) copy-start(bf16[192,256]{1,0:T(8,128)(2,1)} %copy-done.5) | copy-start | bytes 294916
Sparse Core Ops, SparseCore 0:
  40.6 57.9 all-gather.2
  131.1 57.7 reduce-scatter.1

commit v2 on v1

v2 whole, which is shorter than its diff:
```python
import jax
import jax.numpy as jnp
import numpy as np
from jax import lax
from jax.experimental import pallas as pl
from jax.experimental.pallas import tpu as pltpu
from jax.sharding import Mesh, PartitionSpec as P

EPS = 1e-05
AXES = ("x", "zl", "s", "y", "c")
SIZES = {"x": 4, "zl": 2, "s": 4, "y": 8, "c": 2}
D = 3072
TOK = 256
G = 336
F = 192
N_T = 16
N_DP = 8
DS = D // N_DP
N_EARLY = 6
TILE = 112
OFFSETS = ((0, 0), (0, 1), (-1, 0), (1, 0), (-1, 1), (1, 1), (2, 0), (2, 1))

VM = pl.BlockSpec(memory_space=pltpu.VMEM)
HB = pl.BlockSpec(memory_space=pl.ANY)
SM = pl.BlockSpec(memory_space=pltpu.SMEM)


def shift(value, **steps):
    axes = tuple(a for a in AXES if a in steps)
    sizes = [SIZES[a] for a in axes]
    pairs = []
    for i in range(int(np.prod(sizes))):
        at = np.unravel_index(i, sizes)
        to = [(at[k] + steps[a]) % sizes[k] for k, a in enumerate(axes)]
        pairs.append((i, int(np.ravel_multi_index(to, sizes))))
    return lax.ppermute(value, axes if len(axes) > 1 else axes[0], pairs)


def swapped(value, step):
    pairs = []
    for e in range(N_DP):
        for y in range(N_DP):
            d = (((y // 2) + step) % 4) * 2 + y % 2
            pairs.append((e * N_DP + y, d * N_DP + e))
    return lax.ppermute(value, ("x", "zl", "y"), pairs)


def gather_ring(own, rider=None):
    z = shift(own, zl=1)
    behind = shift(own, x=1)
    ahead = shift(own, x=-1)
    z, behind, ahead = lax.optimization_barrier((z, behind, ahead))
    z_behind = shift(z, x=1)
    z_ahead = shift(z, x=-1)
    riders = ()
    if rider is not None:
        riders = tuple(rider(z))
        z_behind, z_ahead, *riders = lax.optimization_barrier((z_behind, z_ahead, *riders))
    across = shift(behind, x=1)
    z_across = shift(z_ahead, x=-1)
    return [own, z, behind, ahead, z_behind, z_ahead, across, z_across], riders


def after(value, earlier):
    return lax.optimization_barrier((value, earlier))[0]


def places():
    x, zl = lax.axis_index("x"), lax.axis_index("zl")
    return jnp.stack([((x + dx) % 4) * 2 + (zl + dz) % 2 for dx, dz in OFFSETS]).astype(jnp.int32)


def normal_into(act_ref, gain_ref, out_ref):
    total = jnp.zeros((1, TOK), jnp.float32)
    for t in range(N_T):
        v = act_ref[t].astype(jnp.float32)
        total = total + jnp.sum(v * v, axis=0, keepdims=True)
    scale = lax.rsqrt(total / D + EPS)
    for t in range(N_T):
        v = act_ref[t].astype(jnp.float32)
        out_ref[t * F : (t + 1) * F, :] = ((v * scale) * gain_ref[t * F : (t + 1) * F, :]).astype(jnp.bfloat16)
    return scale


def fetch(pairs, sems):
    copies = [pltpu.make_async_copy(src, dst, sems.at[i]) for i, (src, dst) in enumerate(pairs)]
    for copy in copies:
        copy.start()
    return copies


def early_kernel(place, *refs):
    w_from = refs[:N_EARLY]
    acts, gain, b_out, f_out, nb_out, nf_out, scale_out, saved, dy, act, w, normal_b, normal_f, sems = refs[N_EARLY:]
    copies = fetch(
        [(acts.at[:, 2], saved), (acts.at[:, 0], act), (acts.at[:, 1], dy)]
        + [(w_from[r], w.at[r]) for r in range(N_EARLY)],
        sems,
    )
    copies[0].wait()
    scale_out[...] = normal_into(saved, gain, normal_b)
    copies[1].wait()
    normal_into(act, gain, normal_f)
    for copy in copies[2:]:
        copy.wait()
    for i in range(N_DP - N_EARLY):
        rows = pl.ds(pl.multiple_of(place[N_EARLY + i] * DS, DS), DS)
        nb_out[i] = normal_b[rows, :]
        nf_out[i] = normal_f[rows, :]
    for m in range(0, G, TILE):
        sums = [jnp.zeros((TILE, TOK), jnp.float32) for _ in range(5)]
        for r in range(N_EARLY):
            d = place[r]
            rows = pl.ds(pl.multiple_of(d * DS, DS), DS)
            n, f = normal_b[rows, :], normal_f[rows, :]
            g = dy[pl.ds(2 * d, 2)].reshape(DS, TOK)
            w_g = w[r, m : m + TILE, :]
            w_u = w[r, G + m : G + m + TILE, :]
            w_d = w[r, 2 * G + m : 2 * G + m + TILE, :]
            for k, (left, right) in enumerate(((w_g, n), (w_u, n), (w_d, g), (w_g, f), (w_u, f))):
                sums[k] = sums[k] + jnp.dot(left, right, preferred_element_type=jnp.float32)
        for k in range(3):
            b_out[k * G + m : k * G + m + TILE, :] = sums[k]
        for k in range(2):
            f_out[k * G + m : k * G + m + TILE, :] = sums[3 + k]


def inner_kernel(place, w_6, w_7, early, normal, acts, weight, scale_ref, dg_out, dgs_out, stat_out, dy, sems):
    w = (w_6, w_7)
    copies = fetch([(acts.at[pl.ds(2 * place[N_EARLY + i], 2), 1], dy.at[i]) for i in range(N_DP - N_EARLY)], sems)
    for copy in copies:
        copy.wait()
    scale = scale_ref[...]
    row = weight[...]
    stat = jnp.zeros((1, TOK), jnp.float32)
    for m in range(0, G, TILE):
        gate, up, hid = (early[k * G + m : k * G + m + TILE, :] for k in range(3))
        for i in range(N_DP - N_EARLY):
            n, g = normal[i], dy[i].reshape(DS, TOK)
            gate = gate + jnp.dot(w[i][m : m + TILE, :], n, preferred_element_type=jnp.float32)
            up = up + jnp.dot(w[i][G + m : G + m + TILE, :], n, preferred_element_type=jnp.float32)
            hid = hid + jnp.dot(w[i][2 * G + m : 2 * G + m + TILE, :], g, preferred_element_type=jnp.float32)
        sg = jax.nn.sigmoid(gate)
        hid = hid * row
        dgate = hid * up * (sg * (1.0 + gate * (1.0 - sg)))
        dup = hid * (gate * sg)
        dgate_r, dup_r = dgate.astype(jnp.bfloat16), dup.astype(jnp.bfloat16)
        dg_out[m : m + TILE, :] = dgate_r
        dg_out[G + m : G + m + TILE, :] = dup_r
        dgs_out[m : m + TILE, :] = (dgate * scale).astype(jnp.bfloat16)
        dgs_out[G + m : G + m + TILE, :] = (dup * scale).astype(jnp.bfloat16)
        stat = stat + jnp.sum(
            dgate_r.astype(jnp.float32) * gate + dup_r.astype(jnp.float32) * up, axis=0, keepdims=True
        )
    stat_out[...] = stat


def outer_kernel(place, *refs):
    w_from = refs[:N_DP]
    dg, early, normal, weight, stat, out, w, hidden, dg_t, hid_t, sems = refs[N_DP:]
    order = list(range(N_EARLY, N_DP)) + list(range(N_EARLY))
    copies = fetch([(w_from[r], w.at[r]) for r in order], sems)
    dg_t[...] = dg[...].astype(jnp.float32).T.astype(jnp.bfloat16)
    row = weight[...]
    last = N_DP - N_EARLY
    for copy in copies[:last]:
        copy.wait()
    for m in range(0, G, TILE):
        gate, up = (early[k * G + m : k * G + m + TILE, :] for k in range(2))
        for i in range(last):
            n = normal[i]
            gate = gate + jnp.dot(w[N_EARLY + i, m : m + TILE, :], n, preferred_element_type=jnp.float32)
            up = up + jnp.dot(w[N_EARLY + i, G + m : G + m + TILE, :], n, preferred_element_type=jnp.float32)
        hidden[m : m + TILE, :] = gate * jax.nn.sigmoid(gate) * up * row
    hid_t[...] = hidden[...].T.astype(jnp.bfloat16)
    for k, r in enumerate(order):
        if k >= last:
            copies[k].wait()
        at = pl.ds(2 * place[r], 2)
        into = jnp.dot(dg_t[...], w[r, : 2 * G, :], preferred_element_type=jnp.float32)
        out[at, 0:F, :] = into.T.astype(jnp.bfloat16).reshape(2, F, TOK)
        part = jnp.dot(hid_t[...], w[r, 2 * G :, :], preferred_element_type=jnp.float32)
        out[at, F : 2 * F, :] = part.T.astype(jnp.bfloat16).reshape(2, F, TOK)
    me = place[N_DP]
    value = stat[...]
    high = value.astype(jnp.bfloat16).astype(jnp.float32)
    rows = lax.broadcasted_iota(jnp.int32, (2 * N_T, TOK), 0)
    block = jnp.where(rows == me, high, jnp.where(rows == me + N_T, value - high, 0.0)).astype(jnp.bfloat16)
    for t in range(N_T):
        out[t, 2 * F :, :] = block


def grad_kernel(place, *refs):
    dgs = refs[:N_DP]
    near, far, gain, near_out, far_out = refs[N_DP:]
    own = place[0]
    opposite = lax.rem(own + 4, N_DP)
    step = 336
    for src, at, out in ((near, own, near_out), (far, opposite, far_out)):
        lanes = gain[:, pl.ds(pl.multiple_of(at * DS, DS), DS)]
        for m in range(0, 2 * G, step):
            total = jnp.zeros((step, DS), jnp.float32)
            for r in range(N_DP):
                v = src[pl.ds(2 * place[r], 2), 0].reshape(DS, TOK)
                total = total + lax.dot_general(
                    dgs[r][m : m + step, :], v, (((1,), (1,)), ((), ())), preferred_element_type=jnp.float32
                )
            out[m : m + step, :] = (total * lanes).astype(jnp.bfloat16)


def assemble_kernel(place, *refs):
    parts = refs[:N_DP]
    gate_out, up_out = refs[N_DP:]
    for r in range(N_DP):
        lanes = pl.ds(pl.multiple_of(place[r] * DS, DS), DS)
        gate_out[:, lanes] = parts[r][:G, :]
        up_out[:, lanes] = parts[r][G:, :]


def params(mib):
    return pltpu.CompilerParams(vmem_limit_bytes=mib << 20)


def cost(flops, nbytes):
    return pl.CostEstimate(flops=flops, bytes_accessed=nbytes, transcendentals=0)


def of(array, k):
    return pl.BlockSpec((N_T, 1, F, TOK), lambda *_: (0, k, 0, 0), memory_space=pltpu.VMEM)


def combine(route_ids, probs):
    return jnp.sum(jnp.where(route_ids == 0, probs, jnp.zeros_like(probs)), axis=-1)[None, :]


def local(
    passed_activations,
    kept_section_input,
    handed_grads,
    norm_gain,
    gate_weight,
    up_weight,
    down_weight,
    routes,
    route_probs,
):
    place = places()
    here = lax.axis_index("y") * 2 + lax.axis_index("c")
    place_t = jnp.concatenate([place, here[None].astype(jnp.int32)])
    saved_t = kept_section_input[0].T
    acts_t = shift(passed_activations[0].T, s=1)
    dy_t = shift(handed_grads[0].T, s=-1)
    own_weights = jnp.concatenate([gate_weight[0].T, up_weight[0].T, down_weight[0]], axis=0)

    def swaps(first):
        block = after(saved_t, first)
        return swapped(block, 0), swapped(block, 2)

    weights, (near, far) = gather_ring(own_weights, swaps)
    acts = lax.all_gather(
        after(jnp.concatenate([acts_t, dy_t, saved_t], axis=0), own_weights), ("y", "c"), axis=0
    ).reshape(N_T, 3, F, TOK)
    far_tokens = lax.all_gather(jnp.concatenate([near, far], axis=0), ("y", "c"), axis=0).reshape(N_T, 2, F, TOK)
    gain = norm_gain[0]
    gain_col = gain[:, None]
    weight_f = combine(routes[0, 0], route_probs[0, 0])
    weight_b = combine(routes[0, 1], route_probs[0, 1])

    bf, f32 = jnp.bfloat16, jnp.float32
    last = N_DP - N_EARLY
    early_b, early_f, normal_b, normal_f, scale_b = pl.pallas_call(
        early_kernel,
        in_specs=[SM] + [HB] * N_EARLY + [HB, VM],
        out_specs=[VM] * 5,
        out_shape=[
            jax.ShapeDtypeStruct((3 * G, TOK), f32),
            jax.ShapeDtypeStruct((2 * G, TOK), f32),
            jax.ShapeDtypeStruct((last, DS, TOK), bf),
            jax.ShapeDtypeStruct((last, DS, TOK), bf),
            jax.ShapeDtypeStruct((1, TOK), f32),
        ],
        scratch_shapes=[
            pltpu.VMEM((N_T, F, TOK), bf),
            pltpu.VMEM((N_T, F, TOK), bf),
            pltpu.VMEM((N_T, F, TOK), bf),
            pltpu.VMEM((N_EARLY, 3 * G, DS), bf),
            pltpu.VMEM((D, TOK), bf),
            pltpu.VMEM((D, TOK), bf),
            pltpu.SemaphoreType.DMA((N_EARLY + 3,)),
        ],
        compiler_params=params(56),
        cost_estimate=cost(10 * D * G * TOK, 32 << 20),
        name="early",
    )(place, *weights[:N_EARLY], acts, gain_col)
    dg, dgs, stat = pl.pallas_call(
        inner_kernel,
        in_specs=[SM] + [VM] * 4 + [HB, VM, VM],
        out_specs=[VM] * 3,
        out_shape=[
            jax.ShapeDtypeStruct((2 * G, TOK), bf),
            jax.ShapeDtypeStruct((2 * G, TOK), bf),
            jax.ShapeDtypeStruct((1, TOK), f32),
        ],
        scratch_shapes=[pltpu.VMEM((last, 2, F, TOK), bf), pltpu.SemaphoreType.DMA((last,))],
        compiler_params=params(32),
        cost_estimate=cost(2 * D * G * TOK, 12 << 20),
        name="inner",
    )(place, *weights[N_EARLY:], early_b, normal_b, acts, weight_b, scale_b)
    dgs_all, _ = gather_ring(dgs)
    payload = pl.pallas_call(
        outer_kernel,
        in_specs=[SM] + [HB] * N_DP + [VM] * 5,
        out_specs=VM,
        out_shape=jax.ShapeDtypeStruct((N_T, 2 * F + 2 * N_T, TOK), bf),
        scratch_shapes=[
            pltpu.VMEM((N_DP, 3 * G, DS), bf),
            pltpu.VMEM((G, TOK), f32),
            pltpu.VMEM((TOK, 2 * G), bf),
            pltpu.VMEM((TOK, G), bf),
            pltpu.SemaphoreType.DMA((N_DP,)),
        ],
        compiler_params=params(56),
        cost_estimate=cost(8 * D * G * TOK, 28 << 20),
        name="outer",
    )(place_t, *weights, dg, early_f, normal_f, weight_f, stat)
    payload = after(payload, tuple(dgs_all[1:4]))
    summed = lax.psum_scatter(payload, ("y", "c"), scatter_dimension=0)

    near_grad, far_grad = pl.pallas_call(
        grad_kernel,
        grid=(1,),
        in_specs=[SM] + [VM] * N_DP + [of(far_tokens, 0), of(far_tokens, 1), VM],
        out_specs=[VM, VM],
        out_shape=[jax.ShapeDtypeStruct((2 * G, DS), bf)] * 2,
        compiler_params=params(24),
        cost_estimate=cost(8 * DS * G * TOK * N_DP, 8 << 20),
        name="grad",
    )(place, *dgs_all, far_tokens, far_tokens, gain[None, :])
    z = shift(near_grad, zl=1)
    behind = shift(near_grad, x=1)
    ahead = shift(near_grad, x=-1)
    z_far = shift(far_grad, zl=1)
    z_behind = shift(z, x=1)
    z_ahead = shift(z, x=-1)
    parts = [near_grad, z, behind, ahead, z_behind, z_ahead, far_grad, z_far]
    grad_g, grad_u = pl.pallas_call(
        assemble_kernel,
        in_specs=[SM] + [VM] * N_DP,
        out_specs=[VM, VM],
        out_shape=[jax.ShapeDtypeStruct((G, D), bf)] * 2,
        compiler_params=params(24),
        cost_estimate=cost(0, 8 << 20),
        name="assemble",
    )(place, *parts)

    into = summed[:F].astype(f32)
    mean_stat = jnp.sum(summed[2 * F :].astype(f32), axis=0, keepdims=True) / D
    gain_here = lax.dynamic_slice_in_dim(gain, here * F, F)[:, None]
    output = (acts_t.astype(f32) + summed[F : 2 * F].astype(f32)).astype(bf)
    hat = saved_t.astype(f32) * scale_b
    stored = (dy_t.astype(f32) + scale_b * (into * gain_here - hat * mean_stat)).astype(bf)
    return (output.T[None], stored.T[None], grad_g.T[None], grad_u.T[None])


def solution(mesh):
    fine = Mesh(mesh.devices.reshape(tuple(SIZES[a] for a in AXES)), AXES)
    dp, tensor = ("x", "zl"), ("y", "c")
    placed = (
        P("s", dp, tensor),
        P("s", dp, tensor),
        P("s", dp, tensor),
        P("s", None),
        P("s", dp, tensor),
        P("s", dp, tensor),
        P("s", tensor, dp),
        P("s", None, dp, None),
        P("s", None, dp, None),
    )
    return jax.shard_map(
        local,
        mesh=fine,
        in_specs=placed,
        out_specs=(
            P("s", dp, tensor),
            P("s", dp, tensor),
            P("s", None, tensor),
            P("s", None, tensor),
        ),
        check_vma=False,
    )
```

time: 246 us -> 209 us (0.85)
  the two profiles are of different devices: /device:TPU:14 before, /device:TPU:6 now
where the time goes in v2:
time: 209 us; the launch traced here: 208 us
  starting transfers between devices  90.9 us (43%)
  waiting for transfers between devices  55.3 us (26%)
  Pallas kernels  28.4 us (14%)
  between operations  14.2 us (7%)
  local copies, waits for them, and re-layouts  13.3 us (6%)
  other arithmetic  5.7 us (3%)
    ppermute x22, starting transfers between devices, shift(): return lax.ppermute(value, axes if len(axes) > 1 else axes[0], pairs)  79.6 us
    ppermute x22, waiting for transfers between devices, shift(): return lax.ppermute(value, axes if len(axes) > 1 else axes[0], pairs)  47.8 us
    ppermute x2, starting transfers between devices, swapped(): return lax.ppermute(value, ('x', 'zl', 'y'), pairs)  11.1 us
    pallas_call x1, Pallas kernels, local(): pl.pallas_call(early_kernel, in_specs=[SM] + [HB] * N_EARLY + [HB, VM], o...  10.3 us
    unnamed x52, local copies, waits for them, and re-layouts  10.2 us
    pallas_call x1, Pallas kernels, local(): pl.pallas_call(outer_kernel, in_specs=[SM] + [HB] * N_DP + [VM] * 5, out_...  9.26 us
    ppermute x2, waiting for transfers between devices, swapped(): return lax.ppermute(value, ('x', 'zl', 'y'), pairs)  7.5 us
  transfers between devices with their start and end apart: 27, of which 17 were waited for; matrix products, arithmetic and copies ran while one was open for 3% of the time, Pallas kernels for 14%

profile of v2, /device:TPU:6, one launch (start us, length us, event | category | flops | bytes accessed | tf_op | source)
XLA Modules:
  0.0 207.8 jit_solution(11833146986557537769)
XLA Ops:
  7.2 10.9 %collective-permute-start.10 = (bf16[192,256]{1,0:T(8,128)(2,1)}, bf16[192,256]{1,0:T(8,128)(2,1)S(1)}, u32[]{:S(2)}, u32[]{:S(2)}) collective-permute-start(bf16[192,256]{1,0:T(8,128)(2,1)} %bitcast.76), channel_id=1, source_target_pairs={{0,48},{16,0},{32,16},{48,32},{1,49},{17,1},{33,17},{49,33},{2,50}... | collective-permute-start | bytes 294920 | tf_op jit(solution)/shard_map/ppermute | solution.py:36
  18.2 1.9 collective-permute-start
  20.1 1.3 pad_maximum_fusion.refs_0_
  21.4 1.3 collective-permute-done.10
  22.7 5.9 %collective-permute-done = bf16[192,256]{1,0:T(8,128)(2,1)S(1)} collective-permute-done((bf16[192,256]{1,0:T(8,128)(2,1)}, bf16[192,256]{1,0:T(8,128)(2,1)S(1)}, u32[]{:S(2)}, u32[]{:S(2)}) %collective-permute-start) | collective-permute-done | bytes 98336 | tf_op jit(solution)/shard_map/ppermute | solution.py:36
  29.4 3.6 %collective-permute-start.1 = (bf16[1008,384]{1,0:T(8,128)(2,1)S(1)}, bf16[1008,384]{1,0:T(8,128)(2,1)S(1)}, u32[]{:S(2)}, u32[]{:S(2)}) collective-permute-start(bf16[1008,384]{1,0:T(8,128)(2,1)S(1)} %pad_maximum_fusion.refs_0_), channel_id=1, source_target_pairs={{0,64},{64,0},{1,65},{65,1},{2,66},{66,2},{3,67},{67,3},{4,68},{68... | collective-permute-start | bytes 2322440 | tf_op jit(solution)/shard_map/ppermute | solution.py:36
  33.0 2.4 %collective-permute-start.2 = (bf16[1008,384]{1,0:T(8,128)(2,1)S(1)}, bf16[1008,384]{1,0:T(8,128)(2,1)}, u32[]{:S(2)}, u32[]{:S(2)}) collective-permute-start(bf16[1008,384]{1,0:T(8,128)(2,1)S(1)} %pad_maximum_fusion.refs_0_), channel_id=1, source_target_pairs={{0,128},{128,256},{256,384},{384,0},{1,129},{129,257},{257,385},{3... | collective-permute-start | bytes 2322440 | tf_op jit(solution)/shard_map/ppermute | solution.py:36
  35.3 3.5 %collective-permute-start.3 = (bf16[1008,384]{1,0:T(8,128)(2,1)S(1)}, bf16[1008,384]{1,0:T(8,128)(2,1)S(1)}, u32[]{:S(2)}, u32[]{:S(2)}) collective-permute-start(bf16[1008,384]{1,0:T(8,128)(2,1)S(1)} %pad_maximum_fusion.refs_0_), channel_id=1, source_target_pairs={{0,384},{128,0},{256,128},{384,256},{1,385},{129,1},{257,129},{385... | collective-permute-start | bytes 2322440 | tf_op jit(solution)/shard_map/ppermute | solution.py:36
  38.8 10.3 %collective-permute-done.1.refs_1_ = bf16[1008,384]{1,0:T(8,128)(2,1)S(1)} collective-permute-done((bf16[1008,384]{1,0:T(8,128)(2,1)S(1)}, bf16[1008,384]{1,0:T(8,128)(2,1)S(1)}, u32[]{:S(2)}, u32[]{:S(2)}) %collective-permute-start.1) | collective-permute-done | bytes 774176 | tf_op jit(solution)/shard_map/ppermute | solution.py:36
  49.1 3.5 %collective-permute-done.2.refs_2_ = bf16[1008,384]{1,0:T(8,128)(2,1)} collective-permute-done((bf16[1008,384]{1,0:T(8,128)(2,1)S(1)}, bf16[1008,384]{1,0:T(8,128)(2,1)}, u32[]{:S(2)}, u32[]{:S(2)}) %collective-permute-start.2) | collective-permute-done | bytes 774176 | tf_op jit(solution)/shard_map/ppermute | solution.py:36
  52.6 3.2 %collective-permute-done.3.refs_3_ = bf16[1008,384]{1,0:T(8,128)(2,1)S(1)} collective-permute-done((bf16[1008,384]{1,0:T(8,128)(2,1)S(1)}, bf16[1008,384]{1,0:T(8,128)(2,1)S(1)}, u32[]{:S(2)}, u32[]{:S(2)}) %collective-permute-start.3) | collective-permute-done | bytes 774176 | tf_op jit(solution)/shard_map/ppermute | solution.py:36
  55.8 2.2 %collective-permute-start.4 = (bf16[1008,384]{1,0:T(8,128)(2,1)S(1)}, bf16[1008,384]{1,0:T(8,128)(2,1)S(1)}, u32[]{:S(2)}, u32[]{:S(2)}) collective-permute-start(bf16[1008,384]{1,0:T(8,128)(2,1)S(1)} %collective-permute-done.1.refs_1_), channel_id=1, source_target_pairs={{0,128},{128,256},{256,384},{384,0},{1,129},{129,257},{257,385},{3... | collective-permute-start | bytes 2322440 | tf_op jit(solution)/shard_map/ppermute | solution.py:36
  58.0 3.7 %collective-permute-start.5 = (bf16[1008,384]{1,0:T(8,128)(2,1)S(1)}, bf16[1008,384]{1,0:T(8,128)(2,1)}, u32[]{:S(2)}, u32[]{:S(2)}) collective-permute-start(bf16[1008,384]{1,0:T(8,128)(2,1)S(1)} %collective-permute-done.1.refs_1_), channel_id=1, source_target_pairs={{0,384},{128,0},{256,128},{384,256},{1,385},{129,1},{257,129},{385... | collective-permute-start | bytes 2322440 | tf_op jit(solution)/shard_map/ppermute | solution.py:36
  61.7 7.1 %collective-permute-start.6 = (bf16[192,256]{1,0:T(8,128)(2,1)S(1)}, bf16[192,256]{1,0:T(8,128)(2,1)S(1)}, u32[]{:S(2)}, u32[]{:S(2)}) collective-permute-start(bf16[192,256]{1,0:T(8,128)(2,1)S(1)} %bitcast.67), channel_id=1, source_target_pairs={{0,0},{2,64},{4,128},{6,192},{8,256},{10,320},{12,384},{14,448},{6... | collective-permute-start | bytes 294920 | tf_op jit(solution)/shard_map/ppermute | solution.py:45
  68.8 4.0 %collective-permute-start.7 = (bf16[192,256]{1,0:T(8,128)(2,1)S(1)}, bf16[192,256]{1,0:T(8,128)(2,1)S(1)}, u32[]{:S(2)}, u32[]{:S(2)}) collective-permute-start(bf16[192,256]{1,0:T(8,128)(2,1)S(1)} %bitcast.68), channel_id=1, source_target_pairs={{0,256},{2,320},{4,384},{6,448},{8,0},{10,64},{12,128},{14,192},{6... | collective-permute-start | bytes 294920 | tf_op jit(solution)/shard_map/ppermute | solution.py:45
  72.8 7.5 %collective-permute-done.6 = bf16[192,256]{1,0:T(8,128)(2,1)S(1)} collective-permute-done((bf16[192,256]{1,0:T(8,128)(2,1)S(1)}, bf16[192,256]{1,0:T(8,128)(2,1)S(1)}, u32[]{:S(2)}, u32[]{:S(2)}) %collective-permute-start.6) | collective-permute-done | bytes 98336 | tf_op jit(solution)/shard_map/ppermute | solution.py:45
  82.5 3.1 %collective-permute-start.8 = (bf16[1008,384]{1,0:T(8,128)(2,1)}, bf16[1008,384]{1,0:T(8,128)(2,1)S(1)}, u32[]{:S(2)}, u32[]{:S(2)}) collective-permute-start(bf16[1008,384]{1,0:T(8,128)(2,1)} %collective-permute-done.2.refs_2_), channel_id=1, source_target_pairs={{0,128},{128,256},{256,384},{384,0},{1,129},{129,257},{257,385},{3... | collective-permute-start | bytes 2322440 | tf_op jit(solution)/shard_map/ppermute | solution.py:36
  85.6 3.2 %collective-permute-start.9 = (bf16[1008,384]{1,0:T(8,128)(2,1)}, bf16[1008,384]{1,0:T(8,128)(2,1)S(1)}, u32[]{:S(2)}, u32[]{:S(2)}) collective-permute-start(bf16[1008,384]{1,0:T(8,128)(2,1)} %collective-permute-done.5.refs_5_), channel_id=1, source_target_pairs={{0,384},{128,0},{256,128},{384,256},{1,385},{129,1},{257,129},{385... | collective-permute-start | bytes 2322440 | tf_op jit(solution)/shard_map/ppermute | solution.py:36
  88.9 1.7 copy.13.refs_7_
  91.8 10.3 %early.1 = (f32[1008,256]{1,0:T(8,128)}, f32[672,256]{1,0:T(8,128)}, bf16[2,384,256]{2,1,0:T(8,128)(2,1)}, bf16[2,384,256]{2,1,0:T(8,128)(2,1)}, f32[1,256]{1,0:T(1,128)}) custom-call(s32[8]{0:T(128)} %stack.35.place, bf16[1008,384]{1,0:T(8,128)(2,1)} %copy-done.15, bf16[1008,384]{1,0:T(8,128)(2,1)} %copy-done.16, ...), custom_call_target="tpu_custom_call" | custom-call | flops 2642411520 | bytes 33554432 | tf_op jit(solution)/shard_map/early/pallas_call | solution.py:271
  102.0 3.6 %collective-permute-done.9.w_7.refs_7_ = bf16[1008,384]{1,0:T(8,128)(2,1)S(1)} collective-permute-done((bf16[1008,384]{1,0:T(8,128)(2,1)}, bf16[1008,384]{1,0:T(8,128)(2,1)S(1)}, u32[]{:S(2)}, u32[]{:S(2)}) %collective-permute-start.9) | collective-permute-done | bytes 774176 | tf_op jit(solution)/shard_map/ppermute | solution.py:36
  105.7 1.5 copy-done.3
  108.8 1.7 inner.1
  111.3 7.3 %collective-permute-start.11 = (bf16[672,256]{1,0:T(8,128)(2,1)S(1)}, bf16[672,256]{1,0:T(8,128)(2,1)S(1)}, u32[]{:S(2)}, u32[]{:S(2)}) collective-permute-start(bf16[672,256]{1,0:T(8,128)(2,1)S(1)} %get-tuple-element.43.refs_0_), channel_id=1, source_target_pairs={{0,64},{64,0},{1,65},{65,1},{2,66},{66,2},{3,67},{67,3},{4,68},{68... | collective-permute-start | bytes 1032200 | tf_op jit(solution)/shard_map/ppermute | solution.py:36
  118.7 3.4 %collective-permute-start.12 = (bf16[672,256]{1,0:T(8,128)(2,1)S(1)}, bf16[672,256]{1,0:T(8,128)(2,1)S(1)}, u32[]{:S(2)}, u32[]{:S(2)}) collective-permute-start(bf16[672,256]{1,0:T(8,128)(2,1)S(1)} %get-tuple-element.43.refs_0_), channel_id=1, source_target_pairs={{0,128},{128,256},{256,384},{384,0},{1,129},{129,257},{257,385},{3... | collective-permute-start | bytes 1032200 | tf_op jit(solution)/shard_map/ppermute | solution.py:36
  122.1 2.4 %collective-permute-start.13 = (bf16[672,256]{1,0:T(8,128)(2,1)S(1)}, bf16[672,256]{1,0:T(8,128)(2,1)S(1)}, u32[]{:S(2)}, u32[]{:S(2)}) collective-permute-start(bf16[672,256]{1,0:T(8,128)(2,1)S(1)} %get-tuple-element.43.refs_0_), channel_id=1, source_target_pairs={{0,384},{128,0},{256,128},{384,256},{1,385},{129,1},{257,129},{385... | collective-permute-start | bytes 1032200 | tf_op jit(solution)/shard_map/ppermute | solution.py:36
  125.2 9.3 %outer.1 = bf16[16,416,256]{2,1,0:T(8,128)(2,1)} custom-call(s32[9]{0:T(128)} %concatenate.13.place, bf16[1008,384]{1,0:T(8,128)(2,1)} %copy-done.15, bf16[1008,384]{1,0:T(8,128)(2,1)} %copy-done.16, bf16[1008,384]{1,0:T(8,128)(2,1)} %collective-permute-done.2.refs_2_, bf16[1008,384]{1,0:T(8,128)(2,1)} %copy-done.17, bf16[1008,384]{1,0:T(8,128)(2,1)} %copy-done.18, ...), custom_call_target="tpu_custom_call" | custom-call | flops 2113929216 | bytes 29360128 | tf_op jit(solution)/shard_map/outer/pallas_call | solution.py:310
  134.5 2.4 %collective-permute-start.15 = (bf16[672,256]{1,0:T(8,128)(2,1)S(1)}, bf16[672,256]{1,0:T(8,128)(2,1)S(1)}, u32[]{:S(2)}, u32[]{:S(2)}) collective-permute-start(bf16[672,256]{1,0:T(8,128)(2,1)S(1)} %collective-permute-done.11.refs_1_), channel_id=1, source_target_pairs={{0,384},{128,0},{256,128},{384,256},{1,385},{129,1},{257,129},{385... | collective-permute-start | bytes 1032200 | tf_op jit(solution)/shard_map/ppermute | solution.py:36
  136.9 4.7 %collective-permute-start.14 = (bf16[672,256]{1,0:T(8,128)(2,1)S(1)}, bf16[672,256]{1,0:T(8,128)(2,1)S(1)}, u32[]{:S(2)}, u32[]{:S(2)}) collective-permute-start(bf16[672,256]{1,0:T(8,128)(2,1)S(1)} %collective-permute-done.11.refs_1_), channel_id=1, source_target_pairs={{0,128},{128,256},{256,384},{384,0},{1,129},{129,257},{257,385},{3... | collective-permute-start | bytes 1032200 | tf_op jit(solution)/shard_map/ppermute | solution.py:36
  141.6 3.4 %collective-permute-start.16 = (bf16[672,256]{1,0:T(8,128)(2,1)S(1)}, bf16[672,256]{1,0:T(8,128)(2,1)S(1)}, u32[]{:S(2)}, u32[]{:S(2)}) collective-permute-start(bf16[672,256]{1,0:T(8,128)(2,1)S(1)} %collective-permute-done.12.refs_2_), channel_id=1, source_target_pairs={{0,128},{128,256},{256,384},{384,0},{1,129},{129,257},{257,385},{3... | collective-permute-start | bytes 1032200 | tf_op jit(solution)/shard_map/ppermute | solution.py:36
  145.4 2.2 %collective-permute-start.17 = (bf16[672,256]{1,0:T(8,128)(2,1)S(1)}, bf16[672,256]{1,0:T(8,128)(2,1)S(1)}, u32[]{:S(2)}, u32[]{:S(2)}) collective-permute-start(bf16[672,256]{1,0:T(8,128)(2,1)S(1)} %collective-permute-done.15.refs_5_), channel_id=1, source_target_pairs={{0,384},{128,0},{256,128},{384,256},{1,385},{129,1},{257,129},{385... | collective-permute-start | bytes 1032200 | tf_op jit(solution)/shard_map/ppermute | solution.py:36
  147.7 2.4 %collective-permute-done.14.refs_4_ = bf16[672,256]{1,0:T(8,128)(2,1)S(1)} collective-permute-done((bf16[672,256]{1,0:T(8,128)(2,1)S(1)}, bf16[672,256]{1,0:T(8,128)(2,1)S(1)}, u32[]{:S(2)}, u32[]{:S(2)}) %collective-permute-start.14) | collective-permute-done | bytes 344096 | tf_op jit(solution)/shard_map/ppermute | solution.py:36
  150.1 3.9 %collective-permute-done.16.refs_6_ = bf16[672,256]{1,0:T(8,128)(2,1)S(1)} collective-permute-done((bf16[672,256]{1,0:T(8,128)(2,1)S(1)}, bf16[672,256]{1,0:T(8,128)(2,1)S(1)}, u32[]{:S(2)}, u32[]{:S(2)}) %collective-permute-start.16) | collective-permute-done | bytes 344096 | tf_op jit(solution)/shard_map/ppermute | solution.py:36
  154.7 1.1 collective-permute-done.17.refs_7_
  156.5 1.9 copy-done
  160.3 3.6 %grad.1 = (bf16[672,384]{1,0:T(8,128)(2,1)S(1)}, bf16[672,384]{1,0:T(8,128)(2,1)S(1)}) custom-call(s32[8]{0:T(128)S(1)} %copy-done.11, bf16[672,256]{1,0:T(8,128)(2,1)S(1)} %get-tuple-element.43.refs_0_, bf16[672,256]{1,0:T(8,128)(2,1)S(1)} %collective-permute-done.11.refs_1_, bf16[672,256]{1,0:T(8,128)(2,1)S(1)} %collective-permute-done.12.refs_2_, ...), custom_call_target="tpu_custom_call" | custom-call | flops 2113929216 | bytes 8388608 | tf_op jit(solution)/shard_map/grad/pallas_call | solution.py:329
  163.9 2.2 %collective-permute-start.18 = (bf16[672,384]{1,0:T(8,128)(2,1)S(1)}, bf16[672,384]{1,0:T(8,128)(2,1)S(1)}, u32[]{:S(2)}, u32[]{:S(2)}) collective-permute-start(bf16[672,384]{1,0:T(8,128)(2,1)S(1)} %get-tuple-element.50.refs_0_), channel_id=1, source_target_pairs={{0,64},{64,0},{1,65},{65,1},{2,66},{66,2},{3,67},{67,3},{4,68},{68... | collective-permute-start | bytes 1548296 | tf_op jit(solution)/shard_map/ppermute | solution.py:36
  166.1 4.6 %collective-permute-start.19 = (bf16[672,384]{1,0:T(8,128)(2,1)S(1)}, bf16[672,384]{1,0:T(8,128)(2,1)S(1)}, u32[]{:S(2)}, u32[]{:S(2)}) collective-permute-start(bf16[672,384]{1,0:T(8,128)(2,1)S(1)} %get-tuple-element.50.refs_0_), channel_id=1, source_target_pairs={{0,128},{128,256},{256,384},{384,0},{1,129},{129,257},{257,385},{3... | collective-permute-start | bytes 1548296 | tf_op jit(solution)/shard_map/ppermute | solution.py:36
  170.7 1.9 collective-permute-start.20
  172.6 3.7 %collective-permute-start.23 = (bf16[672,384]{1,0:T(8,128)(2,1)S(1)}, bf16[672,384]{1,0:T(8,128)(2,1)S(1)}, u32[]{:S(2)}, u32[]{:S(2)}) collective-permute-start(bf16[672,384]{1,0:T(8,128)(2,1)S(1)} %get-tuple-element.51.refs_6_), channel_id=1, source_target_pairs={{0,64},{64,0},{1,65},{65,1},{2,66},{66,2},{3,67},{67,3},{4,68},{68... | collective-permute-start | bytes 1548296 | tf_op jit(solution)/shard_map/ppermute | solution.py:36
  176.3 1.5 collective-permute-done.18.refs_1_
  177.7 5.1 %collective-permute-start.21 = (bf16[672,384]{1,0:T(8,128)(2,1)S(1)}, bf16[672,384]{1,0:T(8,128)(2,1)}, u32[]{:S(2)}, u32[]{:S(2)}) collective-permute-start(bf16[672,384]{1,0:T(8,128)(2,1)S(1)} %collective-permute-done.18.refs_1_), channel_id=1, source_target_pairs={{0,128},{128,256},{256,384},{384,0},{1,129},{129,257},{257,385},{3... | collective-permute-start | bytes 1548296 | tf_op jit(solution)/shard_map/ppermute | solution.py:36
  182.9 1.9 collective-permute-start.22
  185.1 1.5 collective-permute-done.23.refs_7_
  186.7 2.8 %collective-permute-done.21.refs_4_ = bf16[672,384]{1,0:T(8,128)(2,1)} collective-permute-done((bf16[672,384]{1,0:T(8,128)(2,1)S(1)}, bf16[672,384]{1,0:T(8,128)(2,1)}, u32[]{:S(2)}, u32[]{:S(2)}) %collective-permute-start.21) | collective-permute-done | bytes 516128 | tf_op jit(solution)/shard_map/ppermute | solution.py:36
  189.5 5.7 %collective-permute-done.22.refs_5_ = bf16[672,384]{1,0:T(8,128)(2,1)} collective-permute-done((bf16[672,384]{1,0:T(8,128)(2,1)S(1)}, bf16[672,384]{1,0:T(8,128)(2,1)}, u32[]{:S(2)}, u32[]{:S(2)}) %collective-permute-start.22) | collective-permute-done | bytes 516128 | tf_op jit(solution)/shard_map/ppermute | solution.py:36
  195.2 3.6 %assemble.1 = (bf16[336,3072]{1,0:T(8,128)(2,1)}, bf16[336,3072]{1,0:T(8,128)(2,1)}) custom-call(s32[8]{0:T(128)S(1)} %copy-done.11, bf16[672,384]{1,0:T(8,128)(2,1)S(1)} %get-tuple-element.50.refs_0_, bf16[672,384]{1,0:T(8,128)(2,1)S(1)} %collective-permute-done.18.refs_1_, bf16[672,384]{1,0:T(8,128)(2,1)S(1)} %collective-permute-done.19.refs_2_, ...), custom_call_target="tpu_custom_call" | custom-call | bytes 8388608 | tf_op jit(solution)/shard_map/assemble/pallas_call | solution.py:346
  199.5 1.7 fusion.6
  (78 shorter events, 12.3 us)
Async XLA Ops:
  7.2 21.4 %copy-start.19 = (bf16[1,256,192]{1,2,0:T(8,128)(2,1)S(1)}, bf16[1,256,192]{1,2,0:T(8,128)(2,1)}, u32[]{:S(2)}) copy-start(bf16[1,256,192]{1,2,0:T(8,128)(2,1)} %param.10) | copy-start | bytes 294916
  7.2 84.6 %all-gather.5.cloned.1.call-start = ((), (), s32[]{:S(2)}) async-start(), calls=%async_computation.2 | async-start | bytes 5013504 | tf_op jit(solution)/shard_map/all_gather | solution.py:260
  7.2 15.4 %collective-permute-start.10 = (bf16[192,256]{1,0:T(8,128)(2,1)}, bf16[192,256]{1,0:T(8,128)(2,1)S(1)}, u32[]{:S(2)}, u32[]{:S(2)}) collective-permute-start(bf16[192,256]{1,0:T(8,128)(2,1)} %bitcast.76), channel_id=1, source_target_pairs={{0,48},{16,0},{32,16},{48,32},{1,49},{17,1},{33,17},{49,33},{2,50}... | collective-permute-start | bytes 294920 | tf_op jit(solution)/shard_map/ppermute | solution.py:36
  18.2 10.4 %collective-permute-start = (bf16[192,256]{1,0:T(8,128)(2,1)}, bf16[192,256]{1,0:T(8,128)(2,1)S(1)}, u32[]{:S(2)}, u32[]{:S(2)}) collective-permute-start(bf16[192,256]{1,0:T(8,128)(2,1)} %bitcast.77), channel_id=1, source_target_pairs={{0,16},{16,32},{32,48},{48,0},{1,17},{17,33},{33,49},{49,1},{2,18}... | collective-permute-start | bytes 294920 | tf_op jit(solution)/shard_map/ppermute | solution.py:36
  20.1 68.8 %copy-start.10 = (f32[1,3072]{1,0:T(1,128)S(1)}, f32[1,3072]{1,0:T(1,128)}, u32[]{:S(2)}) copy-start(f32[1,3072]{1,0:T(1,128)} %refs_10_.1) | copy-start | bytes 36868
  21.4 69.2 %copy-start.15 = (bf16[1008,384]{1,0:T(8,128)(2,1)}, bf16[1008,384]{1,0:T(8,128)(2,1)S(1)}, u32[]{:S(2)}) copy-start(bf16[1008,384]{1,0:T(8,128)(2,1)S(1)} %pad_maximum_fusion.refs_0_) | copy-start | bytes 2322436
  28.6 62.0 %copy-start.20 = (bf16[192,256]{1,0:T(8,128)(2,1)}, bf16[192,256]{1,0:T(8,128)(2,1)S(1)}, u32[]{:S(2)}) copy-start(bf16[192,256]{1,0:T(8,128)(2,1)S(1)} %collective-permute-done) | copy-start | bytes 294916
  28.6 62.6 %copy-start.22 = (f32[1,2,256,4]{2,3,1,0:T(4,128)S(1)}, f32[1,2,256,4]{2,3,1,0:T(4,128)}, u32[]{:S(2)}) copy-start(f32[1,2,256,4]{2,3,1,0:T(4,128)} %param.17) | copy-start | bytes 24580
  28.6 62.6 %copy-start.23 = (s32[1,2,256,4]{2,3,1,0:T(4,128)S(1)}, s32[1,2,256,4]{2,3,1,0:T(4,128)}, u32[]{:S(2)}) copy-start(s32[1,2,256,4]{2,3,1,0:T(4,128)} %param.16) | copy-start | bytes 24580
  29.3 118.3 %all-gather.7.cloned.1.call-start = ((), (), s32[]{:S(2)}) async-start(), calls=%async_computation.3 | async-start | bytes 3342336 | tf_op jit(solution)/shard_map/all_gather | solution.py:263
  29.4 19.7 %collective-permute-start.1 = (bf16[1008,384]{1,0:T(8,128)(2,1)S(1)}, bf16[1008,384]{1,0:T(8,128)(2,1)S(1)}, u32[]{:S(2)}, u32[]{:S(2)}) collective-permute-start(bf16[1008,384]{1,0:T(8,128)(2,1)S(1)} %pad_maximum_fusion.refs_0_), channel_id=1, source_target_pairs={{0,64},{64,0},{1,65},{65,1},{2,66},{66,2},{3,67},{67,3},{4,68},{68... | collective-permute-start | bytes 2322440 | tf_op jit(solution)/shard_map/ppermute | solution.py:36
  33.0 19.6 %collective-permute-start.2 = (bf16[1008,384]{1,0:T(8,128)(2,1)S(1)}, bf16[1008,384]{1,0:T(8,128)(2,1)}, u32[]{:S(2)}, u32[]{:S(2)}) collective-permute-start(bf16[1008,384]{1,0:T(8,128)(2,1)S(1)} %pad_maximum_fusion.refs_0_), channel_id=1, source_target_pairs={{0,128},{128,256},{256,384},{384,0},{1,129},{129,257},{257,385},{3... | collective-permute-start | bytes 2322440 | tf_op jit(solution)/shard_map/ppermute | solution.py:36
  35.3 20.5 %collective-permute-start.3 = (bf16[1008,384]{1,0:T(8,128)(2,1)S(1)}, bf16[1008,384]{1,0:T(8,128)(2,1)S(1)}, u32[]{:S(2)}, u32[]{:S(2)}) collective-permute-start(bf16[1008,384]{1,0:T(8,128)(2,1)S(1)} %pad_maximum_fusion.refs_0_), channel_id=1, source_target_pairs={{0,384},{128,0},{256,128},{384,256},{1,385},{129,1},{257,129},{385... | collective-permute-start | bytes 2322440 | tf_op jit(solution)/shard_map/ppermute | solution.py:36
  49.1 8.9 %copy-start.16 = (bf16[1008,384]{1,0:T(8,128)(2,1)}, bf16[1008,384]{1,0:T(8,128)(2,1)S(1)}, u32[]{:S(2)}) copy-start(bf16[1008,384]{1,0:T(8,128)(2,1)S(1)} %collective-permute-done.1.refs_1_) | copy-start | bytes 2322436
  55.8 24.5 %copy-start.17 = (bf16[1008,384]{1,0:T(8,128)(2,1)}, bf16[1008,384]{1,0:T(8,128)(2,1)S(1)}, u32[]{:S(2)}) copy-start(bf16[1008,384]{1,0:T(8,128)(2,1)S(1)} %collective-permute-done.3.refs_3_) | copy-start | bytes 2322436
  55.8 24.5 %collective-permute-start.4 = (bf16[1008,384]{1,0:T(8,128)(2,1)S(1)}, bf16[1008,384]{1,0:T(8,128)(2,1)S(1)}, u32[]{:S(2)}, u32[]{:S(2)}) collective-permute-start(bf16[1008,384]{1,0:T(8,128)(2,1)S(1)} %collective-permute-done.1.refs_1_), channel_id=1, source_target_pairs={{0,128},{128,256},{256,384},{384,0},{1,129},{129,257},{257,385},{3... | collective-permute-start | bytes 2322440 | tf_op jit(solution)/shard_map/ppermute | solution.py:36
  58.0 23.7 %collective-permute-start.5 = (bf16[1008,384]{1,0:T(8,128)(2,1)S(1)}, bf16[1008,384]{1,0:T(8,128)(2,1)}, u32[]{:S(2)}, u32[]{:S(2)}) collective-permute-start(bf16[1008,384]{1,0:T(8,128)(2,1)S(1)} %collective-permute-done.1.refs_1_), channel_id=1, source_target_pairs={{0,384},{128,0},{256,128},{384,256},{1,385},{129,1},{257,129},{385... | collective-permute-start | bytes 2322440 | tf_op jit(solution)/shard_map/ppermute | solution.py:36
  61.7 18.6 %collective-permute-start.6 = (bf16[192,256]{1,0:T(8,128)(2,1)S(1)}, bf16[192,256]{1,0:T(8,128)(2,1)S(1)}, u32[]{:S(2)}, u32[]{:S(2)}) collective-permute-start(bf16[192,256]{1,0:T(8,128)(2,1)S(1)} %bitcast.67), channel_id=1, source_target_pairs={{0,0},{2,64},{4,128},{6,192},{8,256},{10,320},{12,384},{14,448},{6... | collective-permute-start | bytes 294920 | tf_op jit(solution)/shard_map/ppermute | solution.py:45
  68.8 11.5 %collective-permute-start.7 = (bf16[192,256]{1,0:T(8,128)(2,1)S(1)}, bf16[192,256]{1,0:T(8,128)(2,1)S(1)}, u32[]{:S(2)}, u32[]{:S(2)}) collective-permute-start(bf16[192,256]{1,0:T(8,128)(2,1)S(1)} %bitcast.68), channel_id=1, source_target_pairs={{0,256},{2,320},{4,384},{6,448},{8,0},{10,64},{12,128},{14,192},{6... | collective-permute-start | bytes 294920 | tf_op jit(solution)/shard_map/ppermute | solution.py:45
  82.4 116.3 %reduce-scatter.2.cloned.1.call-start = ((), (), s32[]{:S(2)}) async-start(), calls=%async_computation.1 | async-start | bytes 3620864 | tf_op jit(solution)/shard_map/reduce_scatter | solution.py:327
  82.5 19.6 %collective-permute-start.8 = (bf16[1008,384]{1,0:T(8,128)(2,1)}, bf16[1008,384]{1,0:T(8,128)(2,1)S(1)}, u32[]{:S(2)}, u32[]{:S(2)}) collective-permute-start(bf16[1008,384]{1,0:T(8,128)(2,1)} %collective-permute-done.2.refs_2_), channel_id=1, source_target_pairs={{0,128},{128,256},{256,384},{384,0},{1,129},{129,257},{257,385},{3... | collective-permute-start | bytes 2322440 | tf_op jit(solution)/shard_map/ppermute | solution.py:36
  85.6 20.1 %collective-permute-start.9 = (bf16[1008,384]{1,0:T(8,128)(2,1)}, bf16[1008,384]{1,0:T(8,128)(2,1)S(1)}, u32[]{:S(2)}, u32[]{:S(2)}) collective-permute-start(bf16[1008,384]{1,0:T(8,128)(2,1)} %collective-permute-done.5.refs_5_), channel_id=1, source_target_pairs={{0,384},{128,0},{256,128},{384,256},{1,385},{129,1},{257,129},{385... | collective-permute-start | bytes 2322440 | tf_op jit(solution)/shard_map/ppermute | solution.py:36
  91.8 13.9 %slice-start = ((s8[4718592]{0:T(1024)(128)(4,1)}), s8[4194304]{0:T(1024)(128)(4,1)S(1)}, s32[]{:S(2)}) async-start(s8[4718592]{0:T(1024)(128)(4,1)} %bitcast.58), calls=%async_computation.4 | async-start | bytes 8388608
  91.8 13.9 %slice-start.1 = ((s8[4718592]{0:T(1024)(128)(4,1)}), s8[524288]{0:T(1024)(128)(4,1)S(1)}, s32[]{:S(2)}) async-start(s8[4718592]{0:T(1024)(128)(4,1)} %bitcast.58), calls=%async_computation.5 | async-start | bytes 1048576
  91.8 13.9 %copy-start.11 = (s32[8]{0:T(128)S(1)}, s32[8]{0:T(128)}, u32[]{:S(2)}) copy-start(s32[8]{0:T(128)} %stack.35.place) | copy-start | bytes 100
  102.0 8.5 %copy-start.1 = (bf16[1008,384]{1,0:T(8,128)(2,1)}, bf16[1008,384]{1,0:T(8,128)(2,1)S(1)}, u32[]{:S(2)}) copy-start(bf16[1008,384]{1,0:T(8,128)(2,1)S(1)} %collective-permute-done.8.w_6.refs_6_) | copy-start | bytes 2322436
  105.6 5.0 %copy-start.2 = (bf16[1008,384]{1,0:T(8,128)(2,1)}, bf16[1008,384]{1,0:T(8,128)(2,1)S(1)}, u32[]{:S(2)}) copy-start(bf16[1008,384]{1,0:T(8,128)(2,1)S(1)} %collective-permute-done.9.w_7.refs_7_) | copy-start | bytes 2322436
  105.6 1.5 copy-start.3
  107.2 1.0 copy-start.4
  111.3 7.4 %copy-start.14 = (f32[1,256]{1,0:T(1,128)}, f32[1,256]{1,0:T(1,128)S(1)}, u32[]{:S(2)}) copy-start(f32[1,256]{1,0:T(1,128)S(1)} %get-tuple-element.42.refs_12_) | copy-start | bytes 3076
  111.3 23.2 %collective-permute-start.11 = (bf16[672,256]{1,0:T(8,128)(2,1)S(1)}, bf16[672,256]{1,0:T(8,128)(2,1)S(1)}, u32[]{:S(2)}, u32[]{:S(2)}) collective-permute-start(bf16[672,256]{1,0:T(8,128)(2,1)S(1)} %get-tuple-element.43.refs_0_), channel_id=1, source_target_pairs={{0,64},{64,0},{1,65},{65,1},{2,66},{66,2},{3,67},{67,3},{4,68},{68... | collective-permute-start | bytes 1032200 | tf_op jit(solution)/shard_map/ppermute | solution.py:36
  118.7 15.8 %collective-permute-start.12 = (bf16[672,256]{1,0:T(8,128)(2,1)S(1)}, bf16[672,256]{1,0:T(8,128)(2,1)S(1)}, u32[]{:S(2)}, u32[]{:S(2)}) collective-permute-start(bf16[672,256]{1,0:T(8,128)(2,1)S(1)} %get-tuple-element.43.refs_0_), channel_id=1, source_target_pairs={{0,128},{128,256},{256,384},{384,0},{1,129},{129,257},{257,385},{3... | collective-permute-start | bytes 1032200 | tf_op jit(solution)/shard_map/ppermute | solution.py:36
  122.1 12.4 %collective-permute-start.13 = (bf16[672,256]{1,0:T(8,128)(2,1)S(1)}, bf16[672,256]{1,0:T(8,128)(2,1)S(1)}, u32[]{:S(2)}, u32[]{:S(2)}) collective-permute-start(bf16[672,256]{1,0:T(8,128)(2,1)S(1)} %get-tuple-element.43.refs_0_), channel_id=1, source_target_pairs={{0,384},{128,0},{256,128},{384,256},{1,385},{129,1},{257,129},{385... | collective-permute-start | bytes 1032200 | tf_op jit(solution)/shard_map/ppermute | solution.py:36
  134.5 10.9 %collective-permute-start.15 = (bf16[672,256]{1,0:T(8,128)(2,1)S(1)}, bf16[672,256]{1,0:T(8,128)(2,1)S(1)}, u32[]{:S(2)}, u32[]{:S(2)}) collective-permute-start(bf16[672,256]{1,0:T(8,128)(2,1)S(1)} %collective-permute-done.11.refs_1_), channel_id=1, source_target_pairs={{0,384},{128,0},{256,128},{384,256},{1,385},{129,1},{257,129},{385... | collective-permute-start | bytes 1032200 | tf_op jit(solution)/shard_map/ppermute | solution.py:36
  136.9 13.2 %collective-permute-start.14 = (bf16[672,256]{1,0:T(8,128)(2,1)S(1)}, bf16[672,256]{1,0:T(8,128)(2,1)S(1)}, u32[]{:S(2)}, u32[]{:S(2)}) collective-permute-start(bf16[672,256]{1,0:T(8,128)(2,1)S(1)} %collective-permute-done.11.refs_1_), channel_id=1, source_target_pairs={{0,128},{128,256},{256,384},{384,0},{1,129},{129,257},{257,385},{3... | collective-permute-start | bytes 1032200 | tf_op jit(solution)/shard_map/ppermute | solution.py:36
  141.6 12.3 %collective-permute-start.16 = (bf16[672,256]{1,0:T(8,128)(2,1)S(1)}, bf16[672,256]{1,0:T(8,128)(2,1)S(1)}, u32[]{:S(2)}, u32[]{:S(2)}) collective-permute-start(bf16[672,256]{1,0:T(8,128)(2,1)S(1)} %collective-permute-done.12.refs_2_), channel_id=1, source_target_pairs={{0,128},{128,256},{256,384},{384,0},{1,129},{129,257},{257,385},{3... | collective-permute-start | bytes 1032200 | tf_op jit(solution)/shard_map/ppermute | solution.py:36
  145.4 10.3 %collective-permute-start.17 = (bf16[672,256]{1,0:T(8,128)(2,1)S(1)}, bf16[672,256]{1,0:T(8,128)(2,1)S(1)}, u32[]{:S(2)}, u32[]{:S(2)}) collective-permute-start(bf16[672,256]{1,0:T(8,128)(2,1)S(1)} %collective-permute-done.15.refs_5_), channel_id=1, source_target_pairs={{0,384},{128,0},{256,128},{384,256},{1,385},{129,1},{257,129},{385... | collective-permute-start | bytes 1032200 | tf_op jit(solution)/shard_map/ppermute | solution.py:36
  156.5 1.9 copy-start
  158.4 1.0 copy-start.7
  159.3 1.0 copy-start.9
  163.9 13.8 %collective-permute-start.18 = (bf16[672,384]{1,0:T(8,128)(2,1)S(1)}, bf16[672,384]{1,0:T(8,128)(2,1)S(1)}, u32[]{:S(2)}, u32[]{:S(2)}) collective-permute-start(bf16[672,384]{1,0:T(8,128)(2,1)S(1)} %get-tuple-element.50.refs_0_), channel_id=1, source_target_pairs={{0,64},{64,0},{1,65},{65,1},{2,66},{66,2},{3,67},{67,3},{4,68},{68... | collective-permute-start | bytes 1548296 | tf_op jit(solution)/shard_map/ppermute | solution.py:36
  166.1 18.8 %collective-permute-start.19 = (bf16[672,384]{1,0:T(8,128)(2,1)S(1)}, bf16[672,384]{1,0:T(8,128)(2,1)S(1)}, u32[]{:S(2)}, u32[]{:S(2)}) collective-permute-start(bf16[672,384]{1,0:T(8,128)(2,1)S(1)} %get-tuple-element.50.refs_0_), channel_id=1, source_target_pairs={{0,128},{128,256},{256,384},{384,0},{1,129},{129,257},{257,385},{3... | collective-permute-start | bytes 1548296 | tf_op jit(solution)/shard_map/ppermute | solution.py:36
  170.7 14.5 %collective-permute-start.20 = (bf16[672,384]{1,0:T(8,128)(2,1)S(1)}, bf16[672,384]{1,0:T(8,128)(2,1)S(1)}, u32[]{:S(2)}, u32[]{:S(2)}) collective-permute-start(bf16[672,384]{1,0:T(8,128)(2,1)S(1)} %get-tuple-element.50.refs_0_), channel_id=1, source_target_pairs={{0,384},{128,0},{256,128},{384,256},{1,385},{129,1},{257,129},{385... | collective-permute-start | bytes 1548296 | tf_op jit(solution)/shard_map/ppermute | solution.py:36
  172.6 14.1 %collective-permute-start.23 = (bf16[672,384]{1,0:T(8,128)(2,1)S(1)}, bf16[672,384]{1,0:T(8,128)(2,1)S(1)}, u32[]{:S(2)}, u32[]{:S(2)}) collective-permute-start(bf16[672,384]{1,0:T(8,128)(2,1)S(1)} %get-tuple-element.51.refs_6_), channel_id=1, source_target_pairs={{0,64},{64,0},{1,65},{65,1},{2,66},{66,2},{3,67},{67,3},{4,68},{68... | collective-permute-start | bytes 1548296 | tf_op jit(solution)/shard_map/ppermute | solution.py:36
  177.7 11.7 %collective-permute-start.21 = (bf16[672,384]{1,0:T(8,128)(2,1)S(1)}, bf16[672,384]{1,0:T(8,128)(2,1)}, u32[]{:S(2)}, u32[]{:S(2)}) collective-permute-start(bf16[672,384]{1,0:T(8,128)(2,1)S(1)} %collective-permute-done.18.refs_1_), channel_id=1, source_target_pairs={{0,128},{128,256},{256,384},{384,0},{1,129},{129,257},{257,385},{3... | collective-permute-start | bytes 1548296 | tf_op jit(solution)/shard_map/ppermute | solution.py:36
  182.9 12.3 %collective-permute-start.22 = (bf16[672,384]{1,0:T(8,128)(2,1)S(1)}, bf16[672,384]{1,0:T(8,128)(2,1)}, u32[]{:S(2)}, u32[]{:S(2)}) collective-permute-start(bf16[672,384]{1,0:T(8,128)(2,1)S(1)} %collective-permute-done.18.refs_1_), channel_id=1, source_target_pairs={{0,384},{128,0},{256,128},{384,256},{1,385},{129,1},{257,129},{385... | collective-permute-start | bytes 1548296 | tf_op jit(solution)/shard_map/ppermute | solution.py:36
  184.9 14.6 %copy-start.13 = (f32[1,256]{1,0:T(1,128)S(1)}, f32[1,256]{1,0:T(1,128)}, u32[]{:S(2)}) copy-start(f32[1,256]{1,0:T(1,128)} %get-tuple-element.38.scale_ref) | copy-start | bytes 3076
  184.9 14.6 %copy-start.21 = (bf16[192,256]{1,0:T(8,128)(2,1)S(1)}, bf16[192,256]{1,0:T(8,128)(2,1)}, u32[]{:S(2)}) copy-start(bf16[192,256]{1,0:T(8,128)(2,1)} %copy-done.20) | copy-start | bytes 294916
  (5 other events, 3.8 us)
Sparse Core Ops, SparseCore 0:
  29.5 42.5 all-gather.4
  82.5 48.5 all-gather.6
  134.7 63.2 reduce-scatter.1

commit v3 on v2

--- a/solution.py
+++ b/solution.py
@@ -16,7 +16,8 @@
 N_T = 16
 N_DP = 8
 DS = D // N_DP
-N_EARLY = 6
+N_EARLY = 7
+CUT = 512
 TILE = 112
 OFFSETS = ((0, 0), (0, 1), (-1, 0), (1, 0), (-1, 1), (1, 1), (2, 0), (2, 1))
 
@@ -45,20 +46,31 @@
     return lax.ppermute(value, ("x", "zl", "y"), pairs)
 
 
-def gather_ring(own, rider=None):
+def gather_ring(own):
+    first = shift(own, zl=1)
+    behind = shift(own, x=1)
+    ahead = shift(own, x=-1)
+    z, behind, ahead = lax.optimization_barrier((first, behind, ahead))
+    z_behind = shift(z, x=1)
+    z_ahead = shift(z, x=-1)
+    across = shift(behind, x=1)
+    z_across = shift(z_ahead, x=-1)
+    return [own, z, behind, ahead, z_behind, z_ahead, across, z_across], first
+
+
+def gather_weights(own, block, ready):
     z = shift(own, zl=1)
     behind = shift(own, x=1)
     ahead = shift(own, x=-1)
-    z, behind, ahead = lax.optimization_barrier((z, behind, ahead))
+    z, behind, ahead, block, ready = lax.optimization_barrier((z, behind, ahead, block, ready))
     z_behind = shift(z, x=1)
-    z_ahead = shift(z, x=-1)
-    riders = ()
-    if rider is not None:
-        riders = tuple(rider(z))
-        z_behind, z_ahead, *riders = lax.optimization_barrier((z_behind, z_ahead, *riders))
-    across = shift(behind, x=1)
-    z_across = shift(z_ahead, x=-1)
-    return [own, z, behind, ahead, z_behind, z_ahead, across, z_across], riders
+    across = shift(ahead, x=-1)
+    z_ahead = shift(ahead, zl=1)
+    near, far = swapped(block, 0), swapped(block, 2)
+    z_behind, across, z_ahead, near, far = lax.optimization_barrier((z_behind, across, z_ahead, near, far))
+    top = shift(z_behind[:CUT], x=1)
+    bottom = shift(z_ahead[CUT:], x=-1)
+    return [own, z, behind, ahead, z_behind, z_ahead, across], (top, bottom), (near, far), ready
 
 
 def after(value, earlier):
@@ -70,16 +82,13 @@
     return jnp.stack([((x + dx) % 4) * 2 + (zl + dz) % 2 for dx, dz in OFFSETS]).astype(jnp.int32)
 
 
-def normal_into(act_ref, gain_ref, out_ref):
-    total = jnp.zeros((1, TOK), jnp.float32)
+def gained_into(act_ref, gain_ref, out_ref):
+    total = jnp.zeros((8, TOK), jnp.float32)
     for t in range(N_T):
         v = act_ref[t].astype(jnp.float32)
-        total = total + jnp.sum(v * v, axis=0, keepdims=True)
-    scale = lax.rsqrt(total / D + EPS)
-    for t in range(N_T):
-        v = act_ref[t].astype(jnp.float32)
-        out_ref[t * F : (t + 1) * F, :] = ((v * scale) * gain_ref[t * F : (t + 1) * F, :]).astype(jnp.bfloat16)
-    return scale
+        total = total + jnp.sum((v * v).reshape(F // 8, 8, TOK), axis=0)
+        out_ref[t * F : (t + 1) * F, :] = (v * gain_ref[t * F : (t + 1) * F, :]).astype(jnp.bfloat16)
+    return lax.rsqrt(jnp.sum(total, axis=0, keepdims=True) / D + EPS)
 
 
 def fetch(pairs, sems):
@@ -91,22 +100,21 @@
 
 def early_kernel(place, *refs):
     w_from = refs[:N_EARLY]
-    acts, gain, b_out, f_out, nb_out, nf_out, scale_out, saved, dy, act, w, normal_b, normal_f, sems = refs[N_EARLY:]
+    acts, gain, b_out, f_out, nb_out, nf_out, scales_out, saved, dy, act, w, normal_b, normal_f, sems = refs[N_EARLY:]
     copies = fetch(
         [(acts.at[:, 2], saved), (acts.at[:, 0], act), (acts.at[:, 1], dy)]
         + [(w_from[r], w.at[r]) for r in range(N_EARLY)],
         sems,
     )
     copies[0].wait()
-    scale_out[...] = normal_into(saved, gain, normal_b)
+    scales_out[0:1, :] = gained_into(saved, gain, normal_b)
     copies[1].wait()
-    normal_into(act, gain, normal_f)
+    scales_out[1:2, :] = gained_into(act, gain, normal_f)
     for copy in copies[2:]:
         copy.wait()
-    for i in range(N_DP - N_EARLY):
-        rows = pl.ds(pl.multiple_of(place[N_EARLY + i] * DS, DS), DS)
-        nb_out[i] = normal_b[rows, :]
-        nf_out[i] = normal_f[rows, :]
+    rows = pl.ds(pl.multiple_of(place[N_EARLY] * DS, DS), DS)
+    nb_out[...] = normal_b[rows, :]
+    nf_out[...] = normal_f[rows, :]
     for m in range(0, G, TILE):
         sums = [jnp.zeros((TILE, TOK), jnp.float32) for _ in range(5)]
         for r in range(N_EARLY):
@@ -125,21 +133,28 @@
             f_out[k * G + m : k * G + m + TILE, :] = sums[3 + k]
 
 
-def inner_kernel(place, w_6, w_7, early, normal, acts, weight, scale_ref, dg_out, dgs_out, stat_out, dy, sems):
-    w = (w_6, w_7)
-    copies = fetch([(acts.at[pl.ds(2 * place[N_EARLY + i], 2), 1], dy.at[i]) for i in range(N_DP - N_EARLY)], sems)
+def inner_kernel(place, top, bottom, early_from, n_from, acts, weight, scales, dg_out, dgs_out, stat_out, w, early, normal, dy, sems):
+    copies = fetch(
+        [
+            (n_from, normal),
+            (acts.at[pl.ds(2 * place[N_EARLY], 2), 1], dy),
+            (top, w.at[:CUT, :]),
+            (bottom, w.at[CUT:, :]),
+            (early_from, early),
+        ],
+        sems,
+    )
+    scale = scales[0:1, :]
+    row = weight[...]
+    stat = jnp.zeros((1, TOK), jnp.float32)
     for copy in copies:
         copy.wait()
-    scale = scale_ref[...]
-    row = weight[...]
-    stat = jnp.zeros((1, TOK), jnp.float32)
+    n, g = normal[...], dy[...].reshape(DS, TOK)
     for m in range(0, G, TILE):
         gate, up, hid = (early[k * G + m : k * G + m + TILE, :] for k in range(3))
-        for i in range(N_DP - N_EARLY):
-            n, g = normal[i], dy[i].reshape(DS, TOK)
-            gate = gate + jnp.dot(w[i][m : m + TILE, :], n, preferred_element_type=jnp.float32)
-            up = up + jnp.dot(w[i][G + m : G + m + TILE, :], n, preferred_element_type=jnp.float32)
-            hid = hid + jnp.dot(w[i][2 * G + m : 2 * G + m + TILE, :], g, preferred_element_type=jnp.float32)
+        gate = scale * (gate + jnp.dot(w[m : m + TILE, :], n, preferred_element_type=jnp.float32))
+        up = scale * (up + jnp.dot(w[G + m : G + m + TILE, :], n, preferred_element_type=jnp.float32))
+        hid = hid + jnp.dot(w[2 * G + m : 2 * G + m + TILE, :], g, preferred_element_type=jnp.float32)
         sg = jax.nn.sigmoid(gate)
         hid = hid * row
         dgate = hid * up * (sg * (1.0 + gate * (1.0 - sg)))
@@ -156,26 +171,26 @@
 
 
 def outer_kernel(place, *refs):
-    w_from = refs[:N_DP]
-    dg, early, normal, weight, stat, out, w, hidden, dg_t, hid_t, sems = refs[N_DP:]
-    order = list(range(N_EARLY, N_DP)) + list(range(N_EARLY))
-    copies = fetch([(w_from[r], w.at[r]) for r in order], sems)
+    w_from = refs[:N_EARLY]
+    top, bottom, dg, early, normal, weight, scales, stat, out, w, hidden, dg_t, hid_t, sems = refs[N_EARLY:]
+    order = [N_EARLY] + list(range(N_EARLY))
+    pairs = [(top, w.at[N_EARLY, :CUT, :]), (bottom, w.at[N_EARLY, CUT:, :])]
+    copies = fetch(pairs + [(w_from[r], w.at[r]) for r in range(N_EARLY)], sems)
     dg_t[...] = dg[...].astype(jnp.float32).T.astype(jnp.bfloat16)
     row = weight[...]
-    last = N_DP - N_EARLY
-    for copy in copies[:last]:
-        copy.wait()
+    scale = scales[1:2, :]
+    copies[0].wait()
+    copies[1].wait()
+    n = normal[...]
     for m in range(0, G, TILE):
         gate, up = (early[k * G + m : k * G + m + TILE, :] for k in range(2))
-        for i in range(last):
-            n = normal[i]
-            gate = gate + jnp.dot(w[N_EARLY + i, m : m + TILE, :], n, preferred_element_type=jnp.float32)
-            up = up + jnp.dot(w[N_EARLY + i, G + m : G + m + TILE, :], n, preferred_element_type=jnp.float32)
+        gate = scale * (gate + jnp.dot(w[N_EARLY, m : m + TILE, :], n, preferred_element_type=jnp.float32))
+        up = scale * (up + jnp.dot(w[N_EARLY, G + m : G + m + TILE, :], n, preferred_element_type=jnp.float32))
         hidden[m : m + TILE, :] = gate * jax.nn.sigmoid(gate) * up * row
     hid_t[...] = hidden[...].T.astype(jnp.bfloat16)
     for k, r in enumerate(order):
-        if k >= last:
-            copies[k].wait()
+        if k:
+            copies[k + 1].wait()
         at = pl.ds(2 * place[r], 2)
         into = jnp.dot(dg_t[...], w[r, : 2 * G, :], preferred_element_type=jnp.float32)
         out[at, 0:F, :] = into.T.astype(jnp.bfloat16).reshape(2, F, TOK)
@@ -191,21 +206,26 @@
 
 
 def grad_kernel(place, *refs):
-    dgs = refs[:N_DP]
-    near, far, gain, near_out, far_out = refs[N_DP:]
+    dgs_from = refs[:N_DP]
+    tokens, gain, near_out, far_out, near, far, dgs, sems = refs[N_DP:]
+    pairs = [(dgs_from[r], dgs.at[r]) for r in range(N_DP)]
+    copies = fetch([(tokens.at[:, 0], near)] + pairs + [(tokens.at[:, 1], far)], sems)
     own = place[0]
     opposite = lax.rem(own + 4, N_DP)
-    step = 336
+    for copy in copies[:-1]:
+        copy.wait()
     for src, at, out in ((near, own, near_out), (far, opposite, far_out)):
+        if src is far:
+            copies[-1].wait()
         lanes = gain[:, pl.ds(pl.multiple_of(at * DS, DS), DS)]
-        for m in range(0, 2 * G, step):
-            total = jnp.zeros((step, DS), jnp.float32)
+        for m in range(0, 2 * G, G):
+            total = jnp.zeros((G, DS), jnp.float32)
             for r in range(N_DP):
-                v = src[pl.ds(2 * place[r], 2), 0].reshape(DS, TOK)
+                v = src[pl.ds(2 * place[r], 2)].reshape(DS, TOK)
                 total = total + lax.dot_general(
-                    dgs[r][m : m + step, :], v, (((1,), (1,)), ((), ())), preferred_element_type=jnp.float32
+                    dgs[r, m : m + G, :], v, (((1,), (1,)), ((), ())), preferred_element_type=jnp.float32
                 )
-            out[m : m + step, :] = (total * lanes).astype(jnp.bfloat16)
+            out[m : m + G, :] = (total * lanes).astype(jnp.bfloat16)
 
 
 def assemble_kernel(place, *refs):
@@ -223,10 +243,6 @@
 
 def cost(flops, nbytes):
     return pl.CostEstimate(flops=flops, bytes_accessed=nbytes, transcendentals=0)
-
-
-def of(array, k):
-    return pl.BlockSpec((N_T, 1, F, TOK), lambda *_: (0, k, 0, 0), memory_space=pltpu.VMEM)
 
 
 def combine(route_ids, probs):
@@ -250,34 +266,27 @@
     saved_t = kept_section_input[0].T
     acts_t = shift(passed_activations[0].T, s=1)
     dy_t = shift(handed_grads[0].T, s=-1)
+    gain = norm_gain[0]
     own_weights = jnp.concatenate([gate_weight[0].T, up_weight[0].T, down_weight[0]], axis=0)
-
-    def swaps(first):
-        block = after(saved_t, first)
-        return swapped(block, 0), swapped(block, 2)
-
-    weights, (near, far) = gather_ring(own_weights, swaps)
+    ready = (gain[:, None], place_t, combine(routes[0, 0], route_probs[0, 0]), combine(routes[0, 1], route_probs[0, 1]))
+    weights, (top, bottom), swaps, ready = gather_weights(own_weights, saved_t, ready)
+    gain_col, place, weight_f, weight_b = ready
     acts = lax.all_gather(
         after(jnp.concatenate([acts_t, dy_t, saved_t], axis=0), own_weights), ("y", "c"), axis=0
     ).reshape(N_T, 3, F, TOK)
-    far_tokens = lax.all_gather(jnp.concatenate([near, far], axis=0), ("y", "c"), axis=0).reshape(N_T, 2, F, TOK)
-    gain = norm_gain[0]
-    gain_col = gain[:, None]
-    weight_f = combine(routes[0, 0], route_probs[0, 0])
-    weight_b = combine(routes[0, 1], route_probs[0, 1])
+    tokens = lax.all_gather(jnp.concatenate(swaps, axis=0), ("y", "c"), axis=0).reshape(N_T, 2, F, TOK)
 
     bf, f32 = jnp.bfloat16, jnp.float32
-    last = N_DP - N_EARLY
-    early_b, early_f, normal_b, normal_f, scale_b = pl.pallas_call(
+    early_b, early_f, normal_b, normal_f, scales = pl.pallas_call(
         early_kernel,
         in_specs=[SM] + [HB] * N_EARLY + [HB, VM],
         out_specs=[VM] * 5,
         out_shape=[
             jax.ShapeDtypeStruct((3 * G, TOK), f32),
             jax.ShapeDtypeStruct((2 * G, TOK), f32),
-            jax.ShapeDtypeStruct((last, DS, TOK), bf),
-            jax.ShapeDtypeStruct((last, DS, TOK), bf),
-            jax.ShapeDtypeStruct((1, TOK), f32),
+            jax.ShapeDtypeStruct((DS, TOK), bf),
+            jax.ShapeDtypeStruct((DS, TOK), bf),
+            jax.ShapeDtypeStruct((2, TOK), f32),
         ],
         scratch_shapes=[
             pltpu.VMEM((N_T, F, TOK), bf),
@@ -291,25 +300,31 @@
         compiler_params=params(56),
         cost_estimate=cost(10 * D * G * TOK, 32 << 20),
         name="early",
-    )(place, *weights[:N_EARLY], acts, gain_col)
+    )(place, *weights, acts, gain_col)
     dg, dgs, stat = pl.pallas_call(
         inner_kernel,
-        in_specs=[SM] + [VM] * 4 + [HB, VM, VM],
+        in_specs=[SM] + [HB] * 5 + [VM, VM],
         out_specs=[VM] * 3,
         out_shape=[
             jax.ShapeDtypeStruct((2 * G, TOK), bf),
             jax.ShapeDtypeStruct((2 * G, TOK), bf),
             jax.ShapeDtypeStruct((1, TOK), f32),
         ],
-        scratch_shapes=[pltpu.VMEM((last, 2, F, TOK), bf), pltpu.SemaphoreType.DMA((last,))],
-        compiler_params=params(32),
+        scratch_shapes=[
+            pltpu.VMEM((3 * G, DS), bf),
+            pltpu.VMEM((3 * G, TOK), f32),
+            pltpu.VMEM((DS, TOK), bf),
+            pltpu.VMEM((2, F, TOK), bf),
+            pltpu.SemaphoreType.DMA((5,)),
+        ],
+        compiler_params=params(56),
         cost_estimate=cost(2 * D * G * TOK, 12 << 20),
         name="inner",
-    )(place, *weights[N_EARLY:], early_b, normal_b, acts, weight_b, scale_b)
-    dgs_all, _ = gather_ring(dgs)
+    )(place, top, bottom, early_b, normal_b, acts, weight_b, scales)
+    dgs_all, dgs_z = gather_ring(dgs)
     payload = pl.pallas_call(
         outer_kernel,
-        in_specs=[SM] + [HB] * N_DP + [VM] * 5,
+        in_specs=[SM] + [HB] * (N_EARLY + 2) + [VM] * 6,
         out_specs=VM,
         out_shape=jax.ShapeDtypeStruct((N_T, 2 * F + 2 * N_T, TOK), bf),
         scratch_shapes=[
@@ -317,25 +332,30 @@
             pltpu.VMEM((G, TOK), f32),
             pltpu.VMEM((TOK, 2 * G), bf),
             pltpu.VMEM((TOK, G), bf),
-            pltpu.SemaphoreType.DMA((N_DP,)),
+            pltpu.SemaphoreType.DMA((N_DP + 1,)),
         ],
         compiler_params=params(56),
         cost_estimate=cost(8 * D * G * TOK, 28 << 20),
         name="outer",
-    )(place_t, *weights, dg, early_f, normal_f, weight_f, stat)
-    payload = after(payload, tuple(dgs_all[1:4]))
+    )(place, *weights, top, bottom, dg, early_f, normal_f, weight_f, scales, stat)
+    payload = after(payload, dgs_z)
     summed = lax.psum_scatter(payload, ("y", "c"), scatter_dimension=0)
 
     near_grad, far_grad = pl.pallas_call(
         grad_kernel,
-        grid=(1,),
-        in_specs=[SM] + [VM] * N_DP + [of(far_tokens, 0), of(far_tokens, 1), VM],
+        in_specs=[SM] + [HB] * (N_DP + 1) + [VM],
         out_specs=[VM, VM],
         out_shape=[jax.ShapeDtypeStruct((2 * G, DS), bf)] * 2,
-        compiler_params=params(24),
+        scratch_shapes=[
+            pltpu.VMEM((N_T, F, TOK), bf),
+            pltpu.VMEM((N_T, F, TOK), bf),
+            pltpu.VMEM((N_DP, 2 * G, TOK), bf),
+            pltpu.SemaphoreType.DMA((N_DP + 2,)),
+        ],
+        compiler_params=params(56),
         cost_estimate=cost(8 * DS * G * TOK * N_DP, 8 << 20),
         name="grad",
-    )(place, *dgs_all, far_tokens, far_tokens, gain[None, :])
+    )(place, *dgs_all, tokens, gain[None, :])
     z = shift(near_grad, zl=1)
     behind = shift(near_grad, x=1)
     ahead = shift(near_grad, x=-1)
@@ -357,6 +377,7 @@
     mean_stat = jnp.sum(summed[2 * F :].astype(f32), axis=0, keepdims=True) / D
     gain_here = lax.dynamic_slice_in_dim(gain, here * F, F)[:, None]
     output = (acts_t.astype(f32) + summed[F : 2 * F].astype(f32)).astype(bf)
+    scale_b = scales[0:1]
     hat = saved_t.astype(f32) * scale_b
     stored = (dy_t.astype(f32) + scale_b * (into * gain_here - hat * mean_stat)).astype(bf)
     return (output.T[None], stored.T[None], grad_g.T[None], grad_u.T[None])

time: 209 us -> 225 us (1.077)
  starting transfers between devices: 90.9 us -> 99.1 us
  waiting for transfers between devices: 55.3 us -> 61.9 us
  Pallas kernels: 28.4 us -> 33.3 us
  local copies, waits for them, and re-layouts: 13.3 us -> 9.34 us
    ppermute x22 -> x23, starting transfers between devices: 79.6 us -> 87.9 us  [shift(): return lax.ppermute(value, axes if len(axes) > 1 else axes[0], pairs)]
    ppermute x22 -> x23, waiting for transfers between devices: 47.8 us -> 55.1 us  [shift(): return lax.ppermute(value, axes if len(axes) > 1 else axes[0], pairs)]
    unnamed x52 -> x54, local copies, waits for them, and re-layouts: 10.2 us -> 4.66 us
    pallas_call x3, Pallas kernels: 14.5 us -> 19.9 us  [the longest x1 9.01 us: local(): pl.pallas_call(outer_kernel, in_specs=[SM] + [HB] * (N_EARLY + 2) + [VM]...]
    another operation x2 -> x0, local copies, waits for them, and re-layouts: 2.32 us -> none  [the longest x1 1.66 us: local(): gain_col = gain[:, None]]
  transfers between devices with their start and end apart: 27 -> 28, of which waited for: 17 -> 16; matrix products, arithmetic and copies ran while one was open for 3% -> 3% of each run, Pallas kernels for 14% -> 15%
where the time goes in v3:
time: 225 us; the launch traced here: 224 us
  starting transfers between devices  99.1 us (44%)
  waiting for transfers between devices  61.9 us (28%)
  Pallas kernels  33.3 us (15%)
  between operations  14.3 us (6%)
  local copies, waits for them, and re-layouts  9.34 us (4%)
  other arithmetic  5.87 us (3%)
    ppermute x23, starting transfers between devices, shift(): return lax.ppermute(value, axes if len(axes) > 1 else axes[0], pairs)  87.9 us
    ppermute x23, waiting for transfers between devices, shift(): return lax.ppermute(value, axes if len(axes) > 1 else axes[0], pairs)  55.1 us
    ppermute x2, starting transfers between devices, swapped(): return lax.ppermute(value, ('x', 'zl', 'y'), pairs)  11.1 us
    pallas_call x1, Pallas kernels, local(): pl.pallas_call(early_kernel, in_specs=[SM] + [HB] * N_EARLY + [HB, VM], o...  10.4 us
    pallas_call x1, Pallas kernels, local(): pl.pallas_call(outer_kernel, in_specs=[SM] + [HB] * (N_EARLY + 2) + [VM]...  9.01 us
    pallas_call x1, Pallas kernels, local(): pl.pallas_call(grad_kernel, in_specs=[SM] + [HB] * (N_DP + 1) + [VM], out...  7.13 us
    ppermute x2, waiting for transfers between devices, swapped(): return lax.ppermute(value, ('x', 'zl', 'y'), pairs)  6.65 us
    unnamed x54, local copies, waits for them, and re-layouts  4.66 us
  transfers between devices with their start and end apart: 28, of which 16 were waited for; matrix products, arithmetic and copies ran while one was open for 3% of the time, Pallas kernels for 15%

profile of v3, /device:TPU:6, one launch (start us, length us, event | category | flops | bytes accessed | tf_op | source)
XLA Modules:
  0.0 223.7 jit_solution(6728019847219147570)
XLA Ops:
  7.2 10.9 %collective-permute-start.11 = (bf16[192,256]{1,0:T(8,128)(2,1)}, bf16[192,256]{1,0:T(8,128)(2,1)S(1)}, u32[]{:S(2)}, u32[]{:S(2)}) collective-permute-start(bf16[192,256]{1,0:T(8,128)(2,1)} %bitcast.73), channel_id=1, source_target_pairs={{0,48},{16,0},{32,16},{48,32},{1,49},{17,1},{33,17},{49,33},{2,50}... | collective-permute-start | bytes 294920 | tf_op jit(solution)/shard_map/ppermute | solution.py:37
  18.2 1.9 collective-permute-start
  20.1 1.3 pad_maximum_fusion.refs_0_
  21.4 1.3 collective-permute-done.11
  22.7 5.9 %collective-permute-done = bf16[192,256]{1,0:T(8,128)(2,1)S(1)} collective-permute-done((bf16[192,256]{1,0:T(8,128)(2,1)}, bf16[192,256]{1,0:T(8,128)(2,1)S(1)}, u32[]{:S(2)}, u32[]{:S(2)}) %collective-permute-start) | collective-permute-done | bytes 98336 | tf_op jit(solution)/shard_map/ppermute | solution.py:37
  29.4 3.6 %collective-permute-start.1 = (bf16[1008,384]{1,0:T(8,128)(2,1)S(1)}, bf16[1008,384]{1,0:T(8,128)(2,1)S(1)}, u32[]{:S(2)}, u32[]{:S(2)}) collective-permute-start(bf16[1008,384]{1,0:T(8,128)(2,1)S(1)} %pad_maximum_fusion.refs_0_), channel_id=1, source_target_pairs={{0,64},{64,0},{1,65},{65,1},{2,66},{66,2},{3,67},{67,3},{4,68},{68... | collective-permute-start | bytes 2322440 | tf_op jit(solution)/shard_map/ppermute | solution.py:37
  33.0 2.4 %collective-permute-start.2 = (bf16[1008,384]{1,0:T(8,128)(2,1)S(1)}, bf16[1008,384]{1,0:T(8,128)(2,1)S(1)}, u32[]{:S(2)}, u32[]{:S(2)}) collective-permute-start(bf16[1008,384]{1,0:T(8,128)(2,1)S(1)} %pad_maximum_fusion.refs_0_), channel_id=1, source_target_pairs={{0,128},{128,256},{256,384},{384,0},{1,129},{129,257},{257,385},{3... | collective-permute-start | bytes 2322440 | tf_op jit(solution)/shard_map/ppermute | solution.py:37
  35.4 3.5 %collective-permute-start.3 = (bf16[1008,384]{1,0:T(8,128)(2,1)S(1)}, bf16[1008,384]{1,0:T(8,128)(2,1)}, u32[]{:S(2)}, u32[]{:S(2)}) collective-permute-start(bf16[1008,384]{1,0:T(8,128)(2,1)S(1)} %pad_maximum_fusion.refs_0_), channel_id=1, source_target_pairs={{0,384},{128,0},{256,128},{384,256},{1,385},{129,1},{257,129},{385... | collective-permute-start | bytes 2322440 | tf_op jit(solution)/shard_map/ppermute | solution.py:37
  40.2 9.0 %collective-permute-done.1.refs_1_ = bf16[1008,384]{1,0:T(8,128)(2,1)S(1)} collective-permute-done((bf16[1008,384]{1,0:T(8,128)(2,1)S(1)}, bf16[1008,384]{1,0:T(8,128)(2,1)S(1)}, u32[]{:S(2)}, u32[]{:S(2)}) %collective-permute-start.1) | collective-permute-done | bytes 774176 | tf_op jit(solution)/shard_map/ppermute | solution.py:37
  49.2 3.4 %collective-permute-done.2.refs_2_ = bf16[1008,384]{1,0:T(8,128)(2,1)S(1)} collective-permute-done((bf16[1008,384]{1,0:T(8,128)(2,1)S(1)}, bf16[1008,384]{1,0:T(8,128)(2,1)S(1)}, u32[]{:S(2)}, u32[]{:S(2)}) %collective-permute-start.2) | collective-permute-done | bytes 774176 | tf_op jit(solution)/shard_map/ppermute | solution.py:37
  52.5 3.4 %collective-permute-done.3.refs_3_ = bf16[1008,384]{1,0:T(8,128)(2,1)} collective-permute-done((bf16[1008,384]{1,0:T(8,128)(2,1)S(1)}, bf16[1008,384]{1,0:T(8,128)(2,1)}, u32[]{:S(2)}, u32[]{:S(2)}) %collective-permute-start.3) | collective-permute-done | bytes 774176 | tf_op jit(solution)/shard_map/ppermute | solution.py:37
  56.0 2.2 collective-permute-start.4
  58.2 3.7 %collective-permute-start.5 = (bf16[1008,384]{1,0:T(8,128)(2,1)}, bf16[1008,384]{1,0:T(8,128)(2,1)}, u32[]{:S(2)}, u32[]{:S(2)}) collective-permute-start(bf16[1008,384]{1,0:T(8,128)(2,1)} %collective-permute-done.3.refs_3_), channel_id=1, source_target_pairs={{0,384},{128,0},{256,128},{384,256},{1,385},{129,1},{257,129},{385... | collective-permute-start | bytes 2322440 | tf_op jit(solution)/shard_map/ppermute | solution.py:37
  61.8 2.2 collective-permute-start.6
  64.0 7.1 %collective-permute-start.7 = (bf16[192,256]{1,0:T(8,128)(2,1)S(1)}, bf16[192,256]{1,0:T(8,128)(2,1)S(1)}, u32[]{:S(2)}, u32[]{:S(2)}) collective-permute-start(bf16[192,256]{1,0:T(8,128)(2,1)S(1)} %bitcast.60), channel_id=1, source_target_pairs={{0,0},{2,64},{4,128},{6,192},{8,256},{10,320},{12,384},{14,448},{6... | collective-permute-start | bytes 294920 | tf_op jit(solution)/shard_map/ppermute | solution.py:46
  71.1 4.0 %collective-permute-start.8 = (bf16[192,256]{1,0:T(8,128)(2,1)S(1)}, bf16[192,256]{1,0:T(8,128)(2,1)S(1)}, u32[]{:S(2)}, u32[]{:S(2)}) collective-permute-start(bf16[192,256]{1,0:T(8,128)(2,1)S(1)} %bitcast.61), channel_id=1, source_target_pairs={{0,256},{2,320},{4,384},{6,448},{8,0},{10,64},{12,128},{14,192},{6... | collective-permute-start | bytes 294920 | tf_op jit(solution)/shard_map/ppermute | solution.py:46
  75.1 6.6 %collective-permute-done.7 = bf16[192,256]{1,0:T(8,128)(2,1)S(1)} collective-permute-done((bf16[192,256]{1,0:T(8,128)(2,1)S(1)}, bf16[192,256]{1,0:T(8,128)(2,1)S(1)}, u32[]{:S(2)}, u32[]{:S(2)}) %collective-permute-start.7) | collective-permute-done | bytes 98336 | tf_op jit(solution)/shard_map/ppermute | solution.py:46
  83.6 15.9 %collective-permute-start.9 = (bf16[512,384]{1,0:T(8,128)(2,1)}, bf16[512,384]{1,0:T(8,128)(2,1)S(1)}, u32[]{:S(2)}, u32[]{:S(2)}) collective-permute-start(bf16[512,384]{1,0:T(8,128)(2,1)} %slice.37), channel_id=1, source_target_pairs={{0,128},{128,256},{256,384},{384,0},{1,129},{129,257},{257,385},{3... | collective-permute-start | bytes 1179656 | tf_op jit(solution)/shard_map/ppermute | solution.py:37
  100.4 1.9 collective-permute-start.10
  102.3 1.7 copy.13.refs_8_
  104.0 10.4 %early.1 = (f32[1008,256]{1,0:T(8,128)}, f32[672,256]{1,0:T(8,128)}, bf16[384,256]{1,0:T(8,128)(2,1)}, bf16[384,256]{1,0:T(8,128)(2,1)}, f32[2,256]{1,0:T(2,128)}) custom-call(s32[9]{0:T(128)} %concatenate.13.place, bf16[1008,384]{1,0:T(8,128)(2,1)} %copy-done.3, bf16[1008,384]{1,0:T(8,128)(2,1)} %copy-done.6, bf16[1008,384]{1,0:T(8,128)(2,1)} %copy-done.7, ...), custom_call_target="tpu_custom_call" | custom-call | flops 2642411520 | bytes 33554432 | tf_op jit(solution)/shard_map/early/pallas_call | solution.py:280
  115.2 3.7 %inner.1 = (bf16[672,256]{1,0:T(8,128)(2,1)}, bf16[672,256]{1,0:T(8,128)(2,1)}, f32[1,256]{1,0:T(1,128)}) custom-call(s32[9]{0:T(128)} %concatenate.13.place, bf16[512,384]{1,0:T(8,128)(2,1)} %copy-done.8, bf16[496,384]{1,0:T(8,128)(2,1)} %collective-permute-done.10.bottom.refs_8_, f32[1008,256]{1,0:T(8,128)} %get-tuple-element.44.early_from, ...), custom_call_target="tpu_custom_call" | custom-call | flops 528482304 | bytes 12582912 | tf_op jit(solution)/shard_map/inner/pallas_call | solution.py:304
  119.0 4.3 %collective-permute-start.12 = (bf16[672,256]{1,0:T(8,128)(2,1)}, bf16[672,256]{1,0:T(8,128)(2,1)S(1)}, u32[]{:S(2)}, u32[]{:S(2)}) collective-permute-start(bf16[672,256]{1,0:T(8,128)(2,1)} %get-tuple-element.53.refs_0_), channel_id=1, source_target_pairs={{0,64},{64,0},{1,65},{65,1},{2,66},{66,2},{3,67},{67,3},{4,68},{68... | collective-permute-start | bytes 1032200 | tf_op jit(solution)/shard_map/ppermute | solution.py:37
  123.3 9.0 %outer.1 = bf16[16,416,256]{2,1,0:T(8,128)(2,1)} custom-call(s32[9]{0:T(128)} %concatenate.13.place, bf16[1008,384]{1,0:T(8,128)(2,1)} %copy-done.3, bf16[1008,384]{1,0:T(8,128)(2,1)} %copy-done.6, bf16[1008,384]{1,0:T(8,128)(2,1)} %copy-done.7, bf16[1008,384]{1,0:T(8,128)(2,1)} %collective-permute-done.3.refs_3_, bf16[1008,384]{1,0:T(8,128)(2,1)} %copy-done.4, ...), custom_call_target="tpu_custom_call" | custom-call | flops 2113929216 | bytes 29360128 | tf_op jit(solution)/shard_map/outer/pallas_call | solution.py:325
  132.3 1.1 copy-done.19
  133.4 5.0 %collective-permute-start.13 = (bf16[672,256]{1,0:T(8,128)(2,1)S(1)}, bf16[672,256]{1,0:T(8,128)(2,1)S(1)}, u32[]{:S(2)}, u32[]{:S(2)}) collective-permute-start(bf16[672,256]{1,0:T(8,128)(2,1)S(1)} %copy-done.19), channel_id=1, source_target_pairs={{0,128},{128,256},{256,384},{384,0},{1,129},{129,257},{257,385},{3... | collective-permute-start | bytes 1032200 | tf_op jit(solution)/shard_map/ppermute | solution.py:37
  138.4 1.9 collective-permute-start.14
  140.3 2.8 %collective-permute-done.13.refs_2_ = bf16[672,256]{1,0:T(8,128)(2,1)S(1)} collective-permute-done((bf16[672,256]{1,0:T(8,128)(2,1)S(1)}, bf16[672,256]{1,0:T(8,128)(2,1)S(1)}, u32[]{:S(2)}, u32[]{:S(2)}) %collective-permute-start.13) | collective-permute-done | bytes 344096 | tf_op jit(solution)/shard_map/ppermute | solution.py:37
  143.1 6.3 %collective-permute-done.14.refs_3_ = bf16[672,256]{1,0:T(8,128)(2,1)S(1)} collective-permute-done((bf16[672,256]{1,0:T(8,128)(2,1)S(1)}, bf16[672,256]{1,0:T(8,128)(2,1)S(1)}, u32[]{:S(2)}, u32[]{:S(2)}) %collective-permute-start.14) | collective-permute-done | bytes 344096 | tf_op jit(solution)/shard_map/ppermute | solution.py:37
  149.4 1.9 collective-permute-start.16
  151.3 5.1 %collective-permute-start.15 = (bf16[672,256]{1,0:T(8,128)(2,1)S(1)}, bf16[672,256]{1,0:T(8,128)(2,1)S(1)}, u32[]{:S(2)}, u32[]{:S(2)}) collective-permute-start(bf16[672,256]{1,0:T(8,128)(2,1)S(1)} %collective-permute-done.12.refs_1_), channel_id=1, source_target_pairs={{0,128},{128,256},{256,384},{384,0},{1,129},{129,257},{257,385},{3... | collective-permute-start | bytes 1032200 | tf_op jit(solution)/shard_map/ppermute | solution.py:37
  156.5 2.1 collective-permute-start.17
  158.6 2.9 %collective-permute-done.16.refs_5_ = bf16[672,256]{1,0:T(8,128)(2,1)S(1)} collective-permute-done((bf16[672,256]{1,0:T(8,128)(2,1)S(1)}, bf16[672,256]{1,0:T(8,128)(2,1)S(1)}, u32[]{:S(2)}, u32[]{:S(2)}) %collective-permute-start.16) | collective-permute-done | bytes 344096 | tf_op jit(solution)/shard_map/ppermute | solution.py:37
  161.5 1.9 collective-permute-start.18
  163.4 2.2 collective-permute-done.17.refs_6_
  165.6 6.2 %collective-permute-done.18.refs_7_ = bf16[672,256]{1,0:T(8,128)(2,1)S(1)} collective-permute-done((bf16[672,256]{1,0:T(8,128)(2,1)S(1)}, bf16[672,256]{1,0:T(8,128)(2,1)S(1)}, u32[]{:S(2)}, u32[]{:S(2)}) %collective-permute-start.18) | collective-permute-done | bytes 344096 | tf_op jit(solution)/shard_map/ppermute | solution.py:37
  172.6 7.1 %grad.1 = (bf16[672,384]{1,0:T(8,128)(2,1)}, bf16[672,384]{1,0:T(8,128)(2,1)}) custom-call(s32[9]{0:T(128)} %concatenate.13.place, bf16[672,256]{1,0:T(8,128)(2,1)} %get-tuple-element.53.refs_0_, bf16[672,256]{1,0:T(8,128)(2,1)} %copy-done.20, bf16[672,256]{1,0:T(8,128)(2,1)} %copy-done.21, bf16[672,256]{1,0:T(8,128)(2,1)} %copy-done.22, ...), custom_call_target="tpu_custom_call" | custom-call | flops 2113929216 | bytes 8388608 | tf_op jit(solution)/shard_map/grad/pallas_call | solution.py:344
  179.7 1.9 collective-permute-start.19
  181.6 1.9 collective-permute-start.20
  183.6 3.9 %collective-permute-start.21 = (bf16[672,384]{1,0:T(8,128)(2,1)}, bf16[672,384]{1,0:T(8,128)(2,1)S(1)}, u32[]{:S(2)}, u32[]{:S(2)}) collective-permute-start(bf16[672,384]{1,0:T(8,128)(2,1)} %get-tuple-element.60.refs_0_), channel_id=1, source_target_pairs={{0,384},{128,0},{256,128},{384,256},{1,385},{129,1},{257,129},{385... | collective-permute-start | bytes 1548296 | tf_op jit(solution)/shard_map/ppermute | solution.py:37
  187.5 3.9 %collective-permute-start.24 = (bf16[672,384]{1,0:T(8,128)(2,1)}, bf16[672,384]{1,0:T(8,128)(2,1)S(1)}, u32[]{:S(2)}, u32[]{:S(2)}) collective-permute-start(bf16[672,384]{1,0:T(8,128)(2,1)} %get-tuple-element.61.refs_6_), channel_id=1, source_target_pairs={{0,64},{64,0},{1,65},{65,1},{2,66},{66,2},{3,67},{67,3},{4,68},{68... | collective-permute-start | bytes 1548296 | tf_op jit(solution)/shard_map/ppermute | solution.py:37
  191.4 2.7 %collective-permute-done.19.refs_1_ = bf16[672,384]{1,0:T(8,128)(2,1)S(1)} collective-permute-done((bf16[672,384]{1,0:T(8,128)(2,1)}, bf16[672,384]{1,0:T(8,128)(2,1)S(1)}, u32[]{:S(2)}, u32[]{:S(2)}) %collective-permute-start.19) | collective-permute-done | bytes 516128 | tf_op jit(solution)/shard_map/ppermute | solution.py:37
  194.1 3.4 %collective-permute-start.22 = (bf16[672,384]{1,0:T(8,128)(2,1)S(1)}, bf16[672,384]{1,0:T(8,128)(2,1)S(1)}, u32[]{:S(2)}, u32[]{:S(2)}) collective-permute-start(bf16[672,384]{1,0:T(8,128)(2,1)S(1)} %collective-permute-done.19.refs_1_), channel_id=1, source_target_pairs={{0,128},{128,256},{256,384},{384,0},{1,129},{129,257},{257,385},{3... | collective-permute-start | bytes 1548296 | tf_op jit(solution)/shard_map/ppermute | solution.py:37
  197.5 2.4 %collective-permute-start.23 = (bf16[672,384]{1,0:T(8,128)(2,1)S(1)}, bf16[672,384]{1,0:T(8,128)(2,1)S(1)}, u32[]{:S(2)}, u32[]{:S(2)}) collective-permute-start(bf16[672,384]{1,0:T(8,128)(2,1)S(1)} %collective-permute-done.19.refs_1_), channel_id=1, source_target_pairs={{0,384},{128,0},{256,128},{384,256},{1,385},{129,1},{257,129},{385... | collective-permute-start | bytes 1548296 | tf_op jit(solution)/shard_map/ppermute | solution.py:37
  201.4 3.7 %collective-permute-done.22.refs_4_ = bf16[672,384]{1,0:T(8,128)(2,1)S(1)} collective-permute-done((bf16[672,384]{1,0:T(8,128)(2,1)S(1)}, bf16[672,384]{1,0:T(8,128)(2,1)S(1)}, u32[]{:S(2)}, u32[]{:S(2)}) %collective-permute-start.22) | collective-permute-done | bytes 516128 | tf_op jit(solution)/shard_map/ppermute | solution.py:37
  205.1 4.6 %collective-permute-done.23.refs_5_ = bf16[672,384]{1,0:T(8,128)(2,1)S(1)} collective-permute-done((bf16[672,384]{1,0:T(8,128)(2,1)S(1)}, bf16[672,384]{1,0:T(8,128)(2,1)S(1)}, u32[]{:S(2)}, u32[]{:S(2)}) %collective-permute-start.23) | collective-permute-done | bytes 516128 | tf_op jit(solution)/shard_map/ppermute | solution.py:37
  211.8 2.9 %assemble.1 = (bf16[336,3072]{1,0:T(8,128)(2,1)}, bf16[336,3072]{1,0:T(8,128)(2,1)}) custom-call(s32[9]{0:T(128)S(1)} %copy-done.2, bf16[672,384]{1,0:T(8,128)(2,1)S(1)} %copy-done, bf16[672,384]{1,0:T(8,128)(2,1)S(1)} %collective-permute-done.19.refs_1_, bf16[672,384]{1,0:T(8,128)(2,1)S(1)} %collective-permute-done.20.refs_2_, ...), custom_call_target="tpu_custom_call" | custom-call | bytes 8388608 | tf_op jit(solution)/shard_map/assemble/pallas_call | solution.py:366
  215.5 1.7 fusion.6
  (83 shorter events, 10.6 us)
Async XLA Ops:
  7.2 21.4 %copy-start.9 = (bf16[1,256,192]{1,2,0:T(8,128)(2,1)S(1)}, bf16[1,256,192]{1,2,0:T(8,128)(2,1)}, u32[]{:S(2)}) copy-start(bf16[1,256,192]{1,2,0:T(8,128)(2,1)} %param.10) | copy-start | bytes 294916
  7.2 32.4 %copy-start.17 = (f32[1,2,256,4]{2,3,1,0:T(4,128)S(1)}, f32[1,2,256,4]{2,3,1,0:T(4,128)}, u32[]{:S(2)}) copy-start(f32[1,2,256,4]{2,3,1,0:T(4,128)} %param.17) | copy-start | bytes 24580
  7.2 32.4 %copy-start.18 = (s32[1,2,256,4]{2,3,1,0:T(4,128)S(1)}, s32[1,2,256,4]{2,3,1,0:T(4,128)}, u32[]{:S(2)}) copy-start(s32[1,2,256,4]{2,3,1,0:T(4,128)} %param.16) | copy-start | bytes 24580
  7.2 96.8 %all-gather.5.cloned.1.call-start = ((), (), s32[]{:S(2)}) async-start(), calls=%async_computation.2 | async-start | bytes 5013504 | tf_op jit(solution)/shard_map/all_gather | solution.py:274
  7.2 15.4 %collective-permute-start.11 = (bf16[192,256]{1,0:T(8,128)(2,1)}, bf16[192,256]{1,0:T(8,128)(2,1)S(1)}, u32[]{:S(2)}, u32[]{:S(2)}) collective-permute-start(bf16[192,256]{1,0:T(8,128)(2,1)} %bitcast.73), channel_id=1, source_target_pairs={{0,48},{16,0},{32,16},{48,32},{1,49},{17,1},{33,17},{49,33},{2,50}... | collective-permute-start | bytes 294920 | tf_op jit(solution)/shard_map/ppermute | solution.py:37
  18.2 10.4 %collective-permute-start = (bf16[192,256]{1,0:T(8,128)(2,1)}, bf16[192,256]{1,0:T(8,128)(2,1)S(1)}, u32[]{:S(2)}, u32[]{:S(2)}) collective-permute-start(bf16[192,256]{1,0:T(8,128)(2,1)} %bitcast.74), channel_id=1, source_target_pairs={{0,16},{16,32},{32,48},{48,0},{1,17},{17,33},{33,49},{49,1},{2,18}... | collective-permute-start | bytes 294920 | tf_op jit(solution)/shard_map/ppermute | solution.py:37
  21.4 79.0 %copy-start.3 = (bf16[1008,384]{1,0:T(8,128)(2,1)}, bf16[1008,384]{1,0:T(8,128)(2,1)S(1)}, u32[]{:S(2)}) copy-start(bf16[1008,384]{1,0:T(8,128)(2,1)S(1)} %pad_maximum_fusion.refs_0_) | copy-start | bytes 2322436
  22.7 6.7 %copy-start.11 = (bf16[192,256]{1,0:T(8,128)(2,1)}, bf16[192,256]{1,0:T(8,128)(2,1)S(1)}, u32[]{:S(2)}) copy-start(bf16[192,256]{1,0:T(8,128)(2,1)S(1)} %collective-permute-done.11) | copy-start | bytes 294916
  28.6 73.7 %copy-start.15 = (f32[1,3072]{1,0:T(1,128)S(1)}, f32[1,3072]{1,0:T(1,128)}, u32[]{:S(2)}) copy-start(f32[1,3072]{1,0:T(1,128)} %refs_9_.1) | copy-start | bytes 36868
  29.4 134.0 %all-gather.7.cloned.1.call-start = ((), (), s32[]{:S(2)}) async-start(), calls=%async_computation.3 | async-start | bytes 3342336 | tf_op jit(solution)/shard_map/all_gather | solution.py:277
  29.4 19.7 %collective-permute-start.1 = (bf16[1008,384]{1,0:T(8,128)(2,1)S(1)}, bf16[1008,384]{1,0:T(8,128)(2,1)S(1)}, u32[]{:S(2)}, u32[]{:S(2)}) collective-permute-start(bf16[1008,384]{1,0:T(8,128)(2,1)S(1)} %pad_maximum_fusion.refs_0_), channel_id=1, source_target_pairs={{0,64},{64,0},{1,65},{65,1},{2,66},{66,2},{3,67},{67,3},{4,68},{68... | collective-permute-start | bytes 2322440 | tf_op jit(solution)/shard_map/ppermute | solution.py:37
  33.0 19.5 %collective-permute-start.2 = (bf16[1008,384]{1,0:T(8,128)(2,1)S(1)}, bf16[1008,384]{1,0:T(8,128)(2,1)S(1)}, u32[]{:S(2)}, u32[]{:S(2)}) collective-permute-start(bf16[1008,384]{1,0:T(8,128)(2,1)S(1)} %pad_maximum_fusion.refs_0_), channel_id=1, source_target_pairs={{0,128},{128,256},{256,384},{384,0},{1,129},{129,257},{257,385},{3... | collective-permute-start | bytes 2322440 | tf_op jit(solution)/shard_map/ppermute | solution.py:37
  35.4 20.6 %collective-permute-start.3 = (bf16[1008,384]{1,0:T(8,128)(2,1)S(1)}, bf16[1008,384]{1,0:T(8,128)(2,1)}, u32[]{:S(2)}, u32[]{:S(2)}) collective-permute-start(bf16[1008,384]{1,0:T(8,128)(2,1)S(1)} %pad_maximum_fusion.refs_0_), channel_id=1, source_target_pairs={{0,384},{128,0},{256,128},{384,256},{1,385},{129,1},{257,129},{385... | collective-permute-start | bytes 2322440 | tf_op jit(solution)/shard_map/ppermute | solution.py:37
  49.2 54.8 %copy-start.6 = (bf16[1008,384]{1,0:T(8,128)(2,1)}, bf16[1008,384]{1,0:T(8,128)(2,1)S(1)}, u32[]{:S(2)}) copy-start(bf16[1008,384]{1,0:T(8,128)(2,1)S(1)} %collective-permute-done.1.refs_1_) | copy-start | bytes 2322436
  56.0 25.8 %collective-permute-start.4 = (bf16[1008,384]{1,0:T(8,128)(2,1)S(1)}, bf16[1008,384]{1,0:T(8,128)(2,1)S(1)}, u32[]{:S(2)}, u32[]{:S(2)}) collective-permute-start(bf16[1008,384]{1,0:T(8,128)(2,1)S(1)} %collective-permute-done.1.refs_1_), channel_id=1, source_target_pairs={{0,128},{128,256},{256,384},{384,0},{1,129},{129,257},{257,385},{3... | collective-permute-start | bytes 2322440 | tf_op jit(solution)/shard_map/ppermute | solution.py:37
  58.2 23.8 %collective-permute-start.5 = (bf16[1008,384]{1,0:T(8,128)(2,1)}, bf16[1008,384]{1,0:T(8,128)(2,1)}, u32[]{:S(2)}, u32[]{:S(2)}) collective-permute-start(bf16[1008,384]{1,0:T(8,128)(2,1)} %collective-permute-done.3.refs_3_), channel_id=1, source_target_pairs={{0,384},{128,0},{256,128},{384,256},{1,385},{129,1},{257,129},{385... | collective-permute-start | bytes 2322440 | tf_op jit(solution)/shard_map/ppermute | solution.py:37
  61.8 20.2 %collective-permute-start.6 = (bf16[1008,384]{1,0:T(8,128)(2,1)}, bf16[1008,384]{1,0:T(8,128)(2,1)S(1)}, u32[]{:S(2)}, u32[]{:S(2)}) collective-permute-start(bf16[1008,384]{1,0:T(8,128)(2,1)} %collective-permute-done.3.refs_3_), channel_id=1, source_target_pairs={{0,64},{64,0},{1,65},{65,1},{2,66},{66,2},{3,67},{67,3},{4,68},{68... | collective-permute-start | bytes 2322440 | tf_op jit(solution)/shard_map/ppermute | solution.py:37
  64.0 17.8 %collective-permute-start.7 = (bf16[192,256]{1,0:T(8,128)(2,1)S(1)}, bf16[192,256]{1,0:T(8,128)(2,1)S(1)}, u32[]{:S(2)}, u32[]{:S(2)}) collective-permute-start(bf16[192,256]{1,0:T(8,128)(2,1)S(1)} %bitcast.60), channel_id=1, source_target_pairs={{0,0},{2,64},{4,128},{6,192},{8,256},{10,320},{12,384},{14,448},{6... | collective-permute-start | bytes 294920 | tf_op jit(solution)/shard_map/ppermute | solution.py:46
  71.1 10.7 %collective-permute-start.8 = (bf16[192,256]{1,0:T(8,128)(2,1)S(1)}, bf16[192,256]{1,0:T(8,128)(2,1)S(1)}, u32[]{:S(2)}, u32[]{:S(2)}) collective-permute-start(bf16[192,256]{1,0:T(8,128)(2,1)S(1)} %bitcast.61), channel_id=1, source_target_pairs={{0,256},{2,320},{4,384},{6,448},{8,0},{10,64},{12,128},{14,192},{6... | collective-permute-start | bytes 294920 | tf_op jit(solution)/shard_map/ppermute | solution.py:46
  81.8 22.2 %copy-start.4 = (bf16[1008,384]{1,0:T(8,128)(2,1)}, bf16[1008,384]{1,0:T(8,128)(2,1)S(1)}, u32[]{:S(2)}) copy-start(bf16[1008,384]{1,0:T(8,128)(2,1)S(1)} %collective-permute-done.4.refs_4_) | copy-start | bytes 2322436
  82.0 22.0 %copy-start.5 = (bf16[1008,384]{1,0:T(8,128)(2,1)}, bf16[1008,384]{1,0:T(8,128)(2,1)S(1)}, u32[]{:S(2)}) copy-start(bf16[1008,384]{1,0:T(8,128)(2,1)S(1)} %collective-permute-done.6.refs_5_) | copy-start | bytes 2322436
  82.8 131.9 %reduce-scatter.2.cloned.1.call-start = ((), (), s32[]{:S(2)}) async-start(), calls=%async_computation.1 | async-start | bytes 3620864 | tf_op jit(solution)/shard_map/reduce_scatter | solution.py:342
  83.6 30.8 %collective-permute-start.9 = (bf16[512,384]{1,0:T(8,128)(2,1)}, bf16[512,384]{1,0:T(8,128)(2,1)S(1)}, u32[]{:S(2)}, u32[]{:S(2)}) collective-permute-start(bf16[512,384]{1,0:T(8,128)(2,1)} %slice.37), channel_id=1, source_target_pairs={{0,128},{128,256},{256,384},{384,0},{1,129},{129,257},{257,385},{3... | collective-permute-start | bytes 1179656 | tf_op jit(solution)/shard_map/ppermute | solution.py:37
  100.4 14.1 %collective-permute-start.10 = (bf16[496,384]{1,0:T(8,128)(2,1)}, bf16[496,384]{1,0:T(8,128)(2,1)}, u32[]{:S(2)}, u32[]{:S(2)}) collective-permute-start(bf16[496,384]{1,0:T(8,128)(2,1)} %slice.38), channel_id=1, source_target_pairs={{0,384},{128,0},{256,128},{384,256},{1,385},{129,1},{257,129},{385... | collective-permute-start | bytes 1142792 | tf_op jit(solution)/shard_map/ppermute | solution.py:37
  119.0 13.4 %collective-permute-start.12 = (bf16[672,256]{1,0:T(8,128)(2,1)}, bf16[672,256]{1,0:T(8,128)(2,1)S(1)}, u32[]{:S(2)}, u32[]{:S(2)}) collective-permute-start(bf16[672,256]{1,0:T(8,128)(2,1)} %get-tuple-element.53.refs_0_), channel_id=1, source_target_pairs={{0,64},{64,0},{1,65},{65,1},{2,66},{66,2},{3,67},{67,3},{4,68},{68... | collective-permute-start | bytes 1032200 | tf_op jit(solution)/shard_map/ppermute | solution.py:37
  132.3 19.0 %copy-start.20 = (bf16[672,256]{1,0:T(8,128)(2,1)}, bf16[672,256]{1,0:T(8,128)(2,1)S(1)}, u32[]{:S(2)}) copy-start(bf16[672,256]{1,0:T(8,128)(2,1)S(1)} %collective-permute-done.12.refs_1_) | copy-start | bytes 1032196
  133.4 9.7 %collective-permute-start.13 = (bf16[672,256]{1,0:T(8,128)(2,1)S(1)}, bf16[672,256]{1,0:T(8,128)(2,1)S(1)}, u32[]{:S(2)}, u32[]{:S(2)}) collective-permute-start(bf16[672,256]{1,0:T(8,128)(2,1)S(1)} %copy-done.19), channel_id=1, source_target_pairs={{0,128},{128,256},{256,384},{384,0},{1,129},{129,257},{257,385},{3... | collective-permute-start | bytes 1032200 | tf_op jit(solution)/shard_map/ppermute | solution.py:37
  138.4 11.0 %collective-permute-start.14 = (bf16[672,256]{1,0:T(8,128)(2,1)S(1)}, bf16[672,256]{1,0:T(8,128)(2,1)S(1)}, u32[]{:S(2)}, u32[]{:S(2)}) collective-permute-start(bf16[672,256]{1,0:T(8,128)(2,1)S(1)} %copy-done.19), channel_id=1, source_target_pairs={{0,384},{128,0},{256,128},{384,256},{1,385},{129,1},{257,129},{385... | collective-permute-start | bytes 1032200 | tf_op jit(solution)/shard_map/ppermute | solution.py:37
  143.1 28.7 %copy-start.21 = (bf16[672,256]{1,0:T(8,128)(2,1)}, bf16[672,256]{1,0:T(8,128)(2,1)S(1)}, u32[]{:S(2)}) copy-start(bf16[672,256]{1,0:T(8,128)(2,1)S(1)} %collective-permute-done.13.refs_2_) | copy-start | bytes 1032196
  149.4 22.4 %copy-start.22 = (bf16[672,256]{1,0:T(8,128)(2,1)}, bf16[672,256]{1,0:T(8,128)(2,1)S(1)}, u32[]{:S(2)}) copy-start(bf16[672,256]{1,0:T(8,128)(2,1)S(1)} %collective-permute-done.14.refs_3_) | copy-start | bytes 1032196
  149.4 12.1 %collective-permute-start.16 = (bf16[672,256]{1,0:T(8,128)(2,1)S(1)}, bf16[672,256]{1,0:T(8,128)(2,1)S(1)}, u32[]{:S(2)}, u32[]{:S(2)}) collective-permute-start(bf16[672,256]{1,0:T(8,128)(2,1)S(1)} %collective-permute-done.12.refs_1_), channel_id=1, source_target_pairs={{0,384},{128,0},{256,128},{384,256},{1,385},{129,1},{257,129},{385... | collective-permute-start | bytes 1032200 | tf_op jit(solution)/shard_map/ppermute | solution.py:37
  151.3 12.1 %collective-permute-start.15 = (bf16[672,256]{1,0:T(8,128)(2,1)S(1)}, bf16[672,256]{1,0:T(8,128)(2,1)S(1)}, u32[]{:S(2)}, u32[]{:S(2)}) collective-permute-start(bf16[672,256]{1,0:T(8,128)(2,1)S(1)} %collective-permute-done.12.refs_1_), channel_id=1, source_target_pairs={{0,128},{128,256},{256,384},{384,0},{1,129},{129,257},{257,385},{3... | collective-permute-start | bytes 1032200 | tf_op jit(solution)/shard_map/ppermute | solution.py:37
  156.5 9.1 %collective-permute-start.17 = (bf16[672,256]{1,0:T(8,128)(2,1)S(1)}, bf16[672,256]{1,0:T(8,128)(2,1)S(1)}, u32[]{:S(2)}, u32[]{:S(2)}) collective-permute-start(bf16[672,256]{1,0:T(8,128)(2,1)S(1)} %collective-permute-done.13.refs_2_), channel_id=1, source_target_pairs={{0,128},{128,256},{256,384},{384,0},{1,129},{129,257},{257,385},{3... | collective-permute-start | bytes 1032200 | tf_op jit(solution)/shard_map/ppermute | solution.py:37
  161.5 10.4 %copy-start.23 = (bf16[672,256]{1,0:T(8,128)(2,1)}, bf16[672,256]{1,0:T(8,128)(2,1)S(1)}, u32[]{:S(2)}) copy-start(bf16[672,256]{1,0:T(8,128)(2,1)S(1)} %collective-permute-done.16.refs_5_) | copy-start | bytes 1032196
  161.5 10.3 %collective-permute-start.18 = (bf16[672,256]{1,0:T(8,128)(2,1)S(1)}, bf16[672,256]{1,0:T(8,128)(2,1)S(1)}, u32[]{:S(2)}, u32[]{:S(2)}) collective-permute-start(bf16[672,256]{1,0:T(8,128)(2,1)S(1)} %collective-permute-done.16.refs_5_), channel_id=1, source_target_pairs={{0,384},{128,0},{256,128},{384,256},{1,385},{129,1},{257,129},{385... | collective-permute-start | bytes 1032200 | tf_op jit(solution)/shard_map/ppermute | solution.py:37
  163.4 8.4 %copy-start.24 = (bf16[672,256]{1,0:T(8,128)(2,1)}, bf16[672,256]{1,0:T(8,128)(2,1)S(1)}, u32[]{:S(2)}) copy-start(bf16[672,256]{1,0:T(8,128)(2,1)S(1)} %collective-permute-done.15.refs_4_) | copy-start | bytes 1032196
  165.6 6.2 %copy-start.25 = (bf16[672,256]{1,0:T(8,128)(2,1)}, bf16[672,256]{1,0:T(8,128)(2,1)S(1)}, u32[]{:S(2)}) copy-start(bf16[672,256]{1,0:T(8,128)(2,1)S(1)} %collective-permute-done.17.refs_6_) | copy-start | bytes 1032196
  172.5 28.2 %copy-start.16 = (f32[2,256]{1,0:T(2,128)S(1)}, f32[2,256]{1,0:T(2,128)}, u32[]{:S(2)}) copy-start(f32[2,256]{1,0:T(2,128)} %get-tuple-element.47.scales.refs_13_) | copy-start | bytes 6148
  172.6 37.1 %copy-start.2 = (s32[9]{0:T(128)S(1)}, s32[9]{0:T(128)}, u32[]{:S(2)}) copy-start(s32[9]{0:T(128)} %concatenate.13.place) | copy-start | bytes 112
  179.7 14.4 %collective-permute-start.19 = (bf16[672,384]{1,0:T(8,128)(2,1)}, bf16[672,384]{1,0:T(8,128)(2,1)S(1)}, u32[]{:S(2)}, u32[]{:S(2)}) collective-permute-start(bf16[672,384]{1,0:T(8,128)(2,1)} %get-tuple-element.60.refs_0_), channel_id=1, source_target_pairs={{0,64},{64,0},{1,65},{65,1},{2,66},{66,2},{3,67},{67,3},{4,68},{68... | collective-permute-start | bytes 1548296 | tf_op jit(solution)/shard_map/ppermute | solution.py:37
  181.6 19.1 %collective-permute-start.20 = (bf16[672,384]{1,0:T(8,128)(2,1)}, bf16[672,384]{1,0:T(8,128)(2,1)S(1)}, u32[]{:S(2)}, u32[]{:S(2)}) collective-permute-start(bf16[672,384]{1,0:T(8,128)(2,1)} %get-tuple-element.60.refs_0_), channel_id=1, source_target_pairs={{0,128},{128,256},{256,384},{384,0},{1,129},{129,257},{257,385},{3... | collective-permute-start | bytes 1548296 | tf_op jit(solution)/shard_map/ppermute | solution.py:37
  183.6 17.8 %collective-permute-start.21 = (bf16[672,384]{1,0:T(8,128)(2,1)}, bf16[672,384]{1,0:T(8,128)(2,1)S(1)}, u32[]{:S(2)}, u32[]{:S(2)}) collective-permute-start(bf16[672,384]{1,0:T(8,128)(2,1)} %get-tuple-element.60.refs_0_), channel_id=1, source_target_pairs={{0,384},{128,0},{256,128},{384,256},{1,385},{129,1},{257,129},{385... | collective-permute-start | bytes 1548296 | tf_op jit(solution)/shard_map/ppermute | solution.py:37
  187.5 13.9 %collective-permute-start.24 = (bf16[672,384]{1,0:T(8,128)(2,1)}, bf16[672,384]{1,0:T(8,128)(2,1)S(1)}, u32[]{:S(2)}, u32[]{:S(2)}) collective-permute-start(bf16[672,384]{1,0:T(8,128)(2,1)} %get-tuple-element.61.refs_6_), channel_id=1, source_target_pairs={{0,64},{64,0},{1,65},{65,1},{2,66},{66,2},{3,67},{67,3},{4,68},{68... | collective-permute-start | bytes 1548296 | tf_op jit(solution)/shard_map/ppermute | solution.py:37
  194.1 11.0 %collective-permute-start.22 = (bf16[672,384]{1,0:T(8,128)(2,1)S(1)}, bf16[672,384]{1,0:T(8,128)(2,1)S(1)}, u32[]{:S(2)}, u32[]{:S(2)}) collective-permute-start(bf16[672,384]{1,0:T(8,128)(2,1)S(1)} %collective-permute-done.19.refs_1_), channel_id=1, source_target_pairs={{0,128},{128,256},{256,384},{384,0},{1,129},{129,257},{257,385},{3... | collective-permute-start | bytes 1548296 | tf_op jit(solution)/shard_map/ppermute | solution.py:37
  197.5 12.2 %collective-permute-start.23 = (bf16[672,384]{1,0:T(8,128)(2,1)S(1)}, bf16[672,384]{1,0:T(8,128)(2,1)S(1)}, u32[]{:S(2)}, u32[]{:S(2)}) collective-permute-start(bf16[672,384]{1,0:T(8,128)(2,1)S(1)} %collective-permute-done.19.refs_1_), channel_id=1, source_target_pairs={{0,384},{128,0},{256,128},{384,256},{1,385},{129,1},{257,129},{385... | collective-permute-start | bytes 1548296 | tf_op jit(solution)/shard_map/ppermute | solution.py:37
  211.8 3.7 %copy-start.10 = (bf16[1,256,192]{1,2,0:T(8,128)(2,1)S(1)}, bf16[1,256,192]{1,2,0:T(8,128)(2,1)}, u32[]{:S(2)}) copy-start(bf16[1,256,192]{1,2,0:T(8,128)(2,1)} %param.10) | copy-start | bytes 294916
  211.8 3.7 %copy-start.12 = (bf16[192,256]{1,0:T(8,128)(2,1)S(1)}, bf16[192,256]{1,0:T(8,128)(2,1)}, u32[]{:S(2)}) copy-start(bf16[192,256]{1,0:T(8,128)(2,1)} %copy-done.11) | copy-start | bytes 294916
  211.8 3.7 %copy-start.14 = (bf16[192,256]{1,0:T(8,128)(2,1)S(1)}, bf16[192,256]{1,0:T(8,128)(2,1)}, u32[]{:S(2)}) copy-start(bf16[192,256]{1,0:T(8,128)(2,1)} %copy-done.13) | copy-start | bytes 294916
  (7 other events, 8.9 us)
Sparse Core Ops, SparseCore 0:
  29.5 42.5 all-gather.4
  82.9 55.1 all-gather.6
  141.0 63.1 reduce-scatter.1

commit v4 on v2

v4 whole, which is shorter than its diff:
```python
import functools

import jax
import jax.numpy as jnp
import numpy as np
from jax import lax
from jax.experimental import pallas as pl
from jax.experimental.pallas import tpu as pltpu
from jax.sharding import Mesh, PartitionSpec as P

EPS = 1e-05
AXES = ("x", "zl", "s", "y", "c")
SIZES = {"x": 4, "zl": 2, "s": 4, "y": 8, "c": 2}
D = 3072
TOK = 256
G = 336
F = 192
N_T = 16
N_DP = 8
DS = D // N_DP
N_EARLY = 6
TILE = 336
OFFSETS = ((0, 0), (0, 1), (-1, 0), (1, 0), (-1, 1), (1, 1), (2, 0), (2, 1))

VM = pl.BlockSpec(memory_space=pltpu.VMEM)
HB = pl.BlockSpec(memory_space=pl.ANY)
SM = pl.BlockSpec(memory_space=pltpu.SMEM)


def shift(value, **steps):
    axes = tuple(a for a in AXES if a in steps)
    sizes = [SIZES[a] for a in axes]
    pairs = []
    for i in range(int(np.prod(sizes))):
        at = np.unravel_index(i, sizes)
        to = [(at[k] + steps[a]) % sizes[k] for k, a in enumerate(axes)]
        pairs.append((i, int(np.ravel_multi_index(to, sizes))))
    return lax.ppermute(value, axes if len(axes) > 1 else axes[0], pairs)


def swapped(value, step):
    pairs = []
    for e in range(N_DP):
        for y in range(N_DP):
            d = (((y // 2) + step) % 4) * 2 + y % 2
            pairs.append((e * N_DP + y, d * N_DP + e))
    return lax.ppermute(value, ("x", "zl", "y"), pairs)


def gather_ring(own, ready=()):
    z = shift(own, zl=1)
    behind = shift(own, x=1)
    ahead = shift(own, x=-1)
    z, behind, ahead, ready = lax.optimization_barrier((z, behind, ahead, ready))
    z_behind = shift(z, x=1)
    z_ahead = shift(z, x=-1)
    if ready:
        z_behind, z_ahead = lax.optimization_barrier((z_behind, z_ahead))
    across = shift(behind, x=1)
    z_across = shift(z_ahead, x=-1)
    return [own, z, behind, ahead, z_behind, z_ahead, across, z_across], ready


def after(value, earlier):
    return lax.optimization_barrier((value, earlier))[0]


def places():
    x, zl = lax.axis_index("x"), lax.axis_index("zl")
    return jnp.stack([((x + dx) % 4) * 2 + (zl + dz) % 2 for dx, dz in OFFSETS]).astype(jnp.int32)


def gained_into(act_ref, gain_ref, out_ref):
    total = jnp.zeros((8, TOK), jnp.float32)
    for t in range(N_T):
        v = act_ref[t].astype(jnp.float32)
        total = total + jnp.sum((v * v).reshape(F // 8, 8, TOK), axis=0)
        out_ref[t * F : (t + 1) * F, :] = (v * gain_ref[t * F : (t + 1) * F, :]).astype(jnp.bfloat16)
    return lax.rsqrt(jnp.sum(total, axis=0, keepdims=True) / D + EPS)


def fetch(pairs, sems):
    copies = [pltpu.make_async_copy(src, dst, sems.at[i]) for i, (src, dst) in enumerate(pairs)]
    for copy in copies:
        copy.start()
    return copies


def norm_kernel(acts, gain, b_out, f_out, scales_out, saved, act, sems):
    copies = fetch([(acts.at[:, 2], saved), (acts.at[:, 0], act)], sems)
    copies[0].wait()
    scales_out[0:1, :] = gained_into(saved, gain, b_out)
    copies[1].wait()
    scales_out[1:2, :] = gained_into(act, gain, f_out)


def early_kernel(place, *refs):
    w_from = refs[:N_EARLY]
    acts, normal_b_from, normal_f_from, b_out, f_out, dy, w, normal_b, normal_f, sems = refs[N_EARLY:]
    copies = fetch(
        [(normal_b_from, normal_b), (normal_f_from, normal_f), (acts.at[:, 1], dy)]
        + [(w_from[r], w.at[r]) for r in range(N_EARLY)],
        sems,
    )
    for copy in copies:
        copy.wait()
    for m in range(0, G, TILE):
        sums = [jnp.zeros((TILE, TOK), jnp.float32) for _ in range(5)]
        for r in range(N_EARLY):
            d = place[r]
            rows = pl.ds(pl.multiple_of(d * DS, DS), DS)
            n, f = normal_b[rows, :], normal_f[rows, :]
            g = dy[pl.ds(2 * d, 2)].reshape(DS, TOK)
            w_g = w[r, m : m + TILE, :]
            w_u = w[r, G + m : G + m + TILE, :]
            w_d = w[r, 2 * G + m : 2 * G + m + TILE, :]
            for k, (left, right) in enumerate(((w_g, n), (w_u, n), (w_d, g), (w_g, f), (w_u, f))):
                sums[k] = sums[k] + jnp.dot(left, right, preferred_element_type=jnp.float32)
        for k in range(3):
            b_out[k * G + m : k * G + m + TILE, :] = sums[k]
        for k in range(2):
            f_out[k * G + m : k * G + m + TILE, :] = sums[3 + k]


def columns(place, i):
    return pl.ds(pl.multiple_of(place[N_EARLY + i] * DS, DS), DS)


def inner_kernel(place, w_6, w_7, early_from, n_from, acts, weight, scales, dg_out, dgs_out, stat_out, w, early, normal, dy, sems):
    last = N_DP - N_EARLY
    copies = fetch(
        [(n_from.at[columns(place, i), :], normal.at[i]) for i in range(last)]
        + [(acts.at[pl.ds(2 * place[N_EARLY + i], 2), 1], dy.at[i]) for i in range(last)]
        + [(w_6, w.at[0]), (w_7, w.at[1]), (early_from, early)],
        sems,
    )
    scale = scales[0:1, :]
    row = weight[...]
    stat = jnp.zeros((1, TOK), jnp.float32)
    for copy in copies:
        copy.wait()
    for m in range(0, G, TILE):
        gate, up, hid = (early[k * G + m : k * G + m + TILE, :] for k in range(3))
        for i in range(last):
            n, g = normal[i], dy[i].reshape(DS, TOK)
            gate = gate + jnp.dot(w[i, m : m + TILE, :], n, preferred_element_type=jnp.float32)
            up = up + jnp.dot(w[i, G + m : G + m + TILE, :], n, preferred_element_type=jnp.float32)
            hid = hid + jnp.dot(w[i, 2 * G + m : 2 * G + m + TILE, :], g, preferred_element_type=jnp.float32)
        gate = scale * gate
        up = scale * up
        sg = jax.nn.sigmoid(gate)
        hid = hid * row
        dgate = hid * up * (sg * (1.0 + gate * (1.0 - sg)))
        dup = hid * (gate * sg)
        dgate_r, dup_r = dgate.astype(jnp.bfloat16), dup.astype(jnp.bfloat16)
        dg_out[m : m + TILE, :] = dgate_r
        dg_out[G + m : G + m + TILE, :] = dup_r
        dgs_out[m : m + TILE, :] = (dgate * scale).astype(jnp.bfloat16)
        dgs_out[G + m : G + m + TILE, :] = (dup * scale).astype(jnp.bfloat16)
        stat = stat + jnp.sum(
            dgate_r.astype(jnp.float32) * gate + dup_r.astype(jnp.float32) * up, axis=0, keepdims=True
        )
    stat_out[...] = stat


def outer_kernel(place, *refs):
    w_from = refs[:N_DP]
    dg, early, n_from, weight, scales, stat, keep, send, w, normal, hidden, dg_t, hid_t, sems = refs[N_DP:]
    last = N_DP - N_EARLY
    order = list(range(N_EARLY, N_DP)) + list(range(N_EARLY))
    pairs = [(n_from.at[columns(place, i), :], normal.at[i]) for i in range(last)]
    copies = fetch(pairs + [(w_from[r], w.at[r]) for r in order], sems)
    dg_t[...] = dg[...].T
    row = weight[...]
    scale = scales[1:2, :]
    for copy in copies[: 2 * last]:
        copy.wait()
    for m in range(0, G, TILE):
        gate, up = (early[k * G + m : k * G + m + TILE, :] for k in range(2))
        for i in range(last):
            n = normal[i]
            gate = gate + jnp.dot(w[N_EARLY + i, m : m + TILE, :], n, preferred_element_type=jnp.float32)
            up = up + jnp.dot(w[N_EARLY + i, G + m : G + m + TILE, :], n, preferred_element_type=jnp.float32)
        gate = scale * gate
        up = scale * up
        hidden[m : m + TILE, :] = (gate * jax.nn.sigmoid(gate) * up * row).astype(jnp.bfloat16)
    hid_t[...] = hidden[...].T
    me = place[N_DP]
    first = lax.rem(me, 2) == 0
    for k, r in enumerate(order):
        if k >= last:
            copies[last + k].wait()
        into = jnp.dot(dg_t[...], w[r, : 2 * G, :], preferred_element_type=jnp.float32)
        part = jnp.dot(hid_t[...], w[r, 2 * G :, :], preferred_element_type=jnp.float32)
        for value, low in ((into, 0), (part, F)):
            value = value.astype(jnp.bfloat16).T
            one, two = value[:F], value[F:]
            keep[place[r], low : low + F, :] = jnp.where(first, one, two)
            send[place[r], low : low + F, :] = jnp.where(first, two, one)
    value = stat[...]
    high = value.astype(jnp.bfloat16).astype(jnp.float32)
    rows = lax.broadcasted_iota(jnp.int32, (2 * N_T, TOK), 0)
    block = jnp.where(rows == me, high, jnp.where(rows == me + N_T, value - high, 0.0)).astype(jnp.bfloat16)
    for y in range(N_T // 2):
        keep[y, 2 * F :, :] = block
        send[y, 2 * F :, :] = block


def grad_kernel(blocks, place, *refs):
    dgs_from = refs[: len(blocks)]
    start = blocks[0] == 0
    if start:
        tokens, near_out, far_out, near, far, dgs, sems = refs[len(blocks) :]
    else:
        tokens, gain, near_sum, far_sum, near_out, far_out, near, far, dgs, sums, sems = refs[len(blocks) :]
    copies = []
    for k, r in enumerate(blocks):
        at = pl.ds(2 * place[r], 2)
        copies += [(tokens.at[at, 0], near.at[k]), (dgs_from[k], dgs.at[k])]
    if not start:
        copies += [(near_sum, sums.at[0]), (far_sum, sums.at[1])]
    for k, r in enumerate(blocks):
        copies.append((tokens.at[pl.ds(2 * place[r], 2), 1], far.at[k]))
    copies = fetch(copies, sems)
    for copy in copies[: -len(blocks)]:
        copy.wait()
    for j, (src, out) in enumerate(((near, near_out), (far, far_out))):
        if j:
            for copy in copies[-len(blocks) :]:
                copy.wait()
        for m in range(0, 2 * G, G):
            total = jnp.zeros((G, DS), jnp.float32) if start else sums[j, m : m + G, :]
            for k in range(len(blocks)):
                v = src[k].reshape(DS, TOK)
                total = total + lax.dot_general(
                    dgs[k, m : m + G, :], v, (((1,), (1,)), ((), ())), preferred_element_type=jnp.float32
                )
            if start:
                out[m : m + G, :] = total
            else:
                at = place[0] if j == 0 else lax.rem(place[0] + 4, N_DP)
                out[m : m + G, :] = (total * gain[:, pl.ds(pl.multiple_of(at * DS, DS), DS)]).astype(jnp.bfloat16)


def assemble_kernel(place, *refs):
    parts = refs[:N_DP]
    gate_out, up_out = refs[N_DP:]
    for r in range(N_DP):
        lanes = pl.ds(pl.multiple_of(place[r] * DS, DS), DS)
        gate_out[:, lanes] = parts[r][:G, :]
        up_out[:, lanes] = parts[r][G:, :]


def params(mib):
    return pltpu.CompilerParams(vmem_limit_bytes=mib << 20)


def cost(flops, nbytes):
    return pl.CostEstimate(flops=flops, bytes_accessed=nbytes, transcendentals=0)


def combine(route_ids, probs):
    return jnp.sum(jnp.where(route_ids == 0, probs, jnp.zeros_like(probs)), axis=-1)[None, :]


def local(
    passed_activations,
    kept_section_input,
    handed_grads,
    norm_gain,
    gate_weight,
    up_weight,
    down_weight,
    routes,
    route_probs,
):
    place = places()
    here = lax.axis_index("y") * 2 + lax.axis_index("c")
    place_t = jnp.concatenate([place, here[None].astype(jnp.int32)])
    saved_t = kept_section_input[0].T
    acts_t = shift(passed_activations[0].T, s=1)
    dy_t = shift(handed_grads[0].T, s=-1)
    gain = norm_gain[0]
    own_weights = jnp.concatenate([gate_weight[0].T, up_weight[0].T, down_weight[0]], axis=0)
    ready = (gain[:, None], place_t, combine(routes[0, 0], route_probs[0, 0]), combine(routes[0, 1], route_probs[0, 1]))
    weights, ready = gather_ring(own_weights, ready)
    gain_col, place, weight_f, weight_b = ready
    acts = lax.all_gather(
        after(jnp.concatenate([acts_t, dy_t, saved_t], axis=0), own_weights), ("y", "c"), axis=0
    ).reshape(N_T, 3, F, TOK)

    bf, f32 = jnp.bfloat16, jnp.float32
    last = N_DP - N_EARLY
    normal_b, normal_f, scales = pl.pallas_call(
        norm_kernel,
        in_specs=[HB, VM],
        out_specs=[VM] * 3,
        out_shape=[
            jax.ShapeDtypeStruct((D, TOK), bf),
            jax.ShapeDtypeStruct((D, TOK), bf),
            jax.ShapeDtypeStruct((2, TOK), f32),
        ],
        scratch_shapes=[pltpu.VMEM((N_T, F, TOK), bf), pltpu.VMEM((N_T, F, TOK), bf), pltpu.SemaphoreType.DMA((2,))],
        compiler_params=params(56),
        cost_estimate=cost(8 * D * TOK, 16 << 20),
        name="norms",
    )(acts, gain_col)
    swap_t = after(saved_t, scales)
    near, far = swapped(swap_t, 0), swapped(swap_t, 2)
    early_b, early_f = pl.pallas_call(
        early_kernel,
        in_specs=[SM] + [HB] * (N_EARLY + 3),
        out_specs=[VM] * 2,
        out_shape=[jax.ShapeDtypeStruct((3 * G, TOK), f32), jax.ShapeDtypeStruct((2 * G, TOK), f32)],
        scratch_shapes=[
            pltpu.VMEM((N_T, F, TOK), bf),
            pltpu.VMEM((N_EARLY, 3 * G, DS), bf),
            pltpu.VMEM((D, TOK), bf),
            pltpu.VMEM((D, TOK), bf),
            pltpu.SemaphoreType.DMA((N_EARLY + 3,)),
        ],
        compiler_params=params(56),
        cost_estimate=cost(10 * D * G * TOK, 32 << 20),
        name="early",
    )(place, *weights[:N_EARLY], acts, normal_b, normal_f)
    near, far, early_b, *weights[N_EARLY:] = lax.optimization_barrier((near, far, early_b, *weights[N_EARLY:]))
    tokens = lax.all_gather(jnp.concatenate([near, far], axis=0), ("y", "c"), axis=0).reshape(N_T, 2, F, TOK)
    dg, dgs, stat = pl.pallas_call(
        inner_kernel,
        in_specs=[SM] + [HB] * 5 + [VM, VM],
        out_specs=[VM] * 3,
        out_shape=[
            jax.ShapeDtypeStruct((2 * G, TOK), bf),
            jax.ShapeDtypeStruct((2 * G, TOK), bf),
            jax.ShapeDtypeStruct((1, TOK), f32),
        ],
        scratch_shapes=[
            pltpu.VMEM((last, 3 * G, DS), bf),
            pltpu.VMEM((3 * G, TOK), f32),
            pltpu.VMEM((last, DS, TOK), bf),
            pltpu.VMEM((last, 2, F, TOK), bf),
            pltpu.SemaphoreType.DMA((3 * last + 1,)),
        ],
        compiler_params=params(56),
        cost_estimate=cost(2 * D * G * TOK, 12 << 20),
        name="inner",
    )(place, *weights[N_EARLY:], early_b, normal_b, acts, weight_b, scales)
    dgs_all, _ = gather_ring(dgs)
    keep, send = pl.pallas_call(
        outer_kernel,
        in_specs=[SM] + [HB] * N_DP + [VM, VM, HB, VM, VM, VM],
        out_specs=[VM, VM],
        out_shape=[jax.ShapeDtypeStruct((N_T // 2, 2 * F + 2 * N_T, TOK), bf)] * 2,
        scratch_shapes=[
            pltpu.VMEM((N_DP, 3 * G, DS), bf),
            pltpu.VMEM((last, DS, TOK), bf),
            pltpu.VMEM((G, TOK), bf),
            pltpu.VMEM((TOK, 2 * G), bf),
            pltpu.VMEM((TOK, G), bf),
            pltpu.SemaphoreType.DMA((N_DP + last,)),
        ],
        compiler_params=params(56),
        cost_estimate=cost(8 * D * G * TOK, 28 << 20),
        name="outer",
    )(place, *weights, dg, early_f, normal_f, weight_f, scales, stat)
    send = after(send, tuple(dgs_all[1:4]))
    got = shift(send, c=1)
    got, keep = lax.optimization_barrier((got, after(keep, tuple(dgs_all[4:7]))))
    both = (keep.astype(f32) + got.astype(f32)).astype(bf)
    summed = lax.psum_scatter(both, "y", scatter_dimension=0)

    half = N_DP // 2
    sums_shape = [jax.ShapeDtypeStruct((2 * G, DS), f32)] * 2
    fetched = [
        pltpu.VMEM((half, 2, F, TOK), bf),
        pltpu.VMEM((half, 2, F, TOK), bf),
        pltpu.VMEM((half, 2 * G, TOK), bf),
    ]
    near_sum, far_sum = pl.pallas_call(
        functools.partial(grad_kernel, range(half)),
        in_specs=[SM] + [HB] * (half + 1),
        out_specs=[VM, VM],
        out_shape=sums_shape,
        scratch_shapes=fetched + [pltpu.SemaphoreType.DMA((3 * half,))],
        compiler_params=params(56),
        cost_estimate=cost(4 * DS * G * TOK * N_DP, 14 << 20),
        name="grad_first",
    )(place, *dgs_all[:half], tokens)
    near_grad, far_grad = pl.pallas_call(
        functools.partial(grad_kernel, range(half, N_DP)),
        in_specs=[SM] + [HB] * (half + 1) + [VM, HB, HB],
        out_specs=[VM, VM],
        out_shape=[jax.ShapeDtypeStruct((2 * G, DS), bf)] * 2,
        scratch_shapes=fetched
        + [pltpu.VMEM((2, 2 * G, DS), f32), pltpu.SemaphoreType.DMA((3 * half + 2,))],
        compiler_params=params(56),
        cost_estimate=cost(4 * DS * G * TOK * N_DP, 14 << 20),
        name="grad_last",
    )(place, *dgs_all[half:], tokens, gain[None, :], near_sum, far_sum)
    z = shift(near_grad, zl=1)
    behind = shift(near_grad, x=1)
    ahead = shift(near_grad, x=-1)
    z_far = shift(far_grad, zl=1)
    z_behind = shift(z, x=1)
    z_ahead = shift(z, x=-1)
    parts = [near_grad, z, behind, ahead, z_behind, z_ahead, far_grad, z_far]
    grad_g, grad_u = pl.pallas_call(
        assemble_kernel,
        in_specs=[SM] + [VM] * N_DP,
        out_specs=[VM, VM],
        out_shape=[jax.ShapeDtypeStruct((G, D), bf)] * 2,
        compiler_params=params(24),
        cost_estimate=cost(0, 8 << 20),
        name="assemble",
    )(place, *parts)

    into = summed[:F].astype(f32)
    mean_stat = jnp.sum(summed[2 * F :].astype(f32), axis=0, keepdims=True) / D
    gain_here = lax.dynamic_slice_in_dim(gain, here * F, F)[:, None]
    output = (acts_t.astype(f32) + summed[F : 2 * F].astype(f32)).astype(bf)
    scale_b = scales[0:1]
    hat = saved_t.astype(f32) * scale_b
    stored = (dy_t.astype(f32) + scale_b * (into * gain_here - hat * mean_stat)).astype(bf)
    return (output.T[None], stored.T[None], grad_g.T[None], grad_u.T[None])


def solution(mesh):
    fine = Mesh(mesh.devices.reshape(tuple(SIZES[a] for a in AXES)), AXES)
    dp, tensor = ("x", "zl"), ("y", "c")
    placed = (
        P("s", dp, tensor),
        P("s", dp, tensor),
        P("s", dp, tensor),
        P("s", None),
        P("s", dp, tensor),
        P("s", dp, tensor),
        P("s", tensor, dp),
        P("s", None, dp, None),
        P("s", None, dp, None),
    )
    return jax.shard_map(
        local,
        mesh=fine,
        in_specs=placed,
        out_specs=(
            P("s", dp, tensor),
            P("s", dp, tensor),
            P("s", None, tensor),
            P("s", None, tensor),
        ),
        check_vma=False,
    )
```

time: 209 us -> 227 us (1.086)
  Pallas kernels: 28.4 us -> 41.3 us
  waiting for transfers between devices: 55.3 us -> 62.2 us
  local copies, waits for them, and re-layouts: 13.3 us -> 6.83 us
  other arithmetic: 5.7 us -> 9.89 us
    ppermute x22 -> x23, waiting for transfers between devices: 47.8 us -> 62.1 us  [shift(): return lax.ppermute(value, axes if len(axes) > 1 else axes[0], pairs)]
    pallas_call x4 -> x6, Pallas kernels: 24.8 us -> 38.3 us  [the longest x1 9.39 us: local(): pl.pallas_call(outer_kernel, in_specs=[SM] + [HB] * N_DP + [VM, VM, HB, V...]
    ppermute x2, waiting for transfers between devices: 7.5 us -> 0.01 us  [swapped(): return lax.ppermute(value, ('x', 'zl', 'y'), pairs)]
    unnamed x52 -> x40, local copies, waits for them, and re-layouts: 10.2 us -> 3.75 us
    convert_element_type x0 -> x1, other arithmetic: none -> 3.25 us  [local(): both = (keep.astype(f32) + got.astype(f32)).astype(bf)]
    another operation x2 -> x0, local copies, waits for them, and re-layouts: 2.32 us -> none  [the longest x1 1.66 us: local(): gain_col = gain[:, None]]
    ppermute x22 -> x23, starting transfers between devices: 79.6 us -> 79.4 us  [shift(): return lax.ppermute(value, axes if len(axes) > 1 else axes[0], pairs)]
  transfers between devices with their start and end apart: 27 -> 28, of which waited for: 17 -> 14; matrix products, arithmetic and copies ran while one was open for 3% -> 5% of each run, Pallas kernels for 14% -> 17%
where the time goes in v4:
time: 227 us; the launch traced here: 225 us
  starting transfers between devices  90.7 us (40%)
  waiting for transfers between devices  62.2 us (27%)
  Pallas kernels  41.3 us (18%)
  between operations  14.3 us (6%)
  other arithmetic  9.89 us (4%)
  local copies, waits for them, and re-layouts  6.83 us (3%)
    ppermute x23, starting transfers between devices, shift(): return lax.ppermute(value, axes if len(axes) > 1 else axes[0], pairs)  79.4 us
    ppermute x23, waiting for transfers between devices, shift(): return lax.ppermute(value, axes if len(axes) > 1 else axes[0], pairs)  62.1 us
    ppermute x2, starting transfers between devices, swapped(): return lax.ppermute(value, ('x', 'zl', 'y'), pairs)  11.1 us
    pallas_call x1, Pallas kernels, local(): pl.pallas_call(outer_kernel, in_specs=[SM] + [HB] * N_DP + [VM, VM, HB, V...  9.39 us
    pallas_call x1, Pallas kernels, local(): pl.pallas_call(early_kernel, in_specs=[SM] + [HB] * (N_EARLY + 3), out_sp...  8.36 us
    pallas_call x1, Pallas kernels, local(): pl.pallas_call(functools.partial(grad_kernel, range(half, N_DP)), in_spec...  5.84 us
    pallas_call x1, Pallas kernels, local(): pl.pallas_call(functools.partial(grad_kernel, range(half)), in_specs=[SM]...  5.15 us
    pallas_call x1, Pallas kernels, local(): pl.pallas_call(norm_kernel, in_specs=[HB, VM], out_specs=[VM] * 3, out_sh...  5.09 us
  transfers between devices with their start and end apart: 28, of which 14 were waited for; matrix products, arithmetic and copies ran while one was open for 5% of the time, Pallas kernels for 17%

profile of v4, /device:TPU:6, one launch (start us, length us, event | category | flops | bytes accessed | tf_op | source)
XLA Modules:
  0.0 225.2 jit_solution(14314560778397743709)
XLA Ops:
  7.2 10.9 %collective-permute-start.6 = (bf16[192,256]{1,0:T(8,128)(2,1)}, bf16[192,256]{1,0:T(8,128)(2,1)S(1)}, u32[]{:S(2)}, u32[]{:S(2)}) collective-permute-start(bf16[192,256]{1,0:T(8,128)(2,1)} %bitcast.75), channel_id=1, source_target_pairs={{0,48},{16,0},{32,16},{48,32},{1,49},{17,1},{33,17},{49,33},{2,50}... | collective-permute-start | bytes 294920 | tf_op jit(solution)/shard_map/ppermute | solution.py:38
  18.2 1.9 collective-permute-start
  22.7 5.9 %collective-permute-done = bf16[192,256]{1,0:T(8,128)(2,1)S(1)} collective-permute-done((bf16[192,256]{1,0:T(8,128)(2,1)}, bf16[192,256]{1,0:T(8,128)(2,1)S(1)}, u32[]{:S(2)}, u32[]{:S(2)}) %collective-permute-start) | collective-permute-done | bytes 98336 | tf_op jit(solution)/shard_map/ppermute | solution.py:38
  28.6 1.6 pad_maximum_fusion.1
  30.3 3.6 %collective-permute-start.1 = (bf16[1008,384]{1,0:T(8,128)(2,1)S(1)}, bf16[1008,384]{1,0:T(8,128)(2,1)S(1)}, u32[]{:S(2)}, u32[]{:S(2)}) collective-permute-start(bf16[1008,384]{1,0:T(8,128)(2,1)S(1)} %pad_maximum_fusion.refs_0_), channel_id=1, source_target_pairs={{0,64},{64,0},{1,65},{65,1},{2,66},{66,2},{3,67},{67,3},{4,68},{68... | collective-permute-start | bytes 2322440 | tf_op jit(solution)/shard_map/ppermute | solution.py:38
  33.9 2.4 %collective-permute-start.2 = (bf16[1008,384]{1,0:T(8,128)(2,1)S(1)}, bf16[1008,384]{1,0:T(8,128)(2,1)S(1)}, u32[]{:S(2)}, u32[]{:S(2)}) collective-permute-start(bf16[1008,384]{1,0:T(8,128)(2,1)S(1)} %pad_maximum_fusion.refs_0_), channel_id=1, source_target_pairs={{0,128},{128,256},{256,384},{384,0},{1,129},{129,257},{257,385},{3... | collective-permute-start | bytes 2322440 | tf_op jit(solution)/shard_map/ppermute | solution.py:38
  36.2 3.5 %collective-permute-start.3 = (bf16[1008,384]{1,0:T(8,128)(2,1)S(1)}, bf16[1008,384]{1,0:T(8,128)(2,1)S(1)}, u32[]{:S(2)}, u32[]{:S(2)}) collective-permute-start(bf16[1008,384]{1,0:T(8,128)(2,1)S(1)} %pad_maximum_fusion.refs_0_), channel_id=1, source_target_pairs={{0,384},{128,0},{256,128},{384,256},{1,385},{129,1},{257,129},{385... | collective-permute-start | bytes 2322440 | tf_op jit(solution)/shard_map/ppermute | solution.py:38
  41.0 9.0 %collective-permute-done.1.refs_1_ = bf16[1008,384]{1,0:T(8,128)(2,1)S(1)} collective-permute-done((bf16[1008,384]{1,0:T(8,128)(2,1)S(1)}, bf16[1008,384]{1,0:T(8,128)(2,1)S(1)}, u32[]{:S(2)}, u32[]{:S(2)}) %collective-permute-start.1) | collective-permute-done | bytes 774176 | tf_op jit(solution)/shard_map/ppermute | solution.py:38
  50.0 3.4 %collective-permute-done.2.refs_2_ = bf16[1008,384]{1,0:T(8,128)(2,1)S(1)} collective-permute-done((bf16[1008,384]{1,0:T(8,128)(2,1)S(1)}, bf16[1008,384]{1,0:T(8,128)(2,1)S(1)}, u32[]{:S(2)}, u32[]{:S(2)}) %collective-permute-start.2) | collective-permute-done | bytes 774176 | tf_op jit(solution)/shard_map/ppermute | solution.py:38
  53.4 3.3 %collective-permute-done.3.refs_3_ = bf16[1008,384]{1,0:T(8,128)(2,1)S(1)} collective-permute-done((bf16[1008,384]{1,0:T(8,128)(2,1)S(1)}, bf16[1008,384]{1,0:T(8,128)(2,1)S(1)}, u32[]{:S(2)}, u32[]{:S(2)}) %collective-permute-start.3) | collective-permute-done | bytes 774176 | tf_op jit(solution)/shard_map/ppermute | solution.py:38
  56.7 2.2 collective-permute-start.4
  58.9 3.7 %collective-permute-start.5 = (bf16[1008,384]{1,0:T(8,128)(2,1)S(1)}, bf16[1008,384]{1,0:T(8,128)(2,1)}, u32[]{:S(2)}, u32[]{:S(2)}) collective-permute-start(bf16[1008,384]{1,0:T(8,128)(2,1)S(1)} %collective-permute-done.1.refs_1_), channel_id=1, source_target_pairs={{0,384},{128,0},{256,128},{384,256},{1,385},{129,1},{257,129},{385... | collective-permute-start | bytes 2322440 | tf_op jit(solution)/shard_map/ppermute | solution.py:38
  62.6 3.4 %collective-permute-start.9 = (bf16[1008,384]{1,0:T(8,128)(2,1)S(1)}, bf16[1008,384]{1,0:T(8,128)(2,1)}, u32[]{:S(2)}, u32[]{:S(2)}) collective-permute-start(bf16[1008,384]{1,0:T(8,128)(2,1)S(1)} %collective-permute-done.2.refs_2_), channel_id=1, source_target_pairs={{0,128},{128,256},{256,384},{384,0},{1,129},{129,257},{257,385},{3... | collective-permute-start | bytes 2322440 | tf_op jit(solution)/shard_map/ppermute | solution.py:38
  66.0 12.8 %collective-permute-done.4.refs_4_ = bf16[1008,384]{1,0:T(8,128)(2,1)S(1)} collective-permute-done((bf16[1008,384]{1,0:T(8,128)(2,1)S(1)}, bf16[1008,384]{1,0:T(8,128)(2,1)S(1)}, u32[]{:S(2)}, u32[]{:S(2)}) %collective-permute-start.4) | collective-permute-done | bytes 774176 | tf_op jit(solution)/shard_map/ppermute | solution.py:38
  79.7 2.2 collective-permute-start.10
  82.0 1.7 copy.13.gain
  83.6 5.1 %norms.1 = (bf16[3072,256]{1,0:T(8,128)(2,1)}, bf16[3072,256]{1,0:T(8,128)(2,1)}, f32[2,256]{1,0:T(2,128)}) custom-call(bf16[16,3,192,256]{3,2,1,0:T(8,128)(2,1)} %bitcast.57, f32[3072,1]{1,0:T(8,128)} %copy.13.gain), custom_call_target="tpu_custom_call" | custom-call | flops 6291456 | bytes 16777216 | tf_op jit(solution)/shard_map/norms/pallas_call | solution.py:294
  88.8 8.5 %collective-permute-start.7 = (bf16[192,256]{1,0:T(8,128)(2,1)S(1)}, bf16[192,256]{1,0:T(8,128)(2,1)S(1)}, u32[]{:S(2)}, u32[]{:S(2)}) collective-permute-start(bf16[192,256]{1,0:T(8,128)(2,1)S(1)} %bitcast.63), channel_id=1, source_target_pairs={{0,0},{2,64},{4,128},{6,192},{8,256},{10,320},{12,384},{14,448},{6... | collective-permute-start | bytes 294920 | tf_op jit(solution)/shard_map/ppermute | solution.py:47
  97.3 2.6 %collective-permute-start.8 = (bf16[192,256]{1,0:T(8,128)(2,1)S(1)}, bf16[192,256]{1,0:T(8,128)(2,1)S(1)}, u32[]{:S(2)}, u32[]{:S(2)}) collective-permute-start(bf16[192,256]{1,0:T(8,128)(2,1)S(1)} %bitcast.64), channel_id=1, source_target_pairs={{0,256},{2,320},{4,384},{6,448},{8,0},{10,64},{12,128},{14,192},{6... | collective-permute-start | bytes 294920 | tf_op jit(solution)/shard_map/ppermute | solution.py:47
  99.9 8.4 %early.1 = (f32[1008,256]{1,0:T(8,128)}, f32[672,256]{1,0:T(8,128)}) custom-call(s32[9]{0:T(128)} %concatenate.13.place, bf16[1008,384]{1,0:T(8,128)(2,1)} %copy-done.3, bf16[1008,384]{1,0:T(8,128)(2,1)} %copy-done.4, bf16[1008,384]{1,0:T(8,128)(2,1)} %copy-done.5, bf16[1008,384]{1,0:T(8,128)(2,1)} %copy-done.6, bf16[1008,384]{1,0:T(8,128)(2,1)} %copy-done.7, ...), custom_call_target="tpu_custom_call" | custom-call | flops 2642411520 | bytes 33554432 | tf_op jit(solution)/shard_map/early/pallas_call | solution.py:310
  109.1 4.5 %inner.1 = (bf16[672,256]{1,0:T(8,128)(2,1)}, bf16[672,256]{1,0:T(8,128)(2,1)}, f32[1,256]{1,0:T(1,128)}) custom-call(s32[9]{0:T(128)} %concatenate.13.place, bf16[1008,384]{1,0:T(8,128)(2,1)} %collective-permute-done.9.w_6.refs_6_, bf16[1008,384]{1,0:T(8,128)(2,1)} %collective-permute-done.10.w_7.refs_7_, f32[1008,256]{1,0:T(8,128)} %get-tuple-element.58.early_from, ...), custom_call_target="tpu_custom_call" | custom-call | flops 528482304 | bytes 12582912 | tf_op jit(solution)/shard_map/inner/pallas_call | solution.py:328
  113.6 4.2 %collective-permute-start.11 = (bf16[672,256]{1,0:T(8,128)(2,1)}, bf16[672,256]{1,0:T(8,128)(2,1)S(1)}, u32[]{:S(2)}, u32[]{:S(2)}) collective-permute-start(bf16[672,256]{1,0:T(8,128)(2,1)} %get-tuple-element.65.refs_0_), channel_id=1, source_target_pairs={{0,64},{64,0},{1,65},{65,1},{2,66},{66,2},{3,67},{67,3},{4,68},{68... | collective-permute-start | bytes 1032200 | tf_op jit(solution)/shard_map/ppermute | solution.py:38
  117.8 5.2 %collective-permute-start.12 = (bf16[672,256]{1,0:T(8,128)(2,1)}, bf16[672,256]{1,0:T(8,128)(2,1)S(1)}, u32[]{:S(2)}, u32[]{:S(2)}) collective-permute-start(bf16[672,256]{1,0:T(8,128)(2,1)} %get-tuple-element.65.refs_0_), channel_id=1, source_target_pairs={{0,128},{128,256},{256,384},{384,0},{1,129},{129,257},{257,385},{3... | collective-permute-start | bytes 1032200 | tf_op jit(solution)/shard_map/ppermute | solution.py:38
  123.0 1.9 collective-permute-start.13
  124.9 9.4 %outer.1 = (bf16[8,416,256]{2,1,0:T(8,128)(2,1)}, bf16[8,416,256]{2,1,0:T(8,128)(2,1)}) custom-call(s32[9]{0:T(128)} %concatenate.13.place, bf16[1008,384]{1,0:T(8,128)(2,1)} %copy-done.3, bf16[1008,384]{1,0:T(8,128)(2,1)} %copy-done.4, bf16[1008,384]{1,0:T(8,128)(2,1)} %copy-done.5, bf16[1008,384]{1,0:T(8,128)(2,1)} %copy-done.6, ...), custom_call_target="tpu_custom_call" | custom-call | flops 2113929216 | bytes 29360128 | tf_op jit(solution)/shard_map/outer/pallas_call | solution.py:349
  134.4 1.9 collective-permute-start.14
  136.3 5.1 %collective-permute-start.15 = (bf16[672,256]{1,0:T(8,128)(2,1)S(1)}, bf16[672,256]{1,0:T(8,128)(2,1)S(1)}, u32[]{:S(2)}, u32[]{:S(2)}) collective-permute-start(bf16[672,256]{1,0:T(8,128)(2,1)S(1)} %collective-permute-done.11.refs_1_), channel_id=1, source_target_pairs={{0,128},{128,256},{256,384},{384,0},{1,129},{129,257},{257,385},{3... | collective-permute-start | bytes 1032200 | tf_op jit(solution)/shard_map/ppermute | solution.py:38
  141.5 1.9 collective-permute-start.16
  143.4 5.1 %collective-permute-start.17 = (bf16[672,256]{1,0:T(8,128)(2,1)S(1)}, bf16[672,256]{1,0:T(8,128)(2,1)S(1)}, u32[]{:S(2)}, u32[]{:S(2)}) collective-permute-start(bf16[672,256]{1,0:T(8,128)(2,1)S(1)} %collective-permute-done.12.refs_2_), channel_id=1, source_target_pairs={{0,128},{128,256},{256,384},{384,0},{1,129},{129,257},{257,385},{3... | collective-permute-start | bytes 1032200 | tf_op jit(solution)/shard_map/ppermute | solution.py:38
  148.5 1.3 collective-permute-done.15.refs_0_
  149.8 4.9 %collective-permute-done.16.refs_1_ = bf16[672,256]{1,0:T(8,128)(2,1)S(1)} collective-permute-done((bf16[672,256]{1,0:T(8,128)(2,1)S(1)}, bf16[672,256]{1,0:T(8,128)(2,1)S(1)}, u32[]{:S(2)}, u32[]{:S(2)}) %collective-permute-start.16) | collective-permute-done | bytes 344096 | tf_op jit(solution)/shard_map/ppermute | solution.py:38
  154.8 2.0 collective-permute-done.17.refs_2_
  156.8 3.2 %add_convert_fusion = bf16[8,416,256]{2,1,0:T(8,128)(2,1)} fusion(bf16[8,416,256]{2,1,0:T(8,128)(2,1)S(1)} %collective-permute-done.14, bf16[8,416,256]{2,1,0:T(8,128)(2,1)} %get-tuple-element.72), kind=kLoop, calls=%fused_computation | loop fusion | flops 3407872 | bytes 5111808 | tf_op jit(solution)/shard_map/convert_element_type | solution.py:369
  160.1 2.8 %collective-permute-start.18 = (bf16[672,256]{1,0:T(8,128)(2,1)S(1)}, bf16[672,256]{1,0:T(8,128)(2,1)S(1)}, u32[]{:S(2)}, u32[]{:S(2)}) collective-permute-start(bf16[672,256]{1,0:T(8,128)(2,1)S(1)} %collective-permute-done.16.refs_1_), channel_id=1, source_target_pairs={{0,384},{128,0},{256,128},{384,256},{1,385},{129,1},{257,129},{385... | collective-permute-start | bytes 1032200 | tf_op jit(solution)/shard_map/ppermute | solution.py:38
  162.9 5.2 %grad_first.1 = (f32[672,384]{1,0:T(8,128)}, f32[672,384]{1,0:T(8,128)}) custom-call(s32[9]{0:T(128)} %concatenate.13.place, bf16[672,256]{1,0:T(8,128)(2,1)} %get-tuple-element.65.refs_0_, bf16[672,256]{1,0:T(8,128)(2,1)} %copy-done.9, bf16[672,256]{1,0:T(8,128)(2,1)} %copy-done.10, bf16[672,256]{1,0:T(8,128)(2,1)} %copy-done.11, ...), custom_call_target="tpu_custom_call" | custom-call | flops 1056964608 | bytes 14680064 | tf_op jit(solution)/shard_map/grad_first/pallas_call | solution.py:379
  168.1 5.6 %collective-permute-done.18.refs_3_ = bf16[672,256]{1,0:T(8,128)(2,1)S(1)} collective-permute-done((bf16[672,256]{1,0:T(8,128)(2,1)S(1)}, bf16[672,256]{1,0:T(8,128)(2,1)S(1)}, u32[]{:S(2)}, u32[]{:S(2)}) %collective-permute-start.18) | collective-permute-done | bytes 344096 | tf_op jit(solution)/shard_map/ppermute | solution.py:38
  174.4 5.8 %grad_last.1 = (bf16[672,384]{1,0:T(8,128)(2,1)}, bf16[672,384]{1,0:T(8,128)(2,1)}) custom-call(s32[9]{0:T(128)} %concatenate.13.place, bf16[672,256]{1,0:T(8,128)(2,1)} %copy-done.12, bf16[672,256]{1,0:T(8,128)(2,1)} %copy-done.13, bf16[672,256]{1,0:T(8,128)(2,1)} %copy-done.14, bf16[672,256]{1,0:T(8,128)(2,1)} %copy-done.15, ...), custom_call_target="tpu_custom_call" | custom-call | flops 1056964608 | bytes 14680064 | tf_op jit(solution)/shard_map/grad_last/pallas_call | solution.py:389
  180.2 2.7 %collective-permute-start.19 = (bf16[672,384]{1,0:T(8,128)(2,1)}, bf16[672,384]{1,0:T(8,128)(2,1)S(1)}, u32[]{:S(2)}, u32[]{:S(2)}) collective-permute-start(bf16[672,384]{1,0:T(8,128)(2,1)} %get-tuple-element.78.refs_0_), channel_id=1, source_target_pairs={{0,64},{64,0},{1,65},{65,1},{2,66},{66,2},{3,67},{67,3},{4,68},{68... | collective-permute-start | bytes 1548296 | tf_op jit(solution)/shard_map/ppermute | solution.py:38
  183.7 3.7 %collective-permute-start.20 = (bf16[672,384]{1,0:T(8,128)(2,1)}, bf16[672,384]{1,0:T(8,128)(2,1)S(1)}, u32[]{:S(2)}, u32[]{:S(2)}) collective-permute-start(bf16[672,384]{1,0:T(8,128)(2,1)} %get-tuple-element.78.refs_0_), channel_id=1, source_target_pairs={{0,128},{128,256},{256,384},{384,0},{1,129},{129,257},{257,385},{3... | collective-permute-start | bytes 1548296 | tf_op jit(solution)/shard_map/ppermute | solution.py:38
  187.4 2.2 collective-permute-start.21
  189.6 3.1 %collective-permute-start.24 = (bf16[672,384]{1,0:T(8,128)(2,1)}, bf16[672,384]{1,0:T(8,128)(2,1)S(1)}, u32[]{:S(2)}, u32[]{:S(2)}) collective-permute-start(bf16[672,384]{1,0:T(8,128)(2,1)} %get-tuple-element.79.refs_6_), channel_id=1, source_target_pairs={{0,64},{64,0},{1,65},{65,1},{2,66},{66,2},{3,67},{67,3},{4,68},{68... | collective-permute-start | bytes 1548296 | tf_op jit(solution)/shard_map/ppermute | solution.py:38
  192.7 4.3 %collective-permute-done.19.refs_1_ = bf16[672,384]{1,0:T(8,128)(2,1)S(1)} collective-permute-done((bf16[672,384]{1,0:T(8,128)(2,1)}, bf16[672,384]{1,0:T(8,128)(2,1)S(1)}, u32[]{:S(2)}, u32[]{:S(2)}) %collective-permute-start.19) | collective-permute-done | bytes 516128 | tf_op jit(solution)/shard_map/ppermute | solution.py:38
  197.0 2.9 %collective-permute-start.22 = (bf16[672,384]{1,0:T(8,128)(2,1)S(1)}, bf16[672,384]{1,0:T(8,128)(2,1)S(1)}, u32[]{:S(2)}, u32[]{:S(2)}) collective-permute-start(bf16[672,384]{1,0:T(8,128)(2,1)S(1)} %collective-permute-done.19.refs_1_), channel_id=1, source_target_pairs={{0,128},{128,256},{256,384},{384,0},{1,129},{129,257},{257,385},{3... | collective-permute-start | bytes 1548296 | tf_op jit(solution)/shard_map/ppermute | solution.py:38
  200.0 2.9 %collective-permute-start.23 = (bf16[672,384]{1,0:T(8,128)(2,1)S(1)}, bf16[672,384]{1,0:T(8,128)(2,1)S(1)}, u32[]{:S(2)}, u32[]{:S(2)}) collective-permute-start(bf16[672,384]{1,0:T(8,128)(2,1)S(1)} %collective-permute-done.19.refs_1_), channel_id=1, source_target_pairs={{0,384},{128,0},{256,128},{384,256},{1,385},{129,1},{257,129},{385... | collective-permute-start | bytes 1548296 | tf_op jit(solution)/shard_map/ppermute | solution.py:38
  203.7 1.7 fusion.6
  206.2 3.2 %collective-permute-done.22.refs_4_ = bf16[672,384]{1,0:T(8,128)(2,1)S(1)} collective-permute-done((bf16[672,384]{1,0:T(8,128)(2,1)S(1)}, bf16[672,384]{1,0:T(8,128)(2,1)S(1)}, u32[]{:S(2)}, u32[]{:S(2)}) %collective-permute-start.22) | collective-permute-done | bytes 516128 | tf_op jit(solution)/shard_map/ppermute | solution.py:38
  209.4 4.3 %collective-permute-done.23.refs_5_ = bf16[672,384]{1,0:T(8,128)(2,1)S(1)} collective-permute-done((bf16[672,384]{1,0:T(8,128)(2,1)S(1)}, bf16[672,384]{1,0:T(8,128)(2,1)S(1)}, u32[]{:S(2)}, u32[]{:S(2)}) %collective-permute-start.23) | collective-permute-done | bytes 516128 | tf_op jit(solution)/shard_map/ppermute | solution.py:38
  215.7 2.9 %assemble.1 = (bf16[336,3072]{1,0:T(8,128)(2,1)}, bf16[336,3072]{1,0:T(8,128)(2,1)}) custom-call(s32[9]{0:T(128)S(1)} %copy-done.2, bf16[672,384]{1,0:T(8,128)(2,1)S(1)} %copy-done, bf16[672,384]{1,0:T(8,128)(2,1)S(1)} %collective-permute-done.19.refs_1_, bf16[672,384]{1,0:T(8,128)(2,1)S(1)} %collective-permute-done.20.refs_2_, ...), custom_call_target="tpu_custom_call" | custom-call | bytes 8388608 | tf_op jit(solution)/shard_map/assemble/pallas_call | solution.py:407
  (70 shorter events, 10.8 us)
Async XLA Ops:
  7.2 33.3 %copy-start.18 = (f32[1,2,256,4]{2,3,1,0:T(4,128)S(1)}, f32[1,2,256,4]{2,3,1,0:T(4,128)}, u32[]{:S(2)}) copy-start(f32[1,2,256,4]{2,3,1,0:T(4,128)} %param.17) | copy-start | bytes 24580
  7.2 33.3 %copy-start.19 = (s32[1,2,256,4]{2,3,1,0:T(4,128)S(1)}, s32[1,2,256,4]{2,3,1,0:T(4,128)}, u32[]{:S(2)}) copy-start(s32[1,2,256,4]{2,3,1,0:T(4,128)} %param.16) | copy-start | bytes 24580
  7.2 74.8 %copy-start.16 = (f32[1,3072]{1,0:T(1,128)S(1)}, f32[1,3072]{1,0:T(1,128)}, u32[]{:S(2)}) copy-start(f32[1,3072]{1,0:T(1,128)} %refs_5_.1) | copy-start | bytes 36868
  7.2 76.4 %all-gather.5.cloned.1.call-start = ((), (), s32[]{:S(2)}) async-start(), calls=%async_computation.2 | async-start | bytes 5013504 | tf_op jit(solution)/shard_map/all_gather | solution.py:288
  7.2 15.4 %collective-permute-start.6 = (bf16[192,256]{1,0:T(8,128)(2,1)}, bf16[192,256]{1,0:T(8,128)(2,1)S(1)}, u32[]{:S(2)}, u32[]{:S(2)}) collective-permute-start(bf16[192,256]{1,0:T(8,128)(2,1)} %bitcast.75), channel_id=1, source_target_pairs={{0,48},{16,0},{32,16},{48,32},{1,49},{17,1},{33,17},{49,33},{2,50}... | collective-permute-start | bytes 294920 | tf_op jit(solution)/shard_map/ppermute | solution.py:38
  18.2 10.4 %collective-permute-start = (bf16[192,256]{1,0:T(8,128)(2,1)}, bf16[192,256]{1,0:T(8,128)(2,1)S(1)}, u32[]{:S(2)}, u32[]{:S(2)}) collective-permute-start(bf16[192,256]{1,0:T(8,128)(2,1)} %bitcast.76), channel_id=1, source_target_pairs={{0,16},{16,32},{32,48},{48,0},{1,17},{17,33},{33,49},{49,1},{2,18}... | collective-permute-start | bytes 294920 | tf_op jit(solution)/shard_map/ppermute | solution.py:38
  21.4 67.3 %copy-start.3 = (bf16[1008,384]{1,0:T(8,128)(2,1)}, bf16[1008,384]{1,0:T(8,128)(2,1)S(1)}, u32[]{:S(2)}) copy-start(bf16[1008,384]{1,0:T(8,128)(2,1)S(1)} %pad_maximum_fusion.refs_0_) | copy-start | bytes 2322436
  30.2 132.7 %all-gather.7.cloned.1.call-start = ((), (), s32[]{:S(2)}) async-start(), calls=%async_computation.3 | async-start | bytes 3342336 | tf_op jit(solution)/shard_map/all_gather | solution.py:327
  30.3 19.7 %collective-permute-start.1 = (bf16[1008,384]{1,0:T(8,128)(2,1)S(1)}, bf16[1008,384]{1,0:T(8,128)(2,1)S(1)}, u32[]{:S(2)}, u32[]{:S(2)}) collective-permute-start(bf16[1008,384]{1,0:T(8,128)(2,1)S(1)} %pad_maximum_fusion.refs_0_), channel_id=1, source_target_pairs={{0,64},{64,0},{1,65},{65,1},{2,66},{66,2},{3,67},{67,3},{4,68},{68... | collective-permute-start | bytes 2322440 | tf_op jit(solution)/shard_map/ppermute | solution.py:38
  33.9 19.5 %collective-permute-start.2 = (bf16[1008,384]{1,0:T(8,128)(2,1)S(1)}, bf16[1008,384]{1,0:T(8,128)(2,1)S(1)}, u32[]{:S(2)}, u32[]{:S(2)}) collective-permute-start(bf16[1008,384]{1,0:T(8,128)(2,1)S(1)} %pad_maximum_fusion.refs_0_), channel_id=1, source_target_pairs={{0,128},{128,256},{256,384},{384,0},{1,129},{129,257},{257,385},{3... | collective-permute-start | bytes 2322440 | tf_op jit(solution)/shard_map/ppermute | solution.py:38
  36.2 20.5 %collective-permute-start.3 = (bf16[1008,384]{1,0:T(8,128)(2,1)S(1)}, bf16[1008,384]{1,0:T(8,128)(2,1)S(1)}, u32[]{:S(2)}, u32[]{:S(2)}) collective-permute-start(bf16[1008,384]{1,0:T(8,128)(2,1)S(1)} %pad_maximum_fusion.refs_0_), channel_id=1, source_target_pairs={{0,384},{128,0},{256,128},{384,256},{1,385},{129,1},{257,129},{385... | collective-permute-start | bytes 2322440 | tf_op jit(solution)/shard_map/ppermute | solution.py:38
  50.0 38.7 %copy-start.4 = (bf16[1008,384]{1,0:T(8,128)(2,1)}, bf16[1008,384]{1,0:T(8,128)(2,1)S(1)}, u32[]{:S(2)}) copy-start(bf16[1008,384]{1,0:T(8,128)(2,1)S(1)} %collective-permute-done.1.refs_1_) | copy-start | bytes 2322436
  53.4 35.3 %copy-start.5 = (bf16[1008,384]{1,0:T(8,128)(2,1)}, bf16[1008,384]{1,0:T(8,128)(2,1)S(1)}, u32[]{:S(2)}) copy-start(bf16[1008,384]{1,0:T(8,128)(2,1)S(1)} %collective-permute-done.2.refs_2_) | copy-start | bytes 2322436
  56.7 32.0 %copy-start.6 = (bf16[1008,384]{1,0:T(8,128)(2,1)}, bf16[1008,384]{1,0:T(8,128)(2,1)S(1)}, u32[]{:S(2)}) copy-start(bf16[1008,384]{1,0:T(8,128)(2,1)S(1)} %collective-permute-done.3.refs_3_) | copy-start | bytes 2322436
  56.7 22.1 %collective-permute-start.4 = (bf16[1008,384]{1,0:T(8,128)(2,1)S(1)}, bf16[1008,384]{1,0:T(8,128)(2,1)S(1)}, u32[]{:S(2)}, u32[]{:S(2)}) collective-permute-start(bf16[1008,384]{1,0:T(8,128)(2,1)S(1)} %collective-permute-done.1.refs_1_), channel_id=1, source_target_pairs={{0,128},{128,256},{256,384},{384,0},{1,129},{129,257},{257,385},{3... | collective-permute-start | bytes 2322440 | tf_op jit(solution)/shard_map/ppermute | solution.py:38
  58.9 19.9 %collective-permute-start.5 = (bf16[1008,384]{1,0:T(8,128)(2,1)S(1)}, bf16[1008,384]{1,0:T(8,128)(2,1)}, u32[]{:S(2)}, u32[]{:S(2)}) collective-permute-start(bf16[1008,384]{1,0:T(8,128)(2,1)S(1)} %collective-permute-done.1.refs_1_), channel_id=1, source_target_pairs={{0,384},{128,0},{256,128},{384,256},{1,385},{129,1},{257,129},{385... | collective-permute-start | bytes 2322440 | tf_op jit(solution)/shard_map/ppermute | solution.py:38
  62.6 45.7 %collective-permute-start.9 = (bf16[1008,384]{1,0:T(8,128)(2,1)S(1)}, bf16[1008,384]{1,0:T(8,128)(2,1)}, u32[]{:S(2)}, u32[]{:S(2)}) collective-permute-start(bf16[1008,384]{1,0:T(8,128)(2,1)S(1)} %collective-permute-done.2.refs_2_), channel_id=1, source_target_pairs={{0,128},{128,256},{256,384},{384,0},{1,129},{129,257},{257,385},{3... | collective-permute-start | bytes 2322440 | tf_op jit(solution)/shard_map/ppermute | solution.py:38
  78.8 0.9 copy-start.7
  79.7 28.6 %collective-permute-start.10 = (bf16[1008,384]{1,0:T(8,128)(2,1)}, bf16[1008,384]{1,0:T(8,128)(2,1)}, u32[]{:S(2)}, u32[]{:S(2)}) collective-permute-start(bf16[1008,384]{1,0:T(8,128)(2,1)} %collective-permute-done.5.refs_5_), channel_id=1, source_target_pairs={{0,384},{128,0},{256,128},{384,256},{1,385},{129,1},{257,129},{385... | collective-permute-start | bytes 2322440 | tf_op jit(solution)/shard_map/ppermute | solution.py:38
  83.6 5.1 %copy-start.8 = (bf16[1,256,192]{1,2,0:T(8,128)(2,1)S(1)}, bf16[1,256,192]{1,2,0:T(8,128)(2,1)}, u32[]{:S(2)}) copy-start(bf16[1,256,192]{1,2,0:T(8,128)(2,1)} %param.10) | copy-start | bytes 294916
  88.8 19.5 %collective-permute-start.7 = (bf16[192,256]{1,0:T(8,128)(2,1)S(1)}, bf16[192,256]{1,0:T(8,128)(2,1)S(1)}, u32[]{:S(2)}, u32[]{:S(2)}) collective-permute-start(bf16[192,256]{1,0:T(8,128)(2,1)S(1)} %bitcast.63), channel_id=1, source_target_pairs={{0,0},{2,64},{4,128},{6,192},{8,256},{10,320},{12,384},{14,448},{6... | collective-permute-start | bytes 294920 | tf_op jit(solution)/shard_map/ppermute | solution.py:47
  97.3 11.0 %collective-permute-start.8 = (bf16[192,256]{1,0:T(8,128)(2,1)S(1)}, bf16[192,256]{1,0:T(8,128)(2,1)S(1)}, u32[]{:S(2)}, u32[]{:S(2)}) collective-permute-start(bf16[192,256]{1,0:T(8,128)(2,1)S(1)} %bitcast.64), channel_id=1, source_target_pairs={{0,256},{2,320},{4,384},{6,448},{8,0},{10,64},{12,128},{14,192},{6... | collective-permute-start | bytes 294920 | tf_op jit(solution)/shard_map/ppermute | solution.py:47
  109.0 93.9 %reduce-scatter.2.cloned.1.call-start = ((), (), s32[]{:S(2)}) async-start(), calls=%async_computation.1 | async-start | bytes 1916928 | tf_op jit(solution)/shard_map/reduce_scatter | solution.py:370
  113.6 20.8 %collective-permute-start.11 = (bf16[672,256]{1,0:T(8,128)(2,1)}, bf16[672,256]{1,0:T(8,128)(2,1)S(1)}, u32[]{:S(2)}, u32[]{:S(2)}) collective-permute-start(bf16[672,256]{1,0:T(8,128)(2,1)} %get-tuple-element.65.refs_0_), channel_id=1, source_target_pairs={{0,64},{64,0},{1,65},{65,1},{2,66},{66,2},{3,67},{67,3},{4,68},{68... | collective-permute-start | bytes 1032200 | tf_op jit(solution)/shard_map/ppermute | solution.py:38
  117.8 16.6 %collective-permute-start.12 = (bf16[672,256]{1,0:T(8,128)(2,1)}, bf16[672,256]{1,0:T(8,128)(2,1)S(1)}, u32[]{:S(2)}, u32[]{:S(2)}) collective-permute-start(bf16[672,256]{1,0:T(8,128)(2,1)} %get-tuple-element.65.refs_0_), channel_id=1, source_target_pairs={{0,128},{128,256},{256,384},{384,0},{1,129},{129,257},{257,385},{3... | collective-permute-start | bytes 1032200 | tf_op jit(solution)/shard_map/ppermute | solution.py:38
  123.0 11.4 %collective-permute-start.13 = (bf16[672,256]{1,0:T(8,128)(2,1)}, bf16[672,256]{1,0:T(8,128)(2,1)S(1)}, u32[]{:S(2)}, u32[]{:S(2)}) collective-permute-start(bf16[672,256]{1,0:T(8,128)(2,1)} %get-tuple-element.65.refs_0_), channel_id=1, source_target_pairs={{0,384},{128,0},{256,128},{384,256},{1,385},{129,1},{257,129},{385... | collective-permute-start | bytes 1032200 | tf_op jit(solution)/shard_map/ppermute | solution.py:38
  134.3 25.7 %copy-start.9 = (bf16[672,256]{1,0:T(8,128)(2,1)}, bf16[672,256]{1,0:T(8,128)(2,1)S(1)}, u32[]{:S(2)}) copy-start(bf16[672,256]{1,0:T(8,128)(2,1)S(1)} %collective-permute-done.11.refs_1_) | copy-start | bytes 1032196
  134.4 25.7 %copy-start.10 = (bf16[672,256]{1,0:T(8,128)(2,1)}, bf16[672,256]{1,0:T(8,128)(2,1)S(1)}, u32[]{:S(2)}) copy-start(bf16[672,256]{1,0:T(8,128)(2,1)S(1)} %collective-permute-done.12.refs_2_) | copy-start | bytes 1032196
  134.4 25.7 %copy-start.11 = (bf16[672,256]{1,0:T(8,128)(2,1)}, bf16[672,256]{1,0:T(8,128)(2,1)S(1)}, u32[]{:S(2)}) copy-start(bf16[672,256]{1,0:T(8,128)(2,1)S(1)} %collective-permute-done.13.refs_3_) | copy-start | bytes 1032196
  134.4 22.4 %collective-permute-start.14 = (bf16[8,416,256]{2,1,0:T(8,128)(2,1)}, bf16[8,416,256]{2,1,0:T(8,128)(2,1)S(1)}, u32[]{:S(2)}, u32[]{:S(2)}) collective-permute-start(bf16[8,416,256]{2,1,0:T(8,128)(2,1)} %get-tuple-element.69), channel_id=1, source_target_pairs={{0,1},{1,0},{2,3},{3,2},{4,5},{5,4},{6,7},{7,6},{8,9},{9,8},{10,11... | collective-permute-start | bytes 5111816 | tf_op jit(solution)/shard_map/ppermute | solution.py:38
  136.3 13.5 %collective-permute-start.15 = (bf16[672,256]{1,0:T(8,128)(2,1)S(1)}, bf16[672,256]{1,0:T(8,128)(2,1)S(1)}, u32[]{:S(2)}, u32[]{:S(2)}) collective-permute-start(bf16[672,256]{1,0:T(8,128)(2,1)S(1)} %collective-permute-done.11.refs_1_), channel_id=1, source_target_pairs={{0,128},{128,256},{256,384},{384,0},{1,129},{129,257},{257,385},{3... | collective-permute-start | bytes 1032200 | tf_op jit(solution)/shard_map/ppermute | solution.py:38
  141.5 13.3 %collective-permute-start.16 = (bf16[672,256]{1,0:T(8,128)(2,1)S(1)}, bf16[672,256]{1,0:T(8,128)(2,1)S(1)}, u32[]{:S(2)}, u32[]{:S(2)}) collective-permute-start(bf16[672,256]{1,0:T(8,128)(2,1)S(1)} %collective-permute-done.11.refs_1_), channel_id=1, source_target_pairs={{0,384},{128,0},{256,128},{384,256},{1,385},{129,1},{257,129},{385... | collective-permute-start | bytes 1032200 | tf_op jit(solution)/shard_map/ppermute | solution.py:38
  143.4 13.4 %collective-permute-start.17 = (bf16[672,256]{1,0:T(8,128)(2,1)S(1)}, bf16[672,256]{1,0:T(8,128)(2,1)S(1)}, u32[]{:S(2)}, u32[]{:S(2)}) collective-permute-start(bf16[672,256]{1,0:T(8,128)(2,1)S(1)} %collective-permute-done.12.refs_2_), channel_id=1, source_target_pairs={{0,128},{128,256},{256,384},{384,0},{1,129},{129,257},{257,385},{3... | collective-permute-start | bytes 1032200 | tf_op jit(solution)/shard_map/ppermute | solution.py:38
  149.8 10.2 %copy-start.12 = (bf16[672,256]{1,0:T(8,128)(2,1)}, bf16[672,256]{1,0:T(8,128)(2,1)S(1)}, u32[]{:S(2)}) copy-start(bf16[672,256]{1,0:T(8,128)(2,1)S(1)} %collective-permute-done.15.refs_0_) | copy-start | bytes 1032196
  154.8 5.4 %copy-start.13 = (bf16[672,256]{1,0:T(8,128)(2,1)}, bf16[672,256]{1,0:T(8,128)(2,1)S(1)}, u32[]{:S(2)}) copy-start(bf16[672,256]{1,0:T(8,128)(2,1)S(1)} %collective-permute-done.16.refs_1_) | copy-start | bytes 1032196
  156.8 3.3 %copy-start.14 = (bf16[672,256]{1,0:T(8,128)(2,1)}, bf16[672,256]{1,0:T(8,128)(2,1)S(1)}, u32[]{:S(2)}) copy-start(bf16[672,256]{1,0:T(8,128)(2,1)S(1)} %collective-permute-done.17.refs_2_) | copy-start | bytes 1032196
  160.1 13.5 %collective-permute-start.18 = (bf16[672,256]{1,0:T(8,128)(2,1)S(1)}, bf16[672,256]{1,0:T(8,128)(2,1)S(1)}, u32[]{:S(2)}, u32[]{:S(2)}) collective-permute-start(bf16[672,256]{1,0:T(8,128)(2,1)S(1)} %collective-permute-done.16.refs_1_), channel_id=1, source_target_pairs={{0,384},{128,0},{256,128},{384,256},{1,385},{129,1},{257,129},{385... | collective-permute-start | bytes 1032200 | tf_op jit(solution)/shard_map/ppermute | solution.py:38
  173.7 0.7 copy-start.15
  174.4 9.3 %copy-start.17 = (f32[2,256]{1,0:T(2,128)S(1)}, f32[2,256]{1,0:T(2,128)}, u32[]{:S(2)}) copy-start(f32[2,256]{1,0:T(2,128)} %get-tuple-element.51.scales.refs_12_) | copy-start | bytes 6148
  174.4 39.3 %copy-start.2 = (s32[9]{0:T(128)S(1)}, s32[9]{0:T(128)}, u32[]{:S(2)}) copy-start(s32[9]{0:T(128)} %concatenate.13.place) | copy-start | bytes 112
  180.2 16.8 %collective-permute-start.19 = (bf16[672,384]{1,0:T(8,128)(2,1)}, bf16[672,384]{1,0:T(8,128)(2,1)S(1)}, u32[]{:S(2)}, u32[]{:S(2)}) collective-permute-start(bf16[672,384]{1,0:T(8,128)(2,1)} %get-tuple-element.78.refs_0_), channel_id=1, source_target_pairs={{0,64},{64,0},{1,65},{65,1},{2,66},{66,2},{3,67},{67,3},{4,68},{68... | collective-permute-start | bytes 1548296 | tf_op jit(solution)/shard_map/ppermute | solution.py:38
  183.7 21.6 %collective-permute-start.20 = (bf16[672,384]{1,0:T(8,128)(2,1)}, bf16[672,384]{1,0:T(8,128)(2,1)S(1)}, u32[]{:S(2)}, u32[]{:S(2)}) collective-permute-start(bf16[672,384]{1,0:T(8,128)(2,1)} %get-tuple-element.78.refs_0_), channel_id=1, source_target_pairs={{0,128},{128,256},{256,384},{384,0},{1,129},{129,257},{257,385},{3... | collective-permute-start | bytes 1548296 | tf_op jit(solution)/shard_map/ppermute | solution.py:38
  187.4 18.0 %collective-permute-start.21 = (bf16[672,384]{1,0:T(8,128)(2,1)}, bf16[672,384]{1,0:T(8,128)(2,1)S(1)}, u32[]{:S(2)}, u32[]{:S(2)}) collective-permute-start(bf16[672,384]{1,0:T(8,128)(2,1)} %get-tuple-element.78.refs_0_), channel_id=1, source_target_pairs={{0,384},{128,0},{256,128},{384,256},{1,385},{129,1},{257,129},{385... | collective-permute-start | bytes 1548296 | tf_op jit(solution)/shard_map/ppermute | solution.py:38
  189.6 16.6 %collective-permute-start.24 = (bf16[672,384]{1,0:T(8,128)(2,1)}, bf16[672,384]{1,0:T(8,128)(2,1)S(1)}, u32[]{:S(2)}, u32[]{:S(2)}) collective-permute-start(bf16[672,384]{1,0:T(8,128)(2,1)} %get-tuple-element.79.refs_6_), channel_id=1, source_target_pairs={{0,64},{64,0},{1,65},{65,1},{2,66},{66,2},{3,67},{67,3},{4,68},{68... | collective-permute-start | bytes 1548296 | tf_op jit(solution)/shard_map/ppermute | solution.py:38
  197.0 12.4 %collective-permute-start.22 = (bf16[672,384]{1,0:T(8,128)(2,1)S(1)}, bf16[672,384]{1,0:T(8,128)(2,1)S(1)}, u32[]{:S(2)}, u32[]{:S(2)}) collective-permute-start(bf16[672,384]{1,0:T(8,128)(2,1)S(1)} %collective-permute-done.19.refs_1_), channel_id=1, source_target_pairs={{0,128},{128,256},{256,384},{384,0},{1,129},{129,257},{257,385},{3... | collective-permute-start | bytes 1548296 | tf_op jit(solution)/shard_map/ppermute | solution.py:38
  200.0 13.7 %collective-permute-start.23 = (bf16[672,384]{1,0:T(8,128)(2,1)S(1)}, bf16[672,384]{1,0:T(8,128)(2,1)S(1)}, u32[]{:S(2)}, u32[]{:S(2)}) collective-permute-start(bf16[672,384]{1,0:T(8,128)(2,1)S(1)} %collective-permute-done.19.refs_1_), channel_id=1, source_target_pairs={{0,384},{128,0},{256,128},{384,256},{1,385},{129,1},{257,129},{385... | collective-permute-start | bytes 1548296 | tf_op jit(solution)/shard_map/ppermute | solution.py:38
  213.7 1.0 copy-start
  214.7 1.0 copy-start.1
Sparse Core Ops, SparseCore 0:
  30.4 42.5 all-gather.4
  109.1 42.5 all-gather.6
  160.2 39.3 reduce-scatter.1

commit v5 on v2

v5 whole, which is shorter than its diff:
```python
import jax
import jax.numpy as jnp
import numpy as np
from jax import lax
from jax.experimental import pallas as pl
from jax.experimental.pallas import tpu as pltpu
from jax.sharding import Mesh, PartitionSpec as P

EPS = 1e-05
AXES = ("x", "zl", "s", "y", "c")
SIZES = {"x": 4, "zl": 2, "s": 4, "y": 8, "c": 2}
D = 3072
TOK = 256
G = 336
F = 192
N_T = 16
N_DP = 8
DS = D // N_DP
N_EARLY = 6
TILE = 336
OFFSETS = ((0, 0), (0, 1), (-1, 0), (1, 0), (-1, 1), (1, 1), (2, 0), (2, 1))

VM = pl.BlockSpec(memory_space=pltpu.VMEM)
HB = pl.BlockSpec(memory_space=pltpu.HBM)
SM = pl.BlockSpec(memory_space=pltpu.SMEM)


def shift(value, **steps):
    axes = tuple(a for a in AXES if a in steps)
    sizes = [SIZES[a] for a in axes]
    pairs = []
    for i in range(int(np.prod(sizes))):
        at = np.unravel_index(i, sizes)
        to = [(at[k] + steps[a]) % sizes[k] for k, a in enumerate(axes)]
        pairs.append((i, int(np.ravel_multi_index(to, sizes))))
    return lax.ppermute(value, axes if len(axes) > 1 else axes[0], pairs)


def swapped(value, step):
    pairs = []
    for e in range(N_DP):
        for y in range(N_DP):
            d = (((y // 2) + step) % 4) * 2 + y % 2
            pairs.append((e * N_DP + y, d * N_DP + e))
    return lax.ppermute(value, ("x", "zl", "y"), pairs)


def gather_ring(own, ready):
    z, behind, ahead = lax.optimization_barrier((shift(own, zl=1), shift(own, x=1), shift(own, x=-1)))
    z_behind = shift(z, x=1)
    z_ahead = shift(z, x=-1)
    across = shift(behind, x=1)
    z_ahead, ready = lax.optimization_barrier((z_ahead, ready))
    z_across = shift(z_ahead, x=-1)
    return [own, z, behind, ahead, z_behind, z_ahead, across, z_across], ready


def gather_weights(own, block, ready):
    z = shift(own, zl=1)
    behind = shift(own, x=1)
    ahead = shift(own, x=-1)
    near = swapped(block, 0)
    z, behind, ahead, near, block, ready = lax.optimization_barrier((z, behind, ahead, near, block, ready))
    z_behind = shift(z, x=1)
    z_ahead = shift(z, x=-1)
    far = swapped(block, 2)
    z_behind, z_ahead, far = lax.optimization_barrier((z_behind, z_ahead, far))
    across = shift(behind, x=1)
    z_across = shift(z_ahead, x=-1)
    return [own, z, behind, ahead, z_behind, z_ahead, across, z_across], (near, far), ready


def after(value, earlier):
    return lax.optimization_barrier((value, earlier))[0]


def places():
    x, zl = lax.axis_index("x"), lax.axis_index("zl")
    return jnp.stack([((x + dx) % 4) * 2 + (zl + dz) % 2 for dx, dz in OFFSETS]).astype(jnp.int32)


def gained_into(act_ref, gain_ref, out_ref):
    total = jnp.zeros((8, TOK), jnp.float32)
    for t in range(N_T):
        v = act_ref[t].astype(jnp.float32)
        total = total + jnp.sum((v * v).reshape(F // 8, 8, TOK), axis=0)
        out_ref[t * F : (t + 1) * F, :] = (v * gain_ref[t * F : (t + 1) * F, :]).astype(jnp.bfloat16)
    return lax.rsqrt(jnp.sum(total, axis=0, keepdims=True) / D + EPS)


def fetch(pairs, sems):
    copies = [pltpu.make_async_copy(src, dst, sems.at[i]) for i, (src, dst) in enumerate(pairs)]
    for copy in copies:
        copy.start()
    return copies


def early_kernel(place, *refs):
    w = refs[:N_EARLY]
    acts, gain, b_out, f_out, nb_out, nf_out, dy_out, scales_out, saved, dy, act, normal_b, normal_f, sems = refs[N_EARLY:]
    copies = fetch([(acts.at[:, 2], saved), (acts.at[:, 0], act), (acts.at[:, 1], dy)], sems)
    copies[0].wait()
    scales_out[0:1, :] = gained_into(saved, gain, normal_b)
    copies[1].wait()
    scales_out[1:2, :] = gained_into(act, gain, normal_f)
    copies[2].wait()
    for i in range(N_DP - N_EARLY):
        d = place[N_EARLY + i]
        rows = pl.ds(pl.multiple_of(d * DS, DS), DS)
        nb_out[i] = normal_b[rows, :]
        nf_out[i] = normal_f[rows, :]
        dy_out[i] = dy[pl.ds(2 * d, 2)].reshape(DS, TOK)
    for m in range(0, G, TILE):
        sums = [jnp.zeros((TILE, TOK), jnp.float32) for _ in range(5)]
        for r in range(N_EARLY):
            d = place[r]
            rows = pl.ds(pl.multiple_of(d * DS, DS), DS)
            n, f = normal_b[rows, :], normal_f[rows, :]
            g = dy[pl.ds(2 * d, 2)].reshape(DS, TOK)
            w_g = w[r][m : m + TILE, :]
            w_u = w[r][G + m : G + m + TILE, :]
            w_d = w[r][2 * G + m : 2 * G + m + TILE, :]
            for k, (left, right) in enumerate(((w_g, n), (w_u, n), (w_d, g), (w_g, f), (w_u, f))):
                sums[k] = sums[k] + jnp.dot(left, right, preferred_element_type=jnp.float32)
        for k in range(3):
            b_out[k * G + m : k * G + m + TILE, :] = sums[k]
        for k in range(2):
            f_out[k * G + m : k * G + m + TILE, :] = sums[3 + k]


def inner_kernel(w_6, w_7, early, normal, dy, weight, scales, dg_out, dgs_out, stat_out):
    w = (w_6, w_7)
    last = N_DP - N_EARLY
    scale = scales[0:1, :]
    row = weight[...]
    stat = jnp.zeros((1, TOK), jnp.float32)
    for m in range(0, G, TILE):
        gate, up, hid = (early[k * G + m : k * G + m + TILE, :] for k in range(3))
        for i in range(last):
            n, g = normal[i], dy[i]
            gate = gate + jnp.dot(w[i][m : m + TILE, :], n, preferred_element_type=jnp.float32)
            up = up + jnp.dot(w[i][G + m : G + m + TILE, :], n, preferred_element_type=jnp.float32)
            hid = hid + jnp.dot(w[i][2 * G + m : 2 * G + m + TILE, :], g, preferred_element_type=jnp.float32)
        gate = scale * gate
        up = scale * up
        sg = jax.nn.sigmoid(gate)
        hid = hid * row
        dgate = hid * up * (sg * (1.0 + gate * (1.0 - sg)))
        dup = hid * (gate * sg)
        dgate_r, dup_r = dgate.astype(jnp.bfloat16), dup.astype(jnp.bfloat16)
        dg_out[m : m + TILE, :] = dgate_r
        dg_out[G + m : G + m + TILE, :] = dup_r
        dgs_out[m : m + TILE, :] = (dgate * scale).astype(jnp.bfloat16)
        dgs_out[G + m : G + m + TILE, :] = (dup * scale).astype(jnp.bfloat16)
        stat = stat + jnp.sum(
            dgate_r.astype(jnp.float32) * gate + dup_r.astype(jnp.float32) * up, axis=0, keepdims=True
        )
    stat_out[...] = stat


def outer_kernel(place, *refs):
    w = refs[:N_DP]
    dg, early, normal, weight, scales, stat, out, chunks, hidden, dg_t, hid_t, sems = refs[N_DP:]
    last = N_DP - N_EARLY
    me = place[N_DP]
    value = stat[...]
    high = value.astype(jnp.bfloat16).astype(jnp.float32)
    rows = lax.broadcasted_iota(jnp.int32, (2 * N_T, TOK), 0)
    block = jnp.where(rows == me, high, jnp.where(rows == me + N_T, value - high, 0.0)).astype(jnp.bfloat16)
    for r in range(N_DP):
        for half in range(2):
            chunks[r, half, 2 * F :, :] = block
    dg_t[...] = dg[...].T
    row = weight[...]
    scale = scales[1:2, :]
    for m in range(0, G, TILE):
        gate, up = (early[k * G + m : k * G + m + TILE, :] for k in range(2))
        for i in range(last):
            n = normal[i]
            gate = gate + jnp.dot(w[N_EARLY + i][m : m + TILE, :], n, preferred_element_type=jnp.float32)
            up = up + jnp.dot(w[N_EARLY + i][G + m : G + m + TILE, :], n, preferred_element_type=jnp.float32)
        gate = scale * gate
        up = scale * up
        hidden[m : m + TILE, :] = (gate * jax.nn.sigmoid(gate) * up * row).astype(jnp.bfloat16)
    hid_t[...] = hidden[...].T
    copies = []
    for r in range(N_DP):
        into = jnp.dot(dg_t[...], w[r][: 2 * G, :], preferred_element_type=jnp.float32)
        chunks[r, :, 0:F, :] = into.astype(jnp.bfloat16).T.reshape(2, F, TOK)
        part = jnp.dot(hid_t[...], w[r][2 * G :, :], preferred_element_type=jnp.float32)
        chunks[r, :, F : 2 * F, :] = part.astype(jnp.bfloat16).T.reshape(2, F, TOK)
        copies.append(pltpu.make_async_copy(chunks.at[r], out.at[pl.ds(2 * place[r], 2)], sems.at[r]))
        copies[r].start()
    for copy in copies:
        copy.wait()


def grad_kernel(place, *refs):
    dgs = refs[:N_DP]
    tokens, gain, near_out, far_out = refs[N_DP:]
    own = place[0]
    for j, (at, out) in enumerate(((own, near_out), (lax.rem(own + 4, N_DP), far_out))):
        lanes = gain[:, pl.ds(pl.multiple_of(at * DS, DS), DS)]
        for m in range(0, 2 * G, G):
            total = jnp.zeros((G, DS), jnp.float32)
            for r in range(N_DP):
                v = tokens[pl.ds(2 * place[r], 2), j].reshape(DS, TOK)
                total = total + lax.dot_general(
                    dgs[r][m : m + G, :], v, (((1,), (1,)), ((), ())), preferred_element_type=jnp.float32
                )
            out[m : m + G, :] = (total * lanes).astype(jnp.bfloat16)


def assemble_kernel(place, *refs):
    parts = refs[:N_DP]
    gate_out, up_out, sems = refs[N_DP:]
    pairs = []
    for r in range(N_DP):
        lanes = pl.ds(pl.multiple_of(place[r] * DS, DS), DS)
        pairs += [(parts[r].at[:G, :], gate_out.at[:, lanes]), (parts[r].at[G:, :], up_out.at[:, lanes])]
    for copy in fetch(pairs, sems):
        copy.wait()


def params(mib):
    return pltpu.CompilerParams(vmem_limit_bytes=mib << 20)


def cost(flops, nbytes):
    return pl.CostEstimate(flops=flops, bytes_accessed=nbytes, transcendentals=0)


def combine(route_ids, probs):
    return jnp.sum(jnp.where(route_ids == 0, probs, jnp.zeros_like(probs)), axis=-1)[None, :]


def local(
    passed_activations,
    kept_section_input,
    handed_grads,
    norm_gain,
    gate_weight,
    up_weight,
    down_weight,
    routes,
    route_probs,
):
    place = places()
    here = lax.axis_index("y") * 2 + lax.axis_index("c")
    place_t = jnp.concatenate([place, here[None].astype(jnp.int32)])
    saved_t = kept_section_input[0].T
    acts_t = shift(passed_activations[0].T, s=1)
    dy_t = shift(handed_grads[0].T, s=-1)
    gain = norm_gain[0]
    own_weights = jnp.concatenate([gate_weight[0].T, up_weight[0].T, down_weight[0]], axis=0)
    ready = (gain[:, None], place_t, combine(routes[0, 0], route_probs[0, 0]), combine(routes[0, 1], route_probs[0, 1]))
    weights, swaps, ready = gather_weights(own_weights, saved_t, ready)
    gain_col, place, weight_f, weight_b = ready
    acts = lax.all_gather(
        after(jnp.concatenate([acts_t, dy_t, saved_t], axis=0), own_weights), ("y", "c"), axis=0
    ).reshape(N_T, 3, F, TOK)
    tokens = lax.all_gather(jnp.concatenate(swaps, axis=0), ("y", "c"), axis=0).reshape(N_T, 2, F, TOK)

    bf, f32 = jnp.bfloat16, jnp.float32
    last = N_DP - N_EARLY
    block = jax.ShapeDtypeStruct((last, DS, TOK), bf)
    early_b, early_f, normal_b, normal_f, dy_last, scales = pl.pallas_call(
        early_kernel,
        in_specs=[SM] + [VM] * N_EARLY + [HB, VM],
        out_specs=[VM] * 6,
        out_shape=[
            jax.ShapeDtypeStruct((3 * G, TOK), f32),
            jax.ShapeDtypeStruct((2 * G, TOK), f32),
            block,
            block,
            block,
            jax.ShapeDtypeStruct((2, TOK), f32),
        ],
        scratch_shapes=[
            pltpu.VMEM((N_T, F, TOK), bf),
            pltpu.VMEM((N_T, F, TOK), bf),
            pltpu.VMEM((N_T, F, TOK), bf),
            pltpu.VMEM((D, TOK), bf),
            pltpu.VMEM((D, TOK), bf),
            pltpu.SemaphoreType.DMA((3,)),
        ],
        compiler_params=params(20),
        cost_estimate=cost(10 * D * G * TOK, 28 << 20),
        name="early",
    )(place, *weights[:N_EARLY], acts, gain_col)
    dg, dgs, stat = pl.pallas_call(
        inner_kernel,
        in_specs=[VM] * 7,
        out_specs=[VM] * 3,
        out_shape=[
            jax.ShapeDtypeStruct((2 * G, TOK), bf),
            jax.ShapeDtypeStruct((2 * G, TOK), bf),
            jax.ShapeDtypeStruct((1, TOK), f32),
        ],
        compiler_params=params(12),
        cost_estimate=cost(2 * D * G * TOK, 8 << 20),
        name="inner",
    )(*weights[N_EARLY:], early_b, normal_b, dy_last, weight_b, scales)
    dgs_all, tokens = gather_ring(dgs, tokens)
    payload = pl.pallas_call(
        outer_kernel,
        in_specs=[SM] + [VM] * (N_DP + 6),
        out_specs=HB,
        out_shape=jax.ShapeDtypeStruct((N_T, 2 * F + 2 * N_T, TOK), bf),
        scratch_shapes=[
            pltpu.VMEM((N_DP, 2, 2 * F + 2 * N_T, TOK), bf),
            pltpu.VMEM((G, TOK), bf),
            pltpu.VMEM((TOK, 2 * G), bf),
            pltpu.VMEM((TOK, G), bf),
            pltpu.SemaphoreType.DMA((N_DP,)),
        ],
        compiler_params=params(16),
        cost_estimate=cost(8 * D * G * TOK, 20 << 20),
        name="outer",
    )(place, *weights, dg, early_f, normal_f, weight_f, scales, stat)
    summed = lax.psum_scatter(payload, ("y", "c"), scatter_dimension=0)

    near_grad, far_grad = pl.pallas_call(
        grad_kernel,
        in_specs=[SM] + [VM] * (N_DP + 2),
        out_specs=[VM, VM],
        out_shape=[jax.ShapeDtypeStruct((2 * G, DS), bf)] * 2,
        compiler_params=params(12),
        cost_estimate=cost(8 * DS * G * TOK * N_DP, 8 << 20),
        name="grad",
    )(place, *dgs_all, tokens, gain[None, :])
    z = shift(near_grad, zl=1)
    behind = shift(near_grad, x=1)
    ahead = shift(near_grad, x=-1)
    z_far = shift(far_grad, zl=1)
    z_behind = shift(z, x=1)
    z_ahead = shift(z, x=-1)
    parts = [near_grad, z, behind, ahead, z_behind, z_ahead, far_grad, z_far]
    grad_g, grad_u = pl.pallas_call(
        assemble_kernel,
        in_specs=[SM] + [VM] * N_DP,
        out_specs=[HB, HB],
        out_shape=[jax.ShapeDtypeStruct((G, D), bf)] * 2,
        scratch_shapes=[pltpu.SemaphoreType.DMA((2 * N_DP,))],
        compiler_params=params(12),
        cost_estimate=cost(0, 8 << 20),
        name="assemble",
    )(place, *parts)

    into = summed[:F].astype(f32)
    mean_stat = jnp.sum(summed[2 * F :].astype(f32), axis=0, keepdims=True) / D
    gain_here = lax.dynamic_slice_in_dim(gain, here * F, F)[:, None]
    output = (acts_t.astype(f32) + summed[F : 2 * F].astype(f32)).astype(bf)
    scale_b = scales[0:1]
    hat = saved_t.astype(f32) * scale_b
    stored = (dy_t.astype(f32) + scale_b * (into * gain_here - hat * mean_stat)).astype(bf)
    return (output.T[None], stored.T[None], grad_g.T[None], grad_u.T[None])


def solution(mesh):
    fine = Mesh(mesh.devices.reshape(tuple(SIZES[a] for a in AXES)), AXES)
    dp, tensor = ("x", "zl"), ("y", "c")
    placed = (
        P("s", dp, tensor),
        P("s", dp, tensor),
        P("s", dp, tensor),
        P("s", None),
        P("s", dp, tensor),
        P("s", dp, tensor),
        P("s", tensor, dp),
        P("s", None, dp, None),
        P("s", None, dp, None),
    )
    return jax.shard_map(
        local,
        mesh=fine,
        in_specs=placed,
        out_specs=(
            P("s", dp, tensor),
            P("s", dp, tensor),
            P("s", None, tensor),
            P("s", None, tensor),
        ),
        check_vma=False,
    )
```

time: 209 us -> 204 us (0.976)
  waiting for transfers between devices: 55.3 us -> 65 us
  Pallas kernels: 28.4 us -> 21.2 us
  local copies, waits for them, and re-layouts: 13.3 us -> 8.94 us
  starting transfers between devices: 90.9 us -> 88.7 us
    pallas_call x5, Pallas kernels: 28.4 us -> 21.2 us  [the longest x1 6.24 us: local(): pl.pallas_call(outer_kernel, in_specs=[SM] + [VM] * (N_DP + 6), out_specs...]
    ppermute x22, starting transfers between devices: 79.6 us -> 73.2 us  [shift(): return lax.ppermute(value, axes if len(axes) > 1 else axes[0], pairs)]
    ppermute x2, waiting for transfers between devices: 7.5 us -> 13.9 us  [swapped(): return lax.ppermute(value, ('x', 'zl', 'y'), pairs)]
    ppermute x2, starting transfers between devices: 11.1 us -> 15.3 us  [swapped(): return lax.ppermute(value, ('x', 'zl', 'y'), pairs)]
    reduce_scatter x1, waiting for transfers between devices: 0.01 us -> 3.97 us  [local(): summed = lax.psum_scatter(payload, ('y', 'c'), scatter_dimension=0)]
    another operation x2 -> x0, local copies, waits for them, and re-layouts: 2.32 us -> none  [the longest x1 1.66 us: local(): gain_col = gain[:, None]]
    unnamed x52 -> x34, local copies, waits for them, and re-layouts: 10.2 us -> 8.27 us
  transfers between devices with their start and end apart: 27 -> 27, of which waited for: 17 -> 19; matrix products, arithmetic and copies ran while one was open for 3% -> 1% of each run, Pallas kernels for 14% -> 10%
where the time goes in v5:
time: 204 us; the launch traced here: 203 us
  starting transfers between devices  88.7 us (43%)
  waiting for transfers between devices  65 us (32%)
  Pallas kernels  21.2 us (10%)
  between operations  14.2 us (7%)
  local copies, waits for them, and re-layouts  8.94 us (4%)
  other arithmetic  5.18 us (3%)
    ppermute x22, starting transfers between devices, shift(): return lax.ppermute(value, axes if len(axes) > 1 else axes[0], pairs)  73.2 us
    ppermute x22, waiting for transfers between devices, shift(): return lax.ppermute(value, axes if len(axes) > 1 else axes[0], pairs)  47.1 us
    ppermute x2, starting transfers between devices, swapped(): return lax.ppermute(value, ('x', 'zl', 'y'), pairs)  15.3 us
    ppermute x2, waiting for transfers between devices, swapped(): return lax.ppermute(value, ('x', 'zl', 'y'), pairs)  13.9 us
    unnamed x34, local copies, waits for them, and re-layouts  8.27 us
    pallas_call x1, Pallas kernels, local(): pl.pallas_call(outer_kernel, in_specs=[SM] + [VM] * (N_DP + 6), out_specs...  6.24 us
    pallas_call x1, Pallas kernels, local(): pl.pallas_call(early_kernel, in_specs=[SM] + [VM] * N_EARLY + [HB, VM], o...  5.67 us
  transfers between devices with their start and end apart: 27, of which 19 were waited for; matrix products, arithmetic and copies ran while one was open for 1% of the time, Pallas kernels for 10%

profile of v5, /device:TPU:6, one launch (start us, length us, event | category | flops | bytes accessed | tf_op | source)
XLA Modules:
  0.0 203.3 jit_solution(3967040123750808268)
XLA Ops:
  7.2 10.9 %collective-permute-start.10 = (bf16[192,256]{1,0:T(8,128)(2,1)}, bf16[192,256]{1,0:T(8,128)(2,1)S(1)}, u32[]{:S(2)}, u32[]{:S(2)}) collective-permute-start(bf16[192,256]{1,0:T(8,128)(2,1)} %bitcast.72), channel_id=1, source_target_pairs={{0,48},{16,0},{32,16},{48,32},{1,49},{17,1},{33,17},{49,33},{2,50}... | collective-permute-start | bytes 294920 | tf_op jit(solution)/shard_map/ppermute | solution.py:36
  18.2 1.9 collective-permute-start
  22.7 5.9 %collective-permute-done = bf16[192,256]{1,0:T(8,128)(2,1)S(1)} collective-permute-done((bf16[192,256]{1,0:T(8,128)(2,1)}, bf16[192,256]{1,0:T(8,128)(2,1)S(1)}, u32[]{:S(2)}, u32[]{:S(2)}) %collective-permute-start) | collective-permute-done | bytes 98336 | tf_op jit(solution)/shard_map/ppermute | solution.py:36
  29.4 3.6 %collective-permute-start.1 = (bf16[1008,384]{1,0:T(8,128)(2,1)S(1)}, bf16[1008,384]{1,0:T(8,128)(2,1)S(1)}, u32[]{:S(2)}, u32[]{:S(2)}) collective-permute-start(bf16[1008,384]{1,0:T(8,128)(2,1)S(1)} %pad_maximum_fusion.refs_0_), channel_id=1, source_target_pairs={{0,64},{64,0},{1,65},{65,1},{2,66},{66,2},{3,67},{67,3},{4,68},{68... | collective-permute-start | bytes 2322440 | tf_op jit(solution)/shard_map/ppermute | solution.py:36
  33.0 2.4 %collective-permute-start.2 = (bf16[1008,384]{1,0:T(8,128)(2,1)S(1)}, bf16[1008,384]{1,0:T(8,128)(2,1)}, u32[]{:S(2)}, u32[]{:S(2)}) collective-permute-start(bf16[1008,384]{1,0:T(8,128)(2,1)S(1)} %pad_maximum_fusion.refs_0_), channel_id=1, source_target_pairs={{0,128},{128,256},{256,384},{384,0},{1,129},{129,257},{257,385},{3... | collective-permute-start | bytes 2322440 | tf_op jit(solution)/shard_map/ppermute | solution.py:36
  35.4 3.5 %collective-permute-start.3 = (bf16[1008,384]{1,0:T(8,128)(2,1)S(1)}, bf16[1008,384]{1,0:T(8,128)(2,1)S(1)}, u32[]{:S(2)}, u32[]{:S(2)}) collective-permute-start(bf16[1008,384]{1,0:T(8,128)(2,1)S(1)} %pad_maximum_fusion.refs_0_), channel_id=1, source_target_pairs={{0,384},{128,0},{256,128},{384,256},{1,385},{129,1},{257,129},{385... | collective-permute-start | bytes 2322440 | tf_op jit(solution)/shard_map/ppermute | solution.py:36
  38.8 7.3 %collective-permute-start.4 = (bf16[192,256]{1,0:T(8,128)(2,1)S(1)}, bf16[192,256]{1,0:T(8,128)(2,1)S(1)}, u32[]{:S(2)}, u32[]{:S(2)}) collective-permute-start(bf16[192,256]{1,0:T(8,128)(2,1)S(1)} %bitcast.63), channel_id=1, source_target_pairs={{0,0},{2,64},{4,128},{6,192},{8,256},{10,320},{12,384},{14,448},{6... | collective-permute-start | bytes 294920 | tf_op jit(solution)/shard_map/ppermute | solution.py:45
  46.3 8.7 %collective-permute-done.4 = bf16[192,256]{1,0:T(8,128)(2,1)S(1)} collective-permute-done((bf16[192,256]{1,0:T(8,128)(2,1)S(1)}, bf16[192,256]{1,0:T(8,128)(2,1)S(1)}, u32[]{:S(2)}, u32[]{:S(2)}) %collective-permute-start.4) | collective-permute-done | bytes 98336 | tf_op jit(solution)/shard_map/ppermute | solution.py:45
  55.0 3.0 %collective-permute-done.3.refs_3_ = bf16[1008,384]{1,0:T(8,128)(2,1)S(1)} collective-permute-done((bf16[1008,384]{1,0:T(8,128)(2,1)S(1)}, bf16[1008,384]{1,0:T(8,128)(2,1)S(1)}, u32[]{:S(2)}, u32[]{:S(2)}) %collective-permute-start.3) | collective-permute-done | bytes 774176 | tf_op jit(solution)/shard_map/ppermute | solution.py:36
  58.8 1.9 collective-permute-start.5
  60.8 3.9 %collective-permute-start.6 = (bf16[1008,384]{1,0:T(8,128)(2,1)S(1)}, bf16[1008,384]{1,0:T(8,128)(2,1)}, u32[]{:S(2)}, u32[]{:S(2)}) collective-permute-start(bf16[1008,384]{1,0:T(8,128)(2,1)S(1)} %collective-permute-done.1.refs_1_), channel_id=1, source_target_pairs={{0,384},{128,0},{256,128},{384,256},{1,385},{129,1},{257,129},{385... | collective-permute-start | bytes 2322440 | tf_op jit(solution)/shard_map/ppermute | solution.py:36
  64.7 8.0 %collective-permute-start.7 = (bf16[192,256]{1,0:T(8,128)(2,1)S(1)}, bf16[192,256]{1,0:T(8,128)(2,1)S(1)}, u32[]{:S(2)}, u32[]{:S(2)}) collective-permute-start(bf16[192,256]{1,0:T(8,128)(2,1)S(1)} %bitcast.64), channel_id=1, source_target_pairs={{0,256},{2,320},{4,384},{6,448},{8,0},{10,64},{12,128},{14,192},{6... | collective-permute-start | bytes 294920 | tf_op jit(solution)/shard_map/ppermute | solution.py:45
  72.7 5.2 %collective-permute-done.7 = bf16[192,256]{1,0:T(8,128)(2,1)S(1)} collective-permute-done((bf16[192,256]{1,0:T(8,128)(2,1)S(1)}, bf16[192,256]{1,0:T(8,128)(2,1)S(1)}, u32[]{:S(2)}, u32[]{:S(2)}) %collective-permute-start.7) | collective-permute-done | bytes 98336 | tf_op jit(solution)/shard_map/ppermute | solution.py:45
  78.8 3.7 %collective-permute-done.6.refs_5_ = bf16[1008,384]{1,0:T(8,128)(2,1)} collective-permute-done((bf16[1008,384]{1,0:T(8,128)(2,1)S(1)}, bf16[1008,384]{1,0:T(8,128)(2,1)}, u32[]{:S(2)}, u32[]{:S(2)}) %collective-permute-start.6) | collective-permute-done | bytes 774176 | tf_op jit(solution)/shard_map/ppermute | solution.py:36
  83.3 1.9 collective-permute-start.8
  85.2 3.9 %collective-permute-start.9 = (bf16[1008,384]{1,0:T(8,128)(2,1)}, bf16[1008,384]{1,0:T(8,128)(2,1)}, u32[]{:S(2)}, u32[]{:S(2)}) collective-permute-start(bf16[1008,384]{1,0:T(8,128)(2,1)} %collective-permute-done.6.refs_5_), channel_id=1, source_target_pairs={{0,384},{128,0},{256,128},{384,256},{1,385},{129,1},{257,129},{385... | collective-permute-start | bytes 2322440 | tf_op jit(solution)/shard_map/ppermute | solution.py:36
  89.7 2.3 %copy-done = bf16[9216,256]{1,0:T(8,128)(2,1)S(1)} copy-done((bf16[9216,256]{1,0:T(8,128)(2,1)S(1)}, bf16[9216,256]{1,0:T(8,128)(2,1)}, u32[]{:S(2)}) %copy-start) | copy-done | bytes 4718616
  94.3 5.7 %early.1 = (f32[1008,256]{1,0:T(8,128)S(1)}, f32[672,256]{1,0:T(8,128)S(1)}, bf16[2,384,256]{2,1,0:T(8,128)(2,1)S(1)}, bf16[2,384,256]{2,1,0:T(8,128)(2,1)S(1)},...) custom-call(s32[9]{0:T(128)S(1)} %concatenate.13.place, bf16[1008,384]{1,0:T(8,128)(2,1)S(1)} %pad_maximum_fusion.refs_0_, ...), custom_call_target="tpu_custom_call" | custom-call | flops 2642411520 | bytes 29360128 | tf_op jit(solution)/shard_map/early/pallas_call | solution.py:267
  101.0 3.1 %collective-permute-done.9.w_7.refs_7_ = bf16[1008,384]{1,0:T(8,128)(2,1)} collective-permute-done((bf16[1008,384]{1,0:T(8,128)(2,1)}, bf16[1008,384]{1,0:T(8,128)(2,1)}, u32[]{:S(2)}, u32[]{:S(2)}) %collective-permute-start.9) | collective-permute-done | bytes 774176 | tf_op jit(solution)/shard_map/ppermute | solution.py:36
  104.2 2.4 %inner.1 = (bf16[672,256]{1,0:T(8,128)(2,1)S(1)}, bf16[672,256]{1,0:T(8,128)(2,1)S(1)}, f32[1,256]{1,0:T(1,128)S(1)}) custom-call(bf16[1008,384]{1,0:T(8,128)(2,1)} %collective-permute-done.8.w_6.refs_6_, bf16[1008,384]{1,0:T(8,128)(2,1)} %collective-permute-done.9.w_7.refs_7_, f32[1008,256]{1,0:T(8,128)S(1)} %get-tuple-element.44.early, ...), custom_call_target="tpu_custom_call" | custom-call | flops 528482304 | bytes 8388608 | tf_op jit(solution)/shard_map/inner/pallas_call | solution.py:291
  106.6 6.2 %outer.1 = bf16[16,416,256]{2,1,0:T(8,128)(2,1)} custom-call(s32[9]{0:T(128)S(1)} %concatenate.13.place, bf16[1008,384]{1,0:T(8,128)(2,1)S(1)} %pad_maximum_fusion.refs_0_, bf16[1008,384]{1,0:T(8,128)(2,1)S(1)} %collective-permute-done.1.refs_1_, bf16[1008,384]{1,0:T(8,128)(2,1)} %collective-permute-done.2.refs_2_, bf16[1008,384]{1,0:T(8,128)(2,1)S(1)} %copy-done.3, ...), custom_call_target="tpu_custom_call" | custom-call | flops 2113929216 | bytes 20971520 | tf_op jit(solution)/shard_map/outer/pallas_call | solution.py:305
  112.9 4.3 %collective-permute-start.11 = (bf16[672,256]{1,0:T(8,128)(2,1)S(1)}, bf16[672,256]{1,0:T(8,128)(2,1)S(1)}, u32[]{:S(2)}, u32[]{:S(2)}) collective-permute-start(bf16[672,256]{1,0:T(8,128)(2,1)S(1)} %get-tuple-element.54.refs_0_), channel_id=1, source_target_pairs={{0,64},{64,0},{1,65},{65,1},{2,66},{66,2},{3,67},{67,3},{4,68},{68... | collective-permute-start | bytes 1032200 | tf_op jit(solution)/shard_map/ppermute | solution.py:36
  117.2 3.6 %collective-permute-start.12 = (bf16[672,256]{1,0:T(8,128)(2,1)S(1)}, bf16[672,256]{1,0:T(8,128)(2,1)S(1)}, u32[]{:S(2)}, u32[]{:S(2)}) collective-permute-start(bf16[672,256]{1,0:T(8,128)(2,1)S(1)} %get-tuple-element.54.refs_0_), channel_id=1, source_target_pairs={{0,128},{128,256},{256,384},{384,0},{1,129},{129,257},{257,385},{3... | collective-permute-start | bytes 1032200 | tf_op jit(solution)/shard_map/ppermute | solution.py:36
  120.8 2.2 %collective-permute-start.13 = (bf16[672,256]{1,0:T(8,128)(2,1)S(1)}, bf16[672,256]{1,0:T(8,128)(2,1)S(1)}, u32[]{:S(2)}, u32[]{:S(2)}) collective-permute-start(bf16[672,256]{1,0:T(8,128)(2,1)S(1)} %get-tuple-element.54.refs_0_), channel_id=1, source_target_pairs={{0,384},{128,0},{256,128},{384,256},{1,385},{129,1},{257,129},{385... | collective-permute-start | bytes 1032200 | tf_op jit(solution)/shard_map/ppermute | solution.py:36
  123.1 3.3 %collective-permute-done.12.refs_2_ = bf16[672,256]{1,0:T(8,128)(2,1)S(1)} collective-permute-done((bf16[672,256]{1,0:T(8,128)(2,1)S(1)}, bf16[672,256]{1,0:T(8,128)(2,1)S(1)}, u32[]{:S(2)}, u32[]{:S(2)}) %collective-permute-start.12) | collective-permute-done | bytes 344096 | tf_op jit(solution)/shard_map/ppermute | solution.py:36
  126.4 5.2 %collective-permute-done.13.refs_3_ = bf16[672,256]{1,0:T(8,128)(2,1)S(1)} collective-permute-done((bf16[672,256]{1,0:T(8,128)(2,1)S(1)}, bf16[672,256]{1,0:T(8,128)(2,1)S(1)}, u32[]{:S(2)}, u32[]{:S(2)}) %collective-permute-start.13) | collective-permute-done | bytes 344096 | tf_op jit(solution)/shard_map/ppermute | solution.py:36
  131.6 1.9 collective-permute-start.15
  133.5 5.1 %collective-permute-start.14 = (bf16[672,256]{1,0:T(8,128)(2,1)S(1)}, bf16[672,256]{1,0:T(8,128)(2,1)S(1)}, u32[]{:S(2)}, u32[]{:S(2)}) collective-permute-start(bf16[672,256]{1,0:T(8,128)(2,1)S(1)} %collective-permute-done.11.refs_1_), channel_id=1, source_target_pairs={{0,128},{128,256},{256,384},{384,0},{1,129},{129,257},{257,385},{3... | collective-permute-start | bytes 1032200 | tf_op jit(solution)/shard_map/ppermute | solution.py:36
  138.7 1.9 collective-permute-start.16
  142.0 2.6 %collective-permute-start.17 = (bf16[672,256]{1,0:T(8,128)(2,1)S(1)}, bf16[672,256]{1,0:T(8,128)(2,1)S(1)}, u32[]{:S(2)}, u32[]{:S(2)}) collective-permute-start(bf16[672,256]{1,0:T(8,128)(2,1)S(1)} %collective-permute-done.15.refs_5_), channel_id=1, source_target_pairs={{0,384},{128,0},{256,128},{384,256},{1,385},{129,1},{257,129},{385... | collective-permute-start | bytes 1032200 | tf_op jit(solution)/shard_map/ppermute | solution.py:36
  144.6 1.8 collective-permute-done.14.refs_4_
  146.3 3.7 %collective-permute-done.16.refs_6_ = bf16[672,256]{1,0:T(8,128)(2,1)S(1)} collective-permute-done((bf16[672,256]{1,0:T(8,128)(2,1)S(1)}, bf16[672,256]{1,0:T(8,128)(2,1)S(1)}, u32[]{:S(2)}, u32[]{:S(2)}) %collective-permute-start.16) | collective-permute-done | bytes 344096 | tf_op jit(solution)/shard_map/ppermute | solution.py:36
  150.0 2.3 %collective-permute-done.17.refs_7_ = bf16[672,256]{1,0:T(8,128)(2,1)S(1)} collective-permute-done((bf16[672,256]{1,0:T(8,128)(2,1)S(1)}, bf16[672,256]{1,0:T(8,128)(2,1)S(1)}, u32[]{:S(2)}, u32[]{:S(2)}) %collective-permute-start.17) | collective-permute-done | bytes 344096 | tf_op jit(solution)/shard_map/ppermute | solution.py:36
  152.3 1.9 copy-done.8
  154.2 3.6 %grad.1 = (bf16[672,384]{1,0:T(8,128)(2,1)S(1)}, bf16[672,384]{1,0:T(8,128)(2,1)S(1)}) custom-call(s32[9]{0:T(128)S(1)} %concatenate.13.place, bf16[672,256]{1,0:T(8,128)(2,1)S(1)} %get-tuple-element.54.refs_0_, bf16[672,256]{1,0:T(8,128)(2,1)S(1)} %collective-permute-done.11.refs_1_, bf16[672,256]{1,0:T(8,128)(2,1)S(1)} %collective-permute-done.12.refs_2_, ...), custom_call_target="tpu_custom_call" | custom-call | flops 2113929216 | bytes 8388608 | tf_op jit(solution)/shard_map/grad/pallas_call | solution.py:323
  157.8 2.2 %collective-permute-start.18 = (bf16[672,384]{1,0:T(8,128)(2,1)S(1)}, bf16[672,384]{1,0:T(8,128)(2,1)S(1)}, u32[]{:S(2)}, u32[]{:S(2)}) collective-permute-start(bf16[672,384]{1,0:T(8,128)(2,1)S(1)} %get-tuple-element.62.refs_0_), channel_id=1, source_target_pairs={{0,64},{64,0},{1,65},{65,1},{2,66},{66,2},{3,67},{67,3},{4,68},{68... | collective-permute-start | bytes 1548296 | tf_op jit(solution)/shard_map/ppermute | solution.py:36
  160.0 3.6 %collective-permute-start.19 = (bf16[672,384]{1,0:T(8,128)(2,1)S(1)}, bf16[672,384]{1,0:T(8,128)(2,1)S(1)}, u32[]{:S(2)}, u32[]{:S(2)}) collective-permute-start(bf16[672,384]{1,0:T(8,128)(2,1)S(1)} %get-tuple-element.62.refs_0_), channel_id=1, source_target_pairs={{0,128},{128,256},{256,384},{384,0},{1,129},{129,257},{257,385},{3... | collective-permute-start | bytes 1548296 | tf_op jit(solution)/shard_map/ppermute | solution.py:36
  163.6 2.3 %collective-permute-start.20 = (bf16[672,384]{1,0:T(8,128)(2,1)S(1)}, bf16[672,384]{1,0:T(8,128)(2,1)S(1)}, u32[]{:S(2)}, u32[]{:S(2)}) collective-permute-start(bf16[672,384]{1,0:T(8,128)(2,1)S(1)} %get-tuple-element.62.refs_0_), channel_id=1, source_target_pairs={{0,384},{128,0},{256,128},{384,256},{1,385},{129,1},{257,129},{385... | collective-permute-start | bytes 1548296 | tf_op jit(solution)/shard_map/ppermute | solution.py:36
  165.8 3.6 %collective-permute-start.23 = (bf16[672,384]{1,0:T(8,128)(2,1)S(1)}, bf16[672,384]{1,0:T(8,128)(2,1)S(1)}, u32[]{:S(2)}, u32[]{:S(2)}) collective-permute-start(bf16[672,384]{1,0:T(8,128)(2,1)S(1)} %get-tuple-element.63.refs_6_), channel_id=1, source_target_pairs={{0,64},{64,0},{1,65},{65,1},{2,66},{66,2},{3,67},{67,3},{4,68},{68... | collective-permute-start | bytes 1548296 | tf_op jit(solution)/shard_map/ppermute | solution.py:36
  169.5 2.5 %collective-permute-done.18.refs_1_ = bf16[672,384]{1,0:T(8,128)(2,1)S(1)} collective-permute-done((bf16[672,384]{1,0:T(8,128)(2,1)S(1)}, bf16[672,384]{1,0:T(8,128)(2,1)S(1)}, u32[]{:S(2)}, u32[]{:S(2)}) %collective-permute-start.18) | collective-permute-done | bytes 516128 | tf_op jit(solution)/shard_map/ppermute | solution.py:36
  172.0 2.1 %collective-permute-start.21 = (bf16[672,384]{1,0:T(8,128)(2,1)S(1)}, bf16[672,384]{1,0:T(8,128)(2,1)}, u32[]{:S(2)}, u32[]{:S(2)}) collective-permute-start(bf16[672,384]{1,0:T(8,128)(2,1)S(1)} %collective-permute-done.18.refs_1_), channel_id=1, source_target_pairs={{0,128},{128,256},{256,384},{384,0},{1,129},{129,257},{257,385},{3... | collective-permute-start | bytes 1548296 | tf_op jit(solution)/shard_map/ppermute | solution.py:36
  174.2 3.7 %collective-permute-start.22 = (bf16[672,384]{1,0:T(8,128)(2,1)S(1)}, bf16[672,384]{1,0:T(8,128)(2,1)}, u32[]{:S(2)}, u32[]{:S(2)}) collective-permute-start(bf16[672,384]{1,0:T(8,128)(2,1)S(1)} %collective-permute-done.18.refs_1_), channel_id=1, source_target_pairs={{0,384},{128,0},{256,128},{384,256},{1,385},{129,1},{257,129},{385... | collective-permute-start | bytes 1548296 | tf_op jit(solution)/shard_map/ppermute | solution.py:36
  178.0 1.8 collective-permute-done.23.refs_7_
  179.8 3.3 %collective-permute-done.21.refs_4_ = bf16[672,384]{1,0:T(8,128)(2,1)} collective-permute-done((bf16[672,384]{1,0:T(8,128)(2,1)S(1)}, bf16[672,384]{1,0:T(8,128)(2,1)}, u32[]{:S(2)}, u32[]{:S(2)}) %collective-permute-start.21) | collective-permute-done | bytes 516128 | tf_op jit(solution)/shard_map/ppermute | solution.py:36
  183.1 3.8 %collective-permute-done.22.refs_5_ = bf16[672,384]{1,0:T(8,128)(2,1)} collective-permute-done((bf16[672,384]{1,0:T(8,128)(2,1)S(1)}, bf16[672,384]{1,0:T(8,128)(2,1)}, u32[]{:S(2)}, u32[]{:S(2)}) %collective-permute-start.22) | collective-permute-done | bytes 516128 | tf_op jit(solution)/shard_map/ppermute | solution.py:36
  186.9 3.3 %assemble.1 = (bf16[336,3072]{1,0:T(8,128)(2,1)}, bf16[336,3072]{1,0:T(8,128)(2,1)}) custom-call(s32[9]{0:T(128)S(1)} %concatenate.13.place, bf16[672,384]{1,0:T(8,128)(2,1)S(1)} %get-tuple-element.62.refs_0_, bf16[672,384]{1,0:T(8,128)(2,1)S(1)} %collective-permute-done.18.refs_1_, bf16[672,384]{1,0:T(8,128)(2,1)S(1)} %collective-permute-done.19.refs_2_, ...), custom_call_target="tpu_custom_call" | custom-call | bytes 8388608 | tf_op jit(solution)/shard_map/assemble/pallas_call | solution.py:339
  190.3 4.0 %reduce-scatter.2.cloned.1.call-done = bf16[1,416,256]{2,1,0:T(8,128)(2,1)} async-done(((bf16[16,416,256]{2,1,0:T(8,128)(2,1)}), bf16[1,416,256]{2,1,0:T(8,128)(2,1)}) %reduce-scatter.2.cloned.1.call-update) | async-done | bytes 213008 | tf_op jit(solution)/shard_map/reduce_scatter | solution.py:321
  195.0 1.7 fusion.6
  (59 shorter events, 12.1 us)
Async XLA Ops:
  7.2 21.4 %copy-start.9 = (bf16[1,256,192]{1,2,0:T(8,128)(2,1)S(1)}, bf16[1,256,192]{1,2,0:T(8,128)(2,1)}, u32[]{:S(2)}) copy-start(bf16[1,256,192]{1,2,0:T(8,128)(2,1)} %param.10) | copy-start | bytes 294916
  7.2 39.1 %copy-start.15 = (f32[1,2,256,4]{2,3,1,0:T(4,128)S(1)}, f32[1,2,256,4]{2,3,1,0:T(4,128)}, u32[]{:S(2)}) copy-start(f32[1,2,256,4]{2,3,1,0:T(4,128)} %param.17) | copy-start | bytes 24580
  7.2 39.1 %copy-start.16 = (s32[1,2,256,4]{2,3,1,0:T(4,128)S(1)}, s32[1,2,256,4]{2,3,1,0:T(4,128)}, u32[]{:S(2)}) copy-start(s32[1,2,256,4]{2,3,1,0:T(4,128)} %param.16) | copy-start | bytes 24580
  7.2 82.5 %all-gather.5.cloned.1.call-start = ((), (), s32[]{:S(2)}) async-start(), calls=%async_computation.2 | async-start | bytes 5013504 | tf_op jit(solution)/shard_map/all_gather | solution.py:259
  7.2 15.4 %collective-permute-start.10 = (bf16[192,256]{1,0:T(8,128)(2,1)}, bf16[192,256]{1,0:T(8,128)(2,1)S(1)}, u32[]{:S(2)}, u32[]{:S(2)}) collective-permute-start(bf16[192,256]{1,0:T(8,128)(2,1)} %bitcast.72), channel_id=1, source_target_pairs={{0,48},{16,0},{32,16},{48,32},{1,49},{17,1},{33,17},{49,33},{2,50}... | collective-permute-start | bytes 294920 | tf_op jit(solution)/shard_map/ppermute | solution.py:36
  18.2 10.4 %collective-permute-start = (bf16[192,256]{1,0:T(8,128)(2,1)}, bf16[192,256]{1,0:T(8,128)(2,1)S(1)}, u32[]{:S(2)}, u32[]{:S(2)}) collective-permute-start(bf16[192,256]{1,0:T(8,128)(2,1)} %bitcast.73), channel_id=1, source_target_pairs={{0,16},{16,32},{32,48},{48,0},{1,17},{17,33},{33,49},{49,1},{2,18}... | collective-permute-start | bytes 294920 | tf_op jit(solution)/shard_map/ppermute | solution.py:36
  20.1 69.0 %copy-start.7 = (f32[1,3072]{1,0:T(1,128)S(1)}, f32[1,3072]{1,0:T(1,128)}, u32[]{:S(2)}) copy-start(f32[1,3072]{1,0:T(1,128)} %refs_9_.1) | copy-start | bytes 36868
  22.7 10.3 %copy-start.11 = (bf16[192,256]{1,0:T(8,128)(2,1)}, bf16[192,256]{1,0:T(8,128)(2,1)S(1)}, u32[]{:S(2)}) copy-start(bf16[192,256]{1,0:T(8,128)(2,1)S(1)} %collective-permute-done.10) | copy-start | bytes 294916
  28.6 4.4 %copy-start.13 = (bf16[192,256]{1,0:T(8,128)(2,1)}, bf16[192,256]{1,0:T(8,128)(2,1)S(1)}, u32[]{:S(2)}) copy-start(bf16[192,256]{1,0:T(8,128)(2,1)S(1)} %collective-permute-done) | copy-start | bytes 294916
  29.4 111.3 %all-gather.7.cloned.1.call-start = ((), (), s32[]{:S(2)}) async-start(), calls=%async_computation.3 | async-start | bytes 3342336 | tf_op jit(solution)/shard_map/all_gather | solution.py:262
  29.4 25.6 %collective-permute-start.1 = (bf16[1008,384]{1,0:T(8,128)(2,1)S(1)}, bf16[1008,384]{1,0:T(8,128)(2,1)S(1)}, u32[]{:S(2)}, u32[]{:S(2)}) collective-permute-start(bf16[1008,384]{1,0:T(8,128)(2,1)S(1)} %pad_maximum_fusion.refs_0_), channel_id=1, source_target_pairs={{0,64},{64,0},{1,65},{65,1},{2,66},{66,2},{3,67},{67,3},{4,68},{68... | collective-permute-start | bytes 2322440 | tf_op jit(solution)/shard_map/ppermute | solution.py:36
  33.0 22.0 %collective-permute-start.2 = (bf16[1008,384]{1,0:T(8,128)(2,1)S(1)}, bf16[1008,384]{1,0:T(8,128)(2,1)}, u32[]{:S(2)}, u32[]{:S(2)}) collective-permute-start(bf16[1008,384]{1,0:T(8,128)(2,1)S(1)} %pad_maximum_fusion.refs_0_), channel_id=1, source_target_pairs={{0,128},{128,256},{256,384},{384,0},{1,129},{129,257},{257,385},{3... | collective-permute-start | bytes 2322440 | tf_op jit(solution)/shard_map/ppermute | solution.py:36
  35.4 22.6 %collective-permute-start.3 = (bf16[1008,384]{1,0:T(8,128)(2,1)S(1)}, bf16[1008,384]{1,0:T(8,128)(2,1)S(1)}, u32[]{:S(2)}, u32[]{:S(2)}) collective-permute-start(bf16[1008,384]{1,0:T(8,128)(2,1)S(1)} %pad_maximum_fusion.refs_0_), channel_id=1, source_target_pairs={{0,384},{128,0},{256,128},{384,256},{1,385},{129,1},{257,129},{385... | collective-permute-start | bytes 2322440 | tf_op jit(solution)/shard_map/ppermute | solution.py:36
  38.8 16.2 %collective-permute-start.4 = (bf16[192,256]{1,0:T(8,128)(2,1)S(1)}, bf16[192,256]{1,0:T(8,128)(2,1)S(1)}, u32[]{:S(2)}, u32[]{:S(2)}) collective-permute-start(bf16[192,256]{1,0:T(8,128)(2,1)S(1)} %bitcast.63), channel_id=1, source_target_pairs={{0,0},{2,64},{4,128},{6,192},{8,256},{10,320},{12,384},{14,448},{6... | collective-permute-start | bytes 294920 | tf_op jit(solution)/shard_map/ppermute | solution.py:45
  58.0 0.9 copy-start.1
  58.8 19.1 %collective-permute-start.5 = (bf16[1008,384]{1,0:T(8,128)(2,1)S(1)}, bf16[1008,384]{1,0:T(8,128)(2,1)S(1)}, u32[]{:S(2)}, u32[]{:S(2)}) collective-permute-start(bf16[1008,384]{1,0:T(8,128)(2,1)S(1)} %collective-permute-done.1.refs_1_), channel_id=1, source_target_pairs={{0,128},{128,256},{256,384},{384,0},{1,129},{129,257},{257,385},{3... | collective-permute-start | bytes 2322440 | tf_op jit(solution)/shard_map/ppermute | solution.py:36
  60.8 21.8 %collective-permute-start.6 = (bf16[1008,384]{1,0:T(8,128)(2,1)S(1)}, bf16[1008,384]{1,0:T(8,128)(2,1)}, u32[]{:S(2)}, u32[]{:S(2)}) collective-permute-start(bf16[1008,384]{1,0:T(8,128)(2,1)S(1)} %collective-permute-done.1.refs_1_), channel_id=1, source_target_pairs={{0,384},{128,0},{256,128},{384,256},{1,385},{129,1},{257,129},{385... | collective-permute-start | bytes 2322440 | tf_op jit(solution)/shard_map/ppermute | solution.py:36
  64.7 13.3 %collective-permute-start.7 = (bf16[192,256]{1,0:T(8,128)(2,1)S(1)}, bf16[192,256]{1,0:T(8,128)(2,1)S(1)}, u32[]{:S(2)}, u32[]{:S(2)}) collective-permute-start(bf16[192,256]{1,0:T(8,128)(2,1)S(1)} %bitcast.64), channel_id=1, source_target_pairs={{0,256},{2,320},{4,384},{6,448},{8,0},{10,64},{12,128},{14,192},{6... | collective-permute-start | bytes 294920 | tf_op jit(solution)/shard_map/ppermute | solution.py:45
  78.0 0.9 copy-start.4
  83.2 111.0 %reduce-scatter.2.cloned.1.call-start = ((), (), s32[]{:S(2)}) async-start(), calls=%async_computation.1 | async-start | bytes 3620864 | tf_op jit(solution)/shard_map/reduce_scatter | solution.py:321
  83.3 17.7 %collective-permute-start.8 = (bf16[1008,384]{1,0:T(8,128)(2,1)}, bf16[1008,384]{1,0:T(8,128)(2,1)}, u32[]{:S(2)}, u32[]{:S(2)}) collective-permute-start(bf16[1008,384]{1,0:T(8,128)(2,1)} %collective-permute-done.2.refs_2_), channel_id=1, source_target_pairs={{0,128},{128,256},{256,384},{384,0},{1,129},{129,257},{257,385},{3... | collective-permute-start | bytes 2322440 | tf_op jit(solution)/shard_map/ppermute | solution.py:36
  85.2 18.9 %collective-permute-start.9 = (bf16[1008,384]{1,0:T(8,128)(2,1)}, bf16[1008,384]{1,0:T(8,128)(2,1)}, u32[]{:S(2)}, u32[]{:S(2)}) collective-permute-start(bf16[1008,384]{1,0:T(8,128)(2,1)} %collective-permute-done.6.refs_5_), channel_id=1, source_target_pairs={{0,384},{128,0},{256,128},{384,256},{1,385},{129,1},{257,129},{385... | collective-permute-start | bytes 2322440 | tf_op jit(solution)/shard_map/ppermute | solution.py:36
  89.7 2.3 %copy-start = (bf16[9216,256]{1,0:T(8,128)(2,1)S(1)}, bf16[9216,256]{1,0:T(8,128)(2,1)}, u32[]{:S(2)}) copy-start(bf16[9216,256]{1,0:T(8,128)(2,1)} %all-gather.5.cloned.1.call-done) | copy-start | bytes 14155780
  92.0 1.1 copy-start.2
  93.2 1.1 copy-start.5
  104.2 2.4 %copy-start.3 = (bf16[1008,384]{1,0:T(8,128)(2,1)S(1)}, bf16[1008,384]{1,0:T(8,128)(2,1)}, u32[]{:S(2)}) copy-start(bf16[1008,384]{1,0:T(8,128)(2,1)} %copy-done.1) | copy-start | bytes 2322436
  104.2 2.4 %copy-start.6 = (bf16[1008,384]{1,0:T(8,128)(2,1)S(1)}, bf16[1008,384]{1,0:T(8,128)(2,1)}, u32[]{:S(2)}) copy-start(bf16[1008,384]{1,0:T(8,128)(2,1)} %copy-done.4) | copy-start | bytes 2322436
  112.9 10.2 %collective-permute-start.11 = (bf16[672,256]{1,0:T(8,128)(2,1)S(1)}, bf16[672,256]{1,0:T(8,128)(2,1)S(1)}, u32[]{:S(2)}, u32[]{:S(2)}) collective-permute-start(bf16[672,256]{1,0:T(8,128)(2,1)S(1)} %get-tuple-element.54.refs_0_), channel_id=1, source_target_pairs={{0,64},{64,0},{1,65},{65,1},{2,66},{66,2},{3,67},{67,3},{4,68},{68... | collective-permute-start | bytes 1032200 | tf_op jit(solution)/shard_map/ppermute | solution.py:36
  117.2 9.1 %collective-permute-start.12 = (bf16[672,256]{1,0:T(8,128)(2,1)S(1)}, bf16[672,256]{1,0:T(8,128)(2,1)S(1)}, u32[]{:S(2)}, u32[]{:S(2)}) collective-permute-start(bf16[672,256]{1,0:T(8,128)(2,1)S(1)} %get-tuple-element.54.refs_0_), channel_id=1, source_target_pairs={{0,128},{128,256},{256,384},{384,0},{1,129},{129,257},{257,385},{3... | collective-permute-start | bytes 1032200 | tf_op jit(solution)/shard_map/ppermute | solution.py:36
  120.8 10.8 %collective-permute-start.13 = (bf16[672,256]{1,0:T(8,128)(2,1)S(1)}, bf16[672,256]{1,0:T(8,128)(2,1)S(1)}, u32[]{:S(2)}, u32[]{:S(2)}) collective-permute-start(bf16[672,256]{1,0:T(8,128)(2,1)S(1)} %get-tuple-element.54.refs_0_), channel_id=1, source_target_pairs={{0,384},{128,0},{256,128},{384,256},{1,385},{129,1},{257,129},{385... | collective-permute-start | bytes 1032200 | tf_op jit(solution)/shard_map/ppermute | solution.py:36
  131.6 10.3 %collective-permute-start.15 = (bf16[672,256]{1,0:T(8,128)(2,1)S(1)}, bf16[672,256]{1,0:T(8,128)(2,1)S(1)}, u32[]{:S(2)}, u32[]{:S(2)}) collective-permute-start(bf16[672,256]{1,0:T(8,128)(2,1)S(1)} %collective-permute-done.11.refs_1_), channel_id=1, source_target_pairs={{0,384},{128,0},{256,128},{384,256},{1,385},{129,1},{257,129},{385... | collective-permute-start | bytes 1032200 | tf_op jit(solution)/shard_map/ppermute | solution.py:36
  133.5 12.8 %collective-permute-start.14 = (bf16[672,256]{1,0:T(8,128)(2,1)S(1)}, bf16[672,256]{1,0:T(8,128)(2,1)S(1)}, u32[]{:S(2)}, u32[]{:S(2)}) collective-permute-start(bf16[672,256]{1,0:T(8,128)(2,1)S(1)} %collective-permute-done.11.refs_1_), channel_id=1, source_target_pairs={{0,128},{128,256},{256,384},{384,0},{1,129},{129,257},{257,385},{3... | collective-permute-start | bytes 1032200 | tf_op jit(solution)/shard_map/ppermute | solution.py:36
  138.7 11.4 %collective-permute-start.16 = (bf16[672,256]{1,0:T(8,128)(2,1)S(1)}, bf16[672,256]{1,0:T(8,128)(2,1)S(1)}, u32[]{:S(2)}, u32[]{:S(2)}) collective-permute-start(bf16[672,256]{1,0:T(8,128)(2,1)S(1)} %collective-permute-done.12.refs_2_), channel_id=1, source_target_pairs={{0,128},{128,256},{256,384},{384,0},{1,129},{129,257},{257,385},{3... | collective-permute-start | bytes 1032200 | tf_op jit(solution)/shard_map/ppermute | solution.py:36
  142.0 10.3 %collective-permute-start.17 = (bf16[672,256]{1,0:T(8,128)(2,1)S(1)}, bf16[672,256]{1,0:T(8,128)(2,1)S(1)}, u32[]{:S(2)}, u32[]{:S(2)}) collective-permute-start(bf16[672,256]{1,0:T(8,128)(2,1)S(1)} %collective-permute-done.15.refs_5_), channel_id=1, source_target_pairs={{0,384},{128,0},{256,128},{384,256},{1,385},{129,1},{257,129},{385... | collective-permute-start | bytes 1032200 | tf_op jit(solution)/shard_map/ppermute | solution.py:36
  152.3 1.9 copy-start.8
  157.8 14.3 %collective-permute-start.18 = (bf16[672,384]{1,0:T(8,128)(2,1)S(1)}, bf16[672,384]{1,0:T(8,128)(2,1)S(1)}, u32[]{:S(2)}, u32[]{:S(2)}) collective-permute-start(bf16[672,384]{1,0:T(8,128)(2,1)S(1)} %get-tuple-element.62.refs_0_), channel_id=1, source_target_pairs={{0,64},{64,0},{1,65},{65,1},{2,66},{66,2},{3,67},{67,3},{4,68},{68... | collective-permute-start | bytes 1548296 | tf_op jit(solution)/shard_map/ppermute | solution.py:36
  160.0 18.0 %collective-permute-start.19 = (bf16[672,384]{1,0:T(8,128)(2,1)S(1)}, bf16[672,384]{1,0:T(8,128)(2,1)S(1)}, u32[]{:S(2)}, u32[]{:S(2)}) collective-permute-start(bf16[672,384]{1,0:T(8,128)(2,1)S(1)} %get-tuple-element.62.refs_0_), channel_id=1, source_target_pairs={{0,128},{128,256},{256,384},{384,0},{1,129},{129,257},{257,385},{3... | collective-permute-start | bytes 1548296 | tf_op jit(solution)/shard_map/ppermute | solution.py:36
  163.6 14.4 %collective-permute-start.20 = (bf16[672,384]{1,0:T(8,128)(2,1)S(1)}, bf16[672,384]{1,0:T(8,128)(2,1)S(1)}, u32[]{:S(2)}, u32[]{:S(2)}) collective-permute-start(bf16[672,384]{1,0:T(8,128)(2,1)S(1)} %get-tuple-element.62.refs_0_), channel_id=1, source_target_pairs={{0,384},{128,0},{256,128},{384,256},{1,385},{129,1},{257,129},{385... | collective-permute-start | bytes 1548296 | tf_op jit(solution)/shard_map/ppermute | solution.py:36
  165.8 14.0 %collective-permute-start.23 = (bf16[672,384]{1,0:T(8,128)(2,1)S(1)}, bf16[672,384]{1,0:T(8,128)(2,1)S(1)}, u32[]{:S(2)}, u32[]{:S(2)}) collective-permute-start(bf16[672,384]{1,0:T(8,128)(2,1)S(1)} %get-tuple-element.63.refs_6_), channel_id=1, source_target_pairs={{0,64},{64,0},{1,65},{65,1},{2,66},{66,2},{3,67},{67,3},{4,68},{68... | collective-permute-start | bytes 1548296 | tf_op jit(solution)/shard_map/ppermute | solution.py:36
  172.0 11.1 %collective-permute-start.21 = (bf16[672,384]{1,0:T(8,128)(2,1)S(1)}, bf16[672,384]{1,0:T(8,128)(2,1)}, u32[]{:S(2)}, u32[]{:S(2)}) collective-permute-start(bf16[672,384]{1,0:T(8,128)(2,1)S(1)} %collective-permute-done.18.refs_1_), channel_id=1, source_target_pairs={{0,128},{128,256},{256,384},{384,0},{1,129},{129,257},{257,385},{3... | collective-permute-start | bytes 1548296 | tf_op jit(solution)/shard_map/ppermute | solution.py:36
  174.2 12.8 %collective-permute-start.22 = (bf16[672,384]{1,0:T(8,128)(2,1)S(1)}, bf16[672,384]{1,0:T(8,128)(2,1)}, u32[]{:S(2)}, u32[]{:S(2)}) collective-permute-start(bf16[672,384]{1,0:T(8,128)(2,1)S(1)} %collective-permute-done.18.refs_1_), channel_id=1, source_target_pairs={{0,384},{128,0},{256,128},{384,256},{1,385},{129,1},{257,129},{385... | collective-permute-start | bytes 1548296 | tf_op jit(solution)/shard_map/ppermute | solution.py:36
  177.9 17.0 %copy-start.10 = (bf16[1,256,192]{1,2,0:T(8,128)(2,1)S(1)}, bf16[1,256,192]{1,2,0:T(8,128)(2,1)}, u32[]{:S(2)}) copy-start(bf16[1,256,192]{1,2,0:T(8,128)(2,1)} %param.10) | copy-start | bytes 294916
  177.9 17.0 %copy-start.12 = (bf16[192,256]{1,0:T(8,128)(2,1)S(1)}, bf16[192,256]{1,0:T(8,128)(2,1)}, u32[]{:S(2)}) copy-start(bf16[192,256]{1,0:T(8,128)(2,1)} %copy-done.11) | copy-start | bytes 294916
  177.9 17.1 %copy-start.14 = (bf16[192,256]{1,0:T(8,128)(2,1)S(1)}, bf16[192,256]{1,0:T(8,128)(2,1)}, u32[]{:S(2)}) copy-start(bf16[192,256]{1,0:T(8,128)(2,1)} %copy-done.13) | copy-start | bytes 294916
Sparse Core Ops, SparseCore 0:
  29.5 50.0 all-gather.4
  83.4 44.4 all-gather.6
  130.7 63.4 reduce-scatter.1

commit v6 on v5

--- a/solution.py
+++ b/solution.py
@@ -167,6 +167,7 @@
     high = value.astype(jnp.bfloat16).astype(jnp.float32)
     rows = lax.broadcasted_iota(jnp.int32, (2 * N_T, TOK), 0)
     block = jnp.where(rows == me, high, jnp.where(rows == me + N_T, value - high, 0.0)).astype(jnp.bfloat16)
+    first = lax.rem(me, 2) == 0
     for r in range(N_DP):
         for half in range(2):
             chunks[r, half, 2 * F :, :] = block
@@ -186,10 +187,13 @@
     copies = []
     for r in range(N_DP):
         into = jnp.dot(dg_t[...], w[r][: 2 * G, :], preferred_element_type=jnp.float32)
-        chunks[r, :, 0:F, :] = into.astype(jnp.bfloat16).T.reshape(2, F, TOK)
         part = jnp.dot(hid_t[...], w[r][2 * G :, :], preferred_element_type=jnp.float32)
-        chunks[r, :, F : 2 * F, :] = part.astype(jnp.bfloat16).T.reshape(2, F, TOK)
-        copies.append(pltpu.make_async_copy(chunks.at[r], out.at[pl.ds(2 * place[r], 2)], sems.at[r]))
+        for value, low in ((into, 0), (part, F)):
+            value = value.astype(jnp.bfloat16).T
+            one, two = value[:F], value[F:]
+            chunks[r, 0, low : low + F, :] = jnp.where(first, one, two)
+            chunks[r, 1, low : low + F, :] = jnp.where(first, two, one)
+        copies.append(pltpu.make_async_copy(chunks.at[r], out.at[place[r]], sems.at[r]))
         copies[r].start()
     for copy in copies:
         copy.wait()
@@ -220,6 +224,19 @@
         pairs += [(parts[r].at[:G, :], gate_out.at[:, lanes]), (parts[r].at[G:, :], up_out.at[:, lanes])]
     for copy in fetch(pairs, sems):
         copy.wait()
+
+
+def finish_kernel(summed, got, act, saved, dy, scales, gain, output, stored):
+    f32 = jnp.float32
+    scale = scales[0:1, :]
+
+    def rows(low, high):
+        return summed[0, low:high, :].astype(f32) + got[low:high, :].astype(f32)
+
+    mean = jnp.sum(rows(2 * F, 2 * F + 2 * N_T), axis=0, keepdims=True) / D
+    output[...] = (act[...].astype(f32) + rows(F, 2 * F)).astype(jnp.bfloat16)
+    hat = saved[...].astype(f32) * scale
+    stored[...] = (dy[...].astype(f32) + scale * (rows(0, F) * gain[...] - hat * mean)).astype(jnp.bfloat16)
 
 
 def params(mib):
@@ -306,7 +323,7 @@
         outer_kernel,
         in_specs=[SM] + [VM] * (N_DP + 6),
         out_specs=HB,
-        out_shape=jax.ShapeDtypeStruct((N_T, 2 * F + 2 * N_T, TOK), bf),
+        out_shape=jax.ShapeDtypeStruct((N_T // 2, 2, 2 * F + 2 * N_T, TOK), bf),
         scratch_shapes=[
             pltpu.VMEM((N_DP, 2, 2 * F + 2 * N_T, TOK), bf),
             pltpu.VMEM((G, TOK), bf),
@@ -318,7 +335,8 @@
         cost_estimate=cost(8 * D * G * TOK, 20 << 20),
         name="outer",
     )(place, *weights, dg, early_f, normal_f, weight_f, scales, stat)
-    summed = lax.psum_scatter(payload, ("y", "c"), scatter_dimension=0)
+    payload = after(payload, tuple(dgs_all[1:4]))
+    summed = lax.psum_scatter(payload, "y", scatter_dimension=0)
 
     near_grad, far_grad = pl.pallas_call(
         grad_kernel,
@@ -333,9 +351,11 @@
     behind = shift(near_grad, x=1)
     ahead = shift(near_grad, x=-1)
     z_far = shift(far_grad, zl=1)
+    got = shift(summed[1], c=1)
     z_behind = shift(z, x=1)
     z_ahead = shift(z, x=-1)
     parts = [near_grad, z, behind, ahead, z_behind, z_ahead, far_grad, z_far]
+    *parts, got = lax.optimization_barrier((*parts, got))
     grad_g, grad_u = pl.pallas_call(
         assemble_kernel,
         in_specs=[SM] + [VM] * N_DP,
@@ -347,13 +367,16 @@
         name="assemble",
     )(place, *parts)
 
-    into = summed[:F].astype(f32)
-    mean_stat = jnp.sum(summed[2 * F :].astype(f32), axis=0, keepdims=True) / D
     gain_here = lax.dynamic_slice_in_dim(gain, here * F, F)[:, None]
-    output = (acts_t.astype(f32) + summed[F : 2 * F].astype(f32)).astype(bf)
-    scale_b = scales[0:1]
-    hat = saved_t.astype(f32) * scale_b
-    stored = (dy_t.astype(f32) + scale_b * (into * gain_here - hat * mean_stat)).astype(bf)
+    output, stored = pl.pallas_call(
+        finish_kernel,
+        in_specs=[VM] * 7,
+        out_specs=[VM, VM],
+        out_shape=[jax.ShapeDtypeStruct((F, TOK), bf)] * 2,
+        compiler_params=params(8),
+        cost_estimate=cost(20 * F * TOK, 2 << 20),
+        name="finish",
+    )(summed, got, acts_t, saved_t, dy_t, scales, gain_here)
     return (output.T[None], stored.T[None], grad_g.T[None], grad_u.T[None])
 
 

time: 204 us -> 199 us (0.975)
  waiting for transfers between devices: 65 us -> 51.8 us
  local copies, waits for them, and re-layouts: 8.94 us -> 14.1 us
  other arithmetic: 5.18 us -> 2.72 us
  starting transfers between devices: 88.7 us -> 91.1 us
    ppermute x22 -> x23, waiting for transfers between devices: 47.1 us -> 31.5 us  [shift(): return lax.ppermute(value, axes if len(axes) > 1 else axes[0], pairs)]
    unnamed x34, local copies, waits for them, and re-layouts: 8.27 us -> 11.7 us
    ppermute x22 -> x23, starting transfers between devices: 73.2 us -> 75.6 us  [shift(): return lax.ppermute(value, axes if len(axes) > 1 else axes[0], pairs)]
    reduce_scatter x1, waiting for transfers between devices: 3.97 us -> 6.3 us  [local(): summed = lax.psum_scatter(payload, 'y', scatter_dimension=0)]
  transfers between devices with their start and end apart: 27 -> 28, of which waited for: 19 -> 17; matrix products, arithmetic and copies ran while one was open for 1% -> 2% of each run, Pallas kernels for 10% -> 9%
where the time goes in v6:
time: 199 us; the launch traced here: 197 us
  starting transfers between devices  91.1 us (46%)
  waiting for transfers between devices  51.8 us (26%)
  Pallas kernels  22.9 us (12%)
  between operations  14.2 us (7%)
  local copies, waits for them, and re-layouts  14.1 us (7%)
  other arithmetic  2.72 us (1%)
    ppermute x23, starting transfers between devices, shift(): return lax.ppermute(value, axes if len(axes) > 1 else axes[0], pairs)  75.6 us
    ppermute x23, waiting for transfers between devices, shift(): return lax.ppermute(value, axes if len(axes) > 1 else axes[0], pairs)  31.5 us
    ppermute x2, starting transfers between devices, swapped(): return lax.ppermute(value, ('x', 'zl', 'y'), pairs)  15.3 us
    ppermute x2, waiting for transfers between devices, swapped(): return lax.ppermute(value, ('x', 'zl', 'y'), pairs)  13.9 us
    unnamed x34, local copies, waits for them, and re-layouts  11.7 us
    reduce_scatter x1, waiting for transfers between devices, local(): summed = lax.psum_scatter(payload, 'y', scatter_dimension=0)  6.3 us
    pallas_call x1, Pallas kernels, local(): pl.pallas_call(outer_kernel, in_specs=[SM] + [VM] * (N_DP + 6), out_specs...  6.2 us
    pallas_call x1, Pallas kernels, local(): pl.pallas_call(early_kernel, in_specs=[SM] + [VM] * N_EARLY + [HB, VM], o...  5.67 us
  transfers between devices with their start and end apart: 28, of which 17 were waited for; matrix products, arithmetic and copies ran while one was open for 2% of the time, Pallas kernels for 9%

profile of v6, /device:TPU:6, one launch (start us, length us, event | category | flops | bytes accessed | tf_op | source)
XLA Modules:
  0.0 196.7 jit_solution(666270846051120453)
XLA Ops:
  7.2 10.9 %collective-permute-start.10 = (bf16[192,256]{1,0:T(8,128)(2,1)}, bf16[192,256]{1,0:T(8,128)(2,1)S(1)}, u32[]{:S(2)}, u32[]{:S(2)}) collective-permute-start(bf16[192,256]{1,0:T(8,128)(2,1)} %bitcast.62), channel_id=1, source_target_pairs={{0,48},{16,0},{32,16},{48,32},{1,49},{17,1},{33,17},{49,33},{2,50}... | collective-permute-start | bytes 294920 | tf_op jit(solution)/shard_map/ppermute | solution.py:36
  18.2 1.9 collective-permute-start.9
  20.1 1.3 pad_maximum_fusion.refs_0_
  22.7 5.9 %collective-permute-done.9.act = bf16[192,256]{1,0:T(8,128)(2,1)S(1)} collective-permute-done((bf16[192,256]{1,0:T(8,128)(2,1)}, bf16[192,256]{1,0:T(8,128)(2,1)S(1)}, u32[]{:S(2)}, u32[]{:S(2)}) %collective-permute-start.9) | collective-permute-done | bytes 98336 | tf_op jit(solution)/shard_map/ppermute | solution.py:36
  29.4 3.6 %collective-permute-start = (bf16[1008,384]{1,0:T(8,128)(2,1)S(1)}, bf16[1008,384]{1,0:T(8,128)(2,1)S(1)}, u32[]{:S(2)}, u32[]{:S(2)}) collective-permute-start(bf16[1008,384]{1,0:T(8,128)(2,1)S(1)} %pad_maximum_fusion.refs_0_), channel_id=1, source_target_pairs={{0,64},{64,0},{1,65},{65,1},{2,66},{66,2},{3,67},{67,3},{4,68},{68... | collective-permute-start | bytes 2322440 | tf_op jit(solution)/shard_map/ppermute | solution.py:36
  33.0 2.4 %collective-permute-start.1 = (bf16[1008,384]{1,0:T(8,128)(2,1)S(1)}, bf16[1008,384]{1,0:T(8,128)(2,1)}, u32[]{:S(2)}, u32[]{:S(2)}) collective-permute-start(bf16[1008,384]{1,0:T(8,128)(2,1)S(1)} %pad_maximum_fusion.refs_0_), channel_id=1, source_target_pairs={{0,128},{128,256},{256,384},{384,0},{1,129},{129,257},{257,385},{3... | collective-permute-start | bytes 2322440 | tf_op jit(solution)/shard_map/ppermute | solution.py:36
  35.4 3.5 %collective-permute-start.2 = (bf16[1008,384]{1,0:T(8,128)(2,1)S(1)}, bf16[1008,384]{1,0:T(8,128)(2,1)S(1)}, u32[]{:S(2)}, u32[]{:S(2)}) collective-permute-start(bf16[1008,384]{1,0:T(8,128)(2,1)S(1)} %pad_maximum_fusion.refs_0_), channel_id=1, source_target_pairs={{0,384},{128,0},{256,128},{384,256},{1,385},{129,1},{257,129},{385... | collective-permute-start | bytes 2322440 | tf_op jit(solution)/shard_map/ppermute | solution.py:36
  38.8 7.3 %collective-permute-start.3 = (bf16[192,256]{1,0:T(8,128)(2,1)S(1)}, bf16[192,256]{1,0:T(8,128)(2,1)S(1)}, u32[]{:S(2)}, u32[]{:S(2)}) collective-permute-start(bf16[192,256]{1,0:T(8,128)(2,1)S(1)} %bitcast.50), channel_id=1, source_target_pairs={{0,0},{2,64},{4,128},{6,192},{8,256},{10,320},{12,384},{14,448},{6... | collective-permute-start | bytes 294920 | tf_op jit(solution)/shard_map/ppermute | solution.py:45
  46.3 8.7 %collective-permute-done.3 = bf16[192,256]{1,0:T(8,128)(2,1)S(1)} collective-permute-done((bf16[192,256]{1,0:T(8,128)(2,1)S(1)}, bf16[192,256]{1,0:T(8,128)(2,1)S(1)}, u32[]{:S(2)}, u32[]{:S(2)}) %collective-permute-start.3) | collective-permute-done | bytes 98336 | tf_op jit(solution)/shard_map/ppermute | solution.py:45
  55.0 3.0 %collective-permute-done.2.refs_3_ = bf16[1008,384]{1,0:T(8,128)(2,1)S(1)} collective-permute-done((bf16[1008,384]{1,0:T(8,128)(2,1)S(1)}, bf16[1008,384]{1,0:T(8,128)(2,1)S(1)}, u32[]{:S(2)}, u32[]{:S(2)}) %collective-permute-start.2) | collective-permute-done | bytes 774176 | tf_op jit(solution)/shard_map/ppermute | solution.py:36
  58.8 1.9 collective-permute-start.4
  60.7 3.9 %collective-permute-start.5 = (bf16[1008,384]{1,0:T(8,128)(2,1)S(1)}, bf16[1008,384]{1,0:T(8,128)(2,1)}, u32[]{:S(2)}, u32[]{:S(2)}) collective-permute-start(bf16[1008,384]{1,0:T(8,128)(2,1)S(1)} %collective-permute-done.refs_1_), channel_id=1, source_target_pairs={{0,384},{128,0},{256,128},{384,256},{1,385},{129,1},{257,129},{385... | collective-permute-start | bytes 2322440 | tf_op jit(solution)/shard_map/ppermute | solution.py:36
  64.7 8.0 %collective-permute-start.6 = (bf16[192,256]{1,0:T(8,128)(2,1)S(1)}, bf16[192,256]{1,0:T(8,128)(2,1)S(1)}, u32[]{:S(2)}, u32[]{:S(2)}) collective-permute-start(bf16[192,256]{1,0:T(8,128)(2,1)S(1)} %bitcast.51), channel_id=1, source_target_pairs={{0,256},{2,320},{4,384},{6,448},{8,0},{10,64},{12,128},{14,192},{6... | collective-permute-start | bytes 294920 | tf_op jit(solution)/shard_map/ppermute | solution.py:45
  72.7 5.2 %collective-permute-done.6 = bf16[192,256]{1,0:T(8,128)(2,1)S(1)} collective-permute-done((bf16[192,256]{1,0:T(8,128)(2,1)S(1)}, bf16[192,256]{1,0:T(8,128)(2,1)S(1)}, u32[]{:S(2)}, u32[]{:S(2)}) %collective-permute-start.6) | collective-permute-done | bytes 98336 | tf_op jit(solution)/shard_map/ppermute | solution.py:45
  78.8 3.7 %collective-permute-done.5.refs_5_ = bf16[1008,384]{1,0:T(8,128)(2,1)} collective-permute-done((bf16[1008,384]{1,0:T(8,128)(2,1)S(1)}, bf16[1008,384]{1,0:T(8,128)(2,1)}, u32[]{:S(2)}, u32[]{:S(2)}) %collective-permute-start.5) | collective-permute-done | bytes 774176 | tf_op jit(solution)/shard_map/ppermute | solution.py:36
  83.2 1.9 collective-permute-start.7
  85.2 3.9 %collective-permute-start.8 = (bf16[1008,384]{1,0:T(8,128)(2,1)}, bf16[1008,384]{1,0:T(8,128)(2,1)}, u32[]{:S(2)}, u32[]{:S(2)}) collective-permute-start(bf16[1008,384]{1,0:T(8,128)(2,1)} %collective-permute-done.5.refs_5_), channel_id=1, source_target_pairs={{0,384},{128,0},{256,128},{384,256},{1,385},{129,1},{257,129},{385... | collective-permute-start | bytes 2322440 | tf_op jit(solution)/shard_map/ppermute | solution.py:36
  89.7 2.3 %copy-done = bf16[9216,256]{1,0:T(8,128)(2,1)S(1)} copy-done((bf16[9216,256]{1,0:T(8,128)(2,1)S(1)}, bf16[9216,256]{1,0:T(8,128)(2,1)}, u32[]{:S(2)}) %copy-start) | copy-done | bytes 4718616
  94.3 5.7 %early.1 = (f32[1008,256]{1,0:T(8,128)S(1)}, f32[672,256]{1,0:T(8,128)S(1)}, bf16[2,384,256]{2,1,0:T(8,128)(2,1)S(1)}, bf16[2,384,256]{2,1,0:T(8,128)(2,1)S(1)},...) custom-call(s32[9]{0:T(128)S(1)} %concatenate.13.place, bf16[1008,384]{1,0:T(8,128)(2,1)S(1)} %pad_maximum_fusion.refs_0_, ...), custom_call_target="tpu_custom_call" | custom-call | flops 2642411520 | bytes 29360128 | tf_op jit(solution)/shard_map/early/pallas_call | solution.py:284
  101.0 3.1 %collective-permute-done.8.w_7.refs_7_ = bf16[1008,384]{1,0:T(8,128)(2,1)} collective-permute-done((bf16[1008,384]{1,0:T(8,128)(2,1)}, bf16[1008,384]{1,0:T(8,128)(2,1)}, u32[]{:S(2)}, u32[]{:S(2)}) %collective-permute-start.8) | collective-permute-done | bytes 774176 | tf_op jit(solution)/shard_map/ppermute | solution.py:36
  104.1 2.4 %inner.1 = (bf16[672,256]{1,0:T(8,128)(2,1)S(1)}, bf16[672,256]{1,0:T(8,128)(2,1)S(1)}, f32[1,256]{1,0:T(1,128)S(1)}) custom-call(bf16[1008,384]{1,0:T(8,128)(2,1)} %collective-permute-done.7.w_6.refs_6_, bf16[1008,384]{1,0:T(8,128)(2,1)} %collective-permute-done.8.w_7.refs_7_, f32[1008,256]{1,0:T(8,128)S(1)} %get-tuple-element.56.early, ...), custom_call_target="tpu_custom_call" | custom-call | flops 528482304 | bytes 8388608 | tf_op jit(solution)/shard_map/inner/pallas_call | solution.py:308
  106.5 4.4 %collective-permute-start.11 = (bf16[672,256]{1,0:T(8,128)(2,1)S(1)}, bf16[672,256]{1,0:T(8,128)(2,1)S(1)}, u32[]{:S(2)}, u32[]{:S(2)}) collective-permute-start(bf16[672,256]{1,0:T(8,128)(2,1)S(1)} %get-tuple-element.66.refs_0_), channel_id=1, source_target_pairs={{0,64},{64,0},{1,65},{65,1},{2,66},{66,2},{3,67},{67,3},{4,68},{68... | collective-permute-start | bytes 1032200 | tf_op jit(solution)/shard_map/ppermute | solution.py:36
  111.0 3.7 %collective-permute-start.12 = (bf16[672,256]{1,0:T(8,128)(2,1)S(1)}, bf16[672,256]{1,0:T(8,128)(2,1)S(1)}, u32[]{:S(2)}, u32[]{:S(2)}) collective-permute-start(bf16[672,256]{1,0:T(8,128)(2,1)S(1)} %get-tuple-element.66.refs_0_), channel_id=1, source_target_pairs={{0,128},{128,256},{256,384},{384,0},{1,129},{129,257},{257,385},{3... | collective-permute-start | bytes 1032200 | tf_op jit(solution)/shard_map/ppermute | solution.py:36
  114.6 2.2 %collective-permute-start.13 = (bf16[672,256]{1,0:T(8,128)(2,1)S(1)}, bf16[672,256]{1,0:T(8,128)(2,1)S(1)}, u32[]{:S(2)}, u32[]{:S(2)}) collective-permute-start(bf16[672,256]{1,0:T(8,128)(2,1)S(1)} %get-tuple-element.66.refs_0_), channel_id=1, source_target_pairs={{0,384},{128,0},{256,128},{384,256},{1,385},{129,1},{257,129},{385... | collective-permute-start | bytes 1032200 | tf_op jit(solution)/shard_map/ppermute | solution.py:36
  116.8 6.2 %outer.1 = bf16[8,2,416,256]{3,2,1,0:T(8,128)(2,1)} custom-call(s32[9]{0:T(128)S(1)} %concatenate.13.place, bf16[1008,384]{1,0:T(8,128)(2,1)S(1)} %pad_maximum_fusion.refs_0_, bf16[1008,384]{1,0:T(8,128)(2,1)S(1)} %collective-permute-done.refs_1_, bf16[1008,384]{1,0:T(8,128)(2,1)} %collective-permute-done.1.refs_2_, bf16[1008,384]{1,0:T(8,128)(2,1)S(1)} %copy-done.3, ...), custom_call_target="tpu_custom_call" | custom-call | flops 2113929216 | bytes 20971520 | tf_op jit(solution)/shard_map/outer/pallas_call | solution.py:322
  123.1 2.3 %collective-permute-done.13.refs_3_ = bf16[672,256]{1,0:T(8,128)(2,1)S(1)} collective-permute-done((bf16[672,256]{1,0:T(8,128)(2,1)S(1)}, bf16[672,256]{1,0:T(8,128)(2,1)S(1)}, u32[]{:S(2)}, u32[]{:S(2)}) %collective-permute-start.13) | collective-permute-done | bytes 344096 | tf_op jit(solution)/shard_map/ppermute | solution.py:36
  126.1 1.9 collective-permute-start.15
  128.0 5.1 %collective-permute-start.14 = (bf16[672,256]{1,0:T(8,128)(2,1)S(1)}, bf16[672,256]{1,0:T(8,128)(2,1)S(1)}, u32[]{:S(2)}, u32[]{:S(2)}) collective-permute-start(bf16[672,256]{1,0:T(8,128)(2,1)S(1)} %collective-permute-done.11.refs_1_), channel_id=1, source_target_pairs={{0,128},{128,256},{256,384},{384,0},{1,129},{129,257},{257,385},{3... | collective-permute-start | bytes 1032200 | tf_op jit(solution)/shard_map/ppermute | solution.py:36
  133.2 1.9 collective-permute-start.16
  135.1 1.3 collective-permute-done.15.refs_5_
  136.5 2.8 %collective-permute-start.17 = (bf16[672,256]{1,0:T(8,128)(2,1)S(1)}, bf16[672,256]{1,0:T(8,128)(2,1)S(1)}, u32[]{:S(2)}, u32[]{:S(2)}) collective-permute-start(bf16[672,256]{1,0:T(8,128)(2,1)S(1)} %collective-permute-done.15.refs_5_), channel_id=1, source_target_pairs={{0,384},{128,0},{256,128},{384,256},{1,385},{129,1},{257,129},{385... | collective-permute-start | bytes 1032200 | tf_op jit(solution)/shard_map/ppermute | solution.py:36
  139.2 1.6 collective-permute-done.14.refs_4_
  140.9 3.7 %collective-permute-done.16.refs_6_ = bf16[672,256]{1,0:T(8,128)(2,1)S(1)} collective-permute-done((bf16[672,256]{1,0:T(8,128)(2,1)S(1)}, bf16[672,256]{1,0:T(8,128)(2,1)S(1)}, u32[]{:S(2)}, u32[]{:S(2)}) %collective-permute-start.16) | collective-permute-done | bytes 344096 | tf_op jit(solution)/shard_map/ppermute | solution.py:36
  145.3 1.5 collective-permute-done.17.refs_7_
  146.8 1.9 copy-done.10
  150.7 3.6 %grad.1 = (bf16[672,384]{1,0:T(8,128)(2,1)S(1)}, bf16[672,384]{1,0:T(8,128)(2,1)S(1)}) custom-call(s32[9]{0:T(128)S(1)} %concatenate.13.place, bf16[672,256]{1,0:T(8,128)(2,1)S(1)} %get-tuple-element.66.refs_0_, bf16[672,256]{1,0:T(8,128)(2,1)S(1)} %collective-permute-done.11.refs_1_, bf16[672,256]{1,0:T(8,128)(2,1)S(1)} %collective-permute-done.12.refs_2_, ...), custom_call_target="tpu_custom_call" | custom-call | flops 2113929216 | bytes 8388608 | tf_op jit(solution)/shard_map/grad/pallas_call | solution.py:341
  154.2 2.2 %collective-permute-start.18 = (bf16[672,384]{1,0:T(8,128)(2,1)S(1)}, bf16[672,384]{1,0:T(8,128)(2,1)S(1)}, u32[]{:S(2)}, u32[]{:S(2)}) collective-permute-start(bf16[672,384]{1,0:T(8,128)(2,1)S(1)} %get-tuple-element.80.refs_0_), channel_id=1, source_target_pairs={{0,64},{64,0},{1,65},{65,1},{2,66},{66,2},{3,67},{67,3},{4,68},{68... | collective-permute-start | bytes 1548296 | tf_op jit(solution)/shard_map/ppermute | solution.py:36
  156.4 4.3 %collective-permute-start.19 = (bf16[672,384]{1,0:T(8,128)(2,1)S(1)}, bf16[672,384]{1,0:T(8,128)(2,1)S(1)}, u32[]{:S(2)}, u32[]{:S(2)}) collective-permute-start(bf16[672,384]{1,0:T(8,128)(2,1)S(1)} %get-tuple-element.80.refs_0_), channel_id=1, source_target_pairs={{0,128},{128,256},{256,384},{384,0},{1,129},{129,257},{257,385},{3... | collective-permute-start | bytes 1548296 | tf_op jit(solution)/shard_map/ppermute | solution.py:36
  160.7 1.9 collective-permute-start.20
  162.7 3.5 %collective-permute-start.23 = (bf16[672,384]{1,0:T(8,128)(2,1)S(1)}, bf16[672,384]{1,0:T(8,128)(2,1)S(1)}, u32[]{:S(2)}, u32[]{:S(2)}) collective-permute-start(bf16[672,384]{1,0:T(8,128)(2,1)S(1)} %get-tuple-element.86.refs_6_), channel_id=1, source_target_pairs={{0,64},{64,0},{1,65},{65,1},{2,66},{66,2},{3,67},{67,3},{4,68},{68... | collective-permute-start | bytes 1548296 | tf_op jit(solution)/shard_map/ppermute | solution.py:36
  166.2 1.5 collective-permute-done.18.refs_1_
  167.7 3.8 %collective-permute-start.21 = (bf16[672,384]{1,0:T(8,128)(2,1)S(1)}, bf16[672,384]{1,0:T(8,128)(2,1)}, u32[]{:S(2)}, u32[]{:S(2)}) collective-permute-start(bf16[672,384]{1,0:T(8,128)(2,1)S(1)} %collective-permute-done.18.refs_1_), channel_id=1, source_target_pairs={{0,128},{128,256},{256,384},{384,0},{1,129},{129,257},{257,385},{3... | collective-permute-start | bytes 1548296 | tf_op jit(solution)/shard_map/ppermute | solution.py:36
  171.5 2.0 %collective-permute-start.22 = (bf16[672,384]{1,0:T(8,128)(2,1)S(1)}, bf16[672,384]{1,0:T(8,128)(2,1)}, u32[]{:S(2)}, u32[]{:S(2)}) collective-permute-start(bf16[672,384]{1,0:T(8,128)(2,1)S(1)} %collective-permute-done.18.refs_1_), channel_id=1, source_target_pairs={{0,384},{128,0},{256,128},{384,256},{1,385},{129,1},{257,129},{385... | collective-permute-start | bytes 1548296 | tf_op jit(solution)/shard_map/ppermute | solution.py:36
  173.5 6.3 %reduce-scatter.2.cloned.1.call-done = bf16[1,2,416,256]{3,2,1,0:T(8,128)(2,1)} async-done(((bf16[8,2,416,256]{3,2,1,0:T(8,128)(2,1)}), bf16[1,2,416,256]{3,2,1,0:T(8,128)(2,1)}) %reduce-scatter.2.cloned.1.call-update) | async-done | bytes 426000 | tf_op jit(solution)/shard_map/reduce_scatter | solution.py:339
  179.8 1.6 slice_bitcast_fusion
  181.4 1.9 collective-permute-start.24
  185.1 3.3 %assemble.1 = (bf16[336,3072]{1,0:T(8,128)(2,1)}, bf16[336,3072]{1,0:T(8,128)(2,1)}) custom-call(s32[9]{0:T(128)S(1)} %concatenate.13.place, bf16[672,384]{1,0:T(8,128)(2,1)S(1)} %get-tuple-element.80.refs_0_, bf16[672,384]{1,0:T(8,128)(2,1)S(1)} %collective-permute-done.18.refs_1_, bf16[672,384]{1,0:T(8,128)(2,1)S(1)} %collective-permute-done.19.refs_2_, ...), custom_call_target="tpu_custom_call" | custom-call | bytes 8388608 | tf_op jit(solution)/shard_map/assemble/pallas_call | solution.py:359
  188.5 1.7 finish.1
  (60 shorter events, 13.7 us)
Async XLA Ops:
  7.2 21.4 %copy-start.8 = (bf16[1,256,192]{1,2,0:T(8,128)(2,1)S(1)}, bf16[1,256,192]{1,2,0:T(8,128)(2,1)}, u32[]{:S(2)}) copy-start(bf16[1,256,192]{1,2,0:T(8,128)(2,1)} %param.10) | copy-start | bytes 294916
  7.2 39.1 %copy-start.15 = (f32[1,2,256,4]{2,3,1,0:T(4,128)S(1)}, f32[1,2,256,4]{2,3,1,0:T(4,128)}, u32[]{:S(2)}) copy-start(f32[1,2,256,4]{2,3,1,0:T(4,128)} %param.17) | copy-start | bytes 24580
  7.2 39.1 %copy-start.16 = (s32[1,2,256,4]{2,3,1,0:T(4,128)S(1)}, s32[1,2,256,4]{2,3,1,0:T(4,128)}, u32[]{:S(2)}) copy-start(s32[1,2,256,4]{2,3,1,0:T(4,128)} %param.16) | copy-start | bytes 24580
  7.2 82.5 %all-gather.5.cloned.1.call-start = ((), (), s32[]{:S(2)}) async-start(), calls=%async_computation.2 | async-start | bytes 5013504 | tf_op jit(solution)/shard_map/all_gather | solution.py:276
  7.2 15.4 %collective-permute-start.10 = (bf16[192,256]{1,0:T(8,128)(2,1)}, bf16[192,256]{1,0:T(8,128)(2,1)S(1)}, u32[]{:S(2)}, u32[]{:S(2)}) collective-permute-start(bf16[192,256]{1,0:T(8,128)(2,1)} %bitcast.62), channel_id=1, source_target_pairs={{0,48},{16,0},{32,16},{48,32},{1,49},{17,1},{33,17},{49,33},{2,50}... | collective-permute-start | bytes 294920 | tf_op jit(solution)/shard_map/ppermute | solution.py:36
  18.2 10.4 %collective-permute-start.9 = (bf16[192,256]{1,0:T(8,128)(2,1)}, bf16[192,256]{1,0:T(8,128)(2,1)S(1)}, u32[]{:S(2)}, u32[]{:S(2)}) collective-permute-start(bf16[192,256]{1,0:T(8,128)(2,1)} %bitcast.63), channel_id=1, source_target_pairs={{0,16},{16,32},{32,48},{48,0},{1,17},{17,33},{33,49},{49,1},{2,18}... | collective-permute-start | bytes 294920 | tf_op jit(solution)/shard_map/ppermute | solution.py:36
  20.1 69.0 %copy-start.9 = (f32[1,3072]{1,0:T(1,128)S(1)}, f32[1,3072]{1,0:T(1,128)}, u32[]{:S(2)}) copy-start(f32[1,3072]{1,0:T(1,128)} %refs_9_.1) | copy-start | bytes 36868
  29.4 105.8 %all-gather.7.cloned.1.call-start = ((), (), s32[]{:S(2)}) async-start(), calls=%async_computation.3 | async-start | bytes 3342336 | tf_op jit(solution)/shard_map/all_gather | solution.py:279
  29.4 25.6 %collective-permute-start = (bf16[1008,384]{1,0:T(8,128)(2,1)S(1)}, bf16[1008,384]{1,0:T(8,128)(2,1)S(1)}, u32[]{:S(2)}, u32[]{:S(2)}) collective-permute-start(bf16[1008,384]{1,0:T(8,128)(2,1)S(1)} %pad_maximum_fusion.refs_0_), channel_id=1, source_target_pairs={{0,64},{64,0},{1,65},{65,1},{2,66},{66,2},{3,67},{67,3},{4,68},{68... | collective-permute-start | bytes 2322440 | tf_op jit(solution)/shard_map/ppermute | solution.py:36
  33.0 22.0 %collective-permute-start.1 = (bf16[1008,384]{1,0:T(8,128)(2,1)S(1)}, bf16[1008,384]{1,0:T(8,128)(2,1)}, u32[]{:S(2)}, u32[]{:S(2)}) collective-permute-start(bf16[1008,384]{1,0:T(8,128)(2,1)S(1)} %pad_maximum_fusion.refs_0_), channel_id=1, source_target_pairs={{0,128},{128,256},{256,384},{384,0},{1,129},{129,257},{257,385},{3... | collective-permute-start | bytes 2322440 | tf_op jit(solution)/shard_map/ppermute | solution.py:36
  35.4 22.6 %collective-permute-start.2 = (bf16[1008,384]{1,0:T(8,128)(2,1)S(1)}, bf16[1008,384]{1,0:T(8,128)(2,1)S(1)}, u32[]{:S(2)}, u32[]{:S(2)}) collective-permute-start(bf16[1008,384]{1,0:T(8,128)(2,1)S(1)} %pad_maximum_fusion.refs_0_), channel_id=1, source_target_pairs={{0,384},{128,0},{256,128},{384,256},{1,385},{129,1},{257,129},{385... | collective-permute-start | bytes 2322440 | tf_op jit(solution)/shard_map/ppermute | solution.py:36
  38.8 16.2 %collective-permute-start.3 = (bf16[192,256]{1,0:T(8,128)(2,1)S(1)}, bf16[192,256]{1,0:T(8,128)(2,1)S(1)}, u32[]{:S(2)}, u32[]{:S(2)}) collective-permute-start(bf16[192,256]{1,0:T(8,128)(2,1)S(1)} %bitcast.50), channel_id=1, source_target_pairs={{0,0},{2,64},{4,128},{6,192},{8,256},{10,320},{12,384},{14,448},{6... | collective-permute-start | bytes 294920 | tf_op jit(solution)/shard_map/ppermute | solution.py:45
  57.9 0.9 copy-start.1
  58.8 19.1 %collective-permute-start.4 = (bf16[1008,384]{1,0:T(8,128)(2,1)S(1)}, bf16[1008,384]{1,0:T(8,128)(2,1)S(1)}, u32[]{:S(2)}, u32[]{:S(2)}) collective-permute-start(bf16[1008,384]{1,0:T(8,128)(2,1)S(1)} %collective-permute-done.refs_1_), channel_id=1, source_target_pairs={{0,128},{128,256},{256,384},{384,0},{1,129},{129,257},{257,385},{3... | collective-permute-start | bytes 2322440 | tf_op jit(solution)/shard_map/ppermute | solution.py:36
  60.7 21.8 %collective-permute-start.5 = (bf16[1008,384]{1,0:T(8,128)(2,1)S(1)}, bf16[1008,384]{1,0:T(8,128)(2,1)}, u32[]{:S(2)}, u32[]{:S(2)}) collective-permute-start(bf16[1008,384]{1,0:T(8,128)(2,1)S(1)} %collective-permute-done.refs_1_), channel_id=1, source_target_pairs={{0,384},{128,0},{256,128},{384,256},{1,385},{129,1},{257,129},{385... | collective-permute-start | bytes 2322440 | tf_op jit(solution)/shard_map/ppermute | solution.py:36
  64.7 13.3 %collective-permute-start.6 = (bf16[192,256]{1,0:T(8,128)(2,1)S(1)}, bf16[192,256]{1,0:T(8,128)(2,1)S(1)}, u32[]{:S(2)}, u32[]{:S(2)}) collective-permute-start(bf16[192,256]{1,0:T(8,128)(2,1)S(1)} %bitcast.51), channel_id=1, source_target_pairs={{0,256},{2,320},{4,384},{6,448},{8,0},{10,64},{12,128},{14,192},{6... | collective-permute-start | bytes 294920 | tf_op jit(solution)/shard_map/ppermute | solution.py:45
  78.0 0.9 copy-start.4
  83.2 96.6 %reduce-scatter.2.cloned.1.call-start = ((), (), s32[]{:S(2)}) async-start(), calls=%async_computation.1 | async-start | bytes 3833856 | tf_op jit(solution)/shard_map/reduce_scatter | solution.py:339
  83.2 17.7 %collective-permute-start.7 = (bf16[1008,384]{1,0:T(8,128)(2,1)}, bf16[1008,384]{1,0:T(8,128)(2,1)}, u32[]{:S(2)}, u32[]{:S(2)}) collective-permute-start(bf16[1008,384]{1,0:T(8,128)(2,1)} %collective-permute-done.1.refs_2_), channel_id=1, source_target_pairs={{0,128},{128,256},{256,384},{384,0},{1,129},{129,257},{257,385},{3... | collective-permute-start | bytes 2322440 | tf_op jit(solution)/shard_map/ppermute | solution.py:36
  85.2 18.9 %collective-permute-start.8 = (bf16[1008,384]{1,0:T(8,128)(2,1)}, bf16[1008,384]{1,0:T(8,128)(2,1)}, u32[]{:S(2)}, u32[]{:S(2)}) collective-permute-start(bf16[1008,384]{1,0:T(8,128)(2,1)} %collective-permute-done.5.refs_5_), channel_id=1, source_target_pairs={{0,384},{128,0},{256,128},{384,256},{1,385},{129,1},{257,129},{385... | collective-permute-start | bytes 2322440 | tf_op jit(solution)/shard_map/ppermute | solution.py:36
  89.7 2.3 %copy-start = (bf16[9216,256]{1,0:T(8,128)(2,1)S(1)}, bf16[9216,256]{1,0:T(8,128)(2,1)}, u32[]{:S(2)}) copy-start(bf16[9216,256]{1,0:T(8,128)(2,1)} %all-gather.5.cloned.1.call-done) | copy-start | bytes 14155780
  92.0 1.1 copy-start.2
  93.1 1.1 copy-start.5
  104.1 12.7 %copy-start.3 = (bf16[1008,384]{1,0:T(8,128)(2,1)S(1)}, bf16[1008,384]{1,0:T(8,128)(2,1)}, u32[]{:S(2)}) copy-start(bf16[1008,384]{1,0:T(8,128)(2,1)} %copy-done.1) | copy-start | bytes 2322436
  104.1 12.7 %copy-start.6 = (bf16[1008,384]{1,0:T(8,128)(2,1)S(1)}, bf16[1008,384]{1,0:T(8,128)(2,1)}, u32[]{:S(2)}) copy-start(bf16[1008,384]{1,0:T(8,128)(2,1)} %copy-done.4) | copy-start | bytes 2322436
  106.5 16.5 %collective-permute-start.11 = (bf16[672,256]{1,0:T(8,128)(2,1)S(1)}, bf16[672,256]{1,0:T(8,128)(2,1)S(1)}, u32[]{:S(2)}, u32[]{:S(2)}) collective-permute-start(bf16[672,256]{1,0:T(8,128)(2,1)S(1)} %get-tuple-element.66.refs_0_), channel_id=1, source_target_pairs={{0,64},{64,0},{1,65},{65,1},{2,66},{66,2},{3,67},{67,3},{4,68},{68... | collective-permute-start | bytes 1032200 | tf_op jit(solution)/shard_map/ppermute | solution.py:36
  111.0 12.1 %collective-permute-start.12 = (bf16[672,256]{1,0:T(8,128)(2,1)S(1)}, bf16[672,256]{1,0:T(8,128)(2,1)S(1)}, u32[]{:S(2)}, u32[]{:S(2)}) collective-permute-start(bf16[672,256]{1,0:T(8,128)(2,1)S(1)} %get-tuple-element.66.refs_0_), channel_id=1, source_target_pairs={{0,128},{128,256},{256,384},{384,0},{1,129},{129,257},{257,385},{3... | collective-permute-start | bytes 1032200 | tf_op jit(solution)/shard_map/ppermute | solution.py:36
  114.6 10.7 %collective-permute-start.13 = (bf16[672,256]{1,0:T(8,128)(2,1)S(1)}, bf16[672,256]{1,0:T(8,128)(2,1)S(1)}, u32[]{:S(2)}, u32[]{:S(2)}) collective-permute-start(bf16[672,256]{1,0:T(8,128)(2,1)S(1)} %get-tuple-element.66.refs_0_), channel_id=1, source_target_pairs={{0,384},{128,0},{256,128},{384,256},{1,385},{129,1},{257,129},{385... | collective-permute-start | bytes 1032200 | tf_op jit(solution)/shard_map/ppermute | solution.py:36
  125.4 0.7 copy-start.11
  126.1 10.3 %collective-permute-start.15 = (bf16[672,256]{1,0:T(8,128)(2,1)S(1)}, bf16[672,256]{1,0:T(8,128)(2,1)S(1)}, u32[]{:S(2)}, u32[]{:S(2)}) collective-permute-start(bf16[672,256]{1,0:T(8,128)(2,1)S(1)} %collective-permute-done.11.refs_1_), channel_id=1, source_target_pairs={{0,384},{128,0},{256,128},{384,256},{1,385},{129,1},{257,129},{385... | collective-permute-start | bytes 1032200 | tf_op jit(solution)/shard_map/ppermute | solution.py:36
  128.0 12.9 %collective-permute-start.14 = (bf16[672,256]{1,0:T(8,128)(2,1)S(1)}, bf16[672,256]{1,0:T(8,128)(2,1)S(1)}, u32[]{:S(2)}, u32[]{:S(2)}) collective-permute-start(bf16[672,256]{1,0:T(8,128)(2,1)S(1)} %collective-permute-done.11.refs_1_), channel_id=1, source_target_pairs={{0,128},{128,256},{256,384},{384,0},{1,129},{129,257},{257,385},{3... | collective-permute-start | bytes 1032200 | tf_op jit(solution)/shard_map/ppermute | solution.py:36
  133.2 11.4 %collective-permute-start.16 = (bf16[672,256]{1,0:T(8,128)(2,1)S(1)}, bf16[672,256]{1,0:T(8,128)(2,1)S(1)}, u32[]{:S(2)}, u32[]{:S(2)}) collective-permute-start(bf16[672,256]{1,0:T(8,128)(2,1)S(1)} %collective-permute-done.12.refs_2_), channel_id=1, source_target_pairs={{0,128},{128,256},{256,384},{384,0},{1,129},{129,257},{257,385},{3... | collective-permute-start | bytes 1032200 | tf_op jit(solution)/shard_map/ppermute | solution.py:36
  136.5 10.3 %collective-permute-start.17 = (bf16[672,256]{1,0:T(8,128)(2,1)S(1)}, bf16[672,256]{1,0:T(8,128)(2,1)S(1)}, u32[]{:S(2)}, u32[]{:S(2)}) collective-permute-start(bf16[672,256]{1,0:T(8,128)(2,1)S(1)} %collective-permute-done.15.refs_5_), channel_id=1, source_target_pairs={{0,384},{128,0},{256,128},{384,256},{1,385},{129,1},{257,129},{385... | collective-permute-start | bytes 1032200 | tf_op jit(solution)/shard_map/ppermute | solution.py:36
  144.6 0.7 copy-start.13
  146.8 1.9 copy-start.10
  148.7 1.0 copy-start.12
  149.7 1.0 copy-start.14
  154.2 13.4 %collective-permute-start.18 = (bf16[672,384]{1,0:T(8,128)(2,1)S(1)}, bf16[672,384]{1,0:T(8,128)(2,1)S(1)}, u32[]{:S(2)}, u32[]{:S(2)}) collective-permute-start(bf16[672,384]{1,0:T(8,128)(2,1)S(1)} %get-tuple-element.80.refs_0_), channel_id=1, source_target_pairs={{0,64},{64,0},{1,65},{65,1},{2,66},{66,2},{3,67},{67,3},{4,68},{68... | collective-permute-start | bytes 1548296 | tf_op jit(solution)/shard_map/ppermute | solution.py:36
  156.4 25.0 %collective-permute-start.19 = (bf16[672,384]{1,0:T(8,128)(2,1)S(1)}, bf16[672,384]{1,0:T(8,128)(2,1)S(1)}, u32[]{:S(2)}, u32[]{:S(2)}) collective-permute-start(bf16[672,384]{1,0:T(8,128)(2,1)S(1)} %get-tuple-element.80.refs_0_), channel_id=1, source_target_pairs={{0,128},{128,256},{256,384},{384,0},{1,129},{129,257},{257,385},{3... | collective-permute-start | bytes 1548296 | tf_op jit(solution)/shard_map/ppermute | solution.py:36
  160.7 22.9 %collective-permute-start.20 = (bf16[672,384]{1,0:T(8,128)(2,1)S(1)}, bf16[672,384]{1,0:T(8,128)(2,1)S(1)}, u32[]{:S(2)}, u32[]{:S(2)}) collective-permute-start(bf16[672,384]{1,0:T(8,128)(2,1)S(1)} %get-tuple-element.80.refs_0_), channel_id=1, source_target_pairs={{0,384},{128,0},{256,128},{384,256},{1,385},{129,1},{257,129},{385... | collective-permute-start | bytes 1548296 | tf_op jit(solution)/shard_map/ppermute | solution.py:36
  162.7 20.9 %collective-permute-start.23 = (bf16[672,384]{1,0:T(8,128)(2,1)S(1)}, bf16[672,384]{1,0:T(8,128)(2,1)S(1)}, u32[]{:S(2)}, u32[]{:S(2)}) collective-permute-start(bf16[672,384]{1,0:T(8,128)(2,1)S(1)} %get-tuple-element.86.refs_6_), channel_id=1, source_target_pairs={{0,64},{64,0},{1,65},{65,1},{2,66},{66,2},{3,67},{67,3},{4,68},{68... | collective-permute-start | bytes 1548296 | tf_op jit(solution)/shard_map/ppermute | solution.py:36
  167.7 15.9 %collective-permute-start.21 = (bf16[672,384]{1,0:T(8,128)(2,1)S(1)}, bf16[672,384]{1,0:T(8,128)(2,1)}, u32[]{:S(2)}, u32[]{:S(2)}) collective-permute-start(bf16[672,384]{1,0:T(8,128)(2,1)S(1)} %collective-permute-done.18.refs_1_), channel_id=1, source_target_pairs={{0,128},{128,256},{256,384},{384,0},{1,129},{129,257},{257,385},{3... | collective-permute-start | bytes 1548296 | tf_op jit(solution)/shard_map/ppermute | solution.py:36
  171.5 12.7 %collective-permute-start.22 = (bf16[672,384]{1,0:T(8,128)(2,1)S(1)}, bf16[672,384]{1,0:T(8,128)(2,1)}, u32[]{:S(2)}, u32[]{:S(2)}) collective-permute-start(bf16[672,384]{1,0:T(8,128)(2,1)S(1)} %collective-permute-done.18.refs_1_), channel_id=1, source_target_pairs={{0,384},{128,0},{256,128},{384,256},{1,385},{129,1},{257,129},{385... | collective-permute-start | bytes 1548296 | tf_op jit(solution)/shard_map/ppermute | solution.py:36
  181.4 3.7 %collective-permute-start.24 = (bf16[416,256]{1,0:T(8,128)(2,1)}, bf16[416,256]{1,0:T(8,128)(2,1)}, u32[]{:S(2)}, u32[]{:S(2)}) collective-permute-start(bf16[416,256]{1,0:T(8,128)(2,1)} %slice_bitcast_fusion), channel_id=1, source_target_pairs={{0,1},{1,0},{2,3},{3,2},{4,5},{5,4},{6,7},{7,6},{8,9},{9,8},{10,11... | collective-permute-start | bytes 638984 | tf_op jit(solution)/shard_map/ppermute | solution.py:36
  183.6 4.9 %copy-start.7 = (bf16[1,2,416,256]{3,2,1,0:T(8,128)(2,1)S(1)}, bf16[1,2,416,256]{3,2,1,0:T(8,128)(2,1)}, u32[]{:S(2)}) copy-start(bf16[1,2,416,256]{3,2,1,0:T(8,128)(2,1)} %reduce-scatter.2.cloned.1.call-done) | copy-start | bytes 1277956
Sparse Core Ops, SparseCore 0:
  29.5 50.3 all-gather.4
  83.3 44.4 all-gather.6
  130.7 49.0 reduce-scatter.1

commit v7 on v6

--- a/solution.py
+++ b/solution.py
@@ -231,7 +231,7 @@
     scale = scales[0:1, :]
 
     def rows(low, high):
-        return summed[0, low:high, :].astype(f32) + got[low:high, :].astype(f32)
+        return summed[0, low:high, :].astype(f32) + got[1, low:high, :].astype(f32)
 
     mean = jnp.sum(rows(2 * F, 2 * F + 2 * N_T), axis=0, keepdims=True) / D
     output[...] = (act[...].astype(f32) + rows(F, 2 * F)).astype(jnp.bfloat16)
@@ -351,11 +351,10 @@
     behind = shift(near_grad, x=1)
     ahead = shift(near_grad, x=-1)
     z_far = shift(far_grad, zl=1)
-    got = shift(summed[1], c=1)
+    got = shift(summed, c=1)
     z_behind = shift(z, x=1)
     z_ahead = shift(z, x=-1)
     parts = [near_grad, z, behind, ahead, z_behind, z_ahead, far_grad, z_far]
-    *parts, got = lax.optimization_barrier((*parts, got))
     grad_g, grad_u = pl.pallas_call(
         assemble_kernel,
         in_specs=[SM] + [VM] * N_DP,

time: 199 us -> 196 us (0.985)
  local copies, waits for them, and re-layouts: 14.1 us -> 9.72 us
  waiting for transfers between devices: 51.8 us -> 54.1 us
    unnamed x34 -> x38, local copies, waits for them, and re-layouts: 11.7 us -> 8.28 us
  transfers between devices with their start and end apart: 28 -> 28, of which waited for: 17 -> 15; matrix products, arithmetic and copies ran while one was open for 2% -> 2% of each run, Pallas kernels for 9% -> 11%
where the time goes in v7:
time: 196 us; the launch traced here: 193 us
  starting transfers between devices  90.6 us (46%)
  waiting for transfers between devices  54.1 us (28%)
  Pallas kernels  22 us (11%)
  between operations  14.3 us (7%)
  local copies, waits for them, and re-layouts  9.72 us (5%)
  other arithmetic  2.73 us (1%)
    ppermute x23, starting transfers between devices, shift(): return lax.ppermute(value, axes if len(axes) > 1 else axes[0], pairs)  75.2 us
    ppermute x23, waiting for transfers between devices, shift(): return lax.ppermute(value, axes if len(axes) > 1 else axes[0], pairs)  32.2 us
    ppermute x2, starting transfers between devices, swapped(): return lax.ppermute(value, ('x', 'zl', 'y'), pairs)  15.3 us
    ppermute x2, waiting for transfers between devices, swapped(): return lax.ppermute(value, ('x', 'zl', 'y'), pairs)  13.9 us
    unnamed x38, local copies, waits for them, and re-layouts  8.28 us
    reduce_scatter x1, waiting for transfers between devices, local(): summed = lax.psum_scatter(payload, 'y', scatter_dimension=0)  7.93 us
    pallas_call x1, Pallas kernels, local(): pl.pallas_call(outer_kernel, in_specs=[SM] + [VM] * (N_DP + 6), out_specs...  6.17 us
    pallas_call x1, Pallas kernels, local(): pl.pallas_call(early_kernel, in_specs=[SM] + [VM] * N_EARLY + [HB, VM], o...  5.67 us
  transfers between devices with their start and end apart: 28, of which 15 were waited for; matrix products, arithmetic and copies ran while one was open for 2% of the time, Pallas kernels for 11%

profile of v7, /device:TPU:6, one launch (start us, length us, event | category | flops | bytes accessed | tf_op | source)
XLA Modules:
  0.0 193.5 jit_solution(3897714953981983032)
XLA Ops:
  7.2 10.9 %collective-permute-start.10 = (bf16[192,256]{1,0:T(8,128)(2,1)}, bf16[192,256]{1,0:T(8,128)(2,1)S(1)}, u32[]{:S(2)}, u32[]{:S(2)}) collective-permute-start(bf16[192,256]{1,0:T(8,128)(2,1)} %bitcast.61), channel_id=1, source_target_pairs={{0,48},{16,0},{32,16},{48,32},{1,49},{17,1},{33,17},{49,33},{2,50}... | collective-permute-start | bytes 294920 | tf_op jit(solution)/shard_map/ppermute | solution.py:36
  18.2 1.9 collective-permute-start.9
  20.1 1.3 pad_maximum_fusion.refs_0_
  21.4 1.3 collective-permute-done.10.dy
  22.7 5.9 %collective-permute-done.9.act = bf16[192,256]{1,0:T(8,128)(2,1)S(1)} collective-permute-done((bf16[192,256]{1,0:T(8,128)(2,1)}, bf16[192,256]{1,0:T(8,128)(2,1)S(1)}, u32[]{:S(2)}, u32[]{:S(2)}) %collective-permute-start.9) | collective-permute-done | bytes 98336 | tf_op jit(solution)/shard_map/ppermute | solution.py:36
  29.4 3.6 %collective-permute-start = (bf16[1008,384]{1,0:T(8,128)(2,1)S(1)}, bf16[1008,384]{1,0:T(8,128)(2,1)S(1)}, u32[]{:S(2)}, u32[]{:S(2)}) collective-permute-start(bf16[1008,384]{1,0:T(8,128)(2,1)S(1)} %pad_maximum_fusion.refs_0_), channel_id=1, source_target_pairs={{0,64},{64,0},{1,65},{65,1},{2,66},{66,2},{3,67},{67,3},{4,68},{68... | collective-permute-start | bytes 2322440 | tf_op jit(solution)/shard_map/ppermute | solution.py:36
  33.0 2.4 %collective-permute-start.1 = (bf16[1008,384]{1,0:T(8,128)(2,1)S(1)}, bf16[1008,384]{1,0:T(8,128)(2,1)}, u32[]{:S(2)}, u32[]{:S(2)}) collective-permute-start(bf16[1008,384]{1,0:T(8,128)(2,1)S(1)} %pad_maximum_fusion.refs_0_), channel_id=1, source_target_pairs={{0,128},{128,256},{256,384},{384,0},{1,129},{129,257},{257,385},{3... | collective-permute-start | bytes 2322440 | tf_op jit(solution)/shard_map/ppermute | solution.py:36
  35.4 3.5 %collective-permute-start.2 = (bf16[1008,384]{1,0:T(8,128)(2,1)S(1)}, bf16[1008,384]{1,0:T(8,128)(2,1)S(1)}, u32[]{:S(2)}, u32[]{:S(2)}) collective-permute-start(bf16[1008,384]{1,0:T(8,128)(2,1)S(1)} %pad_maximum_fusion.refs_0_), channel_id=1, source_target_pairs={{0,384},{128,0},{256,128},{384,256},{1,385},{129,1},{257,129},{385... | collective-permute-start | bytes 2322440 | tf_op jit(solution)/shard_map/ppermute | solution.py:36
  38.8 7.3 %collective-permute-start.3 = (bf16[192,256]{1,0:T(8,128)(2,1)S(1)}, bf16[192,256]{1,0:T(8,128)(2,1)S(1)}, u32[]{:S(2)}, u32[]{:S(2)}) collective-permute-start(bf16[192,256]{1,0:T(8,128)(2,1)S(1)} %bitcast.49), channel_id=1, source_target_pairs={{0,0},{2,64},{4,128},{6,192},{8,256},{10,320},{12,384},{14,448},{6... | collective-permute-start | bytes 294920 | tf_op jit(solution)/shard_map/ppermute | solution.py:45
  46.3 8.7 %collective-permute-done.3 = bf16[192,256]{1,0:T(8,128)(2,1)S(1)} collective-permute-done((bf16[192,256]{1,0:T(8,128)(2,1)S(1)}, bf16[192,256]{1,0:T(8,128)(2,1)S(1)}, u32[]{:S(2)}, u32[]{:S(2)}) %collective-permute-start.3) | collective-permute-done | bytes 98336 | tf_op jit(solution)/shard_map/ppermute | solution.py:45
  55.0 3.0 %collective-permute-done.2.refs_3_ = bf16[1008,384]{1,0:T(8,128)(2,1)S(1)} collective-permute-done((bf16[1008,384]{1,0:T(8,128)(2,1)S(1)}, bf16[1008,384]{1,0:T(8,128)(2,1)S(1)}, u32[]{:S(2)}, u32[]{:S(2)}) %collective-permute-start.2) | collective-permute-done | bytes 774176 | tf_op jit(solution)/shard_map/ppermute | solution.py:36
  58.8 1.9 collective-permute-start.4
  60.8 3.9 %collective-permute-start.5 = (bf16[1008,384]{1,0:T(8,128)(2,1)S(1)}, bf16[1008,384]{1,0:T(8,128)(2,1)}, u32[]{:S(2)}, u32[]{:S(2)}) collective-permute-start(bf16[1008,384]{1,0:T(8,128)(2,1)S(1)} %collective-permute-done.refs_1_), channel_id=1, source_target_pairs={{0,384},{128,0},{256,128},{384,256},{1,385},{129,1},{257,129},{385... | collective-permute-start | bytes 2322440 | tf_op jit(solution)/shard_map/ppermute | solution.py:36
  64.7 8.0 %collective-permute-start.6 = (bf16[192,256]{1,0:T(8,128)(2,1)S(1)}, bf16[192,256]{1,0:T(8,128)(2,1)S(1)}, u32[]{:S(2)}, u32[]{:S(2)}) collective-permute-start(bf16[192,256]{1,0:T(8,128)(2,1)S(1)} %bitcast.50), channel_id=1, source_target_pairs={{0,256},{2,320},{4,384},{6,448},{8,0},{10,64},{12,128},{14,192},{6... | collective-permute-start | bytes 294920 | tf_op jit(solution)/shard_map/ppermute | solution.py:45
  72.7 5.2 %collective-permute-done.6 = bf16[192,256]{1,0:T(8,128)(2,1)S(1)} collective-permute-done((bf16[192,256]{1,0:T(8,128)(2,1)S(1)}, bf16[192,256]{1,0:T(8,128)(2,1)S(1)}, u32[]{:S(2)}, u32[]{:S(2)}) %collective-permute-start.6) | collective-permute-done | bytes 98336 | tf_op jit(solution)/shard_map/ppermute | solution.py:45
  78.8 3.7 %collective-permute-done.5.refs_5_ = bf16[1008,384]{1,0:T(8,128)(2,1)} collective-permute-done((bf16[1008,384]{1,0:T(8,128)(2,1)S(1)}, bf16[1008,384]{1,0:T(8,128)(2,1)}, u32[]{:S(2)}, u32[]{:S(2)}) %collective-permute-start.5) | collective-permute-done | bytes 774176 | tf_op jit(solution)/shard_map/ppermute | solution.py:36
  83.3 1.9 collective-permute-start.7
  85.2 3.9 %collective-permute-start.8 = (bf16[1008,384]{1,0:T(8,128)(2,1)}, bf16[1008,384]{1,0:T(8,128)(2,1)}, u32[]{:S(2)}, u32[]{:S(2)}) collective-permute-start(bf16[1008,384]{1,0:T(8,128)(2,1)} %collective-permute-done.5.refs_5_), channel_id=1, source_target_pairs={{0,384},{128,0},{256,128},{384,256},{1,385},{129,1},{257,129},{385... | collective-permute-start | bytes 2322440 | tf_op jit(solution)/shard_map/ppermute | solution.py:36
  89.7 2.3 %copy-done = bf16[9216,256]{1,0:T(8,128)(2,1)S(1)} copy-done((bf16[9216,256]{1,0:T(8,128)(2,1)S(1)}, bf16[9216,256]{1,0:T(8,128)(2,1)}, u32[]{:S(2)}) %copy-start) | copy-done | bytes 4718616
  92.0 1.1 copy-done.2
  94.3 5.7 %early.1 = (f32[1008,256]{1,0:T(8,128)S(1)}, f32[672,256]{1,0:T(8,128)S(1)}, bf16[2,384,256]{2,1,0:T(8,128)(2,1)S(1)}, bf16[2,384,256]{2,1,0:T(8,128)(2,1)S(1)},...) custom-call(s32[9]{0:T(128)S(1)} %concatenate.13.place, bf16[1008,384]{1,0:T(8,128)(2,1)S(1)} %pad_maximum_fusion.refs_0_, ...), custom_call_target="tpu_custom_call" | custom-call | flops 2642411520 | bytes 29360128 | tf_op jit(solution)/shard_map/early/pallas_call | solution.py:284
  101.0 3.1 %collective-permute-done.8.w_7.refs_7_ = bf16[1008,384]{1,0:T(8,128)(2,1)} collective-permute-done((bf16[1008,384]{1,0:T(8,128)(2,1)}, bf16[1008,384]{1,0:T(8,128)(2,1)}, u32[]{:S(2)}, u32[]{:S(2)}) %collective-permute-start.8) | collective-permute-done | bytes 774176 | tf_op jit(solution)/shard_map/ppermute | solution.py:36
  104.2 2.4 %inner.1 = (bf16[672,256]{1,0:T(8,128)(2,1)S(1)}, bf16[672,256]{1,0:T(8,128)(2,1)S(1)}, f32[1,256]{1,0:T(1,128)S(1)}) custom-call(bf16[1008,384]{1,0:T(8,128)(2,1)} %collective-permute-done.7.w_6.refs_6_, bf16[1008,384]{1,0:T(8,128)(2,1)} %collective-permute-done.8.w_7.refs_7_, f32[1008,256]{1,0:T(8,128)S(1)} %get-tuple-element.47.early, ...), custom_call_target="tpu_custom_call" | custom-call | flops 528482304 | bytes 8388608 | tf_op jit(solution)/shard_map/inner/pallas_call | solution.py:308
  106.6 4.4 %collective-permute-start.11 = (bf16[672,256]{1,0:T(8,128)(2,1)S(1)}, bf16[672,256]{1,0:T(8,128)(2,1)S(1)}, u32[]{:S(2)}, u32[]{:S(2)}) collective-permute-start(bf16[672,256]{1,0:T(8,128)(2,1)S(1)} %get-tuple-element.57.refs_0_), channel_id=1, source_target_pairs={{0,64},{64,0},{1,65},{65,1},{2,66},{66,2},{3,67},{67,3},{4,68},{68... | collective-permute-start | bytes 1032200 | tf_op jit(solution)/shard_map/ppermute | solution.py:36
  111.0 3.7 %collective-permute-start.12 = (bf16[672,256]{1,0:T(8,128)(2,1)S(1)}, bf16[672,256]{1,0:T(8,128)(2,1)S(1)}, u32[]{:S(2)}, u32[]{:S(2)}) collective-permute-start(bf16[672,256]{1,0:T(8,128)(2,1)S(1)} %get-tuple-element.57.refs_0_), channel_id=1, source_target_pairs={{0,128},{128,256},{256,384},{384,0},{1,129},{129,257},{257,385},{3... | collective-permute-start | bytes 1032200 | tf_op jit(solution)/shard_map/ppermute | solution.py:36
  114.7 2.2 %collective-permute-start.13 = (bf16[672,256]{1,0:T(8,128)(2,1)S(1)}, bf16[672,256]{1,0:T(8,128)(2,1)S(1)}, u32[]{:S(2)}, u32[]{:S(2)}) collective-permute-start(bf16[672,256]{1,0:T(8,128)(2,1)S(1)} %get-tuple-element.57.refs_0_), channel_id=1, source_target_pairs={{0,384},{128,0},{256,128},{384,256},{1,385},{129,1},{257,129},{385... | collective-permute-start | bytes 1032200 | tf_op jit(solution)/shard_map/ppermute | solution.py:36
  116.9 6.2 %outer.1 = bf16[8,2,416,256]{3,2,1,0:T(8,128)(2,1)} custom-call(s32[9]{0:T(128)S(1)} %concatenate.13.place, bf16[1008,384]{1,0:T(8,128)(2,1)S(1)} %pad_maximum_fusion.refs_0_, bf16[1008,384]{1,0:T(8,128)(2,1)S(1)} %collective-permute-done.refs_1_, bf16[1008,384]{1,0:T(8,128)(2,1)} %collective-permute-done.1.refs_2_, bf16[1008,384]{1,0:T(8,128)(2,1)S(1)} %copy-done.3, ...), custom_call_target="tpu_custom_call" | custom-call | flops 2113929216 | bytes 20971520 | tf_op jit(solution)/shard_map/outer/pallas_call | solution.py:322
  123.1 2.3 %collective-permute-done.13.refs_3_ = bf16[672,256]{1,0:T(8,128)(2,1)S(1)} collective-permute-done((bf16[672,256]{1,0:T(8,128)(2,1)S(1)}, bf16[672,256]{1,0:T(8,128)(2,1)S(1)}, u32[]{:S(2)}, u32[]{:S(2)}) %collective-permute-start.13) | collective-permute-done | bytes 344096 | tf_op jit(solution)/shard_map/ppermute | solution.py:36
  125.4 1.9 collective-permute-start.16
  127.4 5.1 %collective-permute-start.15 = (bf16[672,256]{1,0:T(8,128)(2,1)S(1)}, bf16[672,256]{1,0:T(8,128)(2,1)S(1)}, u32[]{:S(2)}, u32[]{:S(2)}) collective-permute-start(bf16[672,256]{1,0:T(8,128)(2,1)S(1)} %collective-permute-done.11.refs_1_), channel_id=1, source_target_pairs={{0,128},{128,256},{256,384},{384,0},{1,129},{129,257},{257,385},{3... | collective-permute-start | bytes 1032200 | tf_op jit(solution)/shard_map/ppermute | solution.py:36
  132.5 1.9 collective-permute-start.17
  134.5 1.3 collective-permute-done.16.refs_5_
  135.8 2.6 %collective-permute-start.18 = (bf16[672,256]{1,0:T(8,128)(2,1)S(1)}, bf16[672,256]{1,0:T(8,128)(2,1)S(1)}, u32[]{:S(2)}, u32[]{:S(2)}) collective-permute-start(bf16[672,256]{1,0:T(8,128)(2,1)S(1)} %collective-permute-done.16.refs_5_), channel_id=1, source_target_pairs={{0,384},{128,0},{256,128},{384,256},{1,385},{129,1},{257,129},{385... | collective-permute-start | bytes 1032200 | tf_op jit(solution)/shard_map/ppermute | solution.py:36
  138.4 1.8 collective-permute-done.15.refs_4_
  140.2 3.7 %collective-permute-done.17.refs_6_ = bf16[672,256]{1,0:T(8,128)(2,1)S(1)} collective-permute-done((bf16[672,256]{1,0:T(8,128)(2,1)S(1)}, bf16[672,256]{1,0:T(8,128)(2,1)S(1)}, u32[]{:S(2)}, u32[]{:S(2)}) %collective-permute-start.17) | collective-permute-done | bytes 344096 | tf_op jit(solution)/shard_map/ppermute | solution.py:36
  143.9 2.2 %collective-permute-done.18.refs_7_ = bf16[672,256]{1,0:T(8,128)(2,1)S(1)} collective-permute-done((bf16[672,256]{1,0:T(8,128)(2,1)S(1)}, bf16[672,256]{1,0:T(8,128)(2,1)S(1)}, u32[]{:S(2)}, u32[]{:S(2)}) %collective-permute-start.18) | collective-permute-done | bytes 344096 | tf_op jit(solution)/shard_map/ppermute | solution.py:36
  146.1 1.9 copy-done.16
  148.0 3.6 %grad.1 = (bf16[672,384]{1,0:T(8,128)(2,1)S(1)}, bf16[672,384]{1,0:T(8,128)(2,1)S(1)}) custom-call(s32[9]{0:T(128)S(1)} %concatenate.13.place, bf16[672,256]{1,0:T(8,128)(2,1)S(1)} %get-tuple-element.57.refs_0_, bf16[672,256]{1,0:T(8,128)(2,1)S(1)} %collective-permute-done.11.refs_1_, bf16[672,256]{1,0:T(8,128)(2,1)S(1)} %collective-permute-done.12.refs_2_, ...), custom_call_target="tpu_custom_call" | custom-call | flops 2113929216 | bytes 8388608 | tf_op jit(solution)/shard_map/grad/pallas_call | solution.py:341
  151.6 2.2 %collective-permute-start.19 = (bf16[672,384]{1,0:T(8,128)(2,1)S(1)}, bf16[672,384]{1,0:T(8,128)(2,1)S(1)}, u32[]{:S(2)}, u32[]{:S(2)}) collective-permute-start(bf16[672,384]{1,0:T(8,128)(2,1)S(1)} %get-tuple-element.68.refs_0_), channel_id=1, source_target_pairs={{0,64},{64,0},{1,65},{65,1},{2,66},{66,2},{3,67},{67,3},{4,68},{68... | collective-permute-start | bytes 1548296 | tf_op jit(solution)/shard_map/ppermute | solution.py:36
  153.8 3.6 %collective-permute-start.20 = (bf16[672,384]{1,0:T(8,128)(2,1)S(1)}, bf16[672,384]{1,0:T(8,128)(2,1)S(1)}, u32[]{:S(2)}, u32[]{:S(2)}) collective-permute-start(bf16[672,384]{1,0:T(8,128)(2,1)S(1)} %get-tuple-element.68.refs_0_), channel_id=1, source_target_pairs={{0,128},{128,256},{256,384},{384,0},{1,129},{129,257},{257,385},{3... | collective-permute-start | bytes 1548296 | tf_op jit(solution)/shard_map/ppermute | solution.py:36
  157.4 2.3 %collective-permute-start.21 = (bf16[672,384]{1,0:T(8,128)(2,1)S(1)}, bf16[672,384]{1,0:T(8,128)(2,1)S(1)}, u32[]{:S(2)}, u32[]{:S(2)}) collective-permute-start(bf16[672,384]{1,0:T(8,128)(2,1)S(1)} %get-tuple-element.68.refs_0_), channel_id=1, source_target_pairs={{0,384},{128,0},{256,128},{384,256},{1,385},{129,1},{257,129},{385... | collective-permute-start | bytes 1548296 | tf_op jit(solution)/shard_map/ppermute | solution.py:36
  159.7 3.6 %collective-permute-start.24 = (bf16[672,384]{1,0:T(8,128)(2,1)S(1)}, bf16[672,384]{1,0:T(8,128)(2,1)S(1)}, u32[]{:S(2)}, u32[]{:S(2)}) collective-permute-start(bf16[672,384]{1,0:T(8,128)(2,1)S(1)} %get-tuple-element.69.refs_6_), channel_id=1, source_target_pairs={{0,64},{64,0},{1,65},{65,1},{2,66},{66,2},{3,67},{67,3},{4,68},{68... | collective-permute-start | bytes 1548296 | tf_op jit(solution)/shard_map/ppermute | solution.py:36
  163.3 2.7 %collective-permute-done.19.refs_1_ = bf16[672,384]{1,0:T(8,128)(2,1)S(1)} collective-permute-done((bf16[672,384]{1,0:T(8,128)(2,1)S(1)}, bf16[672,384]{1,0:T(8,128)(2,1)S(1)}, u32[]{:S(2)}, u32[]{:S(2)}) %collective-permute-start.19) | collective-permute-done | bytes 516128 | tf_op jit(solution)/shard_map/ppermute | solution.py:36
  166.0 2.9 %collective-permute-start.22 = (bf16[672,384]{1,0:T(8,128)(2,1)S(1)}, bf16[672,384]{1,0:T(8,128)(2,1)}, u32[]{:S(2)}, u32[]{:S(2)}) collective-permute-start(bf16[672,384]{1,0:T(8,128)(2,1)S(1)} %collective-permute-done.19.refs_1_), channel_id=1, source_target_pairs={{0,128},{128,256},{256,384},{384,0},{1,129},{129,257},{257,385},{3... | collective-permute-start | bytes 1548296 | tf_op jit(solution)/shard_map/ppermute | solution.py:36
  169.0 2.9 %collective-permute-start.23 = (bf16[672,384]{1,0:T(8,128)(2,1)S(1)}, bf16[672,384]{1,0:T(8,128)(2,1)}, u32[]{:S(2)}, u32[]{:S(2)}) collective-permute-start(bf16[672,384]{1,0:T(8,128)(2,1)S(1)} %collective-permute-done.19.refs_1_), channel_id=1, source_target_pairs={{0,384},{128,0},{256,128},{384,256},{1,385},{129,1},{257,129},{385... | collective-permute-start | bytes 1548296 | tf_op jit(solution)/shard_map/ppermute | solution.py:36
  171.9 7.9 %reduce-scatter.2.cloned.1.call-done = bf16[1,2,416,256]{3,2,1,0:T(8,128)(2,1)} async-done(((bf16[8,2,416,256]{3,2,1,0:T(8,128)(2,1)}), bf16[1,2,416,256]{3,2,1,0:T(8,128)(2,1)}) %reduce-scatter.2.cloned.1.call-update) | async-done | bytes 426000 | tf_op jit(solution)/shard_map/reduce_scatter | solution.py:339
  179.8 1.9 collective-permute-start.14
  182.7 3.4 %assemble.1 = (bf16[336,3072]{1,0:T(8,128)(2,1)}, bf16[336,3072]{1,0:T(8,128)(2,1)}) custom-call(s32[9]{0:T(128)S(1)} %concatenate.13.place, bf16[672,384]{1,0:T(8,128)(2,1)S(1)} %get-tuple-element.68.refs_0_, bf16[672,384]{1,0:T(8,128)(2,1)S(1)} %collective-permute-done.19.refs_1_, bf16[672,384]{1,0:T(8,128)(2,1)S(1)} %collective-permute-done.20.refs_2_, ...), custom_call_target="tpu_custom_call" | custom-call | bytes 8388608 | tf_op jit(solution)/shard_map/assemble/pallas_call | solution.py:358
  (63 shorter events, 7.9 us)
Async XLA Ops:
  7.2 21.4 %copy-start.8 = (bf16[1,256,192]{1,2,0:T(8,128)(2,1)S(1)}, bf16[1,256,192]{1,2,0:T(8,128)(2,1)}, u32[]{:S(2)}) copy-start(bf16[1,256,192]{1,2,0:T(8,128)(2,1)} %param.10) | copy-start | bytes 294916
  7.2 39.1 %copy-start.17 = (f32[1,2,256,4]{2,3,1,0:T(4,128)S(1)}, f32[1,2,256,4]{2,3,1,0:T(4,128)}, u32[]{:S(2)}) copy-start(f32[1,2,256,4]{2,3,1,0:T(4,128)} %param.17) | copy-start | bytes 24580
  7.2 39.1 %copy-start.18 = (s32[1,2,256,4]{2,3,1,0:T(4,128)S(1)}, s32[1,2,256,4]{2,3,1,0:T(4,128)}, u32[]{:S(2)}) copy-start(s32[1,2,256,4]{2,3,1,0:T(4,128)} %param.16) | copy-start | bytes 24580
  7.2 82.5 %all-gather.5.cloned.1.call-start = ((), (), s32[]{:S(2)}) async-start(), calls=%async_computation.2 | async-start | bytes 5013504 | tf_op jit(solution)/shard_map/all_gather | solution.py:276
  7.2 15.4 %collective-permute-start.10 = (bf16[192,256]{1,0:T(8,128)(2,1)}, bf16[192,256]{1,0:T(8,128)(2,1)S(1)}, u32[]{:S(2)}, u32[]{:S(2)}) collective-permute-start(bf16[192,256]{1,0:T(8,128)(2,1)} %bitcast.61), channel_id=1, source_target_pairs={{0,48},{16,0},{32,16},{48,32},{1,49},{17,1},{33,17},{49,33},{2,50}... | collective-permute-start | bytes 294920 | tf_op jit(solution)/shard_map/ppermute | solution.py:36
  18.2 10.4 %collective-permute-start.9 = (bf16[192,256]{1,0:T(8,128)(2,1)}, bf16[192,256]{1,0:T(8,128)(2,1)S(1)}, u32[]{:S(2)}, u32[]{:S(2)}) collective-permute-start(bf16[192,256]{1,0:T(8,128)(2,1)} %bitcast.62), channel_id=1, source_target_pairs={{0,16},{16,32},{32,48},{48,0},{1,17},{17,33},{33,49},{49,1},{2,18}... | collective-permute-start | bytes 294920 | tf_op jit(solution)/shard_map/ppermute | solution.py:36
  20.1 69.0 %copy-start.15 = (f32[1,3072]{1,0:T(1,128)S(1)}, f32[1,3072]{1,0:T(1,128)}, u32[]{:S(2)}) copy-start(f32[1,3072]{1,0:T(1,128)} %refs_9_.1) | copy-start | bytes 36868
  22.7 10.3 %copy-start.10 = (bf16[192,256]{1,0:T(8,128)(2,1)}, bf16[192,256]{1,0:T(8,128)(2,1)S(1)}, u32[]{:S(2)}) copy-start(bf16[192,256]{1,0:T(8,128)(2,1)S(1)} %collective-permute-done.10.dy) | copy-start | bytes 294916
  28.6 4.4 %copy-start.12 = (bf16[192,256]{1,0:T(8,128)(2,1)}, bf16[192,256]{1,0:T(8,128)(2,1)S(1)}, u32[]{:S(2)}) copy-start(bf16[192,256]{1,0:T(8,128)(2,1)S(1)} %collective-permute-done.9.act) | copy-start | bytes 294916
  29.4 105.1 %all-gather.7.cloned.1.call-start = ((), (), s32[]{:S(2)}) async-start(), calls=%async_computation.3 | async-start | bytes 3342336 | tf_op jit(solution)/shard_map/all_gather | solution.py:279
  29.4 25.6 %collective-permute-start = (bf16[1008,384]{1,0:T(8,128)(2,1)S(1)}, bf16[1008,384]{1,0:T(8,128)(2,1)S(1)}, u32[]{:S(2)}, u32[]{:S(2)}) collective-permute-start(bf16[1008,384]{1,0:T(8,128)(2,1)S(1)} %pad_maximum_fusion.refs_0_), channel_id=1, source_target_pairs={{0,64},{64,0},{1,65},{65,1},{2,66},{66,2},{3,67},{67,3},{4,68},{68... | collective-permute-start | bytes 2322440 | tf_op jit(solution)/shard_map/ppermute | solution.py:36
  33.0 22.0 %collective-permute-start.1 = (bf16[1008,384]{1,0:T(8,128)(2,1)S(1)}, bf16[1008,384]{1,0:T(8,128)(2,1)}, u32[]{:S(2)}, u32[]{:S(2)}) collective-permute-start(bf16[1008,384]{1,0:T(8,128)(2,1)S(1)} %pad_maximum_fusion.refs_0_), channel_id=1, source_target_pairs={{0,128},{128,256},{256,384},{384,0},{1,129},{129,257},{257,385},{3... | collective-permute-start | bytes 2322440 | tf_op jit(solution)/shard_map/ppermute | solution.py:36
  35.4 22.6 %collective-permute-start.2 = (bf16[1008,384]{1,0:T(8,128)(2,1)S(1)}, bf16[1008,384]{1,0:T(8,128)(2,1)S(1)}, u32[]{:S(2)}, u32[]{:S(2)}) collective-permute-start(bf16[1008,384]{1,0:T(8,128)(2,1)S(1)} %pad_maximum_fusion.refs_0_), channel_id=1, source_target_pairs={{0,384},{128,0},{256,128},{384,256},{1,385},{129,1},{257,129},{385... | collective-permute-start | bytes 2322440 | tf_op jit(solution)/shard_map/ppermute | solution.py:36
  38.8 16.2 %collective-permute-start.3 = (bf16[192,256]{1,0:T(8,128)(2,1)S(1)}, bf16[192,256]{1,0:T(8,128)(2,1)S(1)}, u32[]{:S(2)}, u32[]{:S(2)}) collective-permute-start(bf16[192,256]{1,0:T(8,128)(2,1)S(1)} %bitcast.49), channel_id=1, source_target_pairs={{0,0},{2,64},{4,128},{6,192},{8,256},{10,320},{12,384},{14,448},{6... | collective-permute-start | bytes 294920 | tf_op jit(solution)/shard_map/ppermute | solution.py:45
  58.0 0.9 copy-start.1
  58.8 19.1 %collective-permute-start.4 = (bf16[1008,384]{1,0:T(8,128)(2,1)S(1)}, bf16[1008,384]{1,0:T(8,128)(2,1)S(1)}, u32[]{:S(2)}, u32[]{:S(2)}) collective-permute-start(bf16[1008,384]{1,0:T(8,128)(2,1)S(1)} %collective-permute-done.refs_1_), channel_id=1, source_target_pairs={{0,128},{128,256},{256,384},{384,0},{1,129},{129,257},{257,385},{3... | collective-permute-start | bytes 2322440 | tf_op jit(solution)/shard_map/ppermute | solution.py:36
  60.8 21.8 %collective-permute-start.5 = (bf16[1008,384]{1,0:T(8,128)(2,1)S(1)}, bf16[1008,384]{1,0:T(8,128)(2,1)}, u32[]{:S(2)}, u32[]{:S(2)}) collective-permute-start(bf16[1008,384]{1,0:T(8,128)(2,1)S(1)} %collective-permute-done.refs_1_), channel_id=1, source_target_pairs={{0,384},{128,0},{256,128},{384,256},{1,385},{129,1},{257,129},{385... | collective-permute-start | bytes 2322440 | tf_op jit(solution)/shard_map/ppermute | solution.py:36
  64.7 13.3 %collective-permute-start.6 = (bf16[192,256]{1,0:T(8,128)(2,1)S(1)}, bf16[192,256]{1,0:T(8,128)(2,1)S(1)}, u32[]{:S(2)}, u32[]{:S(2)}) collective-permute-start(bf16[192,256]{1,0:T(8,128)(2,1)S(1)} %bitcast.50), channel_id=1, source_target_pairs={{0,256},{2,320},{4,384},{6,448},{8,0},{10,64},{12,128},{14,192},{6... | collective-permute-start | bytes 294920 | tf_op jit(solution)/shard_map/ppermute | solution.py:45
  78.0 0.9 copy-start.4
  83.2 96.6 %reduce-scatter.2.cloned.1.call-start = ((), (), s32[]{:S(2)}) async-start(), calls=%async_computation.1 | async-start | bytes 3833856 | tf_op jit(solution)/shard_map/reduce_scatter | solution.py:339
  83.3 17.7 %collective-permute-start.7 = (bf16[1008,384]{1,0:T(8,128)(2,1)}, bf16[1008,384]{1,0:T(8,128)(2,1)}, u32[]{:S(2)}, u32[]{:S(2)}) collective-permute-start(bf16[1008,384]{1,0:T(8,128)(2,1)} %collective-permute-done.1.refs_2_), channel_id=1, source_target_pairs={{0,128},{128,256},{256,384},{384,0},{1,129},{129,257},{257,385},{3... | collective-permute-start | bytes 2322440 | tf_op jit(solution)/shard_map/ppermute | solution.py:36
  85.2 18.9 %collective-permute-start.8 = (bf16[1008,384]{1,0:T(8,128)(2,1)}, bf16[1008,384]{1,0:T(8,128)(2,1)}, u32[]{:S(2)}, u32[]{:S(2)}) collective-permute-start(bf16[1008,384]{1,0:T(8,128)(2,1)} %collective-permute-done.5.refs_5_), channel_id=1, source_target_pairs={{0,384},{128,0},{256,128},{384,256},{1,385},{129,1},{257,129},{385... | collective-permute-start | bytes 2322440 | tf_op jit(solution)/shard_map/ppermute | solution.py:36
  89.7 2.3 %copy-start = (bf16[9216,256]{1,0:T(8,128)(2,1)S(1)}, bf16[9216,256]{1,0:T(8,128)(2,1)}, u32[]{:S(2)}) copy-start(bf16[9216,256]{1,0:T(8,128)(2,1)} %all-gather.5.cloned.1.call-done) | copy-start | bytes 14155780
  92.0 1.1 copy-start.2
  93.2 1.1 copy-start.5
  104.2 12.7 %copy-start.3 = (bf16[1008,384]{1,0:T(8,128)(2,1)S(1)}, bf16[1008,384]{1,0:T(8,128)(2,1)}, u32[]{:S(2)}) copy-start(bf16[1008,384]{1,0:T(8,128)(2,1)} %copy-done.1) | copy-start | bytes 2322436
  104.2 12.7 %copy-start.6 = (bf16[1008,384]{1,0:T(8,128)(2,1)S(1)}, bf16[1008,384]{1,0:T(8,128)(2,1)}, u32[]{:S(2)}) copy-start(bf16[1008,384]{1,0:T(8,128)(2,1)} %copy-done.4) | copy-start | bytes 2322436
  106.6 16.5 %collective-permute-start.11 = (bf16[672,256]{1,0:T(8,128)(2,1)S(1)}, bf16[672,256]{1,0:T(8,128)(2,1)S(1)}, u32[]{:S(2)}, u32[]{:S(2)}) collective-permute-start(bf16[672,256]{1,0:T(8,128)(2,1)S(1)} %get-tuple-element.57.refs_0_), channel_id=1, source_target_pairs={{0,64},{64,0},{1,65},{65,1},{2,66},{66,2},{3,67},{67,3},{4,68},{68... | collective-permute-start | bytes 1032200 | tf_op jit(solution)/shard_map/ppermute | solution.py:36
  111.0 12.1 %collective-permute-start.12 = (bf16[672,256]{1,0:T(8,128)(2,1)S(1)}, bf16[672,256]{1,0:T(8,128)(2,1)S(1)}, u32[]{:S(2)}, u32[]{:S(2)}) collective-permute-start(bf16[672,256]{1,0:T(8,128)(2,1)S(1)} %get-tuple-element.57.refs_0_), channel_id=1, source_target_pairs={{0,128},{128,256},{256,384},{384,0},{1,129},{129,257},{257,385},{3... | collective-permute-start | bytes 1032200 | tf_op jit(solution)/shard_map/ppermute | solution.py:36
  114.7 10.7 %collective-permute-start.13 = (bf16[672,256]{1,0:T(8,128)(2,1)S(1)}, bf16[672,256]{1,0:T(8,128)(2,1)S(1)}, u32[]{:S(2)}, u32[]{:S(2)}) collective-permute-start(bf16[672,256]{1,0:T(8,128)(2,1)S(1)} %get-tuple-element.57.refs_0_), channel_id=1, source_target_pairs={{0,384},{128,0},{256,128},{384,256},{1,385},{129,1},{257,129},{385... | collective-permute-start | bytes 1032200 | tf_op jit(solution)/shard_map/ppermute | solution.py:36
  125.4 10.4 %collective-permute-start.16 = (bf16[672,256]{1,0:T(8,128)(2,1)S(1)}, bf16[672,256]{1,0:T(8,128)(2,1)S(1)}, u32[]{:S(2)}, u32[]{:S(2)}) collective-permute-start(bf16[672,256]{1,0:T(8,128)(2,1)S(1)} %collective-permute-done.11.refs_1_), channel_id=1, source_target_pairs={{0,384},{128,0},{256,128},{384,256},{1,385},{129,1},{257,129},{385... | collective-permute-start | bytes 1032200 | tf_op jit(solution)/shard_map/ppermute | solution.py:36
  127.4 12.9 %collective-permute-start.15 = (bf16[672,256]{1,0:T(8,128)(2,1)S(1)}, bf16[672,256]{1,0:T(8,128)(2,1)S(1)}, u32[]{:S(2)}, u32[]{:S(2)}) collective-permute-start(bf16[672,256]{1,0:T(8,128)(2,1)S(1)} %collective-permute-done.11.refs_1_), channel_id=1, source_target_pairs={{0,128},{128,256},{256,384},{384,0},{1,129},{129,257},{257,385},{3... | collective-permute-start | bytes 1032200 | tf_op jit(solution)/shard_map/ppermute | solution.py:36
  132.5 11.4 %collective-permute-start.17 = (bf16[672,256]{1,0:T(8,128)(2,1)S(1)}, bf16[672,256]{1,0:T(8,128)(2,1)S(1)}, u32[]{:S(2)}, u32[]{:S(2)}) collective-permute-start(bf16[672,256]{1,0:T(8,128)(2,1)S(1)} %collective-permute-done.12.refs_2_), channel_id=1, source_target_pairs={{0,128},{128,256},{256,384},{384,0},{1,129},{129,257},{257,385},{3... | collective-permute-start | bytes 1032200 | tf_op jit(solution)/shard_map/ppermute | solution.py:36
  135.8 10.3 %collective-permute-start.18 = (bf16[672,256]{1,0:T(8,128)(2,1)S(1)}, bf16[672,256]{1,0:T(8,128)(2,1)S(1)}, u32[]{:S(2)}, u32[]{:S(2)}) collective-permute-start(bf16[672,256]{1,0:T(8,128)(2,1)S(1)} %collective-permute-done.16.refs_5_), channel_id=1, source_target_pairs={{0,384},{128,0},{256,128},{384,256},{1,385},{129,1},{257,129},{385... | collective-permute-start | bytes 1032200 | tf_op jit(solution)/shard_map/ppermute | solution.py:36
  146.1 1.9 copy-start.16
  151.6 14.4 %collective-permute-start.19 = (bf16[672,384]{1,0:T(8,128)(2,1)S(1)}, bf16[672,384]{1,0:T(8,128)(2,1)S(1)}, u32[]{:S(2)}, u32[]{:S(2)}) collective-permute-start(bf16[672,384]{1,0:T(8,128)(2,1)S(1)} %get-tuple-element.68.refs_0_), channel_id=1, source_target_pairs={{0,64},{64,0},{1,65},{65,1},{2,66},{66,2},{3,67},{67,3},{4,68},{68... | collective-permute-start | bytes 1548296 | tf_op jit(solution)/shard_map/ppermute | solution.py:36
  153.8 18.1 %collective-permute-start.20 = (bf16[672,384]{1,0:T(8,128)(2,1)S(1)}, bf16[672,384]{1,0:T(8,128)(2,1)S(1)}, u32[]{:S(2)}, u32[]{:S(2)}) collective-permute-start(bf16[672,384]{1,0:T(8,128)(2,1)S(1)} %get-tuple-element.68.refs_0_), channel_id=1, source_target_pairs={{0,128},{128,256},{256,384},{384,0},{1,129},{129,257},{257,385},{3... | collective-permute-start | bytes 1548296 | tf_op jit(solution)/shard_map/ppermute | solution.py:36
  157.4 25.3 %collective-permute-start.21 = (bf16[672,384]{1,0:T(8,128)(2,1)S(1)}, bf16[672,384]{1,0:T(8,128)(2,1)S(1)}, u32[]{:S(2)}, u32[]{:S(2)}) collective-permute-start(bf16[672,384]{1,0:T(8,128)(2,1)S(1)} %get-tuple-element.68.refs_0_), channel_id=1, source_target_pairs={{0,384},{128,0},{256,128},{384,256},{1,385},{129,1},{257,129},{385... | collective-permute-start | bytes 1548296 | tf_op jit(solution)/shard_map/ppermute | solution.py:36
  159.7 23.0 %collective-permute-start.24 = (bf16[672,384]{1,0:T(8,128)(2,1)S(1)}, bf16[672,384]{1,0:T(8,128)(2,1)S(1)}, u32[]{:S(2)}, u32[]{:S(2)}) collective-permute-start(bf16[672,384]{1,0:T(8,128)(2,1)S(1)} %get-tuple-element.69.refs_6_), channel_id=1, source_target_pairs={{0,64},{64,0},{1,65},{65,1},{2,66},{66,2},{3,67},{67,3},{4,68},{68... | collective-permute-start | bytes 1548296 | tf_op jit(solution)/shard_map/ppermute | solution.py:36
  166.0 16.6 %collective-permute-start.22 = (bf16[672,384]{1,0:T(8,128)(2,1)S(1)}, bf16[672,384]{1,0:T(8,128)(2,1)}, u32[]{:S(2)}, u32[]{:S(2)}) collective-permute-start(bf16[672,384]{1,0:T(8,128)(2,1)S(1)} %collective-permute-done.19.refs_1_), channel_id=1, source_target_pairs={{0,128},{128,256},{256,384},{384,0},{1,129},{129,257},{257,385},{3... | collective-permute-start | bytes 1548296 | tf_op jit(solution)/shard_map/ppermute | solution.py:36
  169.0 13.7 %collective-permute-start.23 = (bf16[672,384]{1,0:T(8,128)(2,1)S(1)}, bf16[672,384]{1,0:T(8,128)(2,1)}, u32[]{:S(2)}, u32[]{:S(2)}) collective-permute-start(bf16[672,384]{1,0:T(8,128)(2,1)S(1)} %collective-permute-done.19.refs_1_), channel_id=1, source_target_pairs={{0,384},{128,0},{256,128},{384,256},{1,385},{129,1},{257,129},{385... | collective-permute-start | bytes 1548296 | tf_op jit(solution)/shard_map/ppermute | solution.py:36
  179.8 6.2 %collective-permute-start.14 = (bf16[2,416,256]{2,1,0:T(8,128)(2,1)}, bf16[2,416,256]{2,1,0:T(8,128)(2,1)S(1)}, u32[]{:S(2)}, u32[]{:S(2)}) collective-permute-start(bf16[2,416,256]{2,1,0:T(8,128)(2,1)} %bitcast.46), channel_id=1, source_target_pairs={{0,1},{1,0},{2,3},{3,2},{4,5},{5,4},{6,7},{7,6},{8,9},{9,8},{10,11... | collective-permute-start | bytes 1277960 | tf_op jit(solution)/shard_map/ppermute | solution.py:36
  182.6 3.5 %copy-start.7 = (bf16[1,2,416,256]{3,2,1,0:T(8,128)(2,1)S(1)}, bf16[1,2,416,256]{3,2,1,0:T(8,128)(2,1)}, u32[]{:S(2)}) copy-start(bf16[1,2,416,256]{3,2,1,0:T(8,128)(2,1)} %reduce-scatter.2.cloned.1.call-done) | copy-start | bytes 1277956
  182.6 3.5 %copy-start.9 = (bf16[1,256,192]{1,2,0:T(8,128)(2,1)S(1)}, bf16[1,256,192]{1,2,0:T(8,128)(2,1)}, u32[]{:S(2)}) copy-start(bf16[1,256,192]{1,2,0:T(8,128)(2,1)} %param.10) | copy-start | bytes 294916
  182.6 3.5 %copy-start.11 = (bf16[192,256]{1,0:T(8,128)(2,1)S(1)}, bf16[192,256]{1,0:T(8,128)(2,1)}, u32[]{:S(2)}) copy-start(bf16[192,256]{1,0:T(8,128)(2,1)} %copy-done.10) | copy-start | bytes 294916
  182.6 3.5 %copy-start.13 = (bf16[192,256]{1,0:T(8,128)(2,1)S(1)}, bf16[192,256]{1,0:T(8,128)(2,1)}, u32[]{:S(2)}) copy-start(bf16[192,256]{1,0:T(8,128)(2,1)} %copy-done.12) | copy-start | bytes 294916
  182.6 3.5 %copy-start.14 = (f32[192,1]{1,0:T(8,128)S(1)}, f32[192,1]{1,0:T(8,128)}, u32[]{:S(2)}) copy-start(f32[192,1]{1,0:T(8,128)} %copy.14.gain) | copy-start | bytes 2308
Sparse Core Ops, SparseCore 0:
  29.5 50.0 all-gather.4
  83.4 44.4 all-gather.6
  130.7 49.0 reduce-scatter.1
